TPU v7x, 32 devices: a whole 2x2x4 slice. The times are simulated.
32 devices in a mesh: ctx: 8 (over z, x), head: 4 (over y, core).
Axes of the slice: x: 2, y: 2, z: 4, core: 2. Of those that a mesh axis runs over, the one named last changes fastest.
Arguments:
- ssm_input: bfloat16 [2048, 8192], P('ctx', 'head'), may hold values from -32 to 32
- gate_input: bfloat16 [2048, 8192], P('ctx', 'head'), may hold values from -6 to 6
- write_map: bfloat16 [2048, 128], P('ctx'), may hold values from -0.5 to 0.5
- read_map: bfloat16 [2048, 128], P('ctx'), may hold values from -0.5 to 0.5
- log_decay: float32 [2048, 64], P('ctx', 'head'), may hold values from -2.2 to 0
- doc_start: int32 [2048], P('ctx'), may hold values from 0 to 1920, as said below
- ssm_grad: bfloat16 [2048, 8192], P('ctx', 'head'), may hold values from -6 to 6
- att_queries: bfloat16 [2048, 4096], P('ctx', 'head'), may hold values from -32 to 32
- att_keys: bfloat16 [2048, 4096], P('ctx', 'head'), may hold values from -20 to 20
- att_values: bfloat16 [2048, 4096], P('ctx', 'head'), may hold values from -6 to 6
- att_grad: bfloat16 [2048, 4096], P('ctx', 'head'), may hold values from -6 to 6
Outputs:
- mixer_out: bfloat16 [2048, 8192], P('ctx', 'head')
- window_out: bfloat16 [2048, 4096], P('ctx', 'head')
- input_grad: bfloat16 [2048, 8192], P('ctx', 'head')
- gate_grad: bfloat16 [2048, 8192], P('ctx', 'head')
- write_grad: bfloat16 [2048, 128], P('ctx')
- read_grad: bfloat16 [2048, 128], P('ctx')
- query_grad: bfloat16 [2048, 4096], P('ctx', 'head')
- key_grad: bfloat16 [2048, 4096], P('ctx', 'head')
- value_grad: bfloat16 [2048, 4096], P('ctx', 'head')
Inputs may be any that keep to these rules, and one draw needn't show every extreme that they name: doc_start[t] is the position of the first token of the document holding token t; the 8 documents are runs of consecutive positions, the first starts at 0 and the last at 1920; one document other than the first and the last is exactly 4608 tokens long.
All inputs are finite; a program needn't handle non-finite values.
Results may differ from a plain program's by a relative error of at most 0.007.
Values may be sent and summed in bfloat16 or wider, within the bound.
No kernel may reach another device: no remote copies, remote signals or barrier semaphores. Data moves between devices by JAX's collectives and lax.ppermute only.
A program may use at most 128 MiB of HBM per device.

v0:
```python
import jax
import jax.numpy as jnp
from jax import lax
from jax.experimental import pallas as pl
from jax.experimental.pallas import tpu as pltpu
from jax.sharding import PartitionSpec as P

HEAD_DIM = 128
ATT_DIM = 128
WINDOW = 4096
EPSILON = 1e-05
LOG2E = 1.4426950408889634
TAIL = 16
MASKED = -1e30
HIGH = lax.Precision.HIGHEST
F32 = jnp.float32
BF16 = jnp.bfloat16
VMEM_BYTES = 56 * 1024 * 1024


def call(kernel, out_shape, *operands, scratch=(), flops=0, name=None):
    moved = sum(a.size * a.dtype.itemsize for a in jax.tree.leaves((operands, out_shape)))
    return pl.pallas_call(
        kernel,
        out_shape=out_shape,
        in_specs=[pl.BlockSpec(memory_space=pltpu.VMEM)] * len(operands),
        out_specs=jax.tree.map(lambda _: pl.BlockSpec(memory_space=pltpu.VMEM), out_shape),
        scratch_shapes=scratch,
        compiler_params=pltpu.CompilerParams(vmem_limit_bytes=VMEM_BYTES),
        cost_estimate=pl.CostEstimate(flops=flops, bytes_accessed=moved, transcendentals=0),
        name=name,
    )(*operands)


def shape(dims, dtype):
    return jax.ShapeDtypeStruct(dims, dtype)


def dot(a, b):
    return jnp.dot(a, b, preferred_element_type=F32)


def dot_nt(a, b, precision=None):
    return lax.dot_general(
        a, b, (((1,), (1,)), ((), ())), preferred_element_type=F32, precision=precision
    )


def iota(dims, axis):
    return lax.broadcasted_iota(jnp.int32, dims, axis)


def flip(a):
    return a.astype(F32).T.astype(BF16)


def column(row):
    return jnp.broadcast_to(row, (128, row.shape[1])).T


def cols(h):
    return slice(h * HEAD_DIM, (h + 1) * HEAD_DIM)


def first_kernel(ld_ref, rel_ref, w_ref, x_ref, out_ref, lcol_ref, lrow_ref):
    heads, length = ld_ref.shape
    parts, rows = out_ref.shape[0], out_ref.shape[1] - TAIL
    rates = ld_ref[...] * LOG2E
    lower = jnp.where(iota((length, length), 0) >= iota((length, length), 1), 1.0, 0.0)
    upper = jnp.where(iota((length, length), 0) <= iota((length, length), 1), 1.0, 0.0)
    lcol_ref[...] = dot_nt(lower, rates, HIGH)
    lrow = jnp.dot(rates, upper, preferred_element_type=F32, precision=HIGH)
    lrow_ref[...] = lrow
    rel_last = rel_ref[:, length - 1 :]
    last_doc = iota((1, length), 1) >= rel_last
    keeps = rel_last < 0
    writes = w_ref[...].astype(F32).T
    tail_row = iota((TAIL, 128), 0)
    for h in range(heads):
        line = lrow[h : h + 1, :]
        total = line[:, length - 1 :]
        to_end = jnp.where(last_doc, jnp.exp2(total - line), 0.0)
        state = dot((writes * to_end).astype(BF16), x_ref[:, cols(h)]).astype(BF16)
        factor = jnp.where(keeps, jnp.exp2(total), 0.0)
        high = factor.astype(BF16).astype(F32)
        low = factor - high
        first = h * HEAD_DIM
        for part in range(first // rows, (first + HEAD_DIM - 1) // rows + 1):
            begin = max(first, part * rows)
            end = min(first + HEAD_DIM, (part + 1) * rows)
            out_ref[part, begin - part * rows : end - part * rows, :] = state[
                begin - first : end - first, :
            ]
            place = 2 * (begin - part * rows) // HEAD_DIM
            tail = jnp.where(tail_row == place, high, jnp.where(tail_row == place + 1, low, 0.0))
            if place:
                tail = tail + out_ref[part, rows:, :].astype(F32)
            out_ref[part, rows:, :] = tail.astype(BF16)


def carry_kernel(backward, tail_ref, in_ref, out_ref):
    parts, rows = out_ref.shape[0], out_ref.shape[1]
    step = min(rows, HEAD_DIM)
    for k in range(rows // step):
        here = slice(k * step, (k + 1) * step)
        state = jnp.zeros((step, 128), F32)
        for c in range(parts)[:: -1 if backward else 1]:
            out_ref[c, here, :] = state.astype(BF16)
            tail = tail_ref[c].astype(F32)
            factor = tail[2 * k : 2 * k + 1, :] + tail[2 * k + 1 : 2 * k + 2, :]
            state = factor * state + in_ref[c, here, :].astype(F32)


def mix_kernel(
    x_ref, gate_ref, grad_ref, w_ref, r_ref, rel_ref, lcol_ref, lrow_ref, s_ref, mixed_ref, sums_ref
):
    length, heads = lcol_ref.shape
    reads = r_ref[...]
    rel = column(rel_ref[...].astype(F32))
    wide = jnp.concatenate([rel] * (length // 128), axis=1)
    seen = (iota((length, length), 1).astype(F32) >= wide) & (
        iota((length, length), 1) <= iota((length, length), 0)
    )
    scores = jnp.where(seen, dot_nt(reads, w_ref[...]), 0.0)
    squares = jnp.zeros((length, 128), F32)
    inners = jnp.zeros((length, 128), F32)
    for h in range(heads):
        lc = lcol_ref[:, h : h + 1]
        decay = jnp.exp2(jnp.minimum(lc - lrow_ref[h : h + 1, :], 0.0))
        enter = jnp.where(rel < 0, jnp.exp2(jnp.broadcast_to(lc, rel.shape)), 0.0)
        mixed = dot((scores * decay).astype(BF16), x_ref[:, cols(h)]) + enter * dot(
            reads, s_ref[cols(h), :]
        )
        mixed_ref[:, cols(h)] = mixed
        gate = gate_ref[:, cols(h)].astype(F32)
        gated = mixed * (gate / (1.0 + jnp.exp(-gate)))
        squares = squares + gated * gated
        inners = inners + grad_ref[:, cols(h)].astype(F32) * gated
    ones = jnp.ones((8, 128), F32)
    square_row = dot_nt(ones, squares, HIGH)
    inner_row = dot_nt(ones, inners, HIGH)
    sums_ref[...] = jnp.where(iota((8, length), 0) == 0, square_row, inner_row)


def gate_kernel(
    width, sums_ref, mixed_ref, gate_ref, grad_ref, r_ref, rel_ref, lrow_ref,
    mixer_ref, ggrad_ref, dmixed_ref, out_ref,
):
    length = mixed_ref.shape[0]
    heads = lrow_ref.shape[0]
    rows = out_ref.shape[1]
    scale = lax.rsqrt(sums_ref[0:1, :] / width + EPSILON)
    rms = column(scale)
    pull = column(scale * scale * scale * sums_ref[1:2, :] / width)
    reads = r_ref[...].astype(F32).T
    enters = rel_ref[...] < 0
    for h in range(heads):
        mixed = mixed_ref[:, cols(h)]
        gate = gate_ref[:, cols(h)].astype(F32)
        sigma = 1.0 / (1.0 + jnp.exp(-gate))
        swish = gate * sigma
        gated = mixed * swish
        mixer_ref[:, cols(h)] = (gated * rms).astype(BF16)
        dgated = rms * grad_ref[:, cols(h)].astype(F32) - pull * gated
        dmixed = (dgated * swish).astype(BF16)
        dmixed_ref[:, cols(h)] = dmixed
        ggrad_ref[:, cols(h)] = (
            dgated * mixed * sigma * (1.0 + gate * (1.0 - sigma))
        ).astype(BF16)
        enter = jnp.where(enters, jnp.exp2(lrow_ref[h : h + 1, :]), 0.0)
        state = dot((reads * enter).astype(BF16), dmixed).astype(BF16)
        first = h * HEAD_DIM
        for part in range(first // rows, (first + HEAD_DIM - 1) // rows + 1):
            begin = max(first, part * rows)
            end = min(first + HEAD_DIM, (part + 1) * rows)
            out_ref[part, begin - part * rows : end - part * rows, :] = state[
                begin - first : end - first, :
            ]


def inner_kernel(
    dmixed_ref, x_ref, w_ref, r_ref, rel_ref, lcol_ref, lrow_ref, s_ref, gin_ref, read_ref, write_ref
):
    length, heads = lcol_ref.shape
    rel_row = rel_ref[...]
    rel = column(rel_row.astype(F32))
    seen = (iota((length, length), 0) >= rel_row) & (
        iota((length, length), 0) <= iota((length, length), 1)
    )
    scores = jnp.where(seen, dot_nt(w_ref[...], r_ref[...]), 0.0)
    total = jnp.zeros((length, length), F32)
    read = jnp.zeros((length, 128), F32)
    for h in range(heads):
        lc = lcol_ref[:, h : h + 1]
        decay = jnp.exp2(jnp.minimum(lrow_ref[h : h + 1, :] - lc, 0.0))
        dmixed = dmixed_ref[:, cols(h)]
        gin_ref[:, cols(h)] = dot((scores * decay).astype(BF16), dmixed)
        total = total + decay * dot_nt(x_ref[:, cols(h)], dmixed)
        enter = jnp.where(rel < 0, jnp.exp2(jnp.broadcast_to(lc, rel.shape)), 0.0)
        read = read + enter * dot_nt(dmixed, s_ref[cols(h), :])
    total = jnp.where(seen, total, 0.0)
    write_ref[...] = dot(total.astype(BF16), r_ref[...])
    read_ref[...] = read + dot(total.T.astype(BF16), w_ref[...])


def last_kernel(gin_ref, x_ref, w_ref, rel_ref, lcol_ref, back_ref, part_ref, out_ref, write_ref):
    length, heads = lcol_ref.shape
    rel_last = rel_ref[:, length - 1 :]
    last_doc = iota((length, 128), 0) >= rel_last
    writes = w_ref[...]
    write = part_ref[...]
    for h in range(heads):
        lc = lcol_ref[:, h : h + 1]
        line = jnp.broadcast_to(lc[length - 1 :, :] - lc, (length, 128))
        to_end = jnp.where(last_doc, jnp.exp2(line), 0.0)
        back = back_ref[cols(h), :]
        out_ref[:, cols(h)] = (gin_ref[:, cols(h)] + to_end * dot(writes, back)).astype(BF16)
        write = write + to_end * dot_nt(x_ref[:, cols(h)], back)
    write_ref[...] = write


def exchange(blocks):
    return lax.all_to_all(blocks, "ctx", 0, 0)


def pack_kernel(marks_ref, q_ref, k_ref, v_ref, g_ref, out_ref):
    parts, per = out_ref.shape[:2]
    length = q_ref.shape[0]
    for part in range(parts):
        for a in range(per):
            here = cols(part * per + a)
            for place, ref in enumerate((q_ref, k_ref, v_ref, g_ref)):
                out_ref[part, a, place * length : (place + 1) * length, :] = ref[:, here]
            out_ref[part, a, 4 * length :, :] = marks_ref[...]


def unpack_kernel(in_ref, *out_refs):
    parts, per = in_ref.shape[:2]
    length = in_ref.shape[2] // 4
    for part in range(parts):
        for a in range(per):
            here = cols(part * per + a)
            for place, ref in enumerate(out_refs):
                ref[:, here] = in_ref[part, a, place * length : (place + 1) * length, :]


def attend_kernel(length, in_ref, out_ref, expo_ref, kt_ref, vt_ref, dk_ref, dv_ref):
    parts = in_ref.shape[0]
    scale = ATT_DIM ** (-0.5)
    rate = scale * LOG2E
    key_in = iota((length, length), 0)
    causal = key_in <= iota((length, length), 1)
    for a in range(in_ref.shape[1]):

        def piece(block, place):
            return in_ref[block, a, place * length : (place + 1) * length, :]

        for i in range(parts):
            kt_ref[i] = flip(piece(i, 1))
            vt_ref[i] = flip(piece(i, 2))
            queries, grads = piece(i, 0), piece(i, 3)
            marks = in_ref[i, a, 4 * length :, :].astype(F32)
            starts = jnp.concatenate(
                [
                    marks[2 * n : 2 * n + 1] * 128.0 + marks[2 * n + 1 : 2 * n + 2]
                    for n in range(length // 128)
                ],
                axis=1,
            ).astype(jnp.int32)
            query_at = i * length + iota((1, length), 1)
            if parts * length > WINDOW:
                starts = jnp.maximum(starts, query_at - (WINDOW - 1))
            top = jnp.full((1, length), MASKED, F32)
            total = jnp.zeros((1, length), F32)
            tops = []
            for j in range(i + 1):
                seen = key_in >= starts - j * length
                if j == i:
                    seen = seen & causal
                raw = jnp.where(seen, dot_nt(piece(j, 1), queries), MASKED)
                new = jnp.maximum(top, jnp.max(raw, axis=0, keepdims=True))
                expo = jnp.exp2((raw - new) * rate)
                expo_ref[j] = expo
                total = total * jnp.exp2((top - new) * rate) + jnp.sum(expo, axis=0, keepdims=True)
                top = new
                tops.append(new)
            out = jnp.zeros((ATT_DIM, length), F32)
            for j in range(i + 1):
                probs = expo_ref[j] * (jnp.exp2((tops[j] - top) * rate) / total)
                expo_ref[j] = probs
                weights = probs.astype(BF16)
                dvalue = dot(weights, grads)
                dv_ref[j] = dvalue if j == i else dv_ref[j] + dvalue
                out = out + dot(vt_ref[j], weights)
            delta = jnp.sum(out * grads.astype(F32).T, axis=0, keepdims=True)
            dquery = jnp.zeros((ATT_DIM, length), F32)
            for j in range(i + 1):
                dprobs = dot_nt(piece(j, 2), grads)
                dscore = (expo_ref[j] * ((dprobs - delta) * scale)).astype(BF16)
                dkey = dot(dscore, queries)
                dk_ref[j] = dkey if j == i else dk_ref[j] + dkey
                dquery = dquery + dot(kt_ref[j], dscore)
            out_ref[i, a, 0:length, :] = out.T.astype(BF16)
            out_ref[i, a, length : 2 * length, :] = dquery.T.astype(BF16)
        for j in range(parts):
            out_ref[j, a, 2 * length : 3 * length, :] = dk_ref[j].astype(BF16)
            out_ref[j, a, 3 * length :, :] = dv_ref[j].astype(BF16)


def shifted(shard, axis, by):
    devices = lax.axis_size(axis)
    pairs = [(i, i + by) for i in range(devices) if 0 <= i + by < devices]
    return lax.ppermute(shard, axis, pairs)


def head_cols(array, head_index):
    return lax.dynamic_slice_in_dim(array, head_index * ATT_DIM, ATT_DIM, 1)


def ring_attention(att_queries, att_keys, att_values, att_grad, doc_start):
    length = att_queries.shape[0]
    shard_index = lax.axis_index("ctx")
    halo_shards = WINDOW // length
    att_count = att_queries.shape[1] // ATT_DIM
    att_width = att_queries.shape[1]
    score_scale = ATT_DIM ** (-0.5)

    def pass_keys(running, unused):
        moved = shifted((running[0], running[1]), "ctx", 1)
        return (moved, moved)

    _, earlier = lax.scan(pass_keys, (att_keys, att_values), None, length=halo_shards)
    key_all = jnp.concatenate(
        [earlier[0][::-1].reshape(halo_shards * length, att_width), att_keys], axis=0
    )
    value_all = jnp.concatenate(
        [earlier[1][::-1].reshape(halo_shards * length, att_width), att_values], axis=0
    )
    spread_rows = (halo_shards + 1) * length
    query_pos = shard_index * length + jnp.arange(length, dtype=jnp.int32)
    key_pos = (shard_index - halo_shards) * length + jnp.arange(spread_rows, dtype=jnp.int32)
    visible = (
        (key_pos[None, :] <= query_pos[:, None])
        & (query_pos[:, None] - key_pos[None, :] < WINDOW)
        & (key_pos[None, :] >= doc_start[:, None])
    )

    def forward_head(head_index, running):
        out_buf, max_buf, total_buf, delta_buf = running
        query_head = head_cols(att_queries, head_index)
        key_head = head_cols(key_all, head_index)
        value_head = head_cols(value_all, head_index)
        score = (
            jnp.einsum("td,sd->ts", query_head, key_head, preferred_element_type=jnp.float32)
            * score_scale
        )
        row_max = jnp.max(jnp.where(visible, score, -jnp.inf), axis=1)
        expo = jnp.where(visible, jnp.exp(score - row_max[:, None]), 0.0)
        row_total = jnp.sum(expo, axis=1)
        weights = (expo / row_total[:, None]).astype(jnp.bfloat16)
        attended = jnp.dot(weights, value_head, preferred_element_type=jnp.float32)
        delta = jnp.sum(head_cols(att_grad, head_index).astype(jnp.float32) * attended, axis=1)
        out_buf = lax.dynamic_update_slice_in_dim(
            out_buf, attended.astype(jnp.bfloat16), head_index * ATT_DIM, 1
        )
        return (
            out_buf,
            max_buf.at[:, head_index].set(row_max),
            total_buf.at[:, head_index].set(row_total),
            delta_buf.at[:, head_index].set(delta),
        )

    stats_zero = jnp.zeros((length, att_count), jnp.float32)
    window_out, row_maxes, row_totals, row_deltas = lax.fori_loop(
        0,
        att_count,
        forward_head,
        (jnp.zeros((length, att_width), jnp.bfloat16), stats_zero, stats_zero, stats_zero),
    )

    def query_terms(head_index):
        query_head = head_cols(att_queries, head_index)
        key_head = head_cols(key_all, head_index)
        value_head = head_cols(value_all, head_index)
        grad_head = head_cols(att_grad, head_index)
        score = (
            jnp.einsum("td,sd->ts", query_head, key_head, preferred_element_type=jnp.float32)
            * score_scale
        )
        probs = (
            jnp.where(visible, jnp.exp(score - row_maxes[:, head_index][:, None]), 0.0)
            / row_totals[:, head_index][:, None]
        )
        weights = probs.astype(jnp.bfloat16)
        dprobs = jnp.einsum("td,sd->ts", grad_head, value_head, preferred_element_type=jnp.float32)
        dscore = (probs * (dprobs - row_deltas[:, head_index][:, None]) * score_scale).astype(
            jnp.bfloat16
        )
        query_part = jnp.dot(dscore, key_head, preferred_element_type=jnp.float32)
        return (query_head, grad_head, weights, dscore, query_part)

    def backward_head(head_index, running):
        query_buf, key_buf, value_buf = running
        query_head, grad_head, weights, dscore, query_part = query_terms(head_index)
        key_part = jnp.einsum("ts,td->sd", dscore, query_head, preferred_element_type=jnp.float32)
        value_part = jnp.einsum("ts,td->sd", weights, grad_head, preferred_element_type=jnp.float32)
        query_buf = lax.dynamic_update_slice_in_dim(query_buf, query_part, head_index * ATT_DIM, 1)
        key_buf = lax.dynamic_update_slice_in_dim(key_buf, key_part, head_index * ATT_DIM, 1)
        value_buf = lax.dynamic_update_slice_in_dim(value_buf, value_part, head_index * ATT_DIM, 1)
        return (query_buf, key_buf, value_buf)

    part_zero = jnp.zeros((spread_rows, att_width), jnp.float32)
    query_sum, key_parts, value_parts = lax.fori_loop(
        0,
        att_count,
        backward_head,
        (jnp.zeros((length, att_width), jnp.float32), part_zero, part_zero),
    )
    key_blocks = key_parts.reshape(halo_shards + 1, length, att_width)
    value_blocks = value_parts.reshape(halo_shards + 1, length, att_width)

    def send_back(running, block_index):
        moved = shifted((running[0], running[1]), "ctx", -1)
        return ((moved[0] + key_blocks[block_index], moved[1] + value_blocks[block_index]), None)

    (key_sum, value_sum), _ = lax.scan(
        send_back, (key_blocks[0], value_blocks[0]), jnp.arange(1, halo_shards + 1, dtype=jnp.int32)
    )
    return (
        window_out,
        query_sum.astype(jnp.bfloat16),
        key_sum.astype(jnp.bfloat16),
        value_sum.astype(jnp.bfloat16),
    )


def body(
    ssm_input,
    gate_input,
    write_map,
    read_map,
    log_decay,
    doc_start,
    ssm_grad,
    att_queries,
    att_keys,
    att_values,
    att_grad,
):
    length, width = ssm_input.shape
    heads = width // HEAD_DIM
    parts = lax.axis_size("ctx")
    rows = width // parts
    full_width = width * lax.axis_size("head")
    work = 2 * length * length * width
    att_width = att_queries.shape[1]
    per = att_width // ATT_DIM // parts
    dealt = att_width // ATT_DIM % parts == 0
    rel = (doc_start - lax.axis_index("ctx") * length).reshape(1, length)

    sent, lcol, lrow = call(
        first_kernel,
        (
            shape((parts, rows + TAIL, 128), BF16),
            shape((length, heads), F32),
            shape((heads, length), F32),
        ),
        log_decay.T, rel, write_map, ssm_input, flops=work // 2, name="ssm_first",
    )
    got = exchange(sent)
    tail = got[:, rows:, :]
    carried = call(
        lambda *refs: carry_kernel(False, *refs), shape((parts, rows, 128), BF16), tail, got,
        name="ssm_carry",
    )
    state = exchange(carried).reshape(width, 128)

    if dealt:
        marks = doc_start.reshape(length // 128, 128)
        marks = jnp.stack([marks // 128, marks % 128], axis=1).reshape(length // 64, 128)
        marks = jnp.pad(marks, ((0, TAIL - length // 64), (0, 0))).astype(BF16)
        packed = call(
            pack_kernel, shape((parts, per, 4 * length + TAIL, 128), BF16),
            marks, att_queries, att_keys, att_values, att_grad, name="att_pack",
        )
        packed, state = lax.optimization_barrier((packed, state))
        att_got = exchange(packed)
    else:
        att_out = ring_attention(att_queries, att_keys, att_values, att_grad, doc_start)

    mixed, sums = call(
        mix_kernel,
        (shape((length, width), F32), shape((8, length), F32)),
        ssm_input, gate_input, ssm_grad, write_map, read_map, rel, lcol, lrow, state,
        flops=work * 3 // 2, name="ssm_mix",
    )
    sums = lax.psum(sums, "head")
    mixer_out, gate_grad, dmixed, sent = call(
        lambda *refs: gate_kernel(full_width, *refs),
        (
            shape((length, width), BF16),
            shape((length, width), BF16),
            shape((length, width), BF16),
            shape((parts, rows, 128), BF16),
        ),
        sums, mixed, gate_input, ssm_grad, read_map, rel, lrow, flops=work // 2, name="ssm_gate",
    )

    if dealt:
        sent, att_got = lax.optimization_barrier((sent, att_got))
    got = exchange(sent)
    carried = call(
        lambda *refs: carry_kernel(True, *refs), shape((parts, rows, 128), BF16), tail, got,
        name="ssm_carry_back",
    )
    back = exchange(carried).reshape(width, 128)
    if dealt:
        att_done = call(
            lambda *refs: attend_kernel(length, *refs),
            shape((parts, per, 4 * length, 128), BF16),
            att_got,
            scratch=[
                pltpu.VMEM((parts, length, length), F32),
                pltpu.VMEM((parts, ATT_DIM, length), BF16),
                pltpu.VMEM((parts, ATT_DIM, length), BF16),
                pltpu.VMEM((parts, length, ATT_DIM), F32),
                pltpu.VMEM((parts, length, ATT_DIM), F32),
            ],
            flops=6 * per * (parts * length) ** 2 * ATT_DIM, name="att_attend",
        )
        att_done, back = lax.optimization_barrier((att_done, back))
        att_out = call(
            unpack_kernel, (shape((length, att_width), BF16),) * 4, exchange(att_done),
            name="att_unpack",
        )

    gin, read_part, write_part = call(
        inner_kernel,
        (shape((length, width), F32), shape((length, 128), F32), shape((length, 128), F32)),
        dmixed, ssm_input, write_map, read_map, rel, lcol, lrow, state,
        flops=work * 5 // 2, name="ssm_inner",
    )
    input_grad, write_part = call(
        last_kernel,
        (shape((length, width), BF16), shape((length, 128), F32)),
        gin, ssm_input, write_map, rel, lcol, back, write_part, flops=work, name="ssm_last",
    )
    write_sum, read_sum = lax.psum((write_part, read_part), "head")
    window_out, query_grad, key_grad, value_grad = att_out
    return (
        mixer_out,
        window_out,
        input_grad,
        gate_grad,
        write_sum.astype(BF16),
        read_sum.astype(BF16),
        query_grad,
        key_grad,
        value_grad,
    )


def solution(mesh):
    in_specs = (
        P("ctx", "head"),
        P("ctx", "head"),
        P("ctx", None),
        P("ctx", None),
        P("ctx", "head"),
        P("ctx"),
        P("ctx", "head"),
        P("ctx", "head"),
        P("ctx", "head"),
        P("ctx", "head"),
        P("ctx", "head"),
    )
    out_specs = (
        P("ctx", "head"),
        P("ctx", "head"),
        P("ctx", "head"),
        P("ctx", "head"),
        P("ctx", None),
        P("ctx", None),
        P("ctx", "head"),
        P("ctx", "head"),
        P("ctx", "head"),
    )
    return jax.shard_map(body, mesh=mesh, in_specs=in_specs, out_specs=out_specs, check_vma=False)
```

profile of v0, /device:TPU:1, one launch (start us, length us, event | category | flops | bytes accessed | tf_op | source)
XLA Modules:
  0.0 195.9 jit_solution(1326115423442829872)
XLA Ops:
  0.6 1.2 broadcast_subtract_fusion
  1.9 3.0 %ssm_first.1 = (bf16[8,272,128]{2,1,0:T(8,128)(2,1)}, f32[256,16]{1,0:T(8,128)}, f32[16,256]{1,0:T(8,128)}) custom-call(f32[16,256]{1,0:T(8,128)} %bitcast.14, s32[1,256]{1,0:T(1,128)} %bitcast.9, bf16[256,128]{1,0:T(8,128)(2,1)} %w_ref.7, bf16[256,2048]{1,0:T(8,128)(2,1)} %x_ref.7), custom_call_target="tpu_custom_call" | custom-call | flops 134217728 | bytes 1721344 | tf_op jit(solution)/shard_map/ssm_first/pallas_call | solution.py:23
  4.9 21.7 %all_to_all.30.refs_1_ = bf16[8,272,128]{2,1,0:T(8,128)(2,1)S(1)} all-to-all(bf16[8,272,128]{2,1,0:T(8,128)(2,1)} %get-tuple-element.35), channel_id=1, replica_groups=mesh['ctx'=8,'head'=4] {'ctx'}, dimensions={0} | all-to-all | bytes 1114112 | tf_op jit(solution)/shard_map/all_to_all | solution.py:223
  27.4 2.0 %ssm_carry.1 = bf16[8,256,128]{2,1,0:T(8,128)(2,1)} custom-call(bf16[8,16,128]{2,1,0:T(8,128)(2,1)} %slice.4.refs_0_, bf16[8,272,128]{2,1,0:T(8,128)(2,1)} %copy-done.2), custom_call_target="tpu_custom_call" | custom-call | bytes 1114112 | tf_op jit(solution)/shard_map/ssm_carry/pallas_call | solution.py:23
  29.3 3.5 %all-to-all-start.1 = ((bf16[8,256,128]{2,1,0:T(8,128)(2,1)}), bf16[8,256,128]{2,1,0:T(8,128)(2,1)S(1)}, u32[]{:S(2)}, u32[]{:S(2)}) async-start(bf16[8,256,128]{2,1,0:T(8,128)(2,1)} %ssm_carry.1), calls=%async_computation.1 | async-start | bytes 1048576 | tf_op jit(solution)/shard_map/all_to_all | solution.py:223
  33.5 3.3 %att_pack.1 = bf16[8,1,1040,128]{3,2,1,0:T(8,128)(2,1)} custom-call(bf16[16,128]{1,0:T(8,128)(2,1)} %pad.5.marks_ref, bf16[256,1024]{1,0:T(8,128)(2,1)} %q_ref.1, bf16[256,1024]{1,0:T(8,128)(2,1)} %k_ref.1, bf16[256,1024]{1,0:T(8,128)(2,1)} %v_ref.1, bf16[256,1024]{1,0:T(8,128)(2,1)} %g_ref.1), custom_call_target="tpu_custom_call" | custom-call | bytes 4231168 | tf_op jit(solution)/shard_map/att_pack/pallas_call | solution.py:23
  36.8 9.3 %all-to-all-done.1 = bf16[8,256,128]{2,1,0:T(8,128)(2,1)S(1)} async-done(((bf16[8,256,128]{2,1,0:T(8,128)(2,1)}), bf16[8,256,128]{2,1,0:T(8,128)(2,1)S(1)}, u32[]{:S(2)}, u32[]{:S(2)}) %all-to-all-start.1) | async-done | bytes 524320 | tf_op jit(solution)/shard_map/all_to_all | solution.py:223
  46.9 4.3 %all-to-all-start.2 = ((bf16[8,1,1040,128]{3,2,1,0:T(8,128)(2,1)}), bf16[8,1,1040,128]{3,2,1,0:T(8,128)(2,1)}, u32[]{:S(2)}, u32[]{:S(2)}) async-start(bf16[8,1,1040,128]{3,2,1,0:T(8,128)(2,1)} %att_pack.1), calls=%async_computation.2 | async-start | bytes 4259840 | tf_op jit(solution)/shard_map/all_to_all | solution.py:223
  51.2 5.8 %ssm_mix.1 = (f32[256,2048]{1,0:T(8,128)}, f32[8,256]{1,0:T(8,128)}) custom-call(bf16[256,2048]{1,0:T(8,128)(2,1)} %x_ref.7, bf16[256,2048]{1,0:T(8,128)(2,1)} %refs_2_.1, bf16[256,2048]{1,0:T(8,128)(2,1)} %refs_3_.1, bf16[256,128]{1,0:T(8,128)(2,1)} %w_ref.7, bf16[256,128]{1,0:T(8,128)(2,1)} %r_ref.3, s32[1,256]{1,0:T(1,128)} %bitcast.10, ...), custom_call_target="tpu_custom_call" | custom-call | flops 402653184 | bytes 5940224 | tf_op jit(solution)/shard_map/ssm_mix/pallas_call | solution.py:23
  57.0 7.9 %psum.21.refs_0_ = f32[8,256]{1,0:T(8,128)} all-reduce(f32[8,256]{1,0:T(8,128)} %get-tuple-element.37), channel_id=1, replica_groups=mesh['ctx'=8,'head'=4] {'head'}, use_global_device_ids=true, to_apply=%region_0.1 | all-reduce | flops 2048 | bytes 16384 | tf_op jit(solution)/shard_map/psum | solution.py:497
  64.9 5.9 %ssm_gate.1 = (bf16[256,2048]{1,0:T(8,128)(2,1)}, bf16[256,2048]{1,0:T(8,128)(2,1)}, bf16[256,2048]{1,0:T(8,128)(2,1)}, bf16[8,256,128]{2,1,0:T(8,128)(2,1)}) custom-call(f32[8,256]{1,0:T(8,128)} %psum.21.refs_0_, f32[256,2048]{1,0:T(8,128)} %get-tuple-element.38.refs_1_, bf16[256,2048]{1,0:T(8,128)(2,1)} %refs_2_.1, bf16[256,2048]{1,0:T(8,128)(2,1)} %refs_3_.1, ...), custom_call_target="tpu_custom_call" | custom-call | flops 134217728 | bytes 7955456 | tf_op jit(solution)/shard_map/ssm_gate/pallas_call | solution.py:23
  70.8 27.2 %all-to-all-done.2.refs_0_ = bf16[8,1,1040,128]{3,2,1,0:T(8,128)(2,1)} async-done(((bf16[8,1,1040,128]{3,2,1,0:T(8,128)(2,1)}), bf16[8,1,1040,128]{3,2,1,0:T(8,128)(2,1)}, u32[]{:S(2)}, u32[]{:S(2)}) %all-to-all-start.2) | async-done | bytes 2129952 | tf_op jit(solution)/shard_map/all_to_all | solution.py:223
  98.0 19.6 %all_to_all.31.refs_1_ = bf16[8,256,128]{2,1,0:T(8,128)(2,1)} all-to-all(bf16[8,256,128]{2,1,0:T(8,128)(2,1)} %get-tuple-element.43), channel_id=1, replica_groups=mesh['ctx'=8,'head'=4] {'ctx'}, dimensions={0} | all-to-all | bytes 1048576 | tf_op jit(solution)/shard_map/all_to_all | solution.py:223
  117.7 2.0 %ssm_carry_back.1 = bf16[8,256,128]{2,1,0:T(8,128)(2,1)} custom-call(bf16[8,16,128]{2,1,0:T(8,128)(2,1)} %slice.4.refs_0_, bf16[8,256,128]{2,1,0:T(8,128)(2,1)} %all_to_all.31.refs_1_), custom_call_target="tpu_custom_call" | custom-call | bytes 1081344 | tf_op jit(solution)/shard_map/ssm_carry_back/pallas_call | solution.py:23
  119.6 4.1 %all-to-all-start.4 = ((bf16[8,256,128]{2,1,0:T(8,128)(2,1)}), bf16[8,256,128]{2,1,0:T(8,128)(2,1)S(1)}, u32[]{:S(2)}, u32[]{:S(2)}) async-start(bf16[8,256,128]{2,1,0:T(8,128)(2,1)} %ssm_carry_back.1), calls=%async_computation.4 | async-start | bytes 1048576 | tf_op jit(solution)/shard_map/all_to_all | solution.py:223
  123.8 14.6 %att_attend.1 = bf16[8,1,1024,128]{3,2,1,0:T(8,128)(2,1)} custom-call(bf16[8,1,1040,128]{3,2,1,0:T(8,128)(2,1)} %all-to-all-done.2.refs_0_), custom_call_target="tpu_custom_call" | custom-call | flops 3221225472 | bytes 4227072 | tf_op jit(solution)/shard_map/att_attend/pallas_call | solution.py:23
  138.4 0.8 copy-done.3
  139.2 5.4 %all-to-all-start.5 = ((bf16[8,1,1024,128]{3,2,1,0:T(8,128)(2,1)}), bf16[8,1,1024,128]{3,2,1,0:T(8,128)(2,1)S(1)}, u32[]{:S(2)}, u32[]{:S(2)}) async-start(bf16[8,1,1024,128]{3,2,1,0:T(8,128)(2,1)} %att_attend.1), calls=%async_computation.5 | async-start | bytes 4194304 | tf_op jit(solution)/shard_map/all_to_all | solution.py:223
  144.6 4.9 %ssm_inner.1 = (f32[256,2048]{1,0:T(8,128)}, f32[256,128]{1,0:T(8,128)}, f32[256,128]{1,0:T(8,128)}) custom-call(bf16[256,2048]{1,0:T(8,128)(2,1)} %get-tuple-element.46.dmixed_ref, bf16[256,2048]{1,0:T(8,128)(2,1)} %x_ref.7, bf16[256,128]{1,0:T(8,128)(2,1)} %w_ref.7, bf16[256,128]{1,0:T(8,128)(2,1)} %r_ref.3, s32[1,256]{1,0:T(1,128)} %bitcast.12, ...), custom_call_target="tpu_custom_call" | custom-call | flops 671088640 | bytes 5145600 | tf_op jit(solution)/shard_map/ssm_inner/pallas_call | solution.py:23
  149.6 4.1 %ssm_last.1 = (bf16[256,2048]{1,0:T(8,128)(2,1)}, f32[256,128]{1,0:T(8,128)}) custom-call(f32[256,2048]{1,0:T(8,128)} %get-tuple-element.47.gin_ref, bf16[256,2048]{1,0:T(8,128)(2,1)} %x_ref.7, bf16[256,128]{1,0:T(8,128)(2,1)} %w_ref.7, s32[1,256]{1,0:T(1,128)} %bitcast.13, f32[256,16]{1,0:T(8,128)} %get-tuple-element.33.lcol_ref, ...), custom_call_target="tpu_custom_call" | custom-call | flops 268435456 | bytes 5063680 | tf_op jit(solution)/shard_map/ssm_last/pallas_call | solution.py:23
  153.7 16.4 %all-reduce.3 = (bf16[256,128]{1,0:T(8,128)(2,1)}, bf16[256,128]{1,0:T(8,128)(2,1)}) all-reduce(f32[256,128]{1,0:T(8,128)} %get-tuple-element.52, f32[256,128]{1,0:T(8,128)S(1)} %copy-done.4), channel_id=1, replica_groups=mesh['ctx'=8,'head'=4] {'head'}, use_global_device_ids=true, to_apply=%region_1.2 | all-reduce | flops 65536 | bytes 393216 | tf_op jit(solution)/shard_map/psum | solution.py:548
  170.0 21.1 %all-to-all-done.5.in_ref = bf16[8,1,1024,128]{3,2,1,0:T(8,128)(2,1)S(1)} async-done(((bf16[8,1,1024,128]{3,2,1,0:T(8,128)(2,1)}), bf16[8,1,1024,128]{3,2,1,0:T(8,128)(2,1)S(1)}, u32[]{:S(2)}, u32[]{:S(2)}) %all-to-all-start.5) | async-done | bytes 2097184 | tf_op jit(solution)/shard_map/all_to_all | solution.py:223
  191.1 1.3 copy-done
  192.4 3.5 %att_unpack.1 = (bf16[256,1024]{1,0:T(8,128)(2,1)}, bf16[256,1024]{1,0:T(8,128)(2,1)}, bf16[256,1024]{1,0:T(8,128)(2,1)}, bf16[256,1024]{1,0:T(8,128)(2,1)}) custom-call(bf16[8,1,1024,128]{3,2,1,0:T(8,128)(2,1)} %copy-done), custom_call_target="tpu_custom_call" | custom-call | bytes 4194304 | tf_op jit(solution)/shard_map/att_unpack/pallas_call | solution.py:23
  (16 shorter events, 2.2 us)
Async XLA Ops:
  1.9 31.0 %copy-start.5 = (s32[256]{0:T(256)S(1)}, s32[256]{0:T(256)}, u32[]{:S(2)}) copy-start(s32[256]{0:T(256)} %param.16) | copy-start | bytes 3076
  26.5 0.8 copy-start.2
  29.3 16.7 %all-to-all-start.1 = ((bf16[8,256,128]{2,1,0:T(8,128)(2,1)}), bf16[8,256,128]{2,1,0:T(8,128)(2,1)S(1)}, u32[]{:S(2)}, u32[]{:S(2)}) async-start(bf16[8,256,128]{2,1,0:T(8,128)(2,1)} %ssm_carry.1), calls=%async_computation.1 | async-start | bytes 1048576 | tf_op jit(solution)/shard_map/all_to_all | solution.py:223
  46.1 0.8 copy-start.1
  46.9 51.2 %all-to-all-start.2 = ((bf16[8,1,1040,128]{3,2,1,0:T(8,128)(2,1)}), bf16[8,1,1040,128]{3,2,1,0:T(8,128)(2,1)}, u32[]{:S(2)}, u32[]{:S(2)}) async-start(bf16[8,1,1040,128]{3,2,1,0:T(8,128)(2,1)} %att_pack.1), calls=%async_computation.2 | async-start | bytes 4259840 | tf_op jit(solution)/shard_map/all_to_all | solution.py:223
  119.6 18.8 %all-to-all-start.4 = ((bf16[8,256,128]{2,1,0:T(8,128)(2,1)}), bf16[8,256,128]{2,1,0:T(8,128)(2,1)S(1)}, u32[]{:S(2)}, u32[]{:S(2)}) async-start(bf16[8,256,128]{2,1,0:T(8,128)(2,1)} %ssm_carry_back.1), calls=%async_computation.4 | async-start | bytes 1048576 | tf_op jit(solution)/shard_map/all_to_all | solution.py:223
  138.4 0.8 copy-start.3
  139.2 51.9 %all-to-all-start.5 = ((bf16[8,1,1024,128]{3,2,1,0:T(8,128)(2,1)}), bf16[8,1,1024,128]{3,2,1,0:T(8,128)(2,1)S(1)}, u32[]{:S(2)}, u32[]{:S(2)}) async-start(bf16[8,1,1024,128]{3,2,1,0:T(8,128)(2,1)} %att_attend.1), calls=%async_computation.5 | async-start | bytes 4194304 | tf_op jit(solution)/shard_map/all_to_all | solution.py:223
  149.6 4.1 %copy-start.4 = (f32[256,128]{1,0:T(8,128)S(1)}, f32[256,128]{1,0:T(8,128)}, u32[]{:S(2)}) copy-start(f32[256,128]{1,0:T(8,128)} %get-tuple-element.53) | copy-start | bytes 393220
  191.1 1.3 copy-start
where the time goes:
time: 200 us; the launch traced here: 196 us
  blocking collectives  65.6 us (33%)
  waiting for transfers between devices  57.6 us (29%)
  Pallas kernels  49 us (24%)
  starting transfers between devices  17.4 us (9%)
  local copies, waits for them, and re-layouts  4.34 us (2%)
    all_to_all x4, waiting for transfers between devices, exchange(): return lax.all_to_all(blocks, 'ctx', 0, 0)  57.6 us
    pallas_call x10, Pallas kernels, call(): pl.pallas_call(kernel, out_shape=out_shape, in_specs=[pl.BlockSpec(memory...  49 us
    all_to_all x2, blocking collectives, exchange(): return lax.all_to_all(blocks, 'ctx', 0, 0)  41.3 us
    all_to_all x4, starting transfers between devices, exchange(): return lax.all_to_all(blocks, 'ctx', 0, 0)  17.4 us
    psum x1, blocking collectives, body(): write_sum, read_sum = lax.psum((write_part, read_part), 'head')  16.4 us
    psum x1, blocking collectives, body(): sums = lax.psum(sums, 'head')  7.94 us
  transfers between devices with their start and end apart: 4, of which 3 were waited for; matrix products, arithmetic and copies ran while one was open for 0% of the time, Pallas kernels for 20%

commit v1 on v0

--- a/solution.py
+++ b/solution.py
@@ -18,15 +18,20 @@
 VMEM_BYTES = 56 * 1024 * 1024
 
 
-def call(kernel, out_shape, *operands, scratch=(), flops=0, name=None):
+VMEM = pl.BlockSpec(memory_space=pltpu.VMEM)
+SMEM = pl.BlockSpec(memory_space=pltpu.SMEM)
+SMALL = 16 * 1024 * 1024
+
+
+def call(kernel, out_shape, *operands, specs=None, scratch=(), flops=0, vmem=VMEM_BYTES, name=None):
     moved = sum(a.size * a.dtype.itemsize for a in jax.tree.leaves((operands, out_shape)))
     return pl.pallas_call(
         kernel,
         out_shape=out_shape,
-        in_specs=[pl.BlockSpec(memory_space=pltpu.VMEM)] * len(operands),
-        out_specs=jax.tree.map(lambda _: pl.BlockSpec(memory_space=pltpu.VMEM), out_shape),
+        in_specs=specs or [VMEM] * len(operands),
+        out_specs=jax.tree.map(lambda _: VMEM, out_shape),
         scratch_shapes=scratch,
-        compiler_params=pltpu.CompilerParams(vmem_limit_bytes=VMEM_BYTES),
+        compiler_params=pltpu.CompilerParams(vmem_limit_bytes=vmem),
         cost_estimate=pl.CostEstimate(flops=flops, bytes_accessed=moved, transcendentals=0),
         name=name,
     )(*operands)
@@ -62,9 +67,40 @@
     return slice(h * HEAD_DIM, (h + 1) * HEAD_DIM)
 
 
-def first_kernel(ld_ref, rel_ref, w_ref, x_ref, out_ref, lcol_ref, lrow_ref):
+def put_state(x, h, heads, state, mine_ref, other_ref):
+    half = heads // 2
+
+    @pl.when(x == h // half)
+    def _():
+        mine_ref[cols(h % half), :] = state
+
+    @pl.when(x != h // half)
+    def _():
+        other_ref[cols(h % half), :] = state
+
+
+def put_tails(x, factors, mine_ref, other_ref):
+    half = len(factors) // 2
+    row = iota((TAIL, 128), 0)
+    tails = []
+    for part in range(2):
+        tail = jnp.zeros((TAIL, 128), F32)
+        for k in range(half):
+            factor = factors[part * half + k]
+            high = factor.astype(BF16).astype(F32)
+            tail = jnp.where(row == 2 * k, high, jnp.where(row == 2 * k + 1, factor - high, tail))
+        tails.append(tail)
+    mine_ref[half * HEAD_DIM :, :] = jnp.where(x == 0, tails[0], tails[1]).astype(BF16)
+    other_ref[half * HEAD_DIM :, :] = jnp.where(x == 0, tails[1], tails[0]).astype(BF16)
+
+
+def factor_of(tail, k):
+    return tail[2 * k : 2 * k + 1, :] + tail[2 * k + 1 : 2 * k + 2, :]
+
+
+def first_kernel(x_ref, ld_ref, rel_ref, w_ref, in_ref, mine_ref, other_ref, lcol_ref, lrow_ref):
     heads, length = ld_ref.shape
-    parts, rows = out_ref.shape[0], out_ref.shape[1] - TAIL
+    x = x_ref[0]
     rates = ld_ref[...] * LOG2E
     lower = jnp.where(iota((length, length), 0) >= iota((length, length), 1), 1.0, 0.0)
     upper = jnp.where(iota((length, length), 0) <= iota((length, length), 1), 1.0, 0.0)
@@ -73,48 +109,94 @@
     lrow_ref[...] = lrow
     rel_last = rel_ref[:, length - 1 :]
     last_doc = iota((1, length), 1) >= rel_last
-    keeps = rel_last < 0
     writes = w_ref[...].astype(F32).T
-    tail_row = iota((TAIL, 128), 0)
+    factors = []
     for h in range(heads):
         line = lrow[h : h + 1, :]
         total = line[:, length - 1 :]
         to_end = jnp.where(last_doc, jnp.exp2(total - line), 0.0)
-        state = dot((writes * to_end).astype(BF16), x_ref[:, cols(h)]).astype(BF16)
-        factor = jnp.where(keeps, jnp.exp2(total), 0.0)
+        state = dot((writes * to_end).astype(BF16), in_ref[:, cols(h)]).astype(BF16)
+        put_state(x, h, heads, state, mine_ref, other_ref)
+        factors.append(jnp.where(rel_last < 0, jnp.exp2(total), 0.0))
+    put_tails(x, factors, mine_ref, other_ref)
+
+
+def level_kernel(backward, x_ref, mine_ref, got_ref, out_ref):
+    half = out_ref.shape[0] - TAIL
+    is_far = x_ref[0] == (0 if backward else 1)
+    mine_tail, got_tail = mine_ref[half:, :].astype(F32), got_ref[half:, :].astype(F32)
+    row = iota((TAIL, 128), 0)
+    tail = jnp.zeros((TAIL, 128), F32)
+    for k in range(half // HEAD_DIM):
+        mine, got = mine_ref[cols(k), :].astype(F32), got_ref[cols(k), :].astype(F32)
+        mine_factor, got_factor = factor_of(mine_tail, k), factor_of(got_tail, k)
+        out_ref[cols(k), :] = jnp.where(
+            is_far, mine + mine_factor * got, got + got_factor * mine
+        ).astype(BF16)
+        factor = mine_factor * got_factor
         high = factor.astype(BF16).astype(F32)
-        low = factor - high
-        first = h * HEAD_DIM
-        for part in range(first // rows, (first + HEAD_DIM - 1) // rows + 1):
-            begin = max(first, part * rows)
-            end = min(first + HEAD_DIM, (part + 1) * rows)
-            out_ref[part, begin - part * rows : end - part * rows, :] = state[
-                begin - first : end - first, :
-            ]
-            place = 2 * (begin - part * rows) // HEAD_DIM
-            tail = jnp.where(tail_row == place, high, jnp.where(tail_row == place + 1, low, 0.0))
-            if place:
-                tail = tail + out_ref[part, rows:, :].astype(F32)
-            out_ref[part, rows:, :] = tail.astype(BF16)
-
-
-def carry_kernel(backward, tail_ref, in_ref, out_ref):
-    parts, rows = out_ref.shape[0], out_ref.shape[1]
-    step = min(rows, HEAD_DIM)
-    for k in range(rows // step):
-        here = slice(k * step, (k + 1) * step)
-        state = jnp.zeros((step, 128), F32)
-        for c in range(parts)[:: -1 if backward else 1]:
-            out_ref[c, here, :] = state.astype(BF16)
-            tail = tail_ref[c].astype(F32)
-            factor = tail[2 * k : 2 * k + 1, :] + tail[2 * k + 1 : 2 * k + 2, :]
-            state = factor * state + in_ref[c, here, :].astype(F32)
+        tail = jnp.where(row == 2 * k, high, jnp.where(row == 2 * k + 1, factor - high, tail))
+    out_ref[half:, :] = tail.astype(BF16)
+
+
+def reach_kernel(backward, x_ref, mine_ref, got_ref, *refs):
+    steps, (keep_ref, message_ref) = refs[:-2], refs[-2:]
+    half = keep_ref.shape[0]
+    is_far = x_ref[0] == (0 if backward else 1)
+    mine_tail, got_tail = mine_ref[half:, :].astype(F32), got_ref[half:, :].astype(F32)
+    tails = [step[half:, :].astype(F32) for step in steps]
+    for k in range(half // HEAD_DIM):
+        entering = steps[0][cols(k), :].astype(F32)
+        factor = 1.0
+        for n in range(1, len(steps)):
+            factor = factor * factor_of(tails[n - 1], k)
+            entering = entering + factor * steps[n][cols(k), :].astype(F32)
+        near = jnp.where(is_far, got_ref[cols(k), :].astype(F32), mine_ref[cols(k), :].astype(F32))
+        near_factor = jnp.where(is_far, factor_of(got_tail, k), factor_of(mine_tail, k))
+        passed = near + near_factor * entering
+        keep_ref[cols(k), :] = jnp.where(is_far, passed, entering).astype(BF16)
+        message_ref[cols(k), :] = jnp.where(is_far, entering, passed).astype(BF16)
+
+
+def carry_start(other):
+    swap = [(i, i ^ 1) for i in range(lax.axis_size("ctx"))]
+    return lax.ppermute(other, "ctx", swap)
+
+
+def carry_rest(backward, x, mine, got):
+    parts = lax.axis_size("ctx")
+    half = mine.shape[0] - TAIL
+    level = call(
+        lambda *refs: level_kernel(backward, *refs), shape(mine.shape, BF16),
+        x, mine, got, specs=[SMEM, VMEM, VMEM], vmem=SMALL, name="ssm_level",
+    )
+    steps = []
+    for n in range(1, parts // 2):
+        by = -2 * n if backward else 2 * n
+        pairs = [(i, i + by) for i in range(parts) if 0 <= i + by < parts]
+        steps.append(lax.ppermute(level, "ctx", pairs))
+    keep, message = call(
+        lambda *refs: reach_kernel(backward, *refs),
+        (shape((half, 128), BF16), shape((half, 128), BF16)),
+        x, mine, got, *steps,
+        specs=[SMEM] + [VMEM] * (2 + len(steps)), vmem=SMALL, name="ssm_reach",
+    )
+    return keep, carry_start(message)
+
+
+def state_of(x, h, heads, keep_ref, theirs_ref):
+    half = heads // 2
+    here = cols(h % half)
+    keep, theirs = keep_ref[here, :].astype(F32), theirs_ref[here, :].astype(F32)
+    return jnp.where(x == h // half, keep, theirs).astype(BF16)
 
 
 def mix_kernel(
-    x_ref, gate_ref, grad_ref, w_ref, r_ref, rel_ref, lcol_ref, lrow_ref, s_ref, mixed_ref, sums_ref
+    at_ref, x_ref, gate_ref, grad_ref, w_ref, r_ref, rel_ref, lcol_ref, lrow_ref, keep_ref, theirs_ref,
+    mixed_ref, sums_ref, state_ref,
 ):
     length, heads = lcol_ref.shape
+    x = at_ref[0]
     reads = r_ref[...]
     rel = column(rel_ref[...].astype(F32))
     wide = jnp.concatenate([rel] * (length // 128), axis=1)
@@ -128,9 +210,9 @@
         lc = lcol_ref[:, h : h + 1]
         decay = jnp.exp2(jnp.minimum(lc - lrow_ref[h : h + 1, :], 0.0))
         enter = jnp.where(rel < 0, jnp.exp2(jnp.broadcast_to(lc, rel.shape)), 0.0)
-        mixed = dot((scores * decay).astype(BF16), x_ref[:, cols(h)]) + enter * dot(
-            reads, s_ref[cols(h), :]
-        )
+        state = state_of(x, h, heads, keep_ref, theirs_ref)
+        state_ref[cols(h), :] = state
+        mixed = dot((scores * decay).astype(BF16), x_ref[:, cols(h)]) + enter * dot(reads, state)
         mixed_ref[:, cols(h)] = mixed
         gate = gate_ref[:, cols(h)].astype(F32)
         gated = mixed * (gate / (1.0 + jnp.exp(-gate)))
@@ -143,12 +225,14 @@
 
 
 def gate_kernel(
-    width, sums_ref, mixed_ref, gate_ref, grad_ref, r_ref, rel_ref, lrow_ref,
-    mixer_ref, ggrad_ref, dmixed_ref, out_ref,
+    width, x_ref, sums_ref, mixed_ref, gate_ref, grad_ref, r_ref, rel_ref, lrow_ref,
+    mixer_ref, ggrad_ref, dmixed_ref, mine_ref, other_ref,
 ):
     length = mixed_ref.shape[0]
     heads = lrow_ref.shape[0]
-    rows = out_ref.shape[1]
+    x = x_ref[0]
+    rel_last = rel_ref[:, length - 1 :]
+    factors = []
     scale = lax.rsqrt(sums_ref[0:1, :] / width + EPSILON)
     rms = column(scale)
     pull = column(scale * scale * scale * sums_ref[1:2, :] / width)
@@ -169,13 +253,10 @@
         ).astype(BF16)
         enter = jnp.where(enters, jnp.exp2(lrow_ref[h : h + 1, :]), 0.0)
         state = dot((reads * enter).astype(BF16), dmixed).astype(BF16)
-        first = h * HEAD_DIM
-        for part in range(first // rows, (first + HEAD_DIM - 1) // rows + 1):
-            begin = max(first, part * rows)
-            end = min(first + HEAD_DIM, (part + 1) * rows)
-            out_ref[part, begin - part * rows : end - part * rows, :] = state[
-                begin - first : end - first, :
-            ]
+        put_state(x, h, heads, state, mine_ref, other_ref)
+        total = lrow_ref[h : h + 1, length - 1 :]
+        factors.append(jnp.where(rel_last < 0, jnp.exp2(total), 0.0))
+    put_tails(x, factors, mine_ref, other_ref)
 
 
 def inner_kernel(
@@ -203,8 +284,11 @@
     read_ref[...] = read + dot(total.T.astype(BF16), w_ref[...])
 
 
-def last_kernel(gin_ref, x_ref, w_ref, rel_ref, lcol_ref, back_ref, part_ref, out_ref, write_ref):
+def last_kernel(
+    at_ref, gin_ref, x_ref, w_ref, rel_ref, lcol_ref, keep_ref, theirs_ref, part_ref, out_ref, write_ref
+):
     length, heads = lcol_ref.shape
+    x = at_ref[0]
     rel_last = rel_ref[:, length - 1 :]
     last_doc = iota((length, 128), 0) >= rel_last
     writes = w_ref[...]
@@ -213,10 +297,18 @@
         lc = lcol_ref[:, h : h + 1]
         line = jnp.broadcast_to(lc[length - 1 :, :] - lc, (length, 128))
         to_end = jnp.where(last_doc, jnp.exp2(line), 0.0)
-        back = back_ref[cols(h), :]
+        back = state_of(x, h, heads, keep_ref, theirs_ref)
         out_ref[:, cols(h)] = (gin_ref[:, cols(h)] + to_end * dot(writes, back)).astype(BF16)
         write = write + to_end * dot_nt(x_ref[:, cols(h)], back)
     write_ref[...] = write
+
+
+def sum_heads(part):
+    count = lax.axis_size("head")
+    total = part
+    for by in range(1, count):
+        total = total + lax.ppermute(part, "head", [(i, (i + by) % count) for i in range(count)])
+    return total
 
 
 def exchange(blocks):
@@ -450,71 +542,58 @@
     length, width = ssm_input.shape
     heads = width // HEAD_DIM
     parts = lax.axis_size("ctx")
-    rows = width // parts
     full_width = width * lax.axis_size("head")
-    work = 2 * length * length * width
     att_width = att_queries.shape[1]
     per = att_width // ATT_DIM // parts
     dealt = att_width // ATT_DIM % parts == 0
-    rel = (doc_start - lax.axis_index("ctx") * length).reshape(1, length)
-
-    sent, lcol, lrow = call(
+    place = lax.axis_index("ctx")
+    rel = (doc_start - place * length).reshape(1, length)
+    x = (place % 2).reshape(1)
+    half = shape((width // 2 + TAIL, 128), BF16)
+
+    mine, other, lcol, lrow = call(
         first_kernel,
-        (
-            shape((parts, rows + TAIL, 128), BF16),
-            shape((length, heads), F32),
-            shape((heads, length), F32),
-        ),
-        log_decay.T, rel, write_map, ssm_input, flops=work // 2, name="ssm_first",
-    )
-    got = exchange(sent)
-    tail = got[:, rows:, :]
-    carried = call(
-        lambda *refs: carry_kernel(False, *refs), shape((parts, rows, 128), BF16), tail, got,
-        name="ssm_carry",
-    )
-    state = exchange(carried).reshape(width, 128)
-
+        (half, half, shape((length, heads), F32), shape((heads, length), F32)),
+        x, log_decay.T, rel, write_map, ssm_input, specs=[SMEM] + [VMEM] * 4, name="ssm_first",
+    )
     if dealt:
         marks = doc_start.reshape(length // 128, 128)
         marks = jnp.stack([marks // 128, marks % 128], axis=1).reshape(length // 64, 128)
         marks = jnp.pad(marks, ((0, TAIL - length // 64), (0, 0))).astype(BF16)
+        marks, other = lax.optimization_barrier((marks, other))
         packed = call(
             pack_kernel, shape((parts, per, 4 * length + TAIL, 128), BF16),
-            marks, att_queries, att_keys, att_values, att_grad, name="att_pack",
-        )
-        packed, state = lax.optimization_barrier((packed, state))
+            marks, att_queries, att_keys, att_values, att_grad, vmem=SMALL, name="att_pack",
+        )
         att_got = exchange(packed)
+        got = carry_start(other)
+        got, packed = lax.optimization_barrier((got, packed))
     else:
         att_out = ring_attention(att_queries, att_keys, att_values, att_grad, doc_start)
-
-    mixed, sums = call(
+        got = carry_start(other)
+    keep, theirs = carry_rest(False, x, mine, got)
+    mixed, sums, state = call(
         mix_kernel,
-        (shape((length, width), F32), shape((8, length), F32)),
-        ssm_input, gate_input, ssm_grad, write_map, read_map, rel, lcol, lrow, state,
-        flops=work * 3 // 2, name="ssm_mix",
+        (shape((length, width), F32), shape((8, length), F32), shape((width, 128), BF16)),
+        x, ssm_input, gate_input, ssm_grad, write_map, read_map, rel, lcol, lrow, keep, theirs,
+        specs=[SMEM] + [VMEM] * 10, name="ssm_mix",
     )
     sums = lax.psum(sums, "head")
-    mixer_out, gate_grad, dmixed, sent = call(
+    mixer_out, gate_grad, dmixed, mine, other = call(
         lambda *refs: gate_kernel(full_width, *refs),
         (
             shape((length, width), BF16),
             shape((length, width), BF16),
             shape((length, width), BF16),
-            shape((parts, rows, 128), BF16),
+            half,
+            half,
         ),
-        sums, mixed, gate_input, ssm_grad, read_map, rel, lrow, flops=work // 2, name="ssm_gate",
-    )
-
+        x, sums, mixed, gate_input, ssm_grad, read_map, rel, lrow,
+        specs=[SMEM] + [VMEM] * 7, name="ssm_gate",
+    )
+    got = carry_start(other)
     if dealt:
-        sent, att_got = lax.optimization_barrier((sent, att_got))
-    got = exchange(sent)
-    carried = call(
-        lambda *refs: carry_kernel(True, *refs), shape((parts, rows, 128), BF16), tail, got,
-        name="ssm_carry_back",
-    )
-    back = exchange(carried).reshape(width, 128)
-    if dealt:
+        att_got, other = lax.optimization_barrier((att_got, other))
         att_done = call(
             lambda *refs: attend_kernel(length, *refs),
             shape((parts, per, 4 * length, 128), BF16),
@@ -528,24 +607,26 @@
             ],
             flops=6 * per * (parts * length) ** 2 * ATT_DIM, name="att_attend",
         )
-        att_done, back = lax.optimization_barrier((att_done, back))
         att_out = call(
             unpack_kernel, (shape((length, att_width), BF16),) * 4, exchange(att_done),
-            name="att_unpack",
-        )
+            vmem=SMALL, name="att_unpack",
+        )
+        got, att_done = lax.optimization_barrier((got, att_done))
+    keep, theirs = carry_rest(True, x, mine, got)
 
     gin, read_part, write_part = call(
         inner_kernel,
         (shape((length, width), F32), shape((length, 128), F32), shape((length, 128), F32)),
-        dmixed, ssm_input, write_map, read_map, rel, lcol, lrow, state,
-        flops=work * 5 // 2, name="ssm_inner",
+        dmixed, ssm_input, write_map, read_map, rel, lcol, lrow, state, name="ssm_inner",
     )
     input_grad, write_part = call(
         last_kernel,
         (shape((length, width), BF16), shape((length, 128), F32)),
-        gin, ssm_input, write_map, rel, lcol, back, write_part, flops=work, name="ssm_last",
-    )
-    write_sum, read_sum = lax.psum((write_part, read_part), "head")
+        x, gin, ssm_input, write_map, rel, lcol, keep, theirs, write_part,
+        specs=[SMEM] + [VMEM] * 8, name="ssm_last",
+    )
+    read_sum = sum_heads(read_part)
+    write_sum = sum_heads(write_part)
     window_out, query_grad, key_grad, value_grad = att_out
     return (
         mixer_out,

time: 200 us -> 243 us (1.22); the launches traced: 196 us -> 242 us
  waiting for transfers between devices: 57.6 us -> 118 us
  blocking collectives: 65.6 us -> 8.23 us
  starting transfers between devices: 17.4 us -> 54 us
  local copies, waits for them, and re-layouts: 4.34 us -> 8.32 us
  other arithmetic: 1.26 us -> 4.17 us
    ppermute x0 -> x16, waiting for transfers between devices: none -> 118 us  [the longest x6 62.3 us: carry_rest(): steps.append(lax.ppermute(level, 'ctx', pairs))]
    all_to_all x4 -> x2, waiting for transfers between devices: 57.6 us -> 0.01 us  [exchange(): return lax.all_to_all(blocks, 'ctx', 0, 0)]
    all_to_all x2 -> x0, blocking collectives: 41.3 us -> none  [exchange(): return lax.all_to_all(blocks, 'ctx', 0, 0)]
    ppermute x0 -> x16, starting transfers between devices: none -> 23.8 us  [the longest x6 12.3 us: carry_rest(): steps.append(lax.ppermute(level, 'ctx', pairs))]
    psum x1 -> x0, blocking collectives: 16.4 us -> none  [body(): write_sum, read_sum = lax.psum((write_part, read_part), 'head')]
    all_to_all x4 -> x2, starting transfers between devices: 17.4 us -> 30.2 us  [exchange(): return lax.all_to_all(blocks, 'ctx', 0, 0)]
    unnamed x12 -> x28, local copies, waits for them, and re-layouts: 3.07 us -> 8.31 us
    pallas_call x10 -> x12, Pallas kernels: 49 us -> 48.2 us  [call(): pl.pallas_call(kernel, out_shape=out_shape, in_specs=specs or [VMEM] * le...]
  transfers between devices with their start and end apart: 4 -> 18, of which waited for: 3 -> 11; matrix products, arithmetic and copies ran while one was open for 0% -> 1% of each run, Pallas kernels for 20% -> 10%
where the time goes in v1:
time: 243 us; the launch traced here: 242 us
  waiting for transfers between devices  118 us (49%)
  starting transfers between devices  54 us (22%)
  Pallas kernels  48.2 us (20%)
  local copies, waits for them, and re-layouts  8.32 us (3%)
  blocking collectives  8.23 us (3%)
  other arithmetic  4.17 us (2%)
    ppermute x6, waiting for transfers between devices, carry_rest(): steps.append(lax.ppermute(level, 'ctx', pairs))  62.3 us
    ppermute x4, waiting for transfers between devices, carry_start(): return lax.ppermute(other, 'ctx', swap)  49.7 us
    pallas_call x12, Pallas kernels, call(): pl.pallas_call(kernel, out_shape=out_shape, in_specs=specs or [VMEM] * le...  48.2 us
    all_to_all x2, starting transfers between devices, exchange(): return lax.all_to_all(blocks, 'ctx', 0, 0)  30.2 us
    ppermute x6, starting transfers between devices, carry_rest(): steps.append(lax.ppermute(level, 'ctx', pairs))  12.3 us
    unnamed x28, local copies, waits for them, and re-layouts  8.31 us
    psum x1, blocking collectives, body(): sums = lax.psum(sums, 'head')  8.23 us
    ppermute x6, starting transfers between devices, sum_heads(): lax.ppermute(part, 'head', [(i, (i + by) % count) for i in range(count)])  6.1 us
  transfers between devices with their start and end apart: 18, of which 11 were waited for; matrix products, arithmetic and copies ran while one was open for 1% of the time, Pallas kernels for 10%

profile of v1, /device:TPU:1, one launch (start us, length us, event | category | flops | bytes accessed | tf_op | source)
XLA Modules:
  0.0 241.8 jit_solution(14677377009479185451)
XLA Ops:
  2.6 5.4 %ssm_first.1 = (bf16[1040,128]{1,0:T(8,128)(2,1)}, bf16[1040,128]{1,0:T(8,128)(2,1)}, f32[256,16]{1,0:T(8,128)}, f32[16,256]{1,0:T(8,128)}) custom-call(s32[1]{0:T(128)} %bitcast.x_ref.refs_0_.at_ref, f32[16,256]{1,0:T(8,128)} %bitcast.10, s32[1,256]{1,0:T(1,128)} %bitcast.5, bf16[256,128]{1,0:T(8,128)(2,1)} %w_ref.7, bf16[256,2048]{1,0:T(8,128)(2,1)} %x_ref.5), custom_call_target="tpu_custom_call" | custom-call | bytes 1696772 | tf_op jit(solution)/shard_map/ssm_first/pallas_call | solution.py:28
  12.2 1.8 att_pack.1
  14.0 6.5 %all-to-all-start = ((bf16[8,1,1040,128]{3,2,1,0:T(8,128)(2,1)}), bf16[8,1,1040,128]{3,2,1,0:T(8,128)(2,1)S(1)}, u32[]{:S(2)}, u32[]{:S(2)}) async-start(bf16[8,1,1040,128]{3,2,1,0:T(8,128)(2,1)} %att_pack.1), calls=%async_computation | async-start | bytes 4259840 | tf_op jit(solution)/shard_map/all_to_all | solution.py:315
  21.9 22.2 %collective-permute-done.refs_2_ = bf16[1040,128]{1,0:T(8,128)(2,1)S(1)} collective-permute-done((bf16[1040,128]{1,0:T(8,128)(2,1)S(1)}, bf16[1040,128]{1,0:T(8,128)(2,1)S(1)}, u32[]{:S(2)}, u32[]{:S(2)}) %collective-permute-start) | collective-permute-done | bytes 266272 | tf_op jit(solution)/shard_map/ppermute | solution.py:163
  44.3 2.2 collective-permute-start.1
  46.5 4.7 %collective-permute-start.2 = (bf16[1040,128]{1,0:T(8,128)(2,1)S(1)}, bf16[1040,128]{1,0:T(8,128)(2,1)S(1)}, u32[]{:S(2)}, u32[]{:S(2)}) collective-permute-start(bf16[1040,128]{1,0:T(8,128)(2,1)S(1)} %ssm_level.2), channel_id=1, source_target_pairs={{0,16},{4,20},{8,24},{12,28},{1,17},{5,21},{9,25},{13,29},{2,18},{... | collective-permute-start | bytes 798728 | tf_op jit(solution)/shard_map/ppermute | solution.py:177
  52.5 8.6 %collective-permute-done.1.refs_3_ = bf16[1040,128]{1,0:T(8,128)(2,1)S(1)} collective-permute-done((bf16[1040,128]{1,0:T(8,128)(2,1)S(1)}, bf16[1040,128]{1,0:T(8,128)(2,1)S(1)}, u32[]{:S(2)}, u32[]{:S(2)}) %collective-permute-start.1) | collective-permute-done | bytes 266272 | tf_op jit(solution)/shard_map/ppermute | solution.py:177
  61.1 5.7 %collective-permute-done.2.refs_4_ = bf16[1040,128]{1,0:T(8,128)(2,1)S(1)} collective-permute-done((bf16[1040,128]{1,0:T(8,128)(2,1)S(1)}, bf16[1040,128]{1,0:T(8,128)(2,1)S(1)}, u32[]{:S(2)}, u32[]{:S(2)}) %collective-permute-start.2) | collective-permute-done | bytes 266272 | tf_op jit(solution)/shard_map/ppermute | solution.py:177
  66.8 5.7 %collective-permute-done.3.refs_5_ = bf16[1040,128]{1,0:T(8,128)(2,1)S(1)} collective-permute-done((bf16[1040,128]{1,0:T(8,128)(2,1)S(1)}, bf16[1040,128]{1,0:T(8,128)(2,1)S(1)}, u32[]{:S(2)}, u32[]{:S(2)}) %collective-permute-start.3) | collective-permute-done | bytes 266272 | tf_op jit(solution)/shard_map/ppermute | solution.py:177
  74.2 5.6 %collective-permute-done.4.theirs_ref = bf16[1024,128]{1,0:T(8,128)(2,1)S(1)} collective-permute-done((bf16[1024,128]{1,0:T(8,128)(2,1)S(1)}, bf16[1024,128]{1,0:T(8,128)(2,1)S(1)}, u32[]{:S(2)}, u32[]{:S(2)}) %collective-permute-start.4) | collective-permute-done | bytes 262176 | tf_op jit(solution)/shard_map/ppermute | solution.py:163
  80.5 6.0 %ssm_mix.1 = (f32[256,2048]{1,0:T(8,128)}, f32[8,256]{1,0:T(8,128)}, bf16[2048,128]{1,0:T(8,128)(2,1)}) custom-call(s32[1]{0:T(128)} %bitcast.x_ref.refs_0_.at_ref, bf16[256,2048]{1,0:T(8,128)(2,1)} %x_ref.5, bf16[256,2048]{1,0:T(8,128)(2,1)} %refs_3_.1, bf16[256,2048]{1,0:T(8,128)(2,1)} %refs_4_.1, bf16[256,128]{1,0:T(8,128)(2,1)} %w_ref.7, ...), custom_call_target="tpu_custom_call" | custom-call | bytes 6464516 | tf_op jit(solution)/shard_map/ssm_mix/pallas_call | solution.py:28
  86.5 8.2 %psum.7.refs_1_ = f32[8,256]{1,0:T(8,128)} all-reduce(f32[8,256]{1,0:T(8,128)} %get-tuple-element.48), channel_id=1, replica_groups=mesh['ctx'=8,'head'=4] {'head'}, use_global_device_ids=true, to_apply=%region_0.1 | all-reduce | flops 2048 | bytes 16384 | tf_op jit(solution)/shard_map/psum | solution.py:581
  94.7 8.5 %ssm_gate.1 = (bf16[256,2048]{1,0:T(8,128)(2,1)}, bf16[256,2048]{1,0:T(8,128)(2,1)}, bf16[256,2048]{1,0:T(8,128)(2,1)}, bf16[1040,128]{1,0:T(8,128)(2,1)}, bf16[1040,128]{1,0:T(8,128)(2,1)}) custom-call(s32[1]{0:T(128)} %bitcast.x_ref.refs_0_.at_ref, f32[8,256]{1,0:T(8,128)} %psum.7.refs_1_, f32[256,2048]{1,0:T(8,128)} %get-tuple-element.49.refs_2_, ...), custom_call_target="tpu_custom_call" | custom-call | bytes 7963652 | tf_op jit(solution)/shard_map/ssm_gate/pallas_call | solution.py:28
  104.6 14.7 %att_attend.1 = bf16[8,1,1024,128]{3,2,1,0:T(8,128)(2,1)} custom-call(bf16[8,1,1040,128]{3,2,1,0:T(8,128)(2,1)} %copy-done.8), custom_call_target="tpu_custom_call" | custom-call | flops 3221225472 | bytes 4227072 | tf_op jit(solution)/shard_map/att_attend/pallas_call | solution.py:28
  119.2 23.7 %all-to-all-start.1 = ((bf16[8,1,1024,128]{3,2,1,0:T(8,128)(2,1)}), bf16[8,1,1024,128]{3,2,1,0:T(8,128)(2,1)S(1)}, u32[]{:S(2)}, u32[]{:S(2)}) async-start(bf16[8,1,1024,128]{3,2,1,0:T(8,128)(2,1)} %att_attend.1), calls=%async_computation.1 | async-start | bytes 4194304 | tf_op jit(solution)/shard_map/all_to_all | solution.py:315
  144.4 21.9 %collective-permute-done.5.refs_2_ = bf16[1040,128]{1,0:T(8,128)(2,1)S(1)} collective-permute-done((bf16[1040,128]{1,0:T(8,128)(2,1)S(1)}, bf16[1040,128]{1,0:T(8,128)(2,1)S(1)}, u32[]{:S(2)}, u32[]{:S(2)}) %collective-permute-start.5) | collective-permute-done | bytes 266272 | tf_op jit(solution)/shard_map/ppermute | solution.py:163
  170.6 4.9 %collective-permute-done.6.refs_3_ = bf16[1040,128]{1,0:T(8,128)(2,1)S(1)} collective-permute-done((bf16[1040,128]{1,0:T(8,128)(2,1)S(1)}, bf16[1040,128]{1,0:T(8,128)(2,1)S(1)}, u32[]{:S(2)}, u32[]{:S(2)}) %collective-permute-start.6) | collective-permute-done | bytes 266272 | tf_op jit(solution)/shard_map/ppermute | solution.py:177
  175.5 37.3 %collective-permute-done.7.refs_4_ = bf16[1040,128]{1,0:T(8,128)(2,1)S(1)} collective-permute-done((bf16[1040,128]{1,0:T(8,128)(2,1)S(1)}, bf16[1040,128]{1,0:T(8,128)(2,1)S(1)}, u32[]{:S(2)}, u32[]{:S(2)}) %collective-permute-start.7) | collective-permute-done | bytes 266272 | tf_op jit(solution)/shard_map/ppermute | solution.py:177
  213.8 1.9 collective-permute-start.9
  215.7 4.9 %ssm_inner.1 = (f32[256,2048]{1,0:T(8,128)}, f32[256,128]{1,0:T(8,128)}, f32[256,128]{1,0:T(8,128)}) custom-call(bf16[256,2048]{1,0:T(8,128)(2,1)} %get-tuple-element.54.dmixed_ref, bf16[256,2048]{1,0:T(8,128)(2,1)} %x_ref.5, bf16[256,128]{1,0:T(8,128)(2,1)} %w_ref.7, bf16[256,128]{1,0:T(8,128)(2,1)} %r_ref.3, s32[1,256]{1,0:T(1,128)} %bitcast.8, ...), custom_call_target="tpu_custom_call" | custom-call | bytes 5145600 | tf_op jit(solution)/shard_map/ssm_inner/pallas_call | solution.py:28
  220.6 2.9 %collective-permute-start.13 = (f32[256,128]{1,0:T(8,128)}, f32[256,128]{1,0:T(8,128)S(1)}, u32[]{:S(2)}, u32[]{:S(2)}) collective-permute-start(f32[256,128]{1,0:T(8,128)} %get-tuple-element.65), channel_id=1, source_target_pairs={{0,1},{1,2},{2,3},{3,0},{4,5},{5,6},{6,7},{7,4},{8,9},{9,10},{10,1... | collective-permute-start | bytes 393224 | tf_op jit(solution)/shard_map/ppermute | solution.py:310
  224.6 4.1 %ssm_last.1 = (bf16[256,2048]{1,0:T(8,128)(2,1)}, f32[256,128]{1,0:T(8,128)}) custom-call(s32[1]{0:T(128)} %bitcast.x_ref.refs_0_.at_ref, f32[256,2048]{1,0:T(8,128)} %get-tuple-element.56.gin_ref, bf16[256,2048]{1,0:T(8,128)(2,1)} %x_ref.5, bf16[256,128]{1,0:T(8,128)(2,1)} %w_ref.7, s32[1,256]{1,0:T(1,128)} %bitcast.9, ...), custom_call_target="tpu_custom_call" | custom-call | bytes 5063684 | tf_op jit(solution)/shard_map/ssm_last/pallas_call | solution.py:28
  233.3 4.4 %collective-permute-done.11 = f32[256,128]{1,0:T(8,128)S(1)} collective-permute-done((f32[256,128]{1,0:T(8,128)}, f32[256,128]{1,0:T(8,128)S(1)}, u32[]{:S(2)}, u32[]{:S(2)}) %collective-permute-start.11) | collective-permute-done | bytes 131104 | tf_op jit(solution)/shard_map/ppermute | solution.py:310
  239.9 1.9 att_unpack.1
  (60 shorter events, 27.2 us)
Async XLA Ops:
  14.0 6.5 %copy-start.13 = (bf16[1040,128]{1,0:T(8,128)(2,1)S(1)}, bf16[1040,128]{1,0:T(8,128)(2,1)}, u32[]{:S(2)}) copy-start(bf16[1040,128]{1,0:T(8,128)(2,1)} %get-tuple-element.43) | copy-start | bytes 798724
  14.0 30.1 %copy-start.1 = (bf16[1040,128]{1,0:T(8,128)(2,1)S(1)}, bf16[1040,128]{1,0:T(8,128)(2,1)}, u32[]{:S(2)}) copy-start(bf16[1040,128]{1,0:T(8,128)(2,1)} %get-tuple-element.41.refs_1_) | copy-start | bytes 798724
  14.0 89.2 %all-to-all-start = ((bf16[8,1,1040,128]{3,2,1,0:T(8,128)(2,1)}), bf16[8,1,1040,128]{3,2,1,0:T(8,128)(2,1)S(1)}, u32[]{:S(2)}, u32[]{:S(2)}) async-start(bf16[8,1,1040,128]{3,2,1,0:T(8,128)(2,1)} %att_pack.1), calls=%async_computation | async-start | bytes 4259840 | tf_op jit(solution)/shard_map/all_to_all | solution.py:315
  20.5 23.6 %collective-permute-start = (bf16[1040,128]{1,0:T(8,128)(2,1)S(1)}, bf16[1040,128]{1,0:T(8,128)(2,1)S(1)}, u32[]{:S(2)}, u32[]{:S(2)}) collective-permute-start(bf16[1040,128]{1,0:T(8,128)(2,1)S(1)} %copy-done.13), channel_id=1, source_target_pairs={{0,4},{4,0},{8,12},{12,8},{16,20},{20,16},{24,28},{28,24},{1,5},{5... | collective-permute-start | bytes 798728 | tf_op jit(solution)/shard_map/ppermute | solution.py:163
  44.3 16.8 %collective-permute-start.1 = (bf16[1040,128]{1,0:T(8,128)(2,1)S(1)}, bf16[1040,128]{1,0:T(8,128)(2,1)S(1)}, u32[]{:S(2)}, u32[]{:S(2)}) collective-permute-start(bf16[1040,128]{1,0:T(8,128)(2,1)S(1)} %ssm_level.2), channel_id=1, source_target_pairs={{0,8},{4,12},{8,16},{12,20},{16,24},{20,28},{1,9},{5,13},{9,17},{1... | collective-permute-start | bytes 798728 | tf_op jit(solution)/shard_map/ppermute | solution.py:177
  46.5 20.3 %collective-permute-start.2 = (bf16[1040,128]{1,0:T(8,128)(2,1)S(1)}, bf16[1040,128]{1,0:T(8,128)(2,1)S(1)}, u32[]{:S(2)}, u32[]{:S(2)}) collective-permute-start(bf16[1040,128]{1,0:T(8,128)(2,1)S(1)} %ssm_level.2), channel_id=1, source_target_pairs={{0,16},{4,20},{8,24},{12,28},{1,17},{5,21},{9,25},{13,29},{2,18},{... | collective-permute-start | bytes 798728 | tf_op jit(solution)/shard_map/ppermute | solution.py:177
  51.2 21.4 %collective-permute-start.3 = (bf16[1040,128]{1,0:T(8,128)(2,1)S(1)}, bf16[1040,128]{1,0:T(8,128)(2,1)S(1)}, u32[]{:S(2)}, u32[]{:S(2)}) collective-permute-start(bf16[1040,128]{1,0:T(8,128)(2,1)S(1)} %ssm_level.2), channel_id=1, source_target_pairs={{0,24},{4,28},{1,25},{5,29},{2,26},{6,30},{3,27},{7,31}} | collective-permute-start | bytes 798728 | tf_op jit(solution)/shard_map/ppermute | solution.py:177
  73.5 6.3 %collective-permute-start.4 = (bf16[1024,128]{1,0:T(8,128)(2,1)S(1)}, bf16[1024,128]{1,0:T(8,128)(2,1)S(1)}, u32[]{:S(2)}, u32[]{:S(2)}) collective-permute-start(bf16[1024,128]{1,0:T(8,128)(2,1)S(1)} %get-tuple-element.47), channel_id=1, source_target_pairs={{0,4},{4,0},{8,12},{12,8},{16,20},{20,16},{24,28},{28,24},{1,5},{5... | collective-permute-start | bytes 786440 | tf_op jit(solution)/shard_map/ppermute | solution.py:163
  103.2 1.3 copy-start.8
  119.2 23.7 %copy-start.12 = (bf16[1040,128]{1,0:T(8,128)(2,1)S(1)}, bf16[1040,128]{1,0:T(8,128)(2,1)}, u32[]{:S(2)}) copy-start(bf16[1040,128]{1,0:T(8,128)(2,1)} %get-tuple-element.51) | copy-start | bytes 798724
  119.2 47.0 %copy-start = (bf16[1040,128]{1,0:T(8,128)(2,1)S(1)}, bf16[1040,128]{1,0:T(8,128)(2,1)}, u32[]{:S(2)}) copy-start(bf16[1040,128]{1,0:T(8,128)(2,1)} %get-tuple-element.57.refs_1_) | copy-start | bytes 798724
  119.2 120.6 %all-to-all-start.1 = ((bf16[8,1,1024,128]{3,2,1,0:T(8,128)(2,1)}), bf16[8,1,1024,128]{3,2,1,0:T(8,128)(2,1)S(1)}, u32[]{:S(2)}, u32[]{:S(2)}) async-start(bf16[8,1,1024,128]{3,2,1,0:T(8,128)(2,1)} %att_attend.1), calls=%async_computation.1 | async-start | bytes 4194304 | tf_op jit(solution)/shard_map/all_to_all | solution.py:315
  143.0 23.3 %collective-permute-start.5 = (bf16[1040,128]{1,0:T(8,128)(2,1)S(1)}, bf16[1040,128]{1,0:T(8,128)(2,1)S(1)}, u32[]{:S(2)}, u32[]{:S(2)}) collective-permute-start(bf16[1040,128]{1,0:T(8,128)(2,1)S(1)} %copy-done.12), channel_id=1, source_target_pairs={{0,4},{4,0},{8,12},{12,8},{16,20},{20,16},{24,28},{28,24},{1,5},{5... | collective-permute-start | bytes 798728 | tf_op jit(solution)/shard_map/ppermute | solution.py:163
  166.4 9.1 %collective-permute-start.6 = (bf16[1040,128]{1,0:T(8,128)(2,1)S(1)}, bf16[1040,128]{1,0:T(8,128)(2,1)S(1)}, u32[]{:S(2)}, u32[]{:S(2)}) collective-permute-start(bf16[1040,128]{1,0:T(8,128)(2,1)S(1)} %ssm_level.3), channel_id=1, source_target_pairs={{8,0},{12,4},{16,8},{20,12},{24,16},{28,20},{9,1},{13,5},{17,9},{2... | collective-permute-start | bytes 798728 | tf_op jit(solution)/shard_map/ppermute | solution.py:177
  167.7 45.1 %collective-permute-start.7 = (bf16[1040,128]{1,0:T(8,128)(2,1)S(1)}, bf16[1040,128]{1,0:T(8,128)(2,1)S(1)}, u32[]{:S(2)}, u32[]{:S(2)}) collective-permute-start(bf16[1040,128]{1,0:T(8,128)(2,1)S(1)} %ssm_level.3), channel_id=1, source_target_pairs={{16,0},{20,4},{24,8},{28,12},{17,1},{21,5},{25,9},{29,13},{18,2},{... | collective-permute-start | bytes 798728 | tf_op jit(solution)/shard_map/ppermute | solution.py:177
  169.0 43.8 %collective-permute-start.8 = (bf16[1040,128]{1,0:T(8,128)(2,1)S(1)}, bf16[1040,128]{1,0:T(8,128)(2,1)S(1)}, u32[]{:S(2)}, u32[]{:S(2)}) collective-permute-start(bf16[1040,128]{1,0:T(8,128)(2,1)S(1)} %ssm_level.3), channel_id=1, source_target_pairs={{24,0},{28,4},{25,1},{29,5},{26,2},{30,6},{27,3},{31,7}} | collective-permute-start | bytes 798728 | tf_op jit(solution)/shard_map/ppermute | solution.py:177
  213.8 10.1 %collective-permute-start.9 = (bf16[1024,128]{1,0:T(8,128)(2,1)S(1)}, bf16[1024,128]{1,0:T(8,128)(2,1)S(1)}, u32[]{:S(2)}, u32[]{:S(2)}) collective-permute-start(bf16[1024,128]{1,0:T(8,128)(2,1)S(1)} %get-tuple-element.60), channel_id=1, source_target_pairs={{0,4},{4,0},{8,12},{12,8},{16,20},{20,16},{24,28},{28,24},{1,5},{5... | collective-permute-start | bytes 786440 | tf_op jit(solution)/shard_map/ppermute | solution.py:163
  220.6 11.0 %copy-start.11 = (f32[256,128]{1,0:T(8,128)S(1)}, f32[256,128]{1,0:T(8,128)}, u32[]{:S(2)}) copy-start(f32[256,128]{1,0:T(8,128)} %get-tuple-element.65) | copy-start | bytes 393220
  220.6 10.9 %collective-permute-start.13 = (f32[256,128]{1,0:T(8,128)}, f32[256,128]{1,0:T(8,128)S(1)}, u32[]{:S(2)}, u32[]{:S(2)}) collective-permute-start(f32[256,128]{1,0:T(8,128)} %get-tuple-element.65), channel_id=1, source_target_pairs={{0,1},{1,2},{2,3},{3,0},{4,5},{5,6},{6,7},{7,4},{8,9},{9,10},{10,1... | collective-permute-start | bytes 393224 | tf_op jit(solution)/shard_map/ppermute | solution.py:310
  223.5 8.1 %collective-permute-start.14 = (f32[256,128]{1,0:T(8,128)}, f32[256,128]{1,0:T(8,128)S(1)}, u32[]{:S(2)}, u32[]{:S(2)}) collective-permute-start(f32[256,128]{1,0:T(8,128)} %get-tuple-element.65), channel_id=1, source_target_pairs={{0,2},{1,3},{2,0},{3,1},{4,6},{5,7},{6,4},{7,5},{8,10},{9,11},{10,... | collective-permute-start | bytes 393224 | tf_op jit(solution)/shard_map/ppermute | solution.py:310
  223.7 7.9 %collective-permute-start.15 = (f32[256,128]{1,0:T(8,128)}, f32[256,128]{1,0:T(8,128)S(1)}, u32[]{:S(2)}, u32[]{:S(2)}) collective-permute-start(f32[256,128]{1,0:T(8,128)} %get-tuple-element.65), channel_id=1, source_target_pairs={{0,3},{1,0},{2,1},{3,2},{4,7},{5,4},{6,5},{7,6},{8,11},{9,8},{10,9... | collective-permute-start | bytes 393224 | tf_op jit(solution)/shard_map/ppermute | solution.py:310
  228.8 4.6 %collective-permute-start.10 = (f32[256,128]{1,0:T(8,128)}, f32[256,128]{1,0:T(8,128)S(1)}, u32[]{:S(2)}, u32[]{:S(2)}) collective-permute-start(f32[256,128]{1,0:T(8,128)} %get-tuple-element.64), channel_id=1, source_target_pairs={{0,1},{1,2},{2,3},{3,0},{4,5},{5,6},{6,7},{7,4},{8,9},{9,10},{10,1... | collective-permute-start | bytes 393224 | tf_op jit(solution)/shard_map/ppermute | solution.py:310
  230.3 7.5 %collective-permute-start.11 = (f32[256,128]{1,0:T(8,128)}, f32[256,128]{1,0:T(8,128)S(1)}, u32[]{:S(2)}, u32[]{:S(2)}) collective-permute-start(f32[256,128]{1,0:T(8,128)} %get-tuple-element.64), channel_id=1, source_target_pairs={{0,2},{1,3},{2,0},{3,1},{4,6},{5,7},{6,4},{7,5},{8,10},{9,11},{10,... | collective-permute-start | bytes 393224 | tf_op jit(solution)/shard_map/ppermute | solution.py:310
  231.5 6.8 %collective-permute-start.12 = (f32[256,128]{1,0:T(8,128)}, f32[256,128]{1,0:T(8,128)S(1)}, u32[]{:S(2)}, u32[]{:S(2)}) collective-permute-start(f32[256,128]{1,0:T(8,128)} %get-tuple-element.64), channel_id=1, source_target_pairs={{0,3},{1,0},{2,1},{3,2},{4,7},{5,4},{6,5},{7,6},{8,11},{9,8},{10,9... | collective-permute-start | bytes 393224 | tf_op jit(solution)/shard_map/ppermute | solution.py:310
  (8 other events, 7.0 us)

commit v2 on v0

--- a/solution.py
+++ b/solution.py
@@ -18,15 +18,20 @@
 VMEM_BYTES = 56 * 1024 * 1024
 
 
-def call(kernel, out_shape, *operands, scratch=(), flops=0, name=None):
+VMEM = pl.BlockSpec(memory_space=pltpu.VMEM)
+SMEM = pl.BlockSpec(memory_space=pltpu.SMEM)
+SMALL = 16 * 1024 * 1024
+
+
+def call(kernel, out_shape, *operands, specs=None, scratch=(), flops=0, vmem=VMEM_BYTES, name=None):
     moved = sum(a.size * a.dtype.itemsize for a in jax.tree.leaves((operands, out_shape)))
     return pl.pallas_call(
         kernel,
         out_shape=out_shape,
-        in_specs=[pl.BlockSpec(memory_space=pltpu.VMEM)] * len(operands),
-        out_specs=jax.tree.map(lambda _: pl.BlockSpec(memory_space=pltpu.VMEM), out_shape),
+        in_specs=specs or [VMEM] * len(operands),
+        out_specs=jax.tree.map(lambda _: VMEM, out_shape),
         scratch_shapes=scratch,
-        compiler_params=pltpu.CompilerParams(vmem_limit_bytes=VMEM_BYTES),
+        compiler_params=pltpu.CompilerParams(vmem_limit_bytes=vmem),
         cost_estimate=pl.CostEstimate(flops=flops, bytes_accessed=moved, transcendentals=0),
         name=name,
     )(*operands)
@@ -106,7 +111,7 @@
         state = jnp.zeros((step, 128), F32)
         for c in range(parts)[:: -1 if backward else 1]:
             out_ref[c, here, :] = state.astype(BF16)
-            tail = tail_ref[c].astype(F32)
+            tail = tail_ref[c, rows:, :].astype(F32)
             factor = tail[2 * k : 2 * k + 1, :] + tail[2 * k + 1 : 2 * k + 2, :]
             state = factor * state + in_ref[c, here, :].astype(F32)
 
@@ -219,29 +224,46 @@
     write_ref[...] = write
 
 
+def pass_block(block, n):
+    if n == 0:
+        return block
+    return lax.ppermute(block, "ctx", [(i, i ^ n) for i in range(lax.axis_size("ctx"))])
+
+
 def exchange(blocks):
     return lax.all_to_all(blocks, "ctx", 0, 0)
 
 
-def pack_kernel(marks_ref, q_ref, k_ref, v_ref, g_ref, out_ref):
-    parts, per = out_ref.shape[:2]
+def pack_kernel(me_ref, marks_ref, q_ref, k_ref, v_ref, g_ref, *out_refs):
     length = q_ref.shape[0]
-    for part in range(parts):
-        for a in range(per):
-            here = cols(part * per + a)
+    for n, out_ref in enumerate(out_refs):
+        for a in range(out_ref.shape[0]):
+            head = (me_ref[0] ^ n) * out_ref.shape[0] + a
+            here = pl.ds(pl.multiple_of(head * ATT_DIM, ATT_DIM), ATT_DIM)
             for place, ref in enumerate((q_ref, k_ref, v_ref, g_ref)):
-                out_ref[part, a, place * length : (place + 1) * length, :] = ref[:, here]
-            out_ref[part, a, 4 * length :, :] = marks_ref[...]
-
-
-def unpack_kernel(in_ref, *out_refs):
-    parts, per = in_ref.shape[:2]
-    length = in_ref.shape[2] // 4
-    for part in range(parts):
-        for a in range(per):
-            here = cols(part * per + a)
+                out_ref[a, place * length : (place + 1) * length, :] = ref[:, here]
+            out_ref[a, 4 * length :, :] = marks_ref[...]
+
+
+def unpack_kernel(me_ref, *refs):
+    in_refs, out_refs = refs[:-4], refs[-4:]
+    length = out_refs[0].shape[0]
+    for n, in_ref in enumerate(in_refs):
+        for a in range(in_ref.shape[0]):
+            head = (me_ref[0] ^ n) * in_ref.shape[0] + a
+            here = pl.ds(pl.multiple_of(head * ATT_DIM, ATT_DIM), ATT_DIM)
             for place, ref in enumerate(out_refs):
-                ref[:, here] = in_ref[part, a, place * length : (place + 1) * length, :]
+                ref[:, here] = in_ref[a, place * length : (place + 1) * length, :]
+
+
+def attend_blocks(length, parts, me_ref, *refs):
+    in_refs, out_refs = refs[:parts], refs[parts : 2 * parts]
+    all_in, all_out = refs[2 * parts : 2 * parts + 2]
+    for n in range(parts):
+        all_in[me_ref[0] ^ n] = in_refs[n][...]
+    attend_kernel(length, all_in, all_out, *refs[2 * parts + 2 :])
+    for n in range(parts):
+        out_refs[n][...] = all_out[me_ref[0] ^ n]
 
 
 def attend_kernel(length, in_ref, out_ref, expo_ref, kt_ref, vt_ref, dk_ref, dv_ref):
@@ -456,7 +478,9 @@
     att_width = att_queries.shape[1]
     per = att_width // ATT_DIM // parts
     dealt = att_width // ATT_DIM % parts == 0
-    rel = (doc_start - lax.axis_index("ctx") * length).reshape(1, length)
+    place = lax.axis_index("ctx")
+    rel = (doc_start - place * length).reshape(1, length)
+    me = place.reshape(1).astype(jnp.int32)
 
     sent, lcol, lrow = call(
         first_kernel,
@@ -467,26 +491,39 @@
         ),
         log_decay.T, rel, write_map, ssm_input, flops=work // 2, name="ssm_first",
     )
-    got = exchange(sent)
-    tail = got[:, rows:, :]
-    carried = call(
-        lambda *refs: carry_kernel(False, *refs), shape((parts, rows, 128), BF16), tail, got,
-        name="ssm_carry",
-    )
-    state = exchange(carried).reshape(width, 128)
-
     if dealt:
         marks = doc_start.reshape(length // 128, 128)
         marks = jnp.stack([marks // 128, marks % 128], axis=1).reshape(length // 64, 128)
         marks = jnp.pad(marks, ((0, TAIL - length // 64), (0, 0))).astype(BF16)
+        marks, sent = lax.optimization_barrier((marks, sent))
         packed = call(
-            pack_kernel, shape((parts, per, 4 * length + TAIL, 128), BF16),
-            marks, att_queries, att_keys, att_values, att_grad, name="att_pack",
-        )
-        packed, state = lax.optimization_barrier((packed, state))
-        att_got = exchange(packed)
+            pack_kernel, [shape((per, 4 * length + TAIL, 128), BF16)] * parts,
+            me, marks, att_queries, att_keys, att_values, att_grad,
+            specs=[SMEM] + [VMEM] * 5, vmem=SMALL, name="att_pack",
+        )
+        half = parts // 2
+        order = [half] + list(range(1, half)) + list(range(half + 1, parts))
+        early, middle, late = order[:half], order[half:-1], order[-1:]
+        att_got = {0: packed[0]}
+        for n in early:
+            att_got[n] = pass_block(packed[n], n)
     else:
         att_out = ring_attention(att_queries, att_keys, att_values, att_grad, doc_start)
+    got = exchange(sent)
+    first_got = got
+    carried = call(
+        lambda in_ref, out_ref: carry_kernel(False, in_ref, in_ref, out_ref),
+        shape((parts, rows, 128), BF16), got, vmem=SMALL, name="ssm_carry",
+    )
+    state = exchange(carried).reshape(width, 128)
+
+    if dealt:
+        held, done, state = lax.optimization_barrier(
+            ([packed[n] for n in middle], [att_got[n] for n in early], state)
+        )
+        att_got.update(zip(early, done))
+        for n, block in zip(middle, held):
+            att_got[n] = pass_block(block, n)
 
     mixed, sums = call(
         mix_kernel,
@@ -507,19 +544,29 @@
     )
 
     if dealt:
-        sent, att_got = lax.optimization_barrier((sent, att_got))
+        held, done, sent = lax.optimization_barrier(
+            ([packed[n] for n in late], [att_got[n] for n in middle], sent)
+        )
+        att_got.update(zip(middle, done))
+        for n, block in zip(late, held):
+            att_got[n] = pass_block(block, n)
     got = exchange(sent)
     carried = call(
-        lambda *refs: carry_kernel(True, *refs), shape((parts, rows, 128), BF16), tail, got,
-        name="ssm_carry_back",
+        lambda *refs: carry_kernel(True, *refs), shape((parts, rows, 128), BF16), first_got, got,
+        vmem=SMALL, name="ssm_carry_back",
     )
     back = exchange(carried).reshape(width, 128)
     if dealt:
+        last_got, carried = lax.optimization_barrier((att_got[parts - 1], carried))
+        att_got[parts - 1] = last_got
         att_done = call(
-            lambda *refs: attend_kernel(length, *refs),
-            shape((parts, per, 4 * length, 128), BF16),
-            att_got,
+            lambda *refs: attend_blocks(length, parts, *refs),
+            [shape((per, 4 * length, 128), BF16)] * parts,
+            me, *[att_got[n] for n in range(parts)],
+            specs=[SMEM] + [VMEM] * parts,
             scratch=[
+                pltpu.VMEM((parts, per, 4 * length + TAIL, 128), BF16),
+                pltpu.VMEM((parts, per, 4 * length, 128), BF16),
                 pltpu.VMEM((parts, length, length), F32),
                 pltpu.VMEM((parts, ATT_DIM, length), BF16),
                 pltpu.VMEM((parts, ATT_DIM, length), BF16),
@@ -530,8 +577,9 @@
         )
         att_done, back = lax.optimization_barrier((att_done, back))
         att_out = call(
-            unpack_kernel, (shape((length, att_width), BF16),) * 4, exchange(att_done),
-            name="att_unpack",
+            unpack_kernel, (shape((length, att_width), BF16),) * 4,
+            me, *[pass_block(block, n) for n, block in enumerate(att_done)],
+            specs=[SMEM] + [VMEM] * parts, vmem=SMALL, name="att_unpack",
         )
 
     gin, read_part, write_part = call(

time: 200 us -> 201 us (level)
  starting transfers between devices: 17.4 us -> 46.8 us
  waiting for transfers between devices: 57.6 us -> 35.9 us
  Pallas kernels: 49 us -> 43.1 us
  local copies, waits for them, and re-layouts: 4.34 us -> 1.46 us
  blocking collectives: 65.6 us -> 68.3 us
    all_to_all x4 -> x2, waiting for transfers between devices: 57.6 us -> 0.01 us  [exchange(): return lax.all_to_all(blocks, 'ctx', 0, 0)]
    ppermute x0 -> x14, starting transfers between devices: none -> 38.6 us  [pass_block(): lax.ppermute(block, 'ctx', [(i, i ^ n) for i in range(lax.axis_size('ctx'...]
    ppermute x0 -> x14, waiting for transfers between devices: none -> 35.9 us  [pass_block(): lax.ppermute(block, 'ctx', [(i, i ^ n) for i in range(lax.axis_size('ctx'...]
    all_to_all x4 -> x2, starting transfers between devices: 17.4 us -> 8.23 us  [exchange(): return lax.all_to_all(blocks, 'ctx', 0, 0)]
    pallas_call x10, Pallas kernels: 49 us -> 43.1 us  [call(): pl.pallas_call(kernel, out_shape=out_shape, in_specs=specs or [VMEM] * le...]
  transfers between devices with their start and end apart: 4 -> 16, of which waited for: 3 -> 3; matrix products, arithmetic and copies ran while one was open for 0% -> 0% of each run, Pallas kernels for 20% -> 18%
where the time goes in v2:
time: 201 us; the launch traced here: 198 us
  blocking collectives  68.3 us (34%)
  starting transfers between devices  46.8 us (23%)
  Pallas kernels  43.1 us (21%)
  waiting for transfers between devices  35.9 us (18%)
    all_to_all x2, blocking collectives, exchange(): return lax.all_to_all(blocks, 'ctx', 0, 0)  43.2 us
    pallas_call x10, Pallas kernels, call(): pl.pallas_call(kernel, out_shape=out_shape, in_specs=specs or [VMEM] * le...  43.1 us
    ppermute x14, starting transfers between devices, pass_block(): lax.ppermute(block, 'ctx', [(i, i ^ n) for i in range(lax.axis_size('ctx'...  38.6 us
    ppermute x14, waiting for transfers between devices, pass_block(): lax.ppermute(block, 'ctx', [(i, i ^ n) for i in range(lax.axis_size('ctx'...  35.9 us
    psum x1, blocking collectives, body(): write_sum, read_sum = lax.psum((write_part, read_part), 'head')  17.5 us
    all_to_all x2, starting transfers between devices, exchange(): return lax.all_to_all(blocks, 'ctx', 0, 0)  8.23 us
    psum x1, blocking collectives, body(): sums = lax.psum(sums, 'head')  7.51 us
  transfers between devices with their start and end apart: 16, of which 3 were waited for; matrix products, arithmetic and copies ran while one was open for 0% of the time, Pallas kernels for 18%

profile of v2, /device:TPU:1, one launch (start us, length us, event | category | flops | bytes accessed | tf_op | source)
XLA Modules:
  0.0 198.3 jit_solution(5328730106254354152)
XLA Ops:
  0.6 1.3 broadcast_subtract_fusion
  2.7 3.1 %ssm_first.1 = (bf16[8,272,128]{2,1,0:T(8,128)(2,1)}, f32[256,16]{1,0:T(8,128)}, f32[16,256]{1,0:T(8,128)}) custom-call(f32[16,256]{1,0:T(8,128)} %bitcast.13, s32[1,256]{1,0:T(1,128)} %bitcast.8, bf16[256,128]{1,0:T(8,128)(2,1)} %w_ref.7, bf16[256,2048]{1,0:T(8,128)(2,1)} %x_ref.7), custom_call_target="tpu_custom_call" | custom-call | flops 134217728 | bytes 1721344 | tf_op jit(solution)/shard_map/ssm_first/pallas_call | solution.py:28
  5.8 21.7 %all_to_all.20.in_ref.refs_0_ = bf16[8,272,128]{2,1,0:T(8,128)(2,1)S(1)} all-to-all(bf16[8,272,128]{2,1,0:T(8,128)(2,1)} %get-tuple-element.76), channel_id=1, replica_groups=mesh['ctx'=8,'head'=4] {'ctx'}, dimensions={0} | all-to-all | bytes 1114112 | tf_op jit(solution)/shard_map/all_to_all | solution.py:234
  28.4 4.1 %all-to-all-start.1 = ((bf16[8,256,128]{2,1,0:T(8,128)(2,1)}), bf16[8,256,128]{2,1,0:T(8,128)(2,1)}, u32[]{:S(2)}, u32[]{:S(2)}) async-start(bf16[8,256,128]{2,1,0:T(8,128)(2,1)} %ssm_carry.1), calls=%async_computation.1 | async-start | bytes 1048576 | tf_op jit(solution)/shard_map/all_to_all | solution.py:234
  33.8 2.2 %collective-permute-start = (bf16[1,1040,128]{2,1,0:T(8,128)(2,1)S(1)}, bf16[1,1040,128]{2,1,0:T(8,128)(2,1)S(1)}, u32[]{:S(2)}, u32[]{:S(2)}) collective-permute-start(bf16[1,1040,128]{2,1,0:T(8,128)(2,1)S(1)} %get-tuple-element.72), channel_id=1, source_target_pairs={{0,16},{4,20},{8,24},{12,28},{16,0},{20,4},{24,8},{28,12},{1,17},{... | collective-permute-start | bytes 798728 | tf_op jit(solution)/shard_map/ppermute | solution.py:230
  38.7 18.5 %collective-permute-done.refs_5_ = bf16[1,1040,128]{2,1,0:T(8,128)(2,1)S(1)} collective-permute-done((bf16[1,1040,128]{2,1,0:T(8,128)(2,1)S(1)}, bf16[1,1040,128]{2,1,0:T(8,128)(2,1)S(1)}, u32[]{:S(2)}, u32[]{:S(2)}) %collective-permute-start) | collective-permute-done | bytes 266272 | tf_op jit(solution)/shard_map/ppermute | solution.py:230
  57.2 3.5 %collective-permute-done.3.refs_4_ = bf16[1,1040,128]{2,1,0:T(8,128)(2,1)S(1)} collective-permute-done((bf16[1,1040,128]{2,1,0:T(8,128)(2,1)S(1)}, bf16[1,1040,128]{2,1,0:T(8,128)(2,1)S(1)}, u32[]{:S(2)}, u32[]{:S(2)}) %collective-permute-start.3) | collective-permute-done | bytes 266272 | tf_op jit(solution)/shard_map/ppermute | solution.py:230
  61.7 1.4 collective-permute-start.5
  63.1 5.8 %ssm_mix.1 = (f32[256,2048]{1,0:T(8,128)}, f32[8,256]{1,0:T(8,128)}) custom-call(bf16[256,2048]{1,0:T(8,128)(2,1)} %x_ref.7, bf16[256,2048]{1,0:T(8,128)(2,1)} %refs_2_.1, bf16[256,2048]{1,0:T(8,128)(2,1)} %refs_3_.1, bf16[256,128]{1,0:T(8,128)(2,1)} %w_ref.7, bf16[256,128]{1,0:T(8,128)(2,1)} %r_ref.3, s32[1,256]{1,0:T(1,128)} %bitcast.9, ...), custom_call_target="tpu_custom_call" | custom-call | flops 402653184 | bytes 5940224 | tf_op jit(solution)/shard_map/ssm_mix/pallas_call | solution.py:28
  68.9 7.5 %psum.21.refs_0_ = f32[8,256]{1,0:T(8,128)} all-reduce(f32[8,256]{1,0:T(8,128)} %get-tuple-element.78), channel_id=1, replica_groups=mesh['ctx'=8,'head'=4] {'head'}, use_global_device_ids=true, to_apply=%region_0.1 | all-reduce | flops 2048 | bytes 16384 | tf_op jit(solution)/shard_map/psum | solution.py:534
  76.4 5.9 %ssm_gate.1 = (bf16[256,2048]{1,0:T(8,128)(2,1)}, bf16[256,2048]{1,0:T(8,128)(2,1)}, bf16[256,2048]{1,0:T(8,128)(2,1)}, bf16[8,256,128]{2,1,0:T(8,128)(2,1)}) custom-call(f32[8,256]{1,0:T(8,128)} %psum.21.refs_0_, f32[256,2048]{1,0:T(8,128)} %get-tuple-element.79.refs_1_, bf16[256,2048]{1,0:T(8,128)(2,1)} %refs_2_.1, bf16[256,2048]{1,0:T(8,128)(2,1)} %refs_3_.1, ...), custom_call_target="tpu_custom_call" | custom-call | flops 134217728 | bytes 7955456 | tf_op jit(solution)/shard_map/ssm_gate/pallas_call | solution.py:28
  82.3 21.6 %all_to_all.21.refs_1_ = bf16[8,256,128]{2,1,0:T(8,128)(2,1)S(1)} all-to-all(bf16[8,256,128]{2,1,0:T(8,128)(2,1)} %get-tuple-element.93), channel_id=1, replica_groups=mesh['ctx'=8,'head'=4] {'ctx'}, dimensions={0} | all-to-all | bytes 1048576 | tf_op jit(solution)/shard_map/all_to_all | solution.py:234
  104.8 4.1 %all-to-all-start.3 = ((bf16[8,256,128]{2,1,0:T(8,128)(2,1)}), bf16[8,256,128]{2,1,0:T(8,128)(2,1)S(1)}, u32[]{:S(2)}, u32[]{:S(2)}) async-start(bf16[8,256,128]{2,1,0:T(8,128)(2,1)} %ssm_carry_back.1), calls=%async_computation.3 | async-start | bytes 1048576 | tf_op jit(solution)/shard_map/all_to_all | solution.py:234
  108.9 4.2 %collective-permute-start.6 = (bf16[1,1040,128]{2,1,0:T(8,128)(2,1)S(1)}, bf16[1,1040,128]{2,1,0:T(8,128)(2,1)S(1)}, u32[]{:S(2)}, u32[]{:S(2)}) collective-permute-start(bf16[1,1040,128]{2,1,0:T(8,128)(2,1)S(1)} %get-tuple-element.92), channel_id=1, source_target_pairs={{0,28},{4,24},{8,20},{12,16},{16,12},{20,8},{24,4},{28,0},{1,29},{... | collective-permute-start | bytes 798728 | tf_op jit(solution)/shard_map/ppermute | solution.py:230
  113.1 13.8 %collective-permute-done.6.refs_8_ = bf16[1,1040,128]{2,1,0:T(8,128)(2,1)S(1)} collective-permute-done((bf16[1,1040,128]{2,1,0:T(8,128)(2,1)S(1)}, bf16[1,1040,128]{2,1,0:T(8,128)(2,1)S(1)}, u32[]{:S(2)}, u32[]{:S(2)}) %collective-permute-start.6) | collective-permute-done | bytes 266272 | tf_op jit(solution)/shard_map/ppermute | solution.py:230
  127.6 14.8 %att_attend.1 = (bf16[1,1024,128]{2,1,0:T(8,128)(2,1)}, bf16[1,1024,128]{2,1,0:T(8,128)(2,1)}, bf16[1,1024,128]{2,1,0:T(8,128)(2,1)}, bf16[1,1024,128]{2,1,0:T(8...) custom-call(s32[1]{0:T(128)} %bitcast.2.me_ref.refs_0_, ...), custom_call_target="tpu_custom_call" | custom-call | flops 3221225472 | bytes 4227076 | tf_op jit(solution)/shard_map/att_attend/pallas_call | solution.py:28
  142.7 8.4 %collective-permute-start.8 = (bf16[1,1024,128]{2,1,0:T(8,128)(2,1)}, bf16[1,1024,128]{2,1,0:T(8,128)(2,1)S(1)}, u32[]{:S(2)}, u32[]{:S(2)}) collective-permute-start(bf16[1,1024,128]{2,1,0:T(8,128)(2,1)} %get-tuple-element.105), channel_id=1, source_target_pairs={{0,8},{4,12},{8,0},{12,4},{16,24},{20,28},{24,16},{28,20},{1,9},{5... | collective-permute-start | bytes 786440 | tf_op jit(solution)/shard_map/ppermute | solution.py:230
  152.1 2.3 %collective-permute-start.10 = (bf16[1,1024,128]{2,1,0:T(8,128)(2,1)}, bf16[1,1024,128]{2,1,0:T(8,128)(2,1)S(1)}, u32[]{:S(2)}, u32[]{:S(2)}) collective-permute-start(bf16[1,1024,128]{2,1,0:T(8,128)(2,1)} %get-tuple-element.107), channel_id=1, source_target_pairs={{0,16},{4,20},{8,24},{12,28},{16,0},{20,4},{24,8},{28,12},{1,17},{... | collective-permute-start | bytes 786440 | tf_op jit(solution)/shard_map/ppermute | solution.py:230
  154.5 2.0 %collective-permute-start.12 = (bf16[1,1024,128]{2,1,0:T(8,128)(2,1)}, bf16[1,1024,128]{2,1,0:T(8,128)(2,1)S(1)}, u32[]{:S(2)}, u32[]{:S(2)}) collective-permute-start(bf16[1,1024,128]{2,1,0:T(8,128)(2,1)} %get-tuple-element.109), channel_id=1, source_target_pairs={{0,24},{4,28},{8,16},{12,20},{16,8},{20,12},{24,0},{28,4},{1,25},{... | collective-permute-start | bytes 786440 | tf_op jit(solution)/shard_map/ppermute | solution.py:230
  156.5 13.0 %collective-permute-start.13 = (bf16[1,1024,128]{2,1,0:T(8,128)(2,1)}, bf16[1,1024,128]{2,1,0:T(8,128)(2,1)S(1)}, u32[]{:S(2)}, u32[]{:S(2)}) collective-permute-start(bf16[1,1024,128]{2,1,0:T(8,128)(2,1)} %get-tuple-element.110), channel_id=1, source_target_pairs={{0,28},{4,24},{8,20},{12,16},{16,12},{20,8},{24,4},{28,0},{1,29},{... | collective-permute-start | bytes 786440 | tf_op jit(solution)/shard_map/ppermute | solution.py:230
  169.6 5.1 %ssm_inner.1 = (f32[256,2048]{1,0:T(8,128)}, f32[256,128]{1,0:T(8,128)}, f32[256,128]{1,0:T(8,128)}) custom-call(bf16[256,2048]{1,0:T(8,128)(2,1)} %get-tuple-element.112.dmixed_ref, bf16[256,2048]{1,0:T(8,128)(2,1)} %x_ref.7, bf16[256,128]{1,0:T(8,128)(2,1)} %w_ref.7, bf16[256,128]{1,0:T(8,128)(2,1)} %r_ref.3, s32[1,256]{1,0:T(1,128)} %bitcast.11, ...), custom_call_target="tpu_custom_call" | custom-call | flops 671088640 | bytes 5145600 | tf_op jit(solution)/shard_map/ssm_inner/pallas_call | solution.py:28
  174.7 4.1 %ssm_last.1 = (bf16[256,2048]{1,0:T(8,128)(2,1)}, f32[256,128]{1,0:T(8,128)}) custom-call(f32[256,2048]{1,0:T(8,128)} %get-tuple-element.113.gin_ref, bf16[256,2048]{1,0:T(8,128)(2,1)} %x_ref.7, bf16[256,128]{1,0:T(8,128)(2,1)} %w_ref.7, s32[1,256]{1,0:T(1,128)} %bitcast.12, f32[256,16]{1,0:T(8,128)} %get-tuple-element.66.lcol_ref, ...), custom_call_target="tpu_custom_call" | custom-call | flops 268435456 | bytes 5063680 | tf_op jit(solution)/shard_map/ssm_last/pallas_call | solution.py:28
  178.8 17.5 %all-reduce.3 = (bf16[256,128]{1,0:T(8,128)(2,1)}, bf16[256,128]{1,0:T(8,128)(2,1)}) all-reduce(f32[256,128]{1,0:T(8,128)} %get-tuple-element.118, f32[256,128]{1,0:T(8,128)S(1)} %copy-done.7), channel_id=1, replica_groups=mesh['ctx'=8,'head'=4] {'head'}, use_global_device_ids=true, to_apply=%region_1.2 | all-reduce | flops 65536 | bytes 393216 | tf_op jit(solution)/shard_map/psum | solution.py:596
  196.4 1.9 att_unpack.1
  (57 shorter events, 9.6 us)
Async XLA Ops:
  2.6 29.9 %copy-start = (bf16[256,1024]{1,0:T(8,128)(2,1)S(1)}, bf16[256,1024]{1,0:T(8,128)(2,1)}, u32[]{:S(2)}) copy-start(bf16[256,1024]{1,0:T(8,128)(2,1)} %q_ref.1) | copy-start | bytes 1572868
  2.6 29.9 %copy-start.1 = (bf16[256,1024]{1,0:T(8,128)(2,1)S(1)}, bf16[256,1024]{1,0:T(8,128)(2,1)}, u32[]{:S(2)}) copy-start(bf16[256,1024]{1,0:T(8,128)(2,1)} %k_ref.1) | copy-start | bytes 1572868
  2.7 29.9 %copy-start.2 = (bf16[256,1024]{1,0:T(8,128)(2,1)S(1)}, bf16[256,1024]{1,0:T(8,128)(2,1)}, u32[]{:S(2)}) copy-start(bf16[256,1024]{1,0:T(8,128)(2,1)} %v_ref.1) | copy-start | bytes 1572868
  2.7 29.9 %copy-start.3 = (bf16[256,1024]{1,0:T(8,128)(2,1)S(1)}, bf16[256,1024]{1,0:T(8,128)(2,1)}, u32[]{:S(2)}) copy-start(bf16[256,1024]{1,0:T(8,128)(2,1)} %g_ref.1) | copy-start | bytes 1572868
  28.4 32.4 %all-to-all-start.1 = ((bf16[8,256,128]{2,1,0:T(8,128)(2,1)}), bf16[8,256,128]{2,1,0:T(8,128)(2,1)}, u32[]{:S(2)}, u32[]{:S(2)}) async-start(bf16[8,256,128]{2,1,0:T(8,128)(2,1)} %ssm_carry.1), calls=%async_computation.1 | async-start | bytes 1048576 | tf_op jit(solution)/shard_map/all_to_all | solution.py:234
  33.8 23.3 %collective-permute-start = (bf16[1,1040,128]{2,1,0:T(8,128)(2,1)S(1)}, bf16[1,1040,128]{2,1,0:T(8,128)(2,1)S(1)}, u32[]{:S(2)}, u32[]{:S(2)}) collective-permute-start(bf16[1,1040,128]{2,1,0:T(8,128)(2,1)S(1)} %get-tuple-element.72), channel_id=1, source_target_pairs={{0,16},{4,20},{8,24},{12,28},{16,0},{20,4},{24,8},{28,12},{1,17},{... | collective-permute-start | bytes 798728 | tf_op jit(solution)/shard_map/ppermute | solution.py:230
  36.1 21.1 %collective-permute-start.1 = (bf16[1,1040,128]{2,1,0:T(8,128)(2,1)S(1)}, bf16[1,1040,128]{2,1,0:T(8,128)(2,1)S(1)}, u32[]{:S(2)}, u32[]{:S(2)}) collective-permute-start(bf16[1,1040,128]{2,1,0:T(8,128)(2,1)S(1)} %get-tuple-element.73), channel_id=1, source_target_pairs={{0,4},{4,0},{8,12},{12,8},{16,20},{20,16},{24,28},{28,24},{1,5},{5... | collective-permute-start | bytes 798728 | tf_op jit(solution)/shard_map/ppermute | solution.py:230
  37.3 19.9 %collective-permute-start.2 = (bf16[1,1040,128]{2,1,0:T(8,128)(2,1)S(1)}, bf16[1,1040,128]{2,1,0:T(8,128)(2,1)S(1)}, u32[]{:S(2)}, u32[]{:S(2)}) collective-permute-start(bf16[1,1040,128]{2,1,0:T(8,128)(2,1)S(1)} %get-tuple-element.74), channel_id=1, source_target_pairs={{0,8},{4,12},{8,0},{12,4},{16,24},{20,28},{24,16},{28,20},{1,9},{5... | collective-permute-start | bytes 798728 | tf_op jit(solution)/shard_map/ppermute | solution.py:230
  38.5 22.3 %collective-permute-start.3 = (bf16[1,1040,128]{2,1,0:T(8,128)(2,1)S(1)}, bf16[1,1040,128]{2,1,0:T(8,128)(2,1)S(1)}, u32[]{:S(2)}, u32[]{:S(2)}) collective-permute-start(bf16[1,1040,128]{2,1,0:T(8,128)(2,1)S(1)} %get-tuple-element.75), channel_id=1, source_target_pairs={{0,12},{4,8},{8,4},{12,0},{16,28},{20,24},{24,20},{28,16},{1,13},{... | collective-permute-start | bytes 798728 | tf_op jit(solution)/shard_map/ppermute | solution.py:230
  57.2 25.1 %copy-start.8 = (bf16[1,1040,128]{2,1,0:T(8,128)(2,1)}, bf16[1,1040,128]{2,1,0:T(8,128)(2,1)S(1)}, u32[]{:S(2)}) copy-start(bf16[1,1040,128]{2,1,0:T(8,128)(2,1)S(1)} %collective-permute-done.refs_5_) | copy-start | bytes 798724
  57.2 25.1 %copy-start.9 = (bf16[1,1040,128]{2,1,0:T(8,128)(2,1)}, bf16[1,1040,128]{2,1,0:T(8,128)(2,1)S(1)}, u32[]{:S(2)}) copy-start(bf16[1,1040,128]{2,1,0:T(8,128)(2,1)S(1)} %collective-permute-done.1.refs_2_) | copy-start | bytes 798724
  60.8 21.6 %collective-permute-start.4 = (bf16[1,1040,128]{2,1,0:T(8,128)(2,1)S(1)}, bf16[1,1040,128]{2,1,0:T(8,128)(2,1)S(1)}, u32[]{:S(2)}, u32[]{:S(2)}) collective-permute-start(bf16[1,1040,128]{2,1,0:T(8,128)(2,1)S(1)} %get-tuple-element.87), channel_id=1, source_target_pairs={{0,20},{4,16},{8,28},{12,24},{16,4},{20,0},{24,12},{28,8},{1,21},{... | collective-permute-start | bytes 798728 | tf_op jit(solution)/shard_map/ppermute | solution.py:230
  61.7 20.6 %collective-permute-start.5 = (bf16[1,1040,128]{2,1,0:T(8,128)(2,1)S(1)}, bf16[1,1040,128]{2,1,0:T(8,128)(2,1)S(1)}, u32[]{:S(2)}, u32[]{:S(2)}) collective-permute-start(bf16[1,1040,128]{2,1,0:T(8,128)(2,1)S(1)} %get-tuple-element.88), channel_id=1, source_target_pairs={{0,24},{4,28},{8,16},{12,20},{16,8},{20,12},{24,0},{28,4},{1,25},{... | collective-permute-start | bytes 798728 | tf_op jit(solution)/shard_map/ppermute | solution.py:230
  82.3 44.6 %copy-start.12 = (bf16[1,1040,128]{2,1,0:T(8,128)(2,1)}, bf16[1,1040,128]{2,1,0:T(8,128)(2,1)S(1)}, u32[]{:S(2)}) copy-start(bf16[1,1040,128]{2,1,0:T(8,128)(2,1)S(1)} %collective-permute-done.4.refs_6_) | copy-start | bytes 798724
  104.8 37.5 %all-to-all-start.3 = ((bf16[8,256,128]{2,1,0:T(8,128)(2,1)}), bf16[8,256,128]{2,1,0:T(8,128)(2,1)S(1)}, u32[]{:S(2)}, u32[]{:S(2)}) async-start(bf16[8,256,128]{2,1,0:T(8,128)(2,1)} %ssm_carry_back.1), calls=%async_computation.3 | async-start | bytes 1048576 | tf_op jit(solution)/shard_map/all_to_all | solution.py:234
  108.9 18.0 %collective-permute-start.6 = (bf16[1,1040,128]{2,1,0:T(8,128)(2,1)S(1)}, bf16[1,1040,128]{2,1,0:T(8,128)(2,1)S(1)}, u32[]{:S(2)}, u32[]{:S(2)}) collective-permute-start(bf16[1,1040,128]{2,1,0:T(8,128)(2,1)S(1)} %get-tuple-element.92), channel_id=1, source_target_pairs={{0,28},{4,24},{8,20},{12,16},{16,12},{20,8},{24,4},{28,0},{1,29},{... | collective-permute-start | bytes 798728 | tf_op jit(solution)/shard_map/ppermute | solution.py:230
  142.4 32.3 %copy-start.6 = (bf16[8,256,128]{2,1,0:T(8,128)(2,1)}, bf16[8,256,128]{2,1,0:T(8,128)(2,1)S(1)}, u32[]{:S(2)}) copy-start(bf16[8,256,128]{2,1,0:T(8,128)(2,1)S(1)} %all-to-all-done.3) | copy-start | bytes 1572868
  142.4 12.1 %collective-permute-start.7 = (bf16[1,1024,128]{2,1,0:T(8,128)(2,1)}, bf16[1,1024,128]{2,1,0:T(8,128)(2,1)S(1)}, u32[]{:S(2)}, u32[]{:S(2)}) collective-permute-start(bf16[1,1024,128]{2,1,0:T(8,128)(2,1)} %get-tuple-element.104), channel_id=1, source_target_pairs={{0,4},{4,0},{8,12},{12,8},{16,20},{20,16},{24,28},{28,24},{1,5},{5... | collective-permute-start | bytes 786440 | tf_op jit(solution)/shard_map/ppermute | solution.py:230
  142.7 13.9 %collective-permute-start.8 = (bf16[1,1024,128]{2,1,0:T(8,128)(2,1)}, bf16[1,1024,128]{2,1,0:T(8,128)(2,1)S(1)}, u32[]{:S(2)}, u32[]{:S(2)}) collective-permute-start(bf16[1,1024,128]{2,1,0:T(8,128)(2,1)} %get-tuple-element.105), channel_id=1, source_target_pairs={{0,8},{4,12},{8,0},{12,4},{16,24},{20,28},{24,16},{28,20},{1,9},{5... | collective-permute-start | bytes 786440 | tf_op jit(solution)/shard_map/ppermute | solution.py:230
  151.0 45.3 %collective-permute-start.9 = (bf16[1,1024,128]{2,1,0:T(8,128)(2,1)}, bf16[1,1024,128]{2,1,0:T(8,128)(2,1)S(1)}, u32[]{:S(2)}, u32[]{:S(2)}) collective-permute-start(bf16[1,1024,128]{2,1,0:T(8,128)(2,1)} %get-tuple-element.106), channel_id=1, source_target_pairs={{0,12},{4,8},{8,4},{12,0},{16,28},{20,24},{24,20},{28,16},{1,13},{... | collective-permute-start | bytes 786440 | tf_op jit(solution)/shard_map/ppermute | solution.py:230
  152.1 44.2 %collective-permute-start.10 = (bf16[1,1024,128]{2,1,0:T(8,128)(2,1)}, bf16[1,1024,128]{2,1,0:T(8,128)(2,1)S(1)}, u32[]{:S(2)}, u32[]{:S(2)}) collective-permute-start(bf16[1,1024,128]{2,1,0:T(8,128)(2,1)} %get-tuple-element.107), channel_id=1, source_target_pairs={{0,16},{4,20},{8,24},{12,28},{16,0},{20,4},{24,8},{28,12},{1,17},{... | collective-permute-start | bytes 786440 | tf_op jit(solution)/shard_map/ppermute | solution.py:230
  154.4 41.9 %collective-permute-start.11 = (bf16[1,1024,128]{2,1,0:T(8,128)(2,1)}, bf16[1,1024,128]{2,1,0:T(8,128)(2,1)S(1)}, u32[]{:S(2)}, u32[]{:S(2)}) collective-permute-start(bf16[1,1024,128]{2,1,0:T(8,128)(2,1)} %get-tuple-element.108), channel_id=1, source_target_pairs={{0,20},{4,16},{8,28},{12,24},{16,4},{20,0},{24,12},{28,8},{1,21},{... | collective-permute-start | bytes 786440 | tf_op jit(solution)/shard_map/ppermute | solution.py:230
  154.5 41.9 %collective-permute-start.12 = (bf16[1,1024,128]{2,1,0:T(8,128)(2,1)}, bf16[1,1024,128]{2,1,0:T(8,128)(2,1)S(1)}, u32[]{:S(2)}, u32[]{:S(2)}) collective-permute-start(bf16[1,1024,128]{2,1,0:T(8,128)(2,1)} %get-tuple-element.109), channel_id=1, source_target_pairs={{0,24},{4,28},{8,16},{12,20},{16,8},{20,12},{24,0},{28,4},{1,25},{... | collective-permute-start | bytes 786440 | tf_op jit(solution)/shard_map/ppermute | solution.py:230
  156.5 39.8 %collective-permute-start.13 = (bf16[1,1024,128]{2,1,0:T(8,128)(2,1)}, bf16[1,1024,128]{2,1,0:T(8,128)(2,1)S(1)}, u32[]{:S(2)}, u32[]{:S(2)}) collective-permute-start(bf16[1,1024,128]{2,1,0:T(8,128)(2,1)} %get-tuple-element.110), channel_id=1, source_target_pairs={{0,28},{4,24},{8,20},{12,16},{16,12},{20,8},{24,4},{28,0},{1,29},{... | collective-permute-start | bytes 786440 | tf_op jit(solution)/shard_map/ppermute | solution.py:230
  (7 other events, 96.3 us)

commit v3 on v2

--- a/solution.py
+++ b/solution.py
@@ -67,7 +67,25 @@
     return slice(h * HEAD_DIM, (h + 1) * HEAD_DIM)
 
 
-def first_kernel(ld_ref, rel_ref, w_ref, x_ref, out_ref, lcol_ref, lrow_ref):
+def deal(me_ref, held, out_refs):
+    for n, out_ref in enumerate(out_refs):
+        out_ref[...] = held[me_ref[0] ^ n]
+
+
+def collect(me_ref, in_refs, held):
+    for n, in_ref in enumerate(in_refs):
+        held[me_ref[0] ^ n] = in_ref[...]
+
+
+def gather_state(me_ref, in_refs, state_ref):
+    rows = in_refs[0].shape[0]
+    for n, in_ref in enumerate(in_refs):
+        here = pl.ds(pl.multiple_of((me_ref[0] ^ n) * rows, rows), rows)
+        state_ref[here, :] = in_ref[...]
+
+
+def first_kernel(shares, me_ref, ld_ref, rel_ref, w_ref, x_ref, lcol_ref, lrow_ref, *refs):
+    out_refs, out_ref = refs[:shares], refs[shares]
     heads, length = ld_ref.shape
     parts, rows = out_ref.shape[0], out_ref.shape[1] - TAIL
     rates = ld_ref[...] * LOG2E
@@ -101,24 +119,48 @@
             if place:
                 tail = tail + out_ref[part, rows:, :].astype(F32)
             out_ref[part, rows:, :] = tail.astype(BF16)
-
-
-def carry_kernel(backward, tail_ref, in_ref, out_ref):
-    parts, rows = out_ref.shape[0], out_ref.shape[1]
+    deal(me_ref, out_ref, out_refs)
+
+
+def carry(backward, start_ref, tails, held, total_ref, out):
+    shares, rows = tails.shape[0], tails.shape[1] - TAIL
     step = min(rows, HEAD_DIM)
     for k in range(rows // step):
         here = slice(k * step, (k + 1) * step)
-        state = jnp.zeros((step, 128), F32)
-        for c in range(parts)[:: -1 if backward else 1]:
-            out_ref[c, here, :] = state.astype(BF16)
-            tail = tail_ref[c, rows:, :].astype(F32)
+        state = jnp.zeros((step, 128), F32) if start_ref is None else start_ref[here, :].astype(F32)
+        for c in range(shares)[:: -1 if backward else 1]:
+            if out is not None:
+                out[c, here, :] = state.astype(BF16)
+            tail = tails[c, rows:, :].astype(F32)
             factor = tail[2 * k : 2 * k + 1, :] + tail[2 * k + 1 : 2 * k + 2, :]
-            state = factor * state + in_ref[c, here, :].astype(F32)
+            state = factor * state + held[c, here, :].astype(F32)
+        if total_ref is not None:
+            total_ref[here, :] = state.astype(BF16)
+
+
+def total_kernel(backward, shares, me_ref, *refs):
+    count = 2 if backward else 1
+    in_refs, (total_ref, *held) = refs[: count * shares], refs[count * shares :]
+    for n in range(count):
+        collect(me_ref, in_refs[n * shares : (n + 1) * shares], held[n])
+    carry(backward, None, held[0], held[-1], total_ref, None)
+
+
+def carry_kernel(backward, shares, me_ref, start_ref, *refs):
+    count = 2 if backward else 1
+    in_refs, out_refs = refs[: count * shares], refs[count * shares : (count + 1) * shares]
+    *held, out = refs[(count + 1) * shares :]
+    for n in range(count):
+        collect(me_ref, in_refs[n * shares : (n + 1) * shares], held[n])
+    carry(backward, start_ref, held[0], held[-1], None, out)
+    deal(me_ref, out, out_refs)
 
 
 def mix_kernel(
-    x_ref, gate_ref, grad_ref, w_ref, r_ref, rel_ref, lcol_ref, lrow_ref, s_ref, mixed_ref, sums_ref
+    shares, me_ref, x_ref, gate_ref, grad_ref, w_ref, r_ref, rel_ref, lcol_ref, lrow_ref, *refs
 ):
+    state_refs, (mixed_ref, sums_ref, s_ref) = refs[:shares], refs[shares:]
+    gather_state(me_ref, state_refs, s_ref)
     length, heads = lcol_ref.shape
     reads = r_ref[...]
     rel = column(rel_ref[...].astype(F32))
@@ -148,9 +190,10 @@
 
 
 def gate_kernel(
-    width, sums_ref, mixed_ref, gate_ref, grad_ref, r_ref, rel_ref, lrow_ref,
-    mixer_ref, ggrad_ref, dmixed_ref, out_ref,
+    width, shares, me_ref, sums_ref, mixed_ref, gate_ref, grad_ref, r_ref, rel_ref, lrow_ref,
+    mixer_ref, ggrad_ref, dmixed_ref, *refs,
 ):
+    out_refs, out_ref = refs[:shares], refs[shares]
     length = mixed_ref.shape[0]
     heads = lrow_ref.shape[0]
     rows = out_ref.shape[1]
@@ -181,6 +224,7 @@
             out_ref[part, begin - part * rows : end - part * rows, :] = state[
                 begin - first : end - first, :
             ]
+    deal(me_ref, out_ref, out_refs)
 
 
 def inner_kernel(
@@ -208,7 +252,9 @@
     read_ref[...] = read + dot(total.T.astype(BF16), w_ref[...])
 
 
-def last_kernel(gin_ref, x_ref, w_ref, rel_ref, lcol_ref, back_ref, part_ref, out_ref, write_ref):
+def last_kernel(shares, me_ref, gin_ref, x_ref, w_ref, rel_ref, lcol_ref, part_ref, *refs):
+    state_refs, (out_ref, write_ref, back_ref) = refs[:shares], refs[shares:]
+    gather_state(me_ref, state_refs, back_ref)
     length, heads = lcol_ref.shape
     rel_last = rel_ref[:, length - 1 :]
     last_doc = iota((length, 128), 0) >= rel_last
@@ -230,8 +276,11 @@
     return lax.ppermute(block, "ctx", [(i, i ^ n) for i in range(lax.axis_size("ctx"))])
 
 
-def exchange(blocks):
-    return lax.all_to_all(blocks, "ctx", 0, 0)
+def cross(total, backward):
+    count = lax.axis_size("ctx")
+    half = count // 2
+    pairs = [(i + half, i) if backward else (i, i + half) for i in range(half)]
+    return lax.ppermute(total, "ctx", pairs)
 
 
 def pack_kernel(me_ref, marks_ref, q_ref, k_ref, v_ref, g_ref, *out_refs):
@@ -472,25 +521,46 @@
     length, width = ssm_input.shape
     heads = width // HEAD_DIM
     parts = lax.axis_size("ctx")
-    rows = width // parts
+    shares = parts // 2
+    rows = width // shares
     full_width = width * lax.axis_size("head")
-    work = 2 * length * length * width
     att_width = att_queries.shape[1]
     per = att_width // ATT_DIM // parts
     dealt = att_width // ATT_DIM % parts == 0
     place = lax.axis_index("ctx")
     rel = (doc_start - place * length).reshape(1, length)
     me = place.reshape(1).astype(jnp.int32)
-
-    sent, lcol, lrow = call(
-        first_kernel,
-        (
-            shape((parts, rows + TAIL, 128), BF16),
-            shape((length, heads), F32),
-            shape((heads, length), F32),
-        ),
-        log_decay.T, rel, write_map, ssm_input, flops=work // 2, name="ssm_first",
-    )
+    share = (place % shares).reshape(1).astype(jnp.int32)
+    tailed = [shape((rows + TAIL, 128), BF16)] * shares
+    plain = [shape((rows, 128), BF16)] * shares
+    held_tails = pltpu.VMEM((shares, rows + TAIL, 128), BF16)
+    held_plain = pltpu.VMEM((shares, rows, 128), BF16)
+
+    def carry_total(backward, *blocks):
+        return call(
+            lambda *refs: total_kernel(backward, shares, *refs),
+            shape((rows, 128), BF16), share, *blocks,
+            specs=[SMEM] + [VMEM] * len(blocks),
+            scratch=[held_tails, held_plain] if backward else [held_tails],
+            vmem=SMALL, name="ssm_total",
+        )
+
+    def carry_states(backward, start, *blocks):
+        return call(
+            lambda *refs: carry_kernel(backward, shares, *refs),
+            plain, share, start, *blocks,
+            specs=[SMEM] + [VMEM] * (1 + len(blocks)),
+            scratch=[held_tails, held_plain, held_plain] if backward else [held_tails, held_plain],
+            vmem=SMALL, name="ssm_carry",
+        )
+
+    lcol, lrow, *sent = call(
+        lambda *refs: first_kernel(shares, *refs),
+        [shape((length, heads), F32), shape((heads, length), F32)] + tailed,
+        share, log_decay.T, rel, write_map, ssm_input,
+        specs=[SMEM] + [VMEM] * 4, scratch=[held_tails], name="ssm_first",
+    )
+    tails = [pass_block(block, n) for n, block in enumerate(sent)]
     if dealt:
         marks = doc_start.reshape(length // 128, 128)
         marks = jnp.stack([marks // 128, marks % 128], axis=1).reshape(length // 64, 128)
@@ -501,68 +571,51 @@
             me, marks, att_queries, att_keys, att_values, att_grad,
             specs=[SMEM] + [VMEM] * 5, vmem=SMALL, name="att_pack",
         )
-        half = parts // 2
-        order = [half] + list(range(1, half)) + list(range(half + 1, parts))
-        early, middle, late = order[:half], order[half:-1], order[-1:]
+        packed = list(packed)
         att_got = {0: packed[0]}
-        for n in early:
-            att_got[n] = pass_block(packed[n], n)
+        att_got[shares] = pass_block(packed[shares], shares)
     else:
         att_out = ring_attention(att_queries, att_keys, att_values, att_grad, doc_start)
-    got = exchange(sent)
-    first_got = got
-    carried = call(
-        lambda in_ref, out_ref: carry_kernel(False, in_ref, in_ref, out_ref),
-        shape((parts, rows, 128), BF16), got, vmem=SMALL, name="ssm_carry",
-    )
-    state = exchange(carried).reshape(width, 128)
-
+    total = carry_total(False, *tails)
     if dealt:
-        held, done, state = lax.optimization_barrier(
-            ([packed[n] for n in middle], [att_got[n] for n in early], state)
-        )
-        att_got.update(zip(early, done))
-        for n, block in zip(middle, held):
+        total, att_got[shares] = lax.optimization_barrier((total, att_got[shares]))
+    start = cross(total, False)
+    if dealt:
+        start, packed[shares + 1] = lax.optimization_barrier((start, packed[shares + 1]))
+        att_got[shares + 1] = pass_block(packed[shares + 1], shares + 1)
+    state = [
+        pass_block(block, n) for n, block in enumerate(carry_states(False, start, *tails))
+    ]
+    if dealt:
+        rest = [n for n in range(1, parts) if n not in att_got]
+        rest = [n for n in rest if n > shares] + [n for n in rest if n < shares]
+        held, att_got[shares + 1], state = lax.optimization_barrier(
+            ([packed[n] for n in rest], att_got[shares + 1], state)
+        )
+        for n, block in zip(rest, held):
             att_got[n] = pass_block(block, n)
-
-    mixed, sums = call(
-        mix_kernel,
-        (shape((length, width), F32), shape((8, length), F32)),
-        ssm_input, gate_input, ssm_grad, write_map, read_map, rel, lcol, lrow, state,
-        flops=work * 3 // 2, name="ssm_mix",
+    mixed, sums, state = call(
+        lambda *refs: mix_kernel(shares, *refs),
+        (shape((length, width), F32), shape((8, length), F32), shape((width, 128), BF16)),
+        share, ssm_input, gate_input, ssm_grad, write_map, read_map, rel, lcol, lrow, *state,
+        specs=[SMEM] + [VMEM] * (8 + shares), name="ssm_mix",
     )
     sums = lax.psum(sums, "head")
-    mixer_out, gate_grad, dmixed, sent = call(
-        lambda *refs: gate_kernel(full_width, *refs),
-        (
-            shape((length, width), BF16),
-            shape((length, width), BF16),
-            shape((length, width), BF16),
-            shape((parts, rows, 128), BF16),
-        ),
-        sums, mixed, gate_input, ssm_grad, read_map, rel, lrow, flops=work // 2, name="ssm_gate",
-    )
-
+    mixer_out, gate_grad, dmixed, *sent = call(
+        lambda *refs: gate_kernel(full_width, shares, *refs),
+        [shape((length, width), BF16)] * 3 + plain,
+        share, sums, mixed, gate_input, ssm_grad, read_map, rel, lrow,
+        specs=[SMEM] + [VMEM] * 7, scratch=[held_plain], name="ssm_gate",
+    )
+
+    blocks = [pass_block(block, n) for n, block in enumerate(sent)]
+    total = carry_total(True, *tails, *blocks)
+    start = cross(total, True)
     if dealt:
-        held, done, sent = lax.optimization_barrier(
-            ([packed[n] for n in late], [att_got[n] for n in middle], sent)
-        )
-        att_got.update(zip(middle, done))
-        for n, block in zip(late, held):
-            att_got[n] = pass_block(block, n)
-    got = exchange(sent)
-    carried = call(
-        lambda *refs: carry_kernel(True, *refs), shape((parts, rows, 128), BF16), first_got, got,
-        vmem=SMALL, name="ssm_carry_back",
-    )
-    back = exchange(carried).reshape(width, 128)
-    if dealt:
-        last_got, carried = lax.optimization_barrier((att_got[parts - 1], carried))
-        att_got[parts - 1] = last_got
+        att_in, total = lax.optimization_barrier(([att_got[n] for n in range(parts)], total))
         att_done = call(
             lambda *refs: attend_blocks(length, parts, *refs),
-            [shape((per, 4 * length, 128), BF16)] * parts,
-            me, *[att_got[n] for n in range(parts)],
+            [shape((per, 4 * length, 128), BF16)] * parts, me, *att_in,
             specs=[SMEM] + [VMEM] * parts,
             scratch=[
                 pltpu.VMEM((parts, per, 4 * length + TAIL, 128), BF16),
@@ -575,23 +628,32 @@
             ],
             flops=6 * per * (parts * length) ** 2 * ATT_DIM, name="att_attend",
         )
-        att_done, back = lax.optimization_barrier((att_done, back))
+        start, att_done = lax.optimization_barrier((start, att_done))
+    back = [
+        pass_block(block, n) for n, block in enumerate(carry_states(True, start, *tails, *blocks))
+    ]
+    if dealt:
+        att_back = {shares: pass_block(att_done[shares], shares)}
+        held, back = lax.optimization_barrier((att_done, back))
+        for n in [n for n in range(parts)[::-1] if n != shares]:
+            att_back[n] = pass_block(held[n], n)
         att_out = call(
             unpack_kernel, (shape((length, att_width), BF16),) * 4,
-            me, *[pass_block(block, n) for n, block in enumerate(att_done)],
+            me, *[att_back[n] for n in range(parts)],
             specs=[SMEM] + [VMEM] * parts, vmem=SMALL, name="att_unpack",
         )
 
     gin, read_part, write_part = call(
         inner_kernel,
         (shape((length, width), F32), shape((length, 128), F32), shape((length, 128), F32)),
-        dmixed, ssm_input, write_map, read_map, rel, lcol, lrow, state,
-        flops=work * 5 // 2, name="ssm_inner",
+        dmixed, ssm_input, write_map, read_map, rel, lcol, lrow, state, name="ssm_inner",
     )
     input_grad, write_part = call(
-        last_kernel,
+        lambda *refs: last_kernel(shares, *refs),
         (shape((length, width), BF16), shape((length, 128), F32)),
-        gin, ssm_input, write_map, rel, lcol, back, write_part, flops=work, name="ssm_last",
+        share, gin, ssm_input, write_map, rel, lcol, write_part, *back,
+        specs=[SMEM] + [VMEM] * (6 + shares),
+        scratch=[pltpu.VMEM((width, 128), BF16)], name="ssm_last",
     )
     write_sum, read_sum = lax.psum((write_part, read_part), "head")
     window_out, query_grad, key_grad, value_grad = att_out

time: 201 us -> 181 us (0.900); the launches traced: 198 us -> 181 us
  blocking collectives: 68.3 us -> 36.4 us
  waiting for transfers between devices: 35.9 us -> 42.4 us
  local copies, waits for them, and re-layouts: 1.46 us -> 7.81 us
  starting transfers between devices: 46.8 us -> 49.3 us
    all_to_all x2 -> x0, blocking collectives: 43.2 us -> none  [exchange(): return lax.all_to_all(blocks, 'ctx', 0, 0)]
    psum x1, blocking collectives: 17.5 us -> 27.9 us  [body(): write_sum, read_sum = lax.psum((write_part, read_part), 'head')]
    all_to_all x2 -> x0, starting transfers between devices: 8.23 us -> none  [exchange(): return lax.all_to_all(blocks, 'ctx', 0, 0)]
    unnamed x30 -> x56, local copies, waits for them, and re-layouts: 1.46 us -> 7.8 us
    ppermute x0 -> x2, starting transfers between devices: none -> 5.64 us  [cross(): return lax.ppermute(total, 'ctx', pairs)]
    ppermute x14 -> x26, starting transfers between devices: 38.6 us -> 43.7 us  [pass_block(): lax.ppermute(block, 'ctx', [(i, i ^ n) for i in range(lax.axis_size('ctx'...]
    ppermute x14 -> x26, waiting for transfers between devices: 35.9 us -> 40.5 us  [pass_block(): lax.ppermute(block, 'ctx', [(i, i ^ n) for i in range(lax.axis_size('ctx'...]
    pallas_call x10 -> x12, Pallas kernels: 43.1 us -> 41.9 us  [call(): pl.pallas_call(kernel, out_shape=out_shape, in_specs=specs or [VMEM] * le...]
  transfers between devices with their start and end apart: 16 -> 28, of which waited for: 3 -> 14; matrix products, arithmetic and copies ran while one was open for 0% -> 0% of each run, Pallas kernels for 18% -> 13%
where the time goes in v3:
time: 181 us
  starting transfers between devices  49.3 us (27%)
  waiting for transfers between devices  42.4 us (23%)
  Pallas kernels  41.9 us (23%)
  blocking collectives  36.4 us (20%)
  local copies, waits for them, and re-layouts  7.81 us (4%)
  other arithmetic  1.96 us (1%)
    ppermute x26, starting transfers between devices, pass_block(): lax.ppermute(block, 'ctx', [(i, i ^ n) for i in range(lax.axis_size('ctx'...  43.7 us
    pallas_call x12, Pallas kernels, call(): pl.pallas_call(kernel, out_shape=out_shape, in_specs=specs or [VMEM] * le...  41.9 us
    ppermute x26, waiting for transfers between devices, pass_block(): lax.ppermute(block, 'ctx', [(i, i ^ n) for i in range(lax.axis_size('ctx'...  40.5 us
    psum x1, blocking collectives, body(): write_sum, read_sum = lax.psum((write_part, read_part), 'head')  27.9 us
    psum x1, blocking collectives, body(): sums = lax.psum(sums, 'head')  8.54 us
    unnamed x56, local copies, waits for them, and re-layouts  7.8 us
    ppermute x2, starting transfers between devices, cross(): return lax.ppermute(total, 'ctx', pairs)  5.64 us
  transfers between devices with their start and end apart: 28, of which 14 were waited for; matrix products, arithmetic and copies ran while one was open for 0% of the time, Pallas kernels for 13%

profile of v3, /device:TPU:1, one launch (start us, length us, event | category | flops | bytes accessed | tf_op | source)
XLA Modules:
  0.0 180.6 jit_solution(9086833382603934408)
XLA Ops:
  2.6 3.0 %ssm_first.1 = (f32[256,16]{1,0:T(8,128)}, f32[16,256]{1,0:T(8,128)}, bf16[528,128]{1,0:T(8,128)(2,1)}, bf16[528,128]{1,0:T(8,128)(2,1)}, bf16[528,128]{1,0:T(8,128)(2,1)}, /*index=5*/bf16[528,128]{1,0:T(8,128)(2,1)}) custom-call(s32[1]{0:T(128)} %bitcast.refs_0_, f32[16,256]{1,0:T(8,128)} %bitcast.11, s32[1,256]{1,0:T(1,128)} %bitcast.6, ...), custom_call_target="tpu_custom_call" | custom-call | bytes 1704964 | tf_op jit(solution)/shard_map/ssm_first/pallas_call | solution.py:28
  10.4 3.2 %collective-permute-start.3 = (bf16[1,1040,128]{2,1,0:T(8,128)(2,1)S(1)}, bf16[1,1040,128]{2,1,0:T(8,128)(2,1)S(1)}, u32[]{:S(2)}, u32[]{:S(2)}) collective-permute-start(bf16[1,1040,128]{2,1,0:T(8,128)(2,1)S(1)} %get-tuple-element.113), channel_id=1, source_target_pairs={{0,16},{4,20},{8,24},{12,28},{16,0},{20,4},{24,8},{28,12},{1,17},{... | collective-permute-start | bytes 798728 | tf_op jit(solution)/shard_map/ppermute | solution.py:276
  17.8 3.8 %collective-permute-done.1.refs_3_.refs_4_ = bf16[528,128]{1,0:T(8,128)(2,1)S(1)} collective-permute-done((bf16[528,128]{1,0:T(8,128)(2,1)S(1)}, bf16[528,128]{1,0:T(8,128)(2,1)S(1)}, u32[]{:S(2)}, u32[]{:S(2)}) %collective-permute-start.1) | collective-permute-done | bytes 135200 | tf_op jit(solution)/shard_map/ppermute | solution.py:276
  21.6 2.9 %collective-permute-done.2.refs_4_.refs_5_ = bf16[528,128]{1,0:T(8,128)(2,1)S(1)} collective-permute-done((bf16[528,128]{1,0:T(8,128)(2,1)S(1)}, bf16[528,128]{1,0:T(8,128)(2,1)S(1)}, u32[]{:S(2)}, u32[]{:S(2)}) %collective-permute-start.2) | collective-permute-done | bytes 135200 | tf_op jit(solution)/shard_map/ppermute | solution.py:276
  25.5 4.2 %collective-permute-start.4 = (bf16[512,128]{1,0:T(8,128)(2,1)S(1)}, bf16[512,128]{1,0:T(8,128)(2,1)S(1)}, u32[]{:S(2)}, u32[]{:S(2)}) collective-permute-start(bf16[512,128]{1,0:T(8,128)(2,1)S(1)} %ssm_total.2), channel_id=1, source_target_pairs={{0,16},{4,20},{8,24},{12,28},{1,17},{5,21},{9,25},{13,29},{2,18},{... | collective-permute-start | bytes 393224 | tf_op jit(solution)/shard_map/ppermute | solution.py:283
  31.6 2.7 %collective-permute-start.5 = (bf16[1,1040,128]{2,1,0:T(8,128)(2,1)S(1)}, bf16[1,1040,128]{2,1,0:T(8,128)(2,1)S(1)}, u32[]{:S(2)}, u32[]{:S(2)}) collective-permute-start(bf16[1,1040,128]{2,1,0:T(8,128)(2,1)S(1)} %get-tuple-element.116), channel_id=1, source_target_pairs={{0,20},{4,16},{8,28},{12,24},{16,4},{20,0},{24,12},{28,8},{1,21},{... | collective-permute-start | bytes 798728 | tf_op jit(solution)/shard_map/ppermute | solution.py:276
  36.5 10.9 %collective-permute-start.7 = (bf16[512,128]{1,0:T(8,128)(2,1)S(1)}, bf16[512,128]{1,0:T(8,128)(2,1)S(1)}, u32[]{:S(2)}, u32[]{:S(2)}) collective-permute-start(bf16[512,128]{1,0:T(8,128)(2,1)S(1)} %get-tuple-element.120), channel_id=1, source_target_pairs={{0,8},{4,12},{8,0},{12,4},{16,24},{20,28},{24,16},{28,20},{1,9},{5... | collective-permute-start | bytes 393224 | tf_op jit(solution)/shard_map/ppermute | solution.py:276
  47.4 2.3 %collective-permute-done.7.refs_11_ = bf16[512,128]{1,0:T(8,128)(2,1)S(1)} collective-permute-done((bf16[512,128]{1,0:T(8,128)(2,1)S(1)}, bf16[512,128]{1,0:T(8,128)(2,1)S(1)}, u32[]{:S(2)}, u32[]{:S(2)}) %collective-permute-start.7) | collective-permute-done | bytes 131104 | tf_op jit(solution)/shard_map/ppermute | solution.py:276
  49.7 2.8 %collective-permute-done.8.refs_12_ = bf16[512,128]{1,0:T(8,128)(2,1)S(1)} collective-permute-done((bf16[512,128]{1,0:T(8,128)(2,1)S(1)}, bf16[512,128]{1,0:T(8,128)(2,1)S(1)}, u32[]{:S(2)}, u32[]{:S(2)}) %collective-permute-start.8) | collective-permute-done | bytes 131104 | tf_op jit(solution)/shard_map/ppermute | solution.py:276
  53.2 5.9 %ssm_mix.1 = (f32[256,2048]{1,0:T(8,128)}, f32[8,256]{1,0:T(8,128)}, bf16[2048,128]{1,0:T(8,128)(2,1)}) custom-call(s32[1]{0:T(128)} %bitcast.refs_0_, bf16[256,2048]{1,0:T(8,128)(2,1)} %refs_2_.3, bf16[256,2048]{1,0:T(8,128)(2,1)} %refs_3_.6, bf16[256,2048]{1,0:T(8,128)(2,1)} %refs_4_.5, bf16[256,128]{1,0:T(8,128)(2,1)} %refs_3_.7, bf16[256,128]{1,0:T(8,128)(2,1)} %r_ref.1, ...), custom_call_target="tpu_custom_call" | custom-call | bytes 6464516 | tf_op jit(solution)/shard_map/ssm_mix/pallas_call | solution.py:28
  59.2 8.5 %psum.21.refs_1_ = f32[8,256]{1,0:T(8,128)} all-reduce(f32[8,256]{1,0:T(8,128)} %get-tuple-element.126), channel_id=1, replica_groups=mesh['ctx'=8,'head'=4] {'head'}, use_global_device_ids=true, to_apply=%region_0.1 | all-reduce | flops 2048 | bytes 16384 | tf_op jit(solution)/shard_map/psum | solution.py:603
  67.7 5.9 %ssm_gate.1 = (bf16[256,2048]{1,0:T(8,128)(2,1)}, bf16[256,2048]{1,0:T(8,128)(2,1)}, bf16[256,2048]{1,0:T(8,128)(2,1)}, bf16[512,128]{1,0:T(8,128)(2,1)}, bf16[5...) custom-call(s32[1]{0:T(128)} %bitcast.refs_0_, f32[8,256]{1,0:T(8,128)} %psum.21.refs_1_, ...), custom_call_target="tpu_custom_call" | custom-call | bytes 7955460 | tf_op jit(solution)/shard_map/ssm_gate/pallas_call | solution.py:28
  74.1 3.7 %collective-permute-start.10 = (bf16[512,128]{1,0:T(8,128)(2,1)}, bf16[512,128]{1,0:T(8,128)(2,1)S(1)}, u32[]{:S(2)}, u32[]{:S(2)}) collective-permute-start(bf16[512,128]{1,0:T(8,128)(2,1)} %get-tuple-element.131), channel_id=1, source_target_pairs={{0,8},{4,12},{8,0},{12,4},{16,24},{20,28},{24,16},{28,20},{1,9},{5... | collective-permute-start | bytes 393224 | tf_op jit(solution)/shard_map/ppermute | solution.py:276
  81.6 3.3 %collective-permute-start.16 = (bf16[1,1040,128]{2,1,0:T(8,128)(2,1)S(1)}, bf16[1,1040,128]{2,1,0:T(8,128)(2,1)S(1)}, u32[]{:S(2)}, u32[]{:S(2)}) collective-permute-start(bf16[1,1040,128]{2,1,0:T(8,128)(2,1)S(1)} %get-tuple-element.139), channel_id=1, source_target_pairs={{0,24},{4,28},{8,16},{12,20},{16,8},{20,12},{24,0},{28,4},{1,25},{... | collective-permute-start | bytes 798728 | tf_op jit(solution)/shard_map/ppermute | solution.py:276
  89.0 5.8 %collective-permute-done.15.refs_4_ = bf16[1,1040,128]{2,1,0:T(8,128)(2,1)S(1)} collective-permute-done((bf16[1,1040,128]{2,1,0:T(8,128)(2,1)S(1)}, bf16[1,1040,128]{2,1,0:T(8,128)(2,1)S(1)}, u32[]{:S(2)}, u32[]{:S(2)}) %collective-permute-start.15) | collective-permute-done | bytes 266272 | tf_op jit(solution)/shard_map/ppermute | solution.py:276
  94.7 8.3 %collective-permute-done.16.refs_7_ = bf16[1,1040,128]{2,1,0:T(8,128)(2,1)S(1)} collective-permute-done((bf16[1,1040,128]{2,1,0:T(8,128)(2,1)S(1)}, bf16[1,1040,128]{2,1,0:T(8,128)(2,1)S(1)}, u32[]{:S(2)}, u32[]{:S(2)}) %collective-permute-start.16) | collective-permute-done | bytes 266272 | tf_op jit(solution)/shard_map/ppermute | solution.py:276
  103.0 5.2 %collective-permute-done.17.refs_8_ = bf16[1,1040,128]{2,1,0:T(8,128)(2,1)S(1)} collective-permute-done((bf16[1,1040,128]{2,1,0:T(8,128)(2,1)S(1)}, bf16[1,1040,128]{2,1,0:T(8,128)(2,1)S(1)}, u32[]{:S(2)}, u32[]{:S(2)}) %collective-permute-start.17) | collective-permute-done | bytes 266272 | tf_op jit(solution)/shard_map/ppermute | solution.py:276
  109.0 14.8 %att_attend.1 = (bf16[1,1024,128]{2,1,0:T(8,128)(2,1)}, bf16[1,1024,128]{2,1,0:T(8,128)(2,1)}, bf16[1,1024,128]{2,1,0:T(8,128)(2,1)}, bf16[1,1024,128]{2,1,0:T(8...) custom-call(s32[1]{0:T(128)} %bitcast.3.me_ref.refs_0_, ...), custom_call_target="tpu_custom_call" | custom-call | flops 3221225472 | bytes 4227076 | tf_op jit(solution)/shard_map/att_attend/pallas_call | solution.py:28
  134.4 3.1 %collective-permute-done.24.refs_4_ = bf16[1,1024,128]{2,1,0:T(8,128)(2,1)S(1)} collective-permute-done((bf16[1,1024,128]{2,1,0:T(8,128)(2,1)}, bf16[1,1024,128]{2,1,0:T(8,128)(2,1)S(1)}, u32[]{:S(2)}, u32[]{:S(2)}) %collective-permute-start.24) | collective-permute-done | bytes 262176 | tf_op jit(solution)/shard_map/ppermute | solution.py:276
  137.7 4.0 %collective-permute-start.27 = (bf16[1,1024,128]{2,1,0:T(8,128)(2,1)}, bf16[1,1024,128]{2,1,0:T(8,128)(2,1)S(1)}, u32[]{:S(2)}, u32[]{:S(2)}) collective-permute-start(bf16[1,1024,128]{2,1,0:T(8,128)(2,1)} %get-tuple-element.176), channel_id=1, source_target_pairs={{0,28},{4,24},{8,20},{12,16},{16,12},{20,8},{24,4},{28,0},{1,29},{... | collective-permute-start | bytes 786440 | tf_op jit(solution)/shard_map/ppermute | solution.py:276
  141.7 4.9 %ssm_inner.1 = (f32[256,2048]{1,0:T(8,128)}, f32[256,128]{1,0:T(8,128)}, f32[256,128]{1,0:T(8,128)}) custom-call(bf16[256,2048]{1,0:T(8,128)(2,1)} %get-tuple-element.178.dmixed_ref, bf16[256,2048]{1,0:T(8,128)(2,1)} %refs_2_.3, bf16[256,128]{1,0:T(8,128)(2,1)} %refs_3_.7, bf16[256,128]{1,0:T(8,128)(2,1)} %r_ref.1, s32[1,256]{1,0:T(1,128)} %bitcast.9, ...), custom_call_target="tpu_custom_call" | custom-call | bytes 5145600 | tf_op jit(solution)/shard_map/ssm_inner/pallas_call | solution.py:28
  146.6 4.2 %ssm_last.1 = (bf16[256,2048]{1,0:T(8,128)(2,1)}, f32[256,128]{1,0:T(8,128)}) custom-call(s32[1]{0:T(128)} %bitcast.refs_0_, f32[256,2048]{1,0:T(8,128)} %get-tuple-element.180.refs_1_, bf16[256,2048]{1,0:T(8,128)(2,1)} %refs_2_.3, bf16[256,128]{1,0:T(8,128)(2,1)} %refs_3_.7, s32[1,256]{1,0:T(1,128)} %bitcast.10, ...), custom_call_target="tpu_custom_call" | custom-call | bytes 5063684 | tf_op jit(solution)/shard_map/ssm_last/pallas_call | solution.py:28
  150.8 27.9 %all-reduce.3 = (bf16[256,128]{1,0:T(8,128)(2,1)}, bf16[256,128]{1,0:T(8,128)(2,1)}) all-reduce(f32[256,128]{1,0:T(8,128)} %get-tuple-element.188, f32[256,128]{1,0:T(8,128)S(1)} %copy-done.17), channel_id=1, replica_groups=mesh['ctx'=8,'head'=4] {'head'}, use_global_device_ids=true, to_apply=%region_1.2 | all-reduce | flops 65536 | bytes 393216 | tf_op jit(solution)/shard_map/psum | solution.py:658
  178.7 1.9 %att_unpack.1 = (bf16[256,1024]{1,0:T(8,128)(2,1)}, bf16[256,1024]{1,0:T(8,128)(2,1)}, bf16[256,1024]{1,0:T(8,128)(2,1)}, bf16[256,1024]{1,0:T(8,128)(2,1)}) custom-call(s32[1]{0:T(128)} %bitcast.3.me_ref.refs_0_, bf16[1,1024,128]{2,1,0:T(8,128)(2,1)S(1)} %copy-done.7, bf16[1,1024,128]{2,1,0:T(8,128)(2,1)S(1)} %collective-permute-done.21.refs_1_, ...), custom_call_target="tpu_custom_call" | custom-call | bytes 4194308 | tf_op jit(solution)/shard_map/att_unpack/pallas_call | solution.py:28
  (107 shorter events, 36.4 us)
Async XLA Ops:
  10.4 15.1 %collective-permute-start.3 = (bf16[1,1040,128]{2,1,0:T(8,128)(2,1)S(1)}, bf16[1,1040,128]{2,1,0:T(8,128)(2,1)S(1)}, u32[]{:S(2)}, u32[]{:S(2)}) collective-permute-start(bf16[1,1040,128]{2,1,0:T(8,128)(2,1)S(1)} %get-tuple-element.113), channel_id=1, source_target_pairs={{0,16},{4,20},{8,24},{12,28},{16,0},{20,4},{24,8},{28,12},{1,17},{... | collective-permute-start | bytes 798728 | tf_op jit(solution)/shard_map/ppermute | solution.py:276
  14.8 6.8 %collective-permute-start.1 = (bf16[528,128]{1,0:T(8,128)(2,1)S(1)}, bf16[528,128]{1,0:T(8,128)(2,1)S(1)}, u32[]{:S(2)}, u32[]{:S(2)}) collective-permute-start(bf16[528,128]{1,0:T(8,128)(2,1)S(1)} %copy-done.26), channel_id=1, source_target_pairs={{0,8},{4,12},{8,0},{12,4},{16,24},{20,28},{24,16},{28,20},{1,9},{5... | collective-permute-start | bytes 405512 | tf_op jit(solution)/shard_map/ppermute | solution.py:276
  16.1 8.4 %collective-permute-start.2 = (bf16[528,128]{1,0:T(8,128)(2,1)S(1)}, bf16[528,128]{1,0:T(8,128)(2,1)S(1)}, u32[]{:S(2)}, u32[]{:S(2)}) collective-permute-start(bf16[528,128]{1,0:T(8,128)(2,1)S(1)} %copy-done.25), channel_id=1, source_target_pairs={{0,12},{4,8},{8,4},{12,0},{16,28},{20,24},{24,20},{28,16},{1,13},{... | collective-permute-start | bytes 405512 | tf_op jit(solution)/shard_map/ppermute | solution.py:276
  25.5 6.1 %collective-permute-start.4 = (bf16[512,128]{1,0:T(8,128)(2,1)S(1)}, bf16[512,128]{1,0:T(8,128)(2,1)S(1)}, u32[]{:S(2)}, u32[]{:S(2)}) collective-permute-start(bf16[512,128]{1,0:T(8,128)(2,1)S(1)} %ssm_total.2), channel_id=1, source_target_pairs={{0,16},{4,20},{8,24},{12,28},{1,17},{5,21},{9,25},{13,29},{2,18},{... | collective-permute-start | bytes 393224 | tf_op jit(solution)/shard_map/ppermute | solution.py:283
  31.6 21.0 %collective-permute-start.5 = (bf16[1,1040,128]{2,1,0:T(8,128)(2,1)S(1)}, bf16[1,1040,128]{2,1,0:T(8,128)(2,1)S(1)}, u32[]{:S(2)}, u32[]{:S(2)}) collective-permute-start(bf16[1,1040,128]{2,1,0:T(8,128)(2,1)S(1)} %get-tuple-element.116), channel_id=1, source_target_pairs={{0,20},{4,16},{8,28},{12,24},{16,4},{20,0},{24,12},{28,8},{1,21},{... | collective-permute-start | bytes 798728 | tf_op jit(solution)/shard_map/ppermute | solution.py:276
  35.2 12.2 %collective-permute-start.6 = (bf16[512,128]{1,0:T(8,128)(2,1)S(1)}, bf16[512,128]{1,0:T(8,128)(2,1)S(1)}, u32[]{:S(2)}, u32[]{:S(2)}) collective-permute-start(bf16[512,128]{1,0:T(8,128)(2,1)S(1)} %get-tuple-element.119), channel_id=1, source_target_pairs={{0,4},{4,0},{8,12},{12,8},{16,20},{20,16},{24,28},{28,24},{1,5},{5... | collective-permute-start | bytes 393224 | tf_op jit(solution)/shard_map/ppermute | solution.py:276
  36.5 13.3 %collective-permute-start.7 = (bf16[512,128]{1,0:T(8,128)(2,1)S(1)}, bf16[512,128]{1,0:T(8,128)(2,1)S(1)}, u32[]{:S(2)}, u32[]{:S(2)}) collective-permute-start(bf16[512,128]{1,0:T(8,128)(2,1)S(1)} %get-tuple-element.120), channel_id=1, source_target_pairs={{0,8},{4,12},{8,0},{12,4},{16,24},{20,28},{24,16},{28,20},{1,9},{5... | collective-permute-start | bytes 393224 | tf_op jit(solution)/shard_map/ppermute | solution.py:276
  47.4 5.2 %collective-permute-start.8 = (bf16[512,128]{1,0:T(8,128)(2,1)S(1)}, bf16[512,128]{1,0:T(8,128)(2,1)S(1)}, u32[]{:S(2)}, u32[]{:S(2)}) collective-permute-start(bf16[512,128]{1,0:T(8,128)(2,1)S(1)} %get-tuple-element.121), channel_id=1, source_target_pairs={{0,12},{4,8},{8,4},{12,0},{16,28},{20,24},{24,20},{28,16},{1,13},{... | collective-permute-start | bytes 393224 | tf_op jit(solution)/shard_map/ppermute | solution.py:276
  73.6 6.9 %collective-permute-start.9 = (bf16[512,128]{1,0:T(8,128)(2,1)}, bf16[512,128]{1,0:T(8,128)(2,1)S(1)}, u32[]{:S(2)}, u32[]{:S(2)}) collective-permute-start(bf16[512,128]{1,0:T(8,128)(2,1)} %get-tuple-element.130), channel_id=1, source_target_pairs={{0,4},{4,0},{8,12},{12,8},{16,20},{20,16},{24,28},{28,24},{1,5},{5... | collective-permute-start | bytes 393224 | tf_op jit(solution)/shard_map/ppermute | solution.py:276
  74.1 7.5 %collective-permute-start.10 = (bf16[512,128]{1,0:T(8,128)(2,1)}, bf16[512,128]{1,0:T(8,128)(2,1)S(1)}, u32[]{:S(2)}, u32[]{:S(2)}) collective-permute-start(bf16[512,128]{1,0:T(8,128)(2,1)} %get-tuple-element.131), channel_id=1, source_target_pairs={{0,8},{4,12},{8,0},{12,4},{16,24},{20,28},{24,16},{28,20},{1,9},{5... | collective-permute-start | bytes 393224 | tf_op jit(solution)/shard_map/ppermute | solution.py:276
  77.8 7.0 %collective-permute-start.11 = (bf16[512,128]{1,0:T(8,128)(2,1)}, bf16[512,128]{1,0:T(8,128)(2,1)S(1)}, u32[]{:S(2)}, u32[]{:S(2)}) collective-permute-start(bf16[512,128]{1,0:T(8,128)(2,1)} %get-tuple-element.132), channel_id=1, source_target_pairs={{0,12},{4,8},{8,4},{12,0},{16,28},{20,24},{24,20},{28,16},{1,13},{... | collective-permute-start | bytes 393224 | tf_op jit(solution)/shard_map/ppermute | solution.py:276
  77.8 9.6 %collective-permute-start.13 = (bf16[1,1040,128]{2,1,0:T(8,128)(2,1)S(1)}, bf16[1,1040,128]{2,1,0:T(8,128)(2,1)S(1)}, u32[]{:S(2)}, u32[]{:S(2)}) collective-permute-start(bf16[1,1040,128]{2,1,0:T(8,128)(2,1)S(1)} %get-tuple-element.134), channel_id=1, source_target_pairs={{0,4},{4,0},{8,12},{12,8},{16,20},{20,16},{24,28},{28,24},{1,5},{5... | collective-permute-start | bytes 798728 | tf_op jit(solution)/shard_map/ppermute | solution.py:276
  79.0 9.9 %collective-permute-start.14 = (bf16[1,1040,128]{2,1,0:T(8,128)(2,1)S(1)}, bf16[1,1040,128]{2,1,0:T(8,128)(2,1)S(1)}, u32[]{:S(2)}, u32[]{:S(2)}) collective-permute-start(bf16[1,1040,128]{2,1,0:T(8,128)(2,1)S(1)} %get-tuple-element.135), channel_id=1, source_target_pairs={{0,8},{4,12},{8,0},{12,4},{16,24},{20,28},{24,16},{28,20},{1,9},{5... | collective-permute-start | bytes 798728 | tf_op jit(solution)/shard_map/ppermute | solution.py:276
  80.5 14.3 %collective-permute-start.15 = (bf16[1,1040,128]{2,1,0:T(8,128)(2,1)S(1)}, bf16[1,1040,128]{2,1,0:T(8,128)(2,1)S(1)}, u32[]{:S(2)}, u32[]{:S(2)}) collective-permute-start(bf16[1,1040,128]{2,1,0:T(8,128)(2,1)S(1)} %get-tuple-element.136), channel_id=1, source_target_pairs={{0,12},{4,8},{8,4},{12,0},{16,28},{20,24},{24,20},{28,16},{1,13},{... | collective-permute-start | bytes 798728 | tf_op jit(solution)/shard_map/ppermute | solution.py:276
  81.6 21.5 %collective-permute-start.16 = (bf16[1,1040,128]{2,1,0:T(8,128)(2,1)S(1)}, bf16[1,1040,128]{2,1,0:T(8,128)(2,1)S(1)}, u32[]{:S(2)}, u32[]{:S(2)}) collective-permute-start(bf16[1,1040,128]{2,1,0:T(8,128)(2,1)S(1)} %get-tuple-element.139), channel_id=1, source_target_pairs={{0,24},{4,28},{8,16},{12,20},{16,8},{20,12},{24,0},{28,4},{1,25},{... | collective-permute-start | bytes 798728 | tf_op jit(solution)/shard_map/ppermute | solution.py:276
  84.8 23.4 %collective-permute-start.17 = (bf16[1,1040,128]{2,1,0:T(8,128)(2,1)S(1)}, bf16[1,1040,128]{2,1,0:T(8,128)(2,1)S(1)}, u32[]{:S(2)}, u32[]{:S(2)}) collective-permute-start(bf16[1,1040,128]{2,1,0:T(8,128)(2,1)S(1)} %get-tuple-element.140), channel_id=1, source_target_pairs={{0,28},{4,24},{8,20},{12,16},{16,12},{20,8},{24,4},{28,0},{1,29},{... | collective-permute-start | bytes 798728 | tf_op jit(solution)/shard_map/ppermute | solution.py:276
  87.5 36.3 %collective-permute-start.12 = (bf16[512,128]{1,0:T(8,128)(2,1)S(1)}, bf16[512,128]{1,0:T(8,128)(2,1)S(1)}, u32[]{:S(2)}, u32[]{:S(2)}) collective-permute-start(bf16[512,128]{1,0:T(8,128)(2,1)S(1)} %ssm_total.3), channel_id=1, source_target_pairs={{16,0},{20,4},{24,8},{28,12},{17,1},{21,5},{25,9},{29,13},{18,2},{... | collective-permute-start | bytes 393224 | tf_op jit(solution)/shard_map/ppermute | solution.py:283
  127.5 10.0 %collective-permute-start.24 = (bf16[1,1024,128]{2,1,0:T(8,128)(2,1)}, bf16[1,1024,128]{2,1,0:T(8,128)(2,1)S(1)}, u32[]{:S(2)}, u32[]{:S(2)}) collective-permute-start(bf16[1,1024,128]{2,1,0:T(8,128)(2,1)} %get-tuple-element.161), channel_id=1, source_target_pairs={{0,16},{4,20},{8,24},{12,28},{16,0},{20,4},{24,8},{28,12},{1,17},{... | collective-permute-start | bytes 786440 | tf_op jit(solution)/shard_map/ppermute | solution.py:276
  131.3 6.4 %collective-permute-start.21 = (bf16[1,1024,128]{2,1,0:T(8,128)(2,1)}, bf16[1,1024,128]{2,1,0:T(8,128)(2,1)S(1)}, u32[]{:S(2)}, u32[]{:S(2)}) collective-permute-start(bf16[1,1024,128]{2,1,0:T(8,128)(2,1)} %get-tuple-element.171), channel_id=1, source_target_pairs={{0,4},{4,0},{8,12},{12,8},{16,20},{20,16},{24,28},{28,24},{1,5},{5... | collective-permute-start | bytes 786440 | tf_op jit(solution)/shard_map/ppermute | solution.py:276
  133.2 45.5 %collective-permute-start.22 = (bf16[1,1024,128]{2,1,0:T(8,128)(2,1)}, bf16[1,1024,128]{2,1,0:T(8,128)(2,1)S(1)}, u32[]{:S(2)}, u32[]{:S(2)}) collective-permute-start(bf16[1,1024,128]{2,1,0:T(8,128)(2,1)} %get-tuple-element.172), channel_id=1, source_target_pairs={{0,8},{4,12},{8,0},{12,4},{16,24},{20,28},{24,16},{28,20},{1,9},{5... | collective-permute-start | bytes 786440 | tf_op jit(solution)/shard_map/ppermute | solution.py:276
  133.2 45.5 %collective-permute-start.23 = (bf16[1,1024,128]{2,1,0:T(8,128)(2,1)}, bf16[1,1024,128]{2,1,0:T(8,128)(2,1)S(1)}, u32[]{:S(2)}, u32[]{:S(2)}) collective-permute-start(bf16[1,1024,128]{2,1,0:T(8,128)(2,1)} %get-tuple-element.173), channel_id=1, source_target_pairs={{0,12},{4,8},{8,4},{12,0},{16,28},{20,24},{24,20},{28,16},{1,13},{... | collective-permute-start | bytes 786440 | tf_op jit(solution)/shard_map/ppermute | solution.py:276
  134.4 44.3 %collective-permute-start.25 = (bf16[1,1024,128]{2,1,0:T(8,128)(2,1)}, bf16[1,1024,128]{2,1,0:T(8,128)(2,1)S(1)}, u32[]{:S(2)}, u32[]{:S(2)}) collective-permute-start(bf16[1,1024,128]{2,1,0:T(8,128)(2,1)} %get-tuple-element.174), channel_id=1, source_target_pairs={{0,20},{4,16},{8,28},{12,24},{16,4},{20,0},{24,12},{28,8},{1,21},{... | collective-permute-start | bytes 786440 | tf_op jit(solution)/shard_map/ppermute | solution.py:276
  137.5 41.2 %collective-permute-start.26 = (bf16[1,1024,128]{2,1,0:T(8,128)(2,1)}, bf16[1,1024,128]{2,1,0:T(8,128)(2,1)S(1)}, u32[]{:S(2)}, u32[]{:S(2)}) collective-permute-start(bf16[1,1024,128]{2,1,0:T(8,128)(2,1)} %get-tuple-element.175), channel_id=1, source_target_pairs={{0,24},{4,28},{8,16},{12,20},{16,8},{20,12},{24,0},{28,4},{1,25},{... | collective-permute-start | bytes 786440 | tf_op jit(solution)/shard_map/ppermute | solution.py:276
  137.7 41.0 %collective-permute-start.27 = (bf16[1,1024,128]{2,1,0:T(8,128)(2,1)}, bf16[1,1024,128]{2,1,0:T(8,128)(2,1)S(1)}, u32[]{:S(2)}, u32[]{:S(2)}) collective-permute-start(bf16[1,1024,128]{2,1,0:T(8,128)(2,1)} %get-tuple-element.176), channel_id=1, source_target_pairs={{0,28},{4,24},{8,20},{12,16},{16,12},{20,8},{24,4},{28,0},{1,29},{... | collective-permute-start | bytes 786440 | tf_op jit(solution)/shard_map/ppermute | solution.py:276
  (32 other events, 305.2 us)

commit v4 on v3

--- a/solution.py
+++ b/solution.py
@@ -67,26 +67,34 @@
     return slice(h * HEAD_DIM, (h + 1) * HEAD_DIM)
 
 
+def shifted_starts(me_ref, starts_ref):
+    return starts_ref[...] - me_ref[0] * starts_ref.shape[1]
+
+
 def deal(me_ref, held, out_refs):
+    share = me_ref[0] & (len(out_refs) - 1)
     for n, out_ref in enumerate(out_refs):
-        out_ref[...] = held[me_ref[0] ^ n]
+        out_ref[...] = held[share ^ n]
 
 
 def collect(me_ref, in_refs, held):
+    share = me_ref[0] & (len(in_refs) - 1)
     for n, in_ref in enumerate(in_refs):
-        held[me_ref[0] ^ n] = in_ref[...]
+        held[share ^ n] = in_ref[...]
 
 
 def gather_state(me_ref, in_refs, state_ref):
     rows = in_refs[0].shape[0]
+    share = me_ref[0] & (len(in_refs) - 1)
     for n, in_ref in enumerate(in_refs):
-        here = pl.ds(pl.multiple_of((me_ref[0] ^ n) * rows, rows), rows)
+        here = pl.ds(pl.multiple_of((share ^ n) * rows, rows), rows)
         state_ref[here, :] = in_ref[...]
 
 
 def first_kernel(shares, me_ref, ld_ref, rel_ref, w_ref, x_ref, lcol_ref, lrow_ref, *refs):
     out_refs, out_ref = refs[:shares], refs[shares]
     heads, length = ld_ref.shape
+    rel_row = shifted_starts(me_ref, rel_ref)
     parts, rows = out_ref.shape[0], out_ref.shape[1] - TAIL
     rates = ld_ref[...] * LOG2E
     lower = jnp.where(iota((length, length), 0) >= iota((length, length), 1), 1.0, 0.0)
@@ -94,7 +102,7 @@
     lcol_ref[...] = dot_nt(lower, rates, HIGH)
     lrow = jnp.dot(rates, upper, preferred_element_type=F32, precision=HIGH)
     lrow_ref[...] = lrow
-    rel_last = rel_ref[:, length - 1 :]
+    rel_last = rel_row[:, length - 1 :]
     last_doc = iota((1, length), 1) >= rel_last
     keeps = rel_last < 0
     writes = w_ref[...].astype(F32).T
@@ -163,7 +171,7 @@
     gather_state(me_ref, state_refs, s_ref)
     length, heads = lcol_ref.shape
     reads = r_ref[...]
-    rel = column(rel_ref[...].astype(F32))
+    rel = column(shifted_starts(me_ref, rel_ref).astype(F32))
     wide = jnp.concatenate([rel] * (length // 128), axis=1)
     seen = (iota((length, length), 1).astype(F32) >= wide) & (
         iota((length, length), 1) <= iota((length, length), 0)
@@ -201,7 +209,7 @@
     rms = column(scale)
     pull = column(scale * scale * scale * sums_ref[1:2, :] / width)
     reads = r_ref[...].astype(F32).T
-    enters = rel_ref[...] < 0
+    enters = shifted_starts(me_ref, rel_ref) < 0
     for h in range(heads):
         mixed = mixed_ref[:, cols(h)]
         gate = gate_ref[:, cols(h)].astype(F32)
@@ -228,10 +236,10 @@
 
 
 def inner_kernel(
-    dmixed_ref, x_ref, w_ref, r_ref, rel_ref, lcol_ref, lrow_ref, s_ref, gin_ref, read_ref, write_ref
+    me_ref, dmixed_ref, x_ref, w_ref, r_ref, rel_ref, lcol_ref, lrow_ref, s_ref, gin_ref, read_ref, write_ref
 ):
     length, heads = lcol_ref.shape
-    rel_row = rel_ref[...]
+    rel_row = shifted_starts(me_ref, rel_ref)
     rel = column(rel_row.astype(F32))
     seen = (iota((length, length), 0) >= rel_row) & (
         iota((length, length), 0) <= iota((length, length), 1)
@@ -256,7 +264,7 @@
     state_refs, (out_ref, write_ref, back_ref) = refs[:shares], refs[shares:]
     gather_state(me_ref, state_refs, back_ref)
     length, heads = lcol_ref.shape
-    rel_last = rel_ref[:, length - 1 :]
+    rel_last = shifted_starts(me_ref, rel_ref)[:, length - 1 :]
     last_doc = iota((length, 128), 0) >= rel_last
     writes = w_ref[...]
     write = part_ref[...]
@@ -528,9 +536,8 @@
     per = att_width // ATT_DIM // parts
     dealt = att_width // ATT_DIM % parts == 0
     place = lax.axis_index("ctx")
-    rel = (doc_start - place * length).reshape(1, length)
+    starts = doc_start.reshape(1, length)
     me = place.reshape(1).astype(jnp.int32)
-    share = (place % shares).reshape(1).astype(jnp.int32)
     tailed = [shape((rows + TAIL, 128), BF16)] * shares
     plain = [shape((rows, 128), BF16)] * shares
     held_tails = pltpu.VMEM((shares, rows + TAIL, 128), BF16)
@@ -539,7 +546,7 @@
     def carry_total(backward, *blocks):
         return call(
             lambda *refs: total_kernel(backward, shares, *refs),
-            shape((rows, 128), BF16), share, *blocks,
+            shape((rows, 128), BF16), me, *blocks,
             specs=[SMEM] + [VMEM] * len(blocks),
             scratch=[held_tails, held_plain] if backward else [held_tails],
             vmem=SMALL, name="ssm_total",
@@ -548,7 +555,7 @@
     def carry_states(backward, start, *blocks):
         return call(
             lambda *refs: carry_kernel(backward, shares, *refs),
-            plain, share, start, *blocks,
+            plain, me, start, *blocks,
             specs=[SMEM] + [VMEM] * (1 + len(blocks)),
             scratch=[held_tails, held_plain, held_plain] if backward else [held_tails, held_plain],
             vmem=SMALL, name="ssm_carry",
@@ -557,7 +564,7 @@
     lcol, lrow, *sent = call(
         lambda *refs: first_kernel(shares, *refs),
         [shape((length, heads), F32), shape((heads, length), F32)] + tailed,
-        share, log_decay.T, rel, write_map, ssm_input,
+        me, log_decay.T, starts, write_map, ssm_input,
         specs=[SMEM] + [VMEM] * 4, scratch=[held_tails], name="ssm_first",
     )
     tails = [pass_block(block, n) for n, block in enumerate(sent)]
@@ -565,7 +572,7 @@
         marks = doc_start.reshape(length // 128, 128)
         marks = jnp.stack([marks // 128, marks % 128], axis=1).reshape(length // 64, 128)
         marks = jnp.pad(marks, ((0, TAIL - length // 64), (0, 0))).astype(BF16)
-        marks, sent = lax.optimization_barrier((marks, sent))
+        marks, tails[1] = lax.optimization_barrier((marks, tails[1]))
         packed = call(
             pack_kernel, [shape((per, 4 * length + TAIL, 128), BF16)] * parts,
             me, marks, att_queries, att_keys, att_values, att_grad,
@@ -597,17 +604,20 @@
     mixed, sums, state = call(
         lambda *refs: mix_kernel(shares, *refs),
         (shape((length, width), F32), shape((8, length), F32), shape((width, 128), BF16)),
-        share, ssm_input, gate_input, ssm_grad, write_map, read_map, rel, lcol, lrow, *state,
+        me, ssm_input, gate_input, ssm_grad, write_map, read_map, starts, lcol, lrow, *state,
         specs=[SMEM] + [VMEM] * (8 + shares), name="ssm_mix",
     )
     sums = lax.psum(sums, "head")
     mixer_out, gate_grad, dmixed, *sent = call(
         lambda *refs: gate_kernel(full_width, shares, *refs),
         [shape((length, width), BF16)] * 3 + plain,
-        share, sums, mixed, gate_input, ssm_grad, read_map, rel, lrow,
+        me, sums, mixed, gate_input, ssm_grad, read_map, starts, lrow,
         specs=[SMEM] + [VMEM] * 7, scratch=[held_plain], name="ssm_gate",
     )
 
+    if dealt:
+        done, sent = lax.optimization_barrier(([att_got[n] for n in rest], sent))
+        att_got.update(zip(rest, done))
     blocks = [pass_block(block, n) for n, block in enumerate(sent)]
     total = carry_total(True, *tails, *blocks)
     start = cross(total, True)
@@ -646,12 +656,13 @@
     gin, read_part, write_part = call(
         inner_kernel,
         (shape((length, width), F32), shape((length, 128), F32), shape((length, 128), F32)),
-        dmixed, ssm_input, write_map, read_map, rel, lcol, lrow, state, name="ssm_inner",
+        me, dmixed, ssm_input, write_map, read_map, starts, lcol, lrow, state,
+        specs=[SMEM] + [VMEM] * 8, name="ssm_inner",
     )
     input_grad, write_part = call(
         lambda *refs: last_kernel(shares, *refs),
         (shape((length, width), BF16), shape((length, 128), F32)),
-        share, gin, ssm_input, write_map, rel, lcol, write_part, *back,
+        me, gin, ssm_input, write_map, starts, lcol, write_part, *back,
         specs=[SMEM] + [VMEM] * (6 + shares),
         scratch=[pltpu.VMEM((width, 128), BF16)], name="ssm_last",
     )

time: 181 us -> 168 us (0.928)
  waiting for transfers between devices: 42.4 us -> 28.7 us
  starting transfers between devices: 49.3 us -> 56 us
  blocking collectives: 36.4 us -> 33 us
    ppermute x26, waiting for transfers between devices: 40.5 us -> 26.8 us  [pass_block(): lax.ppermute(block, 'ctx', [(i, i ^ n) for i in range(lax.axis_size('ctx'...]
    ppermute x26, starting transfers between devices: 43.7 us -> 51.4 us  [pass_block(): lax.ppermute(block, 'ctx', [(i, i ^ n) for i in range(lax.axis_size('ctx'...]
    psum x1, blocking collectives: 27.9 us -> 25.6 us  [body(): write_sum, read_sum = lax.psum((write_part, read_part), 'head')]
    unnamed x56 -> x52, local copies, waits for them, and re-layouts: 7.8 us -> 6.45 us
  transfers between devices with their start and end apart: 28 -> 28, of which waited for: 14 -> 13; matrix products, arithmetic and copies ran while one was open for 0% -> 0% of each run, Pallas kernels for 13% -> 21%
where the time goes in v4:
time: 168 us
  starting transfers between devices  56 us (33%)
  Pallas kernels  41.9 us (25%)
  blocking collectives  33 us (20%)
  waiting for transfers between devices  28.7 us (17%)
  local copies, waits for them, and re-layouts  6.46 us (4%)
    ppermute x26, starting transfers between devices, pass_block(): lax.ppermute(block, 'ctx', [(i, i ^ n) for i in range(lax.axis_size('ctx'...  51.4 us
    pallas_call x12, Pallas kernels, call(): pl.pallas_call(kernel, out_shape=out_shape, in_specs=specs or [VMEM] * le...  41.9 us
    ppermute x26, waiting for transfers between devices, pass_block(): lax.ppermute(block, 'ctx', [(i, i ^ n) for i in range(lax.axis_size('ctx'...  26.8 us
    psum x1, blocking collectives, body(): write_sum, read_sum = lax.psum((write_part, read_part), 'head')  25.6 us
    psum x1, blocking collectives, body(): sums = lax.psum(sums, 'head')  7.39 us
    unnamed x52, local copies, waits for them, and re-layouts  6.45 us
    ppermute x2, starting transfers between devices, cross(): return lax.ppermute(total, 'ctx', pairs)  4.6 us
  transfers between devices with their start and end apart: 28, of which 13 were waited for; matrix products, arithmetic and copies ran while one was open for 0% of the time, Pallas kernels for 21%

profile of v4, /device:TPU:1, one launch (start us, length us, event | category | flops | bytes accessed | tf_op | source)
XLA Modules:
  0.0 167.7 jit_solution(15017125632957922125)
XLA Ops:
  0.6 3.0 %ssm_first.1 = (f32[256,16]{1,0:T(8,128)}, f32[16,256]{1,0:T(8,128)}, bf16[528,128]{1,0:T(8,128)(2,1)}, bf16[528,128]{1,0:T(8,128)(2,1)}, bf16[528,128]{1,0:T(8,128)(2,1)}, /*index=5*/bf16[528,128]{1,0:T(8,128)(2,1)}) custom-call(s32[1]{0:T(128)} %bitcast.refs_0_.me_ref, f32[16,256]{1,0:T(8,128)} %bitcast.11, s32[1,256]{1,0:T(1,128)} %bitcast.5, ...), custom_call_target="tpu_custom_call" | custom-call | bytes 1704964 | tf_op jit(solution)/shard_map/ssm_first/pallas_call | solution.py:28
  6.4 2.8 %collective-permute-done.refs_2_.refs_3_ = bf16[528,128]{1,0:T(8,128)(2,1)S(1)} collective-permute-done((bf16[528,128]{1,0:T(8,128)(2,1)}, bf16[528,128]{1,0:T(8,128)(2,1)S(1)}, u32[]{:S(2)}, u32[]{:S(2)}) %collective-permute-start) | collective-permute-done | bytes 135200 | tf_op jit(solution)/shard_map/ppermute | solution.py:284
  18.7 4.7 %collective-permute-done.1.refs_3_.refs_4_ = bf16[528,128]{1,0:T(8,128)(2,1)S(1)} collective-permute-done((bf16[528,128]{1,0:T(8,128)(2,1)S(1)}, bf16[528,128]{1,0:T(8,128)(2,1)S(1)}, u32[]{:S(2)}, u32[]{:S(2)}) %collective-permute-start.1) | collective-permute-done | bytes 135200 | tf_op jit(solution)/shard_map/ppermute | solution.py:284
  23.4 2.9 %collective-permute-done.2.refs_4_.refs_5_ = bf16[528,128]{1,0:T(8,128)(2,1)S(1)} collective-permute-done((bf16[528,128]{1,0:T(8,128)(2,1)S(1)}, bf16[528,128]{1,0:T(8,128)(2,1)S(1)}, u32[]{:S(2)}, u32[]{:S(2)}) %collective-permute-start.2) | collective-permute-done | bytes 135200 | tf_op jit(solution)/shard_map/ppermute | solution.py:284
  28.0 3.1 %collective-permute-start.4 = (bf16[512,128]{1,0:T(8,128)(2,1)S(1)}, bf16[512,128]{1,0:T(8,128)(2,1)S(1)}, u32[]{:S(2)}, u32[]{:S(2)}) collective-permute-start(bf16[512,128]{1,0:T(8,128)(2,1)S(1)} %ssm_total.2), channel_id=1, source_target_pairs={{0,16},{4,20},{8,24},{12,28},{1,17},{5,21},{9,25},{13,29},{2,18},{... | collective-permute-start | bytes 393224 | tf_op jit(solution)/shard_map/ppermute | solution.py:291
  33.0 2.7 %collective-permute-start.5 = (bf16[1,1040,128]{2,1,0:T(8,128)(2,1)S(1)}, bf16[1,1040,128]{2,1,0:T(8,128)(2,1)S(1)}, u32[]{:S(2)}, u32[]{:S(2)}) collective-permute-start(bf16[1,1040,128]{2,1,0:T(8,128)(2,1)S(1)} %get-tuple-element.127), channel_id=1, source_target_pairs={{0,20},{4,16},{8,28},{12,24},{16,4},{20,0},{24,12},{28,8},{1,21},{... | collective-permute-start | bytes 798728 | tf_op jit(solution)/shard_map/ppermute | solution.py:284
  37.8 8.5 %collective-permute-start.7 = (bf16[512,128]{1,0:T(8,128)(2,1)S(1)}, bf16[512,128]{1,0:T(8,128)(2,1)S(1)}, u32[]{:S(2)}, u32[]{:S(2)}) collective-permute-start(bf16[512,128]{1,0:T(8,128)(2,1)S(1)} %get-tuple-element.131), channel_id=1, source_target_pairs={{0,8},{4,12},{8,0},{12,4},{16,24},{20,28},{24,16},{28,20},{1,9},{5... | collective-permute-start | bytes 393224 | tf_op jit(solution)/shard_map/ppermute | solution.py:284
  48.8 3.9 %collective-permute-done.8.refs_12_ = bf16[512,128]{1,0:T(8,128)(2,1)S(1)} collective-permute-done((bf16[512,128]{1,0:T(8,128)(2,1)S(1)}, bf16[512,128]{1,0:T(8,128)(2,1)S(1)}, u32[]{:S(2)}, u32[]{:S(2)}) %collective-permute-start.8) | collective-permute-done | bytes 131104 | tf_op jit(solution)/shard_map/ppermute | solution.py:284
  52.6 7.2 %collective-permute-start.9 = (bf16[1,1040,128]{2,1,0:T(8,128)(2,1)S(1)}, bf16[1,1040,128]{2,1,0:T(8,128)(2,1)S(1)}, u32[]{:S(2)}, u32[]{:S(2)}) collective-permute-start(bf16[1,1040,128]{2,1,0:T(8,128)(2,1)S(1)} %get-tuple-element.140), channel_id=1, source_target_pairs={{0,24},{4,28},{8,16},{12,20},{16,8},{20,12},{24,0},{28,4},{1,25},{... | collective-permute-start | bytes 798728 | tf_op jit(solution)/shard_map/ppermute | solution.py:284
  61.3 2.4 %collective-permute-start.13 = (bf16[1,1040,128]{2,1,0:T(8,128)(2,1)S(1)}, bf16[1,1040,128]{2,1,0:T(8,128)(2,1)}, u32[]{:S(2)}, u32[]{:S(2)}) collective-permute-start(bf16[1,1040,128]{2,1,0:T(8,128)(2,1)S(1)} %get-tuple-element.144), channel_id=1, source_target_pairs={{0,12},{4,8},{8,4},{12,0},{16,28},{20,24},{24,20},{28,16},{1,13},{... | collective-permute-start | bytes 798728 | tf_op jit(solution)/shard_map/ppermute | solution.py:284
  63.8 6.0 %ssm_mix.1 = (f32[256,2048]{1,0:T(8,128)}, f32[8,256]{1,0:T(8,128)}, bf16[2048,128]{1,0:T(8,128)(2,1)}) custom-call(s32[1]{0:T(128)} %bitcast.refs_0_.me_ref, bf16[256,2048]{1,0:T(8,128)(2,1)} %refs_2_.3, bf16[256,2048]{1,0:T(8,128)(2,1)} %refs_3_.6, bf16[256,2048]{1,0:T(8,128)(2,1)} %refs_4_.5, bf16[256,128]{1,0:T(8,128)(2,1)} %refs_3_.7, ...), custom_call_target="tpu_custom_call" | custom-call | bytes 6464516 | tf_op jit(solution)/shard_map/ssm_mix/pallas_call | solution.py:28
  69.8 7.4 %psum.21.refs_1_ = f32[8,256]{1,0:T(8,128)} all-reduce(f32[8,256]{1,0:T(8,128)} %get-tuple-element.137), channel_id=1, replica_groups=mesh['ctx'=8,'head'=4] {'head'}, use_global_device_ids=true, to_apply=%region_0.1 | all-reduce | flops 2048 | bytes 16384 | tf_op jit(solution)/shard_map/psum | solution.py:610
  77.1 5.9 %ssm_gate.1 = (bf16[256,2048]{1,0:T(8,128)(2,1)}, bf16[256,2048]{1,0:T(8,128)(2,1)}, bf16[256,2048]{1,0:T(8,128)(2,1)}, bf16[512,128]{1,0:T(8,128)(2,1)}, bf16[5...) custom-call(s32[1]{0:T(128)} %bitcast.refs_0_.me_ref, f32[8,256]{1,0:T(8,128)} %psum.21.refs_1_, ...), custom_call_target="tpu_custom_call" | custom-call | bytes 7955460 | tf_op jit(solution)/shard_map/ssm_gate/pallas_call | solution.py:28
  83.1 2.8 %collective-permute-done.13.refs_4_ = bf16[1,1040,128]{2,1,0:T(8,128)(2,1)} collective-permute-done((bf16[1,1040,128]{2,1,0:T(8,128)(2,1)S(1)}, bf16[1,1040,128]{2,1,0:T(8,128)(2,1)}, u32[]{:S(2)}, u32[]{:S(2)}) %collective-permute-start.13) | collective-permute-done | bytes 266272 | tf_op jit(solution)/shard_map/ppermute | solution.py:284
  86.6 2.8 %collective-permute-start.15 = (bf16[512,128]{1,0:T(8,128)(2,1)}, bf16[512,128]{1,0:T(8,128)(2,1)S(1)}, u32[]{:S(2)}, u32[]{:S(2)}) collective-permute-start(bf16[512,128]{1,0:T(8,128)(2,1)} %get-tuple-element.151), channel_id=1, source_target_pairs={{0,8},{4,12},{8,0},{12,4},{16,24},{20,28},{24,16},{28,20},{1,9},{5... | collective-permute-start | bytes 393224 | tf_op jit(solution)/shard_map/ppermute | solution.py:284
  89.9 2.4 %collective-permute-done.15.refs_7_.refs_8_ = bf16[512,128]{1,0:T(8,128)(2,1)S(1)} collective-permute-done((bf16[512,128]{1,0:T(8,128)(2,1)}, bf16[512,128]{1,0:T(8,128)(2,1)S(1)}, u32[]{:S(2)}, u32[]{:S(2)}) %collective-permute-start.15) | collective-permute-done | bytes 131104 | tf_op jit(solution)/shard_map/ppermute | solution.py:284
  92.3 3.4 %collective-permute-done.16.refs_8_.refs_9_ = bf16[512,128]{1,0:T(8,128)(2,1)S(1)} collective-permute-done((bf16[512,128]{1,0:T(8,128)(2,1)}, bf16[512,128]{1,0:T(8,128)(2,1)S(1)}, u32[]{:S(2)}, u32[]{:S(2)}) %collective-permute-start.16) | collective-permute-done | bytes 131104 | tf_op jit(solution)/shard_map/ppermute | solution.py:284
  98.2 14.8 %att_attend.1 = (bf16[1,1024,128]{2,1,0:T(8,128)(2,1)}, bf16[1,1024,128]{2,1,0:T(8,128)(2,1)}, bf16[1,1024,128]{2,1,0:T(8,128)(2,1)}, bf16[1,1024,128]{2,1,0:T(8...) custom-call(s32[1]{0:T(128)} %bitcast.refs_0_.me_ref, ...), custom_call_target="tpu_custom_call" | custom-call | flops 3221225472 | bytes 4227076 | tf_op jit(solution)/shard_map/att_attend/pallas_call | solution.py:28
  116.6 3.0 %collective-permute-start.24 = (bf16[1,1024,128]{2,1,0:T(8,128)(2,1)}, bf16[1,1024,128]{2,1,0:T(8,128)(2,1)S(1)}, u32[]{:S(2)}, u32[]{:S(2)}) collective-permute-start(bf16[1,1024,128]{2,1,0:T(8,128)(2,1)} %get-tuple-element.181), channel_id=1, source_target_pairs={{0,16},{4,20},{8,24},{12,28},{16,0},{20,4},{24,8},{28,12},{1,17},{... | collective-permute-start | bytes 786440 | tf_op jit(solution)/shard_map/ppermute | solution.py:284
  123.1 3.3 %collective-permute-start.25 = (bf16[1,1024,128]{2,1,0:T(8,128)(2,1)}, bf16[1,1024,128]{2,1,0:T(8,128)(2,1)S(1)}, u32[]{:S(2)}, u32[]{:S(2)}) collective-permute-start(bf16[1,1024,128]{2,1,0:T(8,128)(2,1)} %get-tuple-element.194), channel_id=1, source_target_pairs={{0,20},{4,16},{8,28},{12,24},{16,4},{20,0},{24,12},{28,8},{1,21},{... | collective-permute-start | bytes 786440 | tf_op jit(solution)/shard_map/ppermute | solution.py:284
  126.7 3.2 %collective-permute-start.26 = (bf16[1,1024,128]{2,1,0:T(8,128)(2,1)}, bf16[1,1024,128]{2,1,0:T(8,128)(2,1)S(1)}, u32[]{:S(2)}, u32[]{:S(2)}) collective-permute-start(bf16[1,1024,128]{2,1,0:T(8,128)(2,1)} %get-tuple-element.195), channel_id=1, source_target_pairs={{0,24},{4,28},{8,16},{12,20},{16,8},{20,12},{24,0},{28,4},{1,25},{... | collective-permute-start | bytes 786440 | tf_op jit(solution)/shard_map/ppermute | solution.py:284
  131.0 4.9 %ssm_inner.1 = (f32[256,2048]{1,0:T(8,128)}, f32[256,128]{1,0:T(8,128)}, f32[256,128]{1,0:T(8,128)}) custom-call(s32[1]{0:T(128)} %bitcast.refs_0_.me_ref, bf16[256,2048]{1,0:T(8,128)(2,1)} %get-tuple-element.198.dmixed_ref, bf16[256,2048]{1,0:T(8,128)(2,1)} %refs_2_.3, bf16[256,128]{1,0:T(8,128)(2,1)} %refs_3_.7, bf16[256,128]{1,0:T(8,128)(2,1)} %r_ref.1, ...), custom_call_target="tpu_custom_call" | custom-call | bytes 5145604 | tf_op jit(solution)/shard_map/ssm_inner/pallas_call | solution.py:28
  136.0 4.2 %ssm_last.1 = (bf16[256,2048]{1,0:T(8,128)(2,1)}, f32[256,128]{1,0:T(8,128)}) custom-call(s32[1]{0:T(128)} %bitcast.refs_0_.me_ref, f32[256,2048]{1,0:T(8,128)} %get-tuple-element.200.refs_1_, bf16[256,2048]{1,0:T(8,128)(2,1)} %refs_2_.3, bf16[256,128]{1,0:T(8,128)(2,1)} %refs_3_.7, s32[1,256]{1,0:T(1,128)} %bitcast.10, ...), custom_call_target="tpu_custom_call" | custom-call | bytes 5063684 | tf_op jit(solution)/shard_map/ssm_last/pallas_call | solution.py:28
  140.2 25.6 %all-reduce.3 = (bf16[256,128]{1,0:T(8,128)(2,1)}, bf16[256,128]{1,0:T(8,128)(2,1)}) all-reduce(f32[256,128]{1,0:T(8,128)} %get-tuple-element.208, f32[256,128]{1,0:T(8,128)S(1)} %copy-done.17), channel_id=1, replica_groups=mesh['ctx'=8,'head'=4] {'head'}, use_global_device_ids=true, to_apply=%region_1.2 | all-reduce | flops 65536 | bytes 393216 | tf_op jit(solution)/shard_map/psum | solution.py:669
  (102 shorter events, 36.0 us)
Async XLA Ops:
  14.0 14.0 %collective-permute-start.3 = (bf16[1,1040,128]{2,1,0:T(8,128)(2,1)S(1)}, bf16[1,1040,128]{2,1,0:T(8,128)(2,1)S(1)}, u32[]{:S(2)}, u32[]{:S(2)}) collective-permute-start(bf16[1,1040,128]{2,1,0:T(8,128)(2,1)S(1)} %get-tuple-element.124), channel_id=1, source_target_pairs={{0,16},{4,20},{8,24},{12,28},{16,0},{20,4},{24,8},{28,12},{1,17},{... | collective-permute-start | bytes 798728 | tf_op jit(solution)/shard_map/ppermute | solution.py:284
  16.3 7.1 %collective-permute-start.1 = (bf16[528,128]{1,0:T(8,128)(2,1)S(1)}, bf16[528,128]{1,0:T(8,128)(2,1)S(1)}, u32[]{:S(2)}, u32[]{:S(2)}) collective-permute-start(bf16[528,128]{1,0:T(8,128)(2,1)S(1)} %copy-done.25), channel_id=1, source_target_pairs={{0,8},{4,12},{8,0},{12,4},{16,24},{20,28},{24,16},{28,20},{1,9},{5... | collective-permute-start | bytes 405512 | tf_op jit(solution)/shard_map/ppermute | solution.py:284
  17.6 8.7 %collective-permute-start.2 = (bf16[528,128]{1,0:T(8,128)(2,1)S(1)}, bf16[528,128]{1,0:T(8,128)(2,1)S(1)}, u32[]{:S(2)}, u32[]{:S(2)}) collective-permute-start(bf16[528,128]{1,0:T(8,128)(2,1)S(1)} %copy-done.24), channel_id=1, source_target_pairs={{0,12},{4,8},{8,4},{12,0},{16,28},{20,24},{24,20},{28,16},{1,13},{... | collective-permute-start | bytes 405512 | tf_op jit(solution)/shard_map/ppermute | solution.py:284
  33.0 19.6 %collective-permute-start.5 = (bf16[1,1040,128]{2,1,0:T(8,128)(2,1)S(1)}, bf16[1,1040,128]{2,1,0:T(8,128)(2,1)S(1)}, u32[]{:S(2)}, u32[]{:S(2)}) collective-permute-start(bf16[1,1040,128]{2,1,0:T(8,128)(2,1)S(1)} %get-tuple-element.127), channel_id=1, source_target_pairs={{0,20},{4,16},{8,28},{12,24},{16,4},{20,0},{24,12},{28,8},{1,21},{... | collective-permute-start | bytes 798728 | tf_op jit(solution)/shard_map/ppermute | solution.py:284
  36.6 11.0 %collective-permute-start.6 = (bf16[512,128]{1,0:T(8,128)(2,1)S(1)}, bf16[512,128]{1,0:T(8,128)(2,1)S(1)}, u32[]{:S(2)}, u32[]{:S(2)}) collective-permute-start(bf16[512,128]{1,0:T(8,128)(2,1)S(1)} %get-tuple-element.130), channel_id=1, source_target_pairs={{0,4},{4,0},{8,12},{12,8},{16,20},{20,16},{24,28},{28,24},{1,5},{5... | collective-permute-start | bytes 393224 | tf_op jit(solution)/shard_map/ppermute | solution.py:284
  37.8 10.9 %collective-permute-start.7 = (bf16[512,128]{1,0:T(8,128)(2,1)S(1)}, bf16[512,128]{1,0:T(8,128)(2,1)S(1)}, u32[]{:S(2)}, u32[]{:S(2)}) collective-permute-start(bf16[512,128]{1,0:T(8,128)(2,1)S(1)} %get-tuple-element.131), channel_id=1, source_target_pairs={{0,8},{4,12},{8,0},{12,4},{16,24},{20,28},{24,16},{28,20},{1,9},{5... | collective-permute-start | bytes 393224 | tf_op jit(solution)/shard_map/ppermute | solution.py:284
  46.4 6.2 %collective-permute-start.8 = (bf16[512,128]{1,0:T(8,128)(2,1)S(1)}, bf16[512,128]{1,0:T(8,128)(2,1)S(1)}, u32[]{:S(2)}, u32[]{:S(2)}) collective-permute-start(bf16[512,128]{1,0:T(8,128)(2,1)S(1)} %get-tuple-element.132), channel_id=1, source_target_pairs={{0,12},{4,8},{8,4},{12,0},{16,28},{20,24},{24,20},{28,16},{1,13},{... | collective-permute-start | bytes 393224 | tf_op jit(solution)/shard_map/ppermute | solution.py:284
  52.6 30.4 %collective-permute-start.9 = (bf16[1,1040,128]{2,1,0:T(8,128)(2,1)S(1)}, bf16[1,1040,128]{2,1,0:T(8,128)(2,1)S(1)}, u32[]{:S(2)}, u32[]{:S(2)}) collective-permute-start(bf16[1,1040,128]{2,1,0:T(8,128)(2,1)S(1)} %get-tuple-element.140), channel_id=1, source_target_pairs={{0,24},{4,28},{8,16},{12,20},{16,8},{20,12},{24,0},{28,4},{1,25},{... | collective-permute-start | bytes 798728 | tf_op jit(solution)/shard_map/ppermute | solution.py:284
  59.8 23.2 %collective-permute-start.10 = (bf16[1,1040,128]{2,1,0:T(8,128)(2,1)S(1)}, bf16[1,1040,128]{2,1,0:T(8,128)(2,1)S(1)}, u32[]{:S(2)}, u32[]{:S(2)}) collective-permute-start(bf16[1,1040,128]{2,1,0:T(8,128)(2,1)S(1)} %get-tuple-element.141), channel_id=1, source_target_pairs={{0,28},{4,24},{8,20},{12,16},{16,12},{20,8},{24,4},{28,0},{1,29},{... | collective-permute-start | bytes 798728 | tf_op jit(solution)/shard_map/ppermute | solution.py:284
  61.1 21.9 %collective-permute-start.11 = (bf16[1,1040,128]{2,1,0:T(8,128)(2,1)S(1)}, bf16[1,1040,128]{2,1,0:T(8,128)(2,1)S(1)}, u32[]{:S(2)}, u32[]{:S(2)}) collective-permute-start(bf16[1,1040,128]{2,1,0:T(8,128)(2,1)S(1)} %get-tuple-element.142), channel_id=1, source_target_pairs={{0,4},{4,0},{8,12},{12,8},{16,20},{20,16},{24,28},{28,24},{1,5},{5... | collective-permute-start | bytes 798728 | tf_op jit(solution)/shard_map/ppermute | solution.py:284
  61.3 21.7 %collective-permute-start.12 = (bf16[1,1040,128]{2,1,0:T(8,128)(2,1)S(1)}, bf16[1,1040,128]{2,1,0:T(8,128)(2,1)S(1)}, u32[]{:S(2)}, u32[]{:S(2)}) collective-permute-start(bf16[1,1040,128]{2,1,0:T(8,128)(2,1)S(1)} %get-tuple-element.143), channel_id=1, source_target_pairs={{0,8},{4,12},{8,0},{12,4},{16,24},{20,28},{24,16},{28,20},{1,9},{5... | collective-permute-start | bytes 798728 | tf_op jit(solution)/shard_map/ppermute | solution.py:284
  61.3 24.5 %collective-permute-start.13 = (bf16[1,1040,128]{2,1,0:T(8,128)(2,1)S(1)}, bf16[1,1040,128]{2,1,0:T(8,128)(2,1)}, u32[]{:S(2)}, u32[]{:S(2)}) collective-permute-start(bf16[1,1040,128]{2,1,0:T(8,128)(2,1)S(1)} %get-tuple-element.144), channel_id=1, source_target_pairs={{0,12},{4,8},{8,4},{12,0},{16,28},{20,24},{24,20},{28,16},{1,13},{... | collective-permute-start | bytes 798728 | tf_op jit(solution)/shard_map/ppermute | solution.py:284
  86.6 5.7 %collective-permute-start.15 = (bf16[512,128]{1,0:T(8,128)(2,1)}, bf16[512,128]{1,0:T(8,128)(2,1)S(1)}, u32[]{:S(2)}, u32[]{:S(2)}) collective-permute-start(bf16[512,128]{1,0:T(8,128)(2,1)} %get-tuple-element.151), channel_id=1, source_target_pairs={{0,8},{4,12},{8,0},{12,4},{16,24},{20,28},{24,16},{28,20},{1,9},{5... | collective-permute-start | bytes 393224 | tf_op jit(solution)/shard_map/ppermute | solution.py:284
  89.4 6.2 %collective-permute-start.16 = (bf16[512,128]{1,0:T(8,128)(2,1)}, bf16[512,128]{1,0:T(8,128)(2,1)S(1)}, u32[]{:S(2)}, u32[]{:S(2)}) collective-permute-start(bf16[512,128]{1,0:T(8,128)(2,1)} %get-tuple-element.152), channel_id=1, source_target_pairs={{0,12},{4,8},{8,4},{12,0},{16,28},{20,24},{24,20},{28,16},{1,13},{... | collective-permute-start | bytes 393224 | tf_op jit(solution)/shard_map/ppermute | solution.py:284
  96.7 16.3 %collective-permute-start.17 = (bf16[512,128]{1,0:T(8,128)(2,1)S(1)}, bf16[512,128]{1,0:T(8,128)(2,1)S(1)}, u32[]{:S(2)}, u32[]{:S(2)}) collective-permute-start(bf16[512,128]{1,0:T(8,128)(2,1)S(1)} %ssm_total.3), channel_id=1, source_target_pairs={{16,0},{20,4},{24,8},{28,12},{17,1},{21,5},{25,9},{29,13},{18,2},{... | collective-permute-start | bytes 393224 | tf_op jit(solution)/shard_map/ppermute | solution.py:291
  113.9 5.6 %collective-permute-start.18 = (bf16[512,128]{1,0:T(8,128)(2,1)S(1)}, bf16[512,128]{1,0:T(8,128)(2,1)S(1)}, u32[]{:S(2)}, u32[]{:S(2)}) collective-permute-start(bf16[512,128]{1,0:T(8,128)(2,1)S(1)} %get-tuple-element.187), channel_id=1, source_target_pairs={{0,4},{4,0},{8,12},{12,8},{16,20},{20,16},{24,28},{28,24},{1,5},{5... | collective-permute-start | bytes 393224 | tf_op jit(solution)/shard_map/ppermute | solution.py:284
  114.8 5.7 %collective-permute-start.20 = (bf16[512,128]{1,0:T(8,128)(2,1)S(1)}, bf16[512,128]{1,0:T(8,128)(2,1)S(1)}, u32[]{:S(2)}, u32[]{:S(2)}) collective-permute-start(bf16[512,128]{1,0:T(8,128)(2,1)S(1)} %get-tuple-element.189), channel_id=1, source_target_pairs={{0,12},{4,8},{8,4},{12,0},{16,28},{20,24},{24,20},{28,16},{1,13},{... | collective-permute-start | bytes 393224 | tf_op jit(solution)/shard_map/ppermute | solution.py:284
  116.6 10.1 %collective-permute-start.24 = (bf16[1,1024,128]{2,1,0:T(8,128)(2,1)}, bf16[1,1024,128]{2,1,0:T(8,128)(2,1)S(1)}, u32[]{:S(2)}, u32[]{:S(2)}) collective-permute-start(bf16[1,1024,128]{2,1,0:T(8,128)(2,1)} %get-tuple-element.181), channel_id=1, source_target_pairs={{0,16},{4,20},{8,24},{12,28},{16,0},{20,4},{24,8},{28,12},{1,17},{... | collective-permute-start | bytes 786440 | tf_op jit(solution)/shard_map/ppermute | solution.py:284
  120.5 9.5 %collective-permute-start.21 = (bf16[1,1024,128]{2,1,0:T(8,128)(2,1)}, bf16[1,1024,128]{2,1,0:T(8,128)(2,1)S(1)}, u32[]{:S(2)}, u32[]{:S(2)}) collective-permute-start(bf16[1,1024,128]{2,1,0:T(8,128)(2,1)} %get-tuple-element.191), channel_id=1, source_target_pairs={{0,4},{4,0},{8,12},{12,8},{16,20},{20,16},{24,28},{28,24},{1,5},{5... | collective-permute-start | bytes 786440 | tf_op jit(solution)/shard_map/ppermute | solution.py:284
  121.0 44.7 %collective-permute-start.22 = (bf16[1,1024,128]{2,1,0:T(8,128)(2,1)}, bf16[1,1024,128]{2,1,0:T(8,128)(2,1)S(1)}, u32[]{:S(2)}, u32[]{:S(2)}) collective-permute-start(bf16[1,1024,128]{2,1,0:T(8,128)(2,1)} %get-tuple-element.192), channel_id=1, source_target_pairs={{0,8},{4,12},{8,0},{12,4},{16,24},{20,28},{24,16},{28,20},{1,9},{5... | collective-permute-start | bytes 786440 | tf_op jit(solution)/shard_map/ppermute | solution.py:284
  121.7 44.0 %collective-permute-start.23 = (bf16[1,1024,128]{2,1,0:T(8,128)(2,1)}, bf16[1,1024,128]{2,1,0:T(8,128)(2,1)S(1)}, u32[]{:S(2)}, u32[]{:S(2)}) collective-permute-start(bf16[1,1024,128]{2,1,0:T(8,128)(2,1)} %get-tuple-element.193), channel_id=1, source_target_pairs={{0,12},{4,8},{8,4},{12,0},{16,28},{20,24},{24,20},{28,16},{1,13},{... | collective-permute-start | bytes 786440 | tf_op jit(solution)/shard_map/ppermute | solution.py:284
  123.1 42.6 %collective-permute-start.25 = (bf16[1,1024,128]{2,1,0:T(8,128)(2,1)}, bf16[1,1024,128]{2,1,0:T(8,128)(2,1)S(1)}, u32[]{:S(2)}, u32[]{:S(2)}) collective-permute-start(bf16[1,1024,128]{2,1,0:T(8,128)(2,1)} %get-tuple-element.194), channel_id=1, source_target_pairs={{0,20},{4,16},{8,28},{12,24},{16,4},{20,0},{24,12},{28,8},{1,21},{... | collective-permute-start | bytes 786440 | tf_op jit(solution)/shard_map/ppermute | solution.py:284
  126.7 39.0 %collective-permute-start.26 = (bf16[1,1024,128]{2,1,0:T(8,128)(2,1)}, bf16[1,1024,128]{2,1,0:T(8,128)(2,1)S(1)}, u32[]{:S(2)}, u32[]{:S(2)}) collective-permute-start(bf16[1,1024,128]{2,1,0:T(8,128)(2,1)} %get-tuple-element.195), channel_id=1, source_target_pairs={{0,24},{4,28},{8,16},{12,20},{16,8},{20,12},{24,0},{28,4},{1,25},{... | collective-permute-start | bytes 786440 | tf_op jit(solution)/shard_map/ppermute | solution.py:284
  130.0 35.8 %collective-permute-start.27 = (bf16[1,1024,128]{2,1,0:T(8,128)(2,1)}, bf16[1,1024,128]{2,1,0:T(8,128)(2,1)S(1)}, u32[]{:S(2)}, u32[]{:S(2)}) collective-permute-start(bf16[1,1024,128]{2,1,0:T(8,128)(2,1)} %get-tuple-element.196), channel_id=1, source_target_pairs={{0,28},{4,24},{8,20},{12,16},{16,12},{20,8},{24,4},{28,0},{1,29},{... | collective-permute-start | bytes 786440 | tf_op jit(solution)/shard_map/ppermute | solution.py:284
  (30 other events, 350.0 us)

commit v5 on v4

--- a/solution.py
+++ b/solution.py
@@ -572,35 +572,22 @@
         marks = doc_start.reshape(length // 128, 128)
         marks = jnp.stack([marks // 128, marks % 128], axis=1).reshape(length // 64, 128)
         marks = jnp.pad(marks, ((0, TAIL - length // 64), (0, 0))).astype(BF16)
-        marks, tails[1] = lax.optimization_barrier((marks, tails[1]))
+        marks, tails = lax.optimization_barrier((marks, tails))
         packed = call(
             pack_kernel, [shape((per, 4 * length + TAIL, 128), BF16)] * parts,
             me, marks, att_queries, att_keys, att_values, att_grad,
             specs=[SMEM] + [VMEM] * 5, vmem=SMALL, name="att_pack",
         )
-        packed = list(packed)
-        att_got = {0: packed[0]}
-        att_got[shares] = pass_block(packed[shares], shares)
+        att_got = {n: pass_block(block, n) for n, block in enumerate(packed)}
     else:
         att_out = ring_attention(att_queries, att_keys, att_values, att_grad, doc_start)
     total = carry_total(False, *tails)
-    if dealt:
-        total, att_got[shares] = lax.optimization_barrier((total, att_got[shares]))
     start = cross(total, False)
-    if dealt:
-        start, packed[shares + 1] = lax.optimization_barrier((start, packed[shares + 1]))
-        att_got[shares + 1] = pass_block(packed[shares + 1], shares + 1)
     state = [
         pass_block(block, n) for n, block in enumerate(carry_states(False, start, *tails))
     ]
     if dealt:
-        rest = [n for n in range(1, parts) if n not in att_got]
-        rest = [n for n in rest if n > shares] + [n for n in rest if n < shares]
-        held, att_got[shares + 1], state = lax.optimization_barrier(
-            ([packed[n] for n in rest], att_got[shares + 1], state)
-        )
-        for n, block in zip(rest, held):
-            att_got[n] = pass_block(block, n)
+        att_got[shares], state = lax.optimization_barrier((att_got[shares], state))
     mixed, sums, state = call(
         lambda *refs: mix_kernel(shares, *refs),
         (shape((length, width), F32), shape((8, length), F32), shape((width, 128), BF16)),
@@ -616,6 +603,7 @@
     )
 
     if dealt:
+        rest = [n for n in range(1, parts - 1) if n != shares]
         done, sent = lax.optimization_barrier(([att_got[n] for n in rest], sent))
         att_got.update(zip(rest, done))
     blocks = [pass_block(block, n) for n, block in enumerate(sent)]
@@ -642,9 +630,15 @@
     back = [
         pass_block(block, n) for n, block in enumerate(carry_states(True, start, *tails, *blocks))
     ]
+    gin, read_part, write_part = call(
+        inner_kernel,
+        (shape((length, width), F32), shape((length, 128), F32), shape((length, 128), F32)),
+        me, dmixed, ssm_input, write_map, read_map, starts, lcol, lrow, state,
+        specs=[SMEM] + [VMEM] * 8, name="ssm_inner",
+    )
     if dealt:
         att_back = {shares: pass_block(att_done[shares], shares)}
-        held, back = lax.optimization_barrier((att_done, back))
+        held, back, gin = lax.optimization_barrier((att_done, back, gin))
         for n in [n for n in range(parts)[::-1] if n != shares]:
             att_back[n] = pass_block(held[n], n)
         att_out = call(
@@ -653,12 +647,6 @@
             specs=[SMEM] + [VMEM] * parts, vmem=SMALL, name="att_unpack",
         )
 
-    gin, read_part, write_part = call(
-        inner_kernel,
-        (shape((length, width), F32), shape((length, 128), F32), shape((length, 128), F32)),
-        me, dmixed, ssm_input, write_map, read_map, starts, lcol, lrow, state,
-        specs=[SMEM] + [VMEM] * 8, name="ssm_inner",
-    )
     input_grad, write_part = call(
         lambda *refs: last_kernel(shares, *refs),
         (shape((length, width), BF16), shape((length, 128), F32)),

time: 168 us -> 163 us (0.970)
  waiting for transfers between devices: 28.7 us -> 18.7 us
  blocking collectives: 33 us -> 40.6 us
  starting transfers between devices: 56 us -> 52.5 us
    ppermute x26, waiting for transfers between devices: 26.8 us -> 14.4 us  [pass_block(): lax.ppermute(block, 'ctx', [(i, i ^ n) for i in range(lax.axis_size('ctx'...]
    psum x1, blocking collectives: 25.6 us -> 30.7 us  [body(): write_sum, read_sum = lax.psum((write_part, read_part), 'head')]
    psum x1, blocking collectives: 7.39 us -> 9.82 us  [body(): sums = lax.psum(sums, 'head')]
    ppermute x2, waiting for transfers between devices: 1.93 us -> 4.33 us  [cross(): return lax.ppermute(total, 'ctx', pairs)]
    ppermute x26, starting transfers between devices: 51.4 us -> 49.1 us  [pass_block(): lax.ppermute(block, 'ctx', [(i, i ^ n) for i in range(lax.axis_size('ctx'...]
    unnamed x52 -> x62, local copies, waits for them, and re-layouts: 6.45 us -> 6.47 us
  transfers between devices with their start and end apart: 28 -> 28, of which waited for: 13 -> 8; matrix products, arithmetic and copies ran while one was open for 0% -> 0% of each run, Pallas kernels for 21% -> 22%
where the time goes in v5:
time: 163 us; the launch traced here: 162 us
  starting transfers between devices  52.5 us (32%)
  Pallas kernels  42.1 us (26%)
  blocking collectives  40.6 us (25%)
  waiting for transfers between devices  18.7 us (11%)
  local copies, waits for them, and re-layouts  6.47 us (4%)
    ppermute x26, starting transfers between devices, pass_block(): lax.ppermute(block, 'ctx', [(i, i ^ n) for i in range(lax.axis_size('ctx'...  49.1 us
    pallas_call x12, Pallas kernels, call(): pl.pallas_call(kernel, out_shape=out_shape, in_specs=specs or [VMEM] * le...  42.1 us
    psum x1, blocking collectives, body(): write_sum, read_sum = lax.psum((write_part, read_part), 'head')  30.7 us
    ppermute x26, waiting for transfers between devices, pass_block(): lax.ppermute(block, 'ctx', [(i, i ^ n) for i in range(lax.axis_size('ctx'...  14.4 us
    psum x1, blocking collectives, body(): sums = lax.psum(sums, 'head')  9.82 us
    unnamed x62, local copies, waits for them, and re-layouts  6.47 us
    ppermute x2, waiting for transfers between devices, cross(): return lax.ppermute(total, 'ctx', pairs)  4.33 us
    ppermute x2, starting transfers between devices, cross(): return lax.ppermute(total, 'ctx', pairs)  3.41 us
  transfers between devices with their start and end apart: 28, of which 8 were waited for; matrix products, arithmetic and copies ran while one was open for 0% of the time, Pallas kernels for 22%

profile of v5, /device:TPU:1, one launch (start us, length us, event | category | flops | bytes accessed | tf_op | source)
XLA Modules:
  0.0 162.1 jit_solution(15356445380652485749)
XLA Ops:
  0.6 3.0 %ssm_first.1 = (f32[256,16]{1,0:T(8,128)}, f32[16,256]{1,0:T(8,128)}, bf16[528,128]{1,0:T(8,128)(2,1)}, bf16[528,128]{1,0:T(8,128)(2,1)}, bf16[528,128]{1,0:T(8,128)(2,1)}, /*index=5*/bf16[528,128]{1,0:T(8,128)(2,1)}) custom-call(s32[1]{0:T(128)} %bitcast.refs_0_.me_ref, f32[16,256]{1,0:T(8,128)} %bitcast.11, s32[1,256]{1,0:T(1,128)} %bitcast.5, ...), custom_call_target="tpu_custom_call" | custom-call | bytes 1704964 | tf_op jit(solution)/shard_map/ssm_first/pallas_call | solution.py:28
  3.7 2.0 %collective-permute-start = (bf16[528,128]{1,0:T(8,128)(2,1)}, bf16[528,128]{1,0:T(8,128)(2,1)S(1)}, u32[]{:S(2)}, u32[]{:S(2)}) collective-permute-start(bf16[528,128]{1,0:T(8,128)(2,1)} %get-tuple-element.109), channel_id=1, source_target_pairs={{0,4},{4,0},{8,12},{12,8},{16,20},{20,16},{24,28},{28,24},{1,5},{5... | collective-permute-start | bytes 405512 | tf_op jit(solution)/shard_map/ppermute | solution.py:284
  10.1 2.9 %collective-permute-done.2.refs_4_.refs_5_ = bf16[528,128]{1,0:T(8,128)(2,1)S(1)} collective-permute-done((bf16[528,128]{1,0:T(8,128)(2,1)}, bf16[528,128]{1,0:T(8,128)(2,1)S(1)}, u32[]{:S(2)}, u32[]{:S(2)}) %collective-permute-start.2) | collective-permute-done | bytes 135200 | tf_op jit(solution)/shard_map/ppermute | solution.py:284
  17.7 2.7 %collective-permute-start.3 = (bf16[1,1040,128]{2,1,0:T(8,128)(2,1)S(1)}, bf16[1,1040,128]{2,1,0:T(8,128)(2,1)S(1)}, u32[]{:S(2)}, u32[]{:S(2)}) collective-permute-start(bf16[1,1040,128]{2,1,0:T(8,128)(2,1)S(1)} %get-tuple-element.113), channel_id=1, source_target_pairs={{0,16},{4,20},{8,24},{12,28},{16,0},{20,4},{24,8},{28,12},{1,17},{... | collective-permute-start | bytes 798728 | tf_op jit(solution)/shard_map/ppermute | solution.py:284
  20.5 1.9 %collective-permute-start.4 = (bf16[512,128]{1,0:T(8,128)(2,1)S(1)}, bf16[512,128]{1,0:T(8,128)(2,1)S(1)}, u32[]{:S(2)}, u32[]{:S(2)}) collective-permute-start(bf16[512,128]{1,0:T(8,128)(2,1)S(1)} %ssm_total.2), channel_id=1, source_target_pairs={{0,16},{4,20},{8,24},{12,28},{1,17},{5,21},{9,25},{13,29},{2,18},{... | collective-permute-start | bytes 393224 | tf_op jit(solution)/shard_map/ppermute | solution.py:291
  23.1 4.3 %collective-permute-done.4.refs_1_ = bf16[512,128]{1,0:T(8,128)(2,1)S(1)} collective-permute-done((bf16[512,128]{1,0:T(8,128)(2,1)S(1)}, bf16[512,128]{1,0:T(8,128)(2,1)S(1)}, u32[]{:S(2)}, u32[]{:S(2)}) %collective-permute-start.4) | collective-permute-done | bytes 131104 | tf_op jit(solution)/shard_map/ppermute | solution.py:291
  28.3 12.1 %collective-permute-start.6 = (bf16[512,128]{1,0:T(8,128)(2,1)S(1)}, bf16[512,128]{1,0:T(8,128)(2,1)S(1)}, u32[]{:S(2)}, u32[]{:S(2)}) collective-permute-start(bf16[512,128]{1,0:T(8,128)(2,1)S(1)} %get-tuple-element.120), channel_id=1, source_target_pairs={{0,8},{4,12},{8,0},{12,4},{16,24},{20,28},{24,16},{28,20},{1,9},{5... | collective-permute-start | bytes 393224 | tf_op jit(solution)/shard_map/ppermute | solution.py:284
  40.4 2.7 %collective-permute-start.9 = (bf16[1,1040,128]{2,1,0:T(8,128)(2,1)S(1)}, bf16[1,1040,128]{2,1,0:T(8,128)(2,1)S(1)}, u32[]{:S(2)}, u32[]{:S(2)}) collective-permute-start(bf16[1,1040,128]{2,1,0:T(8,128)(2,1)S(1)} %get-tuple-element.130), channel_id=1, source_target_pairs={{0,8},{4,12},{8,0},{12,4},{16,24},{20,28},{24,16},{28,20},{1,9},{5... | collective-permute-start | bytes 798728 | tf_op jit(solution)/shard_map/ppermute | solution.py:284
  45.3 5.0 %collective-permute-start.11 = (bf16[1,1040,128]{2,1,0:T(8,128)(2,1)S(1)}, bf16[1,1040,128]{2,1,0:T(8,128)(2,1)S(1)}, u32[]{:S(2)}, u32[]{:S(2)}) collective-permute-start(bf16[1,1040,128]{2,1,0:T(8,128)(2,1)S(1)} %get-tuple-element.132), channel_id=1, source_target_pairs={{0,20},{4,16},{8,28},{12,24},{16,4},{20,0},{24,12},{28,8},{1,21},{... | collective-permute-start | bytes 798728 | tf_op jit(solution)/shard_map/ppermute | solution.py:284
  50.5 2.1 %collective-permute-start.17 = (bf16[1,1040,128]{2,1,0:T(8,128)(2,1)S(1)}, bf16[1,1040,128]{2,1,0:T(8,128)(2,1)}, u32[]{:S(2)}, u32[]{:S(2)}) collective-permute-start(bf16[1,1040,128]{2,1,0:T(8,128)(2,1)S(1)} %get-tuple-element.149), channel_id=1, source_target_pairs={{0,28},{4,24},{8,20},{12,16},{16,12},{20,8},{24,4},{28,0},{1,29},{... | collective-permute-start | bytes 798728 | tf_op jit(solution)/shard_map/ppermute | solution.py:284
  52.6 6.0 %ssm_mix.1 = (f32[256,2048]{1,0:T(8,128)}, f32[8,256]{1,0:T(8,128)}, bf16[2048,128]{1,0:T(8,128)(2,1)}) custom-call(s32[1]{0:T(128)} %bitcast.refs_0_.me_ref, bf16[256,2048]{1,0:T(8,128)(2,1)} %refs_2_.3, bf16[256,2048]{1,0:T(8,128)(2,1)} %refs_3_.6, bf16[256,2048]{1,0:T(8,128)(2,1)} %refs_4_.5, bf16[256,128]{1,0:T(8,128)(2,1)} %refs_3_.7, ...), custom_call_target="tpu_custom_call" | custom-call | bytes 6464516 | tf_op jit(solution)/shard_map/ssm_mix/pallas_call | solution.py:28
  58.6 9.8 %psum.21.refs_1_ = f32[8,256]{1,0:T(8,128)} all-reduce(f32[8,256]{1,0:T(8,128)} %get-tuple-element.126), channel_id=1, replica_groups=mesh['ctx'=8,'head'=4] {'head'}, use_global_device_ids=true, to_apply=%region_0.1 | all-reduce | flops 2048 | bytes 16384 | tf_op jit(solution)/shard_map/psum | solution.py:597
  68.4 5.9 %ssm_gate.1 = (bf16[256,2048]{1,0:T(8,128)(2,1)}, bf16[256,2048]{1,0:T(8,128)(2,1)}, bf16[256,2048]{1,0:T(8,128)(2,1)}, bf16[512,128]{1,0:T(8,128)(2,1)}, bf16[5...) custom-call(s32[1]{0:T(128)} %bitcast.refs_0_.me_ref, f32[8,256]{1,0:T(8,128)} %psum.21.refs_1_, ...), custom_call_target="tpu_custom_call" | custom-call | bytes 7955460 | tf_op jit(solution)/shard_map/ssm_gate/pallas_call | solution.py:28
  77.0 5.5 %collective-permute-done.13.refs_6_.refs_7_ = bf16[512,128]{1,0:T(8,128)(2,1)S(1)} collective-permute-done((bf16[512,128]{1,0:T(8,128)(2,1)}, bf16[512,128]{1,0:T(8,128)(2,1)S(1)}, u32[]{:S(2)}, u32[]{:S(2)}) %collective-permute-start.13) | collective-permute-done | bytes 131104 | tf_op jit(solution)/shard_map/ppermute | solution.py:284
  85.2 14.8 %att_attend.1 = (bf16[1,1024,128]{2,1,0:T(8,128)(2,1)}, bf16[1,1024,128]{2,1,0:T(8,128)(2,1)}, bf16[1,1024,128]{2,1,0:T(8,128)(2,1)}, bf16[1,1024,128]{2,1,0:T(8...) custom-call(s32[1]{0:T(128)} %bitcast.refs_0_.me_ref, ...), custom_call_target="tpu_custom_call" | custom-call | flops 3221225472 | bytes 4227076 | tf_op jit(solution)/shard_map/att_attend/pallas_call | solution.py:28
  103.6 5.1 %ssm_inner.1 = (f32[256,2048]{1,0:T(8,128)}, f32[256,128]{1,0:T(8,128)}, f32[256,128]{1,0:T(8,128)}) custom-call(s32[1]{0:T(128)} %bitcast.refs_0_.me_ref, bf16[256,2048]{1,0:T(8,128)(2,1)} %get-tuple-element.179.dmixed_ref, bf16[256,2048]{1,0:T(8,128)(2,1)} %refs_2_.3, bf16[256,128]{1,0:T(8,128)(2,1)} %refs_3_.7, bf16[256,128]{1,0:T(8,128)(2,1)} %r_ref.1, ...), custom_call_target="tpu_custom_call" | custom-call | bytes 5145604 | tf_op jit(solution)/shard_map/ssm_inner/pallas_call | solution.py:28
  108.8 5.6 %collective-permute-start.24 = (bf16[1,1024,128]{2,1,0:T(8,128)(2,1)S(1)}, bf16[1,1024,128]{2,1,0:T(8,128)(2,1)S(1)}, u32[]{:S(2)}, u32[]{:S(2)}) collective-permute-start(bf16[1,1024,128]{2,1,0:T(8,128)(2,1)S(1)} %copy-done.30), channel_id=1, source_target_pairs={{0,16},{4,20},{8,24},{12,28},{16,0},{20,4},{24,8},{28,12},{1,17},{... | collective-permute-start | bytes 786440 | tf_op jit(solution)/shard_map/ppermute | solution.py:284
  114.4 1.5 collective-permute-start.21
  118.3 2.7 %collective-permute-done.24.refs_4_ = bf16[1,1024,128]{2,1,0:T(8,128)(2,1)S(1)} collective-permute-done((bf16[1,1024,128]{2,1,0:T(8,128)(2,1)S(1)}, bf16[1,1024,128]{2,1,0:T(8,128)(2,1)S(1)}, u32[]{:S(2)}, u32[]{:S(2)}) %collective-permute-start.24) | collective-permute-done | bytes 262176 | tf_op jit(solution)/shard_map/ppermute | solution.py:284
  121.0 2.6 %collective-permute-start.26 = (bf16[1,1024,128]{2,1,0:T(8,128)(2,1)S(1)}, bf16[1,1024,128]{2,1,0:T(8,128)(2,1)S(1)}, u32[]{:S(2)}, u32[]{:S(2)}) collective-permute-start(bf16[1,1024,128]{2,1,0:T(8,128)(2,1)S(1)} %copy-done.25), channel_id=1, source_target_pairs={{0,24},{4,28},{8,16},{12,20},{16,8},{20,12},{24,0},{28,4},{1,25},{... | collective-permute-start | bytes 786440 | tf_op jit(solution)/shard_map/ppermute | solution.py:284
  123.6 1.6 collective-permute-start.27
  125.2 4.2 %ssm_last.1 = (bf16[256,2048]{1,0:T(8,128)(2,1)}, f32[256,128]{1,0:T(8,128)}) custom-call(s32[1]{0:T(128)} %bitcast.refs_0_.me_ref, f32[256,2048]{1,0:T(8,128)} %get-tuple-element.190.refs_1_, bf16[256,2048]{1,0:T(8,128)(2,1)} %refs_2_.3, bf16[256,128]{1,0:T(8,128)(2,1)} %refs_3_.7, s32[1,256]{1,0:T(1,128)} %bitcast.10, ...), custom_call_target="tpu_custom_call" | custom-call | bytes 5063684 | tf_op jit(solution)/shard_map/ssm_last/pallas_call | solution.py:28
  129.4 30.7 %all-reduce.3 = (bf16[256,128]{1,0:T(8,128)(2,1)}, bf16[256,128]{1,0:T(8,128)(2,1)}) all-reduce(f32[256,128]{1,0:T(8,128)} %get-tuple-element.198, f32[256,128]{1,0:T(8,128)S(1)} %copy-done.17), channel_id=1, replica_groups=mesh['ctx'=8,'head'=4] {'head'}, use_global_device_ids=true, to_apply=%region_1.2 | all-reduce | flops 65536 | bytes 393216 | tf_op jit(solution)/shard_map/psum | solution.py:657
  160.1 1.9 %att_unpack.1 = (bf16[256,1024]{1,0:T(8,128)(2,1)}, bf16[256,1024]{1,0:T(8,128)(2,1)}, bf16[256,1024]{1,0:T(8,128)(2,1)}, bf16[256,1024]{1,0:T(8,128)(2,1)}) custom-call(s32[1]{0:T(128)} %bitcast.refs_0_.me_ref, bf16[1,1024,128]{2,1,0:T(8,128)(2,1)S(1)} %copy-done.7, bf16[1,1024,128]{2,1,0:T(8,128)(2,1)S(1)} %collective-permute-done.21.refs_1_, ...), custom_call_target="tpu_custom_call" | custom-call | bytes 4194308 | tf_op jit(solution)/shard_map/att_unpack/pallas_call | solution.py:28
  (112 shorter events, 24.3 us)
Async XLA Ops:
  17.7 32.7 %collective-permute-start.3 = (bf16[1,1040,128]{2,1,0:T(8,128)(2,1)S(1)}, bf16[1,1040,128]{2,1,0:T(8,128)(2,1)S(1)}, u32[]{:S(2)}, u32[]{:S(2)}) collective-permute-start(bf16[1,1040,128]{2,1,0:T(8,128)(2,1)S(1)} %get-tuple-element.113), channel_id=1, source_target_pairs={{0,16},{4,20},{8,24},{12,28},{16,0},{20,4},{24,8},{28,12},{1,17},{... | collective-permute-start | bytes 798728 | tf_op jit(solution)/shard_map/ppermute | solution.py:284
  20.5 6.9 %collective-permute-start.4 = (bf16[512,128]{1,0:T(8,128)(2,1)S(1)}, bf16[512,128]{1,0:T(8,128)(2,1)S(1)}, u32[]{:S(2)}, u32[]{:S(2)}) collective-permute-start(bf16[512,128]{1,0:T(8,128)(2,1)S(1)} %ssm_total.2), channel_id=1, source_target_pairs={{0,16},{4,20},{8,24},{12,28},{1,17},{5,21},{9,25},{13,29},{2,18},{... | collective-permute-start | bytes 393224 | tf_op jit(solution)/shard_map/ppermute | solution.py:291
  22.5 28.0 %collective-permute-start.8 = (bf16[1,1040,128]{2,1,0:T(8,128)(2,1)S(1)}, bf16[1,1040,128]{2,1,0:T(8,128)(2,1)S(1)}, u32[]{:S(2)}, u32[]{:S(2)}) collective-permute-start(bf16[1,1040,128]{2,1,0:T(8,128)(2,1)S(1)} %get-tuple-element.129), channel_id=1, source_target_pairs={{0,4},{4,0},{8,12},{12,8},{16,20},{20,16},{24,28},{28,24},{1,5},{5... | collective-permute-start | bytes 798728 | tf_op jit(solution)/shard_map/ppermute | solution.py:284
  28.3 12.1 %collective-permute-start.5 = (bf16[512,128]{1,0:T(8,128)(2,1)S(1)}, bf16[512,128]{1,0:T(8,128)(2,1)S(1)}, u32[]{:S(2)}, u32[]{:S(2)}) collective-permute-start(bf16[512,128]{1,0:T(8,128)(2,1)S(1)} %get-tuple-element.119), channel_id=1, source_target_pairs={{0,4},{4,0},{8,12},{12,8},{16,20},{20,16},{24,28},{28,24},{1,5},{5... | collective-permute-start | bytes 393224 | tf_op jit(solution)/shard_map/ppermute | solution.py:284
  28.3 15.2 %collective-permute-start.6 = (bf16[512,128]{1,0:T(8,128)(2,1)S(1)}, bf16[512,128]{1,0:T(8,128)(2,1)S(1)}, u32[]{:S(2)}, u32[]{:S(2)}) collective-permute-start(bf16[512,128]{1,0:T(8,128)(2,1)S(1)} %get-tuple-element.120), channel_id=1, source_target_pairs={{0,8},{4,12},{8,0},{12,4},{16,24},{20,28},{24,16},{28,20},{1,9},{5... | collective-permute-start | bytes 393224 | tf_op jit(solution)/shard_map/ppermute | solution.py:284
  40.4 33.8 %collective-permute-start.9 = (bf16[1,1040,128]{2,1,0:T(8,128)(2,1)S(1)}, bf16[1,1040,128]{2,1,0:T(8,128)(2,1)S(1)}, u32[]{:S(2)}, u32[]{:S(2)}) collective-permute-start(bf16[1,1040,128]{2,1,0:T(8,128)(2,1)S(1)} %get-tuple-element.130), channel_id=1, source_target_pairs={{0,8},{4,12},{8,0},{12,4},{16,24},{20,28},{24,16},{28,20},{1,9},{5... | collective-permute-start | bytes 798728 | tf_op jit(solution)/shard_map/ppermute | solution.py:284
  43.5 30.7 %collective-permute-start.10 = (bf16[1,1040,128]{2,1,0:T(8,128)(2,1)S(1)}, bf16[1,1040,128]{2,1,0:T(8,128)(2,1)S(1)}, u32[]{:S(2)}, u32[]{:S(2)}) collective-permute-start(bf16[1,1040,128]{2,1,0:T(8,128)(2,1)S(1)} %get-tuple-element.131), channel_id=1, source_target_pairs={{0,12},{4,8},{8,4},{12,0},{16,28},{20,24},{24,20},{28,16},{1,13},{... | collective-permute-start | bytes 798728 | tf_op jit(solution)/shard_map/ppermute | solution.py:284
  45.3 29.0 %collective-permute-start.11 = (bf16[1,1040,128]{2,1,0:T(8,128)(2,1)S(1)}, bf16[1,1040,128]{2,1,0:T(8,128)(2,1)S(1)}, u32[]{:S(2)}, u32[]{:S(2)}) collective-permute-start(bf16[1,1040,128]{2,1,0:T(8,128)(2,1)S(1)} %get-tuple-element.132), channel_id=1, source_target_pairs={{0,20},{4,16},{8,28},{12,24},{16,4},{20,0},{24,12},{28,8},{1,21},{... | collective-permute-start | bytes 798728 | tf_op jit(solution)/shard_map/ppermute | solution.py:284
  50.4 24.0 %collective-permute-start.12 = (bf16[1,1040,128]{2,1,0:T(8,128)(2,1)S(1)}, bf16[1,1040,128]{2,1,0:T(8,128)(2,1)S(1)}, u32[]{:S(2)}, u32[]{:S(2)}) collective-permute-start(bf16[1,1040,128]{2,1,0:T(8,128)(2,1)S(1)} %get-tuple-element.133), channel_id=1, source_target_pairs={{0,24},{4,28},{8,16},{12,20},{16,8},{20,12},{24,0},{28,4},{1,25},{... | collective-permute-start | bytes 798728 | tf_op jit(solution)/shard_map/ppermute | solution.py:284
  50.5 34.7 %collective-permute-start.17 = (bf16[1,1040,128]{2,1,0:T(8,128)(2,1)S(1)}, bf16[1,1040,128]{2,1,0:T(8,128)(2,1)}, u32[]{:S(2)}, u32[]{:S(2)}) collective-permute-start(bf16[1,1040,128]{2,1,0:T(8,128)(2,1)S(1)} %get-tuple-element.149), channel_id=1, source_target_pairs={{0,28},{4,24},{8,20},{12,16},{16,12},{20,8},{24,4},{28,0},{1,29},{... | collective-permute-start | bytes 798728 | tf_op jit(solution)/shard_map/ppermute | solution.py:284
  74.3 8.2 %collective-permute-start.13 = (bf16[512,128]{1,0:T(8,128)(2,1)}, bf16[512,128]{1,0:T(8,128)(2,1)S(1)}, u32[]{:S(2)}, u32[]{:S(2)}) collective-permute-start(bf16[512,128]{1,0:T(8,128)(2,1)} %get-tuple-element.139), channel_id=1, source_target_pairs={{0,4},{4,0},{8,12},{12,8},{16,20},{20,16},{24,28},{28,24},{1,5},{5... | collective-permute-start | bytes 393224 | tf_op jit(solution)/shard_map/ppermute | solution.py:284
  75.7 6.9 %collective-permute-start.14 = (bf16[512,128]{1,0:T(8,128)(2,1)}, bf16[512,128]{1,0:T(8,128)(2,1)S(1)}, u32[]{:S(2)}, u32[]{:S(2)}) collective-permute-start(bf16[512,128]{1,0:T(8,128)(2,1)} %get-tuple-element.140), channel_id=1, source_target_pairs={{0,8},{4,12},{8,0},{12,4},{16,24},{20,28},{24,16},{28,20},{1,9},{5... | collective-permute-start | bytes 393224 | tf_op jit(solution)/shard_map/ppermute | solution.py:284
  75.7 6.9 %collective-permute-start.15 = (bf16[512,128]{1,0:T(8,128)(2,1)}, bf16[512,128]{1,0:T(8,128)(2,1)S(1)}, u32[]{:S(2)}, u32[]{:S(2)}) collective-permute-start(bf16[512,128]{1,0:T(8,128)(2,1)} %get-tuple-element.141), channel_id=1, source_target_pairs={{0,12},{4,8},{8,4},{12,0},{16,28},{20,24},{24,20},{28,16},{1,13},{... | collective-permute-start | bytes 393224 | tf_op jit(solution)/shard_map/ppermute | solution.py:284
  83.7 16.4 %collective-permute-start.16 = (bf16[512,128]{1,0:T(8,128)(2,1)S(1)}, bf16[512,128]{1,0:T(8,128)(2,1)S(1)}, u32[]{:S(2)}, u32[]{:S(2)}) collective-permute-start(bf16[512,128]{1,0:T(8,128)(2,1)S(1)} %ssm_total.3), channel_id=1, source_target_pairs={{16,0},{20,4},{24,8},{28,12},{17,1},{21,5},{25,9},{29,13},{18,2},{... | collective-permute-start | bytes 393224 | tf_op jit(solution)/shard_map/ppermute | solution.py:291
  101.0 13.4 %collective-permute-start.18 = (bf16[512,128]{1,0:T(8,128)(2,1)S(1)}, bf16[512,128]{1,0:T(8,128)(2,1)S(1)}, u32[]{:S(2)}, u32[]{:S(2)}) collective-permute-start(bf16[512,128]{1,0:T(8,128)(2,1)S(1)} %get-tuple-element.176), channel_id=1, source_target_pairs={{0,4},{4,0},{8,12},{12,8},{16,20},{20,16},{24,28},{28,24},{1,5},{5... | collective-permute-start | bytes 393224 | tf_op jit(solution)/shard_map/ppermute | solution.py:284
  102.4 11.9 %collective-permute-start.19 = (bf16[512,128]{1,0:T(8,128)(2,1)S(1)}, bf16[512,128]{1,0:T(8,128)(2,1)S(1)}, u32[]{:S(2)}, u32[]{:S(2)}) collective-permute-start(bf16[512,128]{1,0:T(8,128)(2,1)S(1)} %get-tuple-element.177), channel_id=1, source_target_pairs={{0,8},{4,12},{8,0},{12,4},{16,24},{20,28},{24,16},{28,20},{1,9},{5... | collective-permute-start | bytes 393224 | tf_op jit(solution)/shard_map/ppermute | solution.py:284
  102.4 11.9 %collective-permute-start.20 = (bf16[512,128]{1,0:T(8,128)(2,1)S(1)}, bf16[512,128]{1,0:T(8,128)(2,1)S(1)}, u32[]{:S(2)}, u32[]{:S(2)}) collective-permute-start(bf16[512,128]{1,0:T(8,128)(2,1)S(1)} %get-tuple-element.178), channel_id=1, source_target_pairs={{0,12},{4,8},{8,4},{12,0},{16,28},{20,24},{24,20},{28,16},{1,13},{... | collective-permute-start | bytes 393224 | tf_op jit(solution)/shard_map/ppermute | solution.py:284
  108.8 12.2 %collective-permute-start.24 = (bf16[1,1024,128]{2,1,0:T(8,128)(2,1)S(1)}, bf16[1,1024,128]{2,1,0:T(8,128)(2,1)S(1)}, u32[]{:S(2)}, u32[]{:S(2)}) collective-permute-start(bf16[1,1024,128]{2,1,0:T(8,128)(2,1)S(1)} %copy-done.30), channel_id=1, source_target_pairs={{0,16},{4,20},{8,24},{12,28},{16,0},{20,4},{24,8},{28,12},{1,17},{... | collective-permute-start | bytes 786440 | tf_op jit(solution)/shard_map/ppermute | solution.py:284
  114.4 9.2 %collective-permute-start.21 = (bf16[1,1024,128]{2,1,0:T(8,128)(2,1)S(1)}, bf16[1,1024,128]{2,1,0:T(8,128)(2,1)S(1)}, u32[]{:S(2)}, u32[]{:S(2)}) collective-permute-start(bf16[1,1024,128]{2,1,0:T(8,128)(2,1)S(1)} %copy-done.29), channel_id=1, source_target_pairs={{0,4},{4,0},{8,12},{12,8},{16,20},{20,16},{24,28},{28,24},{1,5},{5... | collective-permute-start | bytes 786440 | tf_op jit(solution)/shard_map/ppermute | solution.py:284
  115.9 44.2 %collective-permute-start.22 = (bf16[1,1024,128]{2,1,0:T(8,128)(2,1)S(1)}, bf16[1,1024,128]{2,1,0:T(8,128)(2,1)S(1)}, u32[]{:S(2)}, u32[]{:S(2)}) collective-permute-start(bf16[1,1024,128]{2,1,0:T(8,128)(2,1)S(1)} %copy-done.28), channel_id=1, source_target_pairs={{0,8},{4,12},{8,0},{12,4},{16,24},{20,28},{24,16},{28,20},{1,9},{5... | collective-permute-start | bytes 786440 | tf_op jit(solution)/shard_map/ppermute | solution.py:284
  115.9 44.2 %collective-permute-start.23 = (bf16[1,1024,128]{2,1,0:T(8,128)(2,1)S(1)}, bf16[1,1024,128]{2,1,0:T(8,128)(2,1)S(1)}, u32[]{:S(2)}, u32[]{:S(2)}) collective-permute-start(bf16[1,1024,128]{2,1,0:T(8,128)(2,1)S(1)} %copy-done.27), channel_id=1, source_target_pairs={{0,12},{4,8},{8,4},{12,0},{16,28},{20,24},{24,20},{28,16},{1,13},{... | collective-permute-start | bytes 786440 | tf_op jit(solution)/shard_map/ppermute | solution.py:284
  117.2 42.9 %collective-permute-start.25 = (bf16[1,1024,128]{2,1,0:T(8,128)(2,1)S(1)}, bf16[1,1024,128]{2,1,0:T(8,128)(2,1)S(1)}, u32[]{:S(2)}, u32[]{:S(2)}) collective-permute-start(bf16[1,1024,128]{2,1,0:T(8,128)(2,1)S(1)} %copy-done.26), channel_id=1, source_target_pairs={{0,20},{4,16},{8,28},{12,24},{16,4},{20,0},{24,12},{28,8},{1,21},{... | collective-permute-start | bytes 786440 | tf_op jit(solution)/shard_map/ppermute | solution.py:284
  121.0 39.1 %collective-permute-start.26 = (bf16[1,1024,128]{2,1,0:T(8,128)(2,1)S(1)}, bf16[1,1024,128]{2,1,0:T(8,128)(2,1)S(1)}, u32[]{:S(2)}, u32[]{:S(2)}) collective-permute-start(bf16[1,1024,128]{2,1,0:T(8,128)(2,1)S(1)} %copy-done.25), channel_id=1, source_target_pairs={{0,24},{4,28},{8,16},{12,20},{16,8},{20,12},{24,0},{28,4},{1,25},{... | collective-permute-start | bytes 786440 | tf_op jit(solution)/shard_map/ppermute | solution.py:284
  123.6 36.5 %collective-permute-start.27 = (bf16[1,1024,128]{2,1,0:T(8,128)(2,1)S(1)}, bf16[1,1024,128]{2,1,0:T(8,128)(2,1)S(1)}, u32[]{:S(2)}, u32[]{:S(2)}) collective-permute-start(bf16[1,1024,128]{2,1,0:T(8,128)(2,1)S(1)} %copy-done.24), channel_id=1, source_target_pairs={{0,28},{4,24},{8,20},{12,16},{16,12},{20,8},{24,4},{28,0},{1,29},{... | collective-permute-start | bytes 786440 | tf_op jit(solution)/shard_map/ppermute | solution.py:284
  (35 other events, 393.1 us)

commit v6 on v5

--- a/solution.py
+++ b/solution.py
@@ -568,21 +568,22 @@
         specs=[SMEM] + [VMEM] * 4, scratch=[held_tails], name="ssm_first",
     )
     tails = [pass_block(block, n) for n, block in enumerate(sent)]
+    total = carry_total(False, *tails)
+    start = cross(total, False)
     if dealt:
         marks = doc_start.reshape(length // 128, 128)
         marks = jnp.stack([marks // 128, marks % 128], axis=1).reshape(length // 64, 128)
         marks = jnp.pad(marks, ((0, TAIL - length // 64), (0, 0))).astype(BF16)
-        marks, tails = lax.optimization_barrier((marks, tails))
+        marks, total = lax.optimization_barrier((marks, total))
         packed = call(
             pack_kernel, [shape((per, 4 * length + TAIL, 128), BF16)] * parts,
             me, marks, att_queries, att_keys, att_values, att_grad,
             specs=[SMEM] + [VMEM] * 5, vmem=SMALL, name="att_pack",
         )
+        packed, start = lax.optimization_barrier((packed, start))
         att_got = {n: pass_block(block, n) for n, block in enumerate(packed)}
     else:
         att_out = ring_attention(att_queries, att_keys, att_values, att_grad, doc_start)
-    total = carry_total(False, *tails)
-    start = cross(total, False)
     state = [
         pass_block(block, n) for n, block in enumerate(carry_states(False, start, *tails))
     ]
@@ -607,10 +608,8 @@
         done, sent = lax.optimization_barrier(([att_got[n] for n in rest], sent))
         att_got.update(zip(rest, done))
     blocks = [pass_block(block, n) for n, block in enumerate(sent)]
-    total = carry_total(True, *tails, *blocks)
-    start = cross(total, True)
     if dealt:
-        att_in, total = lax.optimization_barrier(([att_got[n] for n in range(parts)], total))
+        att_in, sent = lax.optimization_barrier(([att_got[n] for n in range(parts)], sent))
         att_done = call(
             lambda *refs: attend_blocks(length, parts, *refs),
             [shape((per, 4 * length, 128), BF16)] * parts, me, *att_in,
@@ -626,7 +625,9 @@
             ],
             flops=6 * per * (parts * length) ** 2 * ATT_DIM, name="att_attend",
         )
-        start, att_done = lax.optimization_barrier((start, att_done))
+        blocks, att_done = lax.optimization_barrier((blocks, att_done))
+    total = carry_total(True, *tails, *blocks)
+    start = cross(total, True)
     back = [
         pass_block(block, n) for n, block in enumerate(carry_states(True, start, *tails, *blocks))
     ]
@@ -637,10 +638,17 @@
         specs=[SMEM] + [VMEM] * 8, name="ssm_inner",
     )
     if dealt:
-        att_back = {shares: pass_block(att_done[shares], shares)}
+        early = [shares, shares + 1]
+        late = [*range(shares + 2, parts), *range(1, shares)]
+        att_back = {0: att_done[0]}
+        held, total = lax.optimization_barrier((att_done, total))
+        att_back[early[0]] = pass_block(held[early[0]], early[0])
+        held, start = lax.optimization_barrier((att_done, start))
+        att_back[early[1]] = pass_block(held[early[1]], early[1])
         held, back, gin = lax.optimization_barrier((att_done, back, gin))
-        for n in [n for n in range(parts)[::-1] if n != shares]:
-            att_back[n] = pass_block(held[n], n)
+        att_back.update((n, pass_block(held[n], n)) for n in late)
+        done, back = lax.optimization_barrier(([att_back[n] for n in early], back))
+        att_back.update(zip(early, done))
         att_out = call(
             unpack_kernel, (shape((length, att_width), BF16),) * 4,
             me, *[att_back[n] for n in range(parts)],

time: 163 us -> 164 us (level)
  waiting for transfers between devices: 18.7 us -> 33 us
  starting transfers between devices: 52.5 us -> 41.4 us
  local copies, waits for them, and re-layouts: 6.47 us -> 4.38 us
    psum x1, blocking collectives: 30.7 us -> 16.1 us  [body(): write_sum, read_sum = lax.psum((write_part, read_part), 'head')]
    psum x1, blocking collectives: 9.82 us -> 24.3 us  [body(): sums = lax.psum(sums, 'head')]
    ppermute x26, starting transfers between devices: 49.1 us -> 35.4 us  [pass_block(): lax.ppermute(block, 'ctx', [(i, i ^ n) for i in range(lax.axis_size('ctx'...]
    ppermute x2, waiting for transfers between devices: 4.33 us -> 17.4 us  [cross(): return lax.ppermute(total, 'ctx', pairs)]
    ppermute x2, starting transfers between devices: 3.41 us -> 5.98 us  [cross(): return lax.ppermute(total, 'ctx', pairs)]
    unnamed x62 -> x54, local copies, waits for them, and re-layouts: 6.47 us -> 4.38 us
  transfers between devices with their start and end apart: 28 -> 28, of which waited for: 8 -> 9; matrix products, arithmetic and copies ran while one was open for 0% -> 0% of each run, Pallas kernels for 22% -> 23%
where the time goes in v6:
time: 164 us; the launch traced here: 163 us
  Pallas kernels  42.2 us (26%)
  starting transfers between devices  41.4 us (25%)
  blocking collectives  40.4 us (25%)
  waiting for transfers between devices  33 us (20%)
  local copies, waits for them, and re-layouts  4.38 us (3%)
    pallas_call x12, Pallas kernels, call(): pl.pallas_call(kernel, out_shape=out_shape, in_specs=specs or [VMEM] * le...  42.2 us
    ppermute x26, starting transfers between devices, pass_block(): lax.ppermute(block, 'ctx', [(i, i ^ n) for i in range(lax.axis_size('ctx'...  35.4 us
    psum x1, blocking collectives, body(): sums = lax.psum(sums, 'head')  24.3 us
    ppermute x2, waiting for transfers between devices, cross(): return lax.ppermute(total, 'ctx', pairs)  17.4 us
    psum x1, blocking collectives, body(): write_sum, read_sum = lax.psum((write_part, read_part), 'head')  16.1 us
    ppermute x26, waiting for transfers between devices, pass_block(): lax.ppermute(block, 'ctx', [(i, i ^ n) for i in range(lax.axis_size('ctx'...  15.7 us
    ppermute x2, starting transfers between devices, cross(): return lax.ppermute(total, 'ctx', pairs)  5.98 us
    unnamed x54, local copies, waits for them, and re-layouts  4.38 us
  transfers between devices with their start and end apart: 28, of which 9 were waited for; matrix products, arithmetic and copies ran while one was open for 0% of the time, Pallas kernels for 23%

profile of v6, /device:TPU:1, one launch (start us, length us, event | category | flops | bytes accessed | tf_op | source)
XLA Modules:
  0.0 163.1 jit_solution(16842775129481247041)
XLA Ops:
  0.7 3.1 %ssm_first.1 = (f32[256,16]{1,0:T(8,128)}, f32[16,256]{1,0:T(8,128)}, bf16[528,128]{1,0:T(8,128)(2,1)}, bf16[528,128]{1,0:T(8,128)(2,1)}, bf16[528,128]{1,0:T(8,128)(2,1)}, /*index=5*/bf16[528,128]{1,0:T(8,128)(2,1)}) custom-call(s32[1]{0:T(128)} %bitcast.refs_0_.me_ref, f32[16,256]{1,0:T(8,128)} %bitcast.11, s32[1,256]{1,0:T(1,128)} %bitcast.5, ...), custom_call_target="tpu_custom_call" | custom-call | bytes 1704964 | tf_op jit(solution)/shard_map/ssm_first/pallas_call | solution.py:28
  3.8 2.0 %collective-permute-start = (bf16[528,128]{1,0:T(8,128)(2,1)}, bf16[528,128]{1,0:T(8,128)(2,1)S(1)}, u32[]{:S(2)}, u32[]{:S(2)}) collective-permute-start(bf16[528,128]{1,0:T(8,128)(2,1)} %get-tuple-element.123), channel_id=1, source_target_pairs={{0,4},{4,0},{8,12},{12,8},{16,20},{20,16},{24,28},{28,24},{1,5},{5... | collective-permute-start | bytes 405512 | tf_op jit(solution)/shard_map/ppermute | solution.py:284
  7.8 1.5 collective-permute-done.refs_2_.refs_3_
  10.2 2.9 %collective-permute-done.2.refs_4_.refs_5_ = bf16[528,128]{1,0:T(8,128)(2,1)S(1)} collective-permute-done((bf16[528,128]{1,0:T(8,128)(2,1)}, bf16[528,128]{1,0:T(8,128)(2,1)S(1)}, u32[]{:S(2)}, u32[]{:S(2)}) %collective-permute-start.2) | collective-permute-done | bytes 135200 | tf_op jit(solution)/shard_map/ppermute | solution.py:284
  14.1 4.6 %collective-permute-start.3 = (bf16[512,128]{1,0:T(8,128)(2,1)S(1)}, bf16[512,128]{1,0:T(8,128)(2,1)S(1)}, u32[]{:S(2)}, u32[]{:S(2)}) collective-permute-start(bf16[512,128]{1,0:T(8,128)(2,1)S(1)} %ssm_total.2), channel_id=1, source_target_pairs={{0,16},{4,20},{8,24},{12,28},{1,17},{5,21},{9,25},{13,29},{2,18},{... | collective-permute-start | bytes 393224 | tf_op jit(solution)/shard_map/ppermute | solution.py:291
  21.4 2.1 %collective-permute-start.4 = (bf16[1,1040,128]{2,1,0:T(8,128)(2,1)S(1)}, bf16[1,1040,128]{2,1,0:T(8,128)(2,1)S(1)}, u32[]{:S(2)}, u32[]{:S(2)}) collective-permute-start(bf16[1,1040,128]{2,1,0:T(8,128)(2,1)S(1)} %get-tuple-element.135), channel_id=1, source_target_pairs={{0,16},{4,20},{8,24},{12,28},{16,0},{20,4},{24,8},{28,12},{1,17},{... | collective-permute-start | bytes 798728 | tf_op jit(solution)/shard_map/ppermute | solution.py:284
  25.8 3.8 %collective-permute-start.6 = (bf16[512,128]{1,0:T(8,128)(2,1)S(1)}, bf16[512,128]{1,0:T(8,128)(2,1)S(1)}, u32[]{:S(2)}, u32[]{:S(2)}) collective-permute-start(bf16[512,128]{1,0:T(8,128)(2,1)S(1)} %get-tuple-element.139), channel_id=1, source_target_pairs={{0,8},{4,12},{8,0},{12,4},{16,24},{20,28},{24,16},{28,20},{1,9},{5... | collective-permute-start | bytes 393224 | tf_op jit(solution)/shard_map/ppermute | solution.py:284
  31.2 3.2 %collective-permute-start.9 = (bf16[1,1040,128]{2,1,0:T(8,128)(2,1)S(1)}, bf16[1,1040,128]{2,1,0:T(8,128)(2,1)S(1)}, u32[]{:S(2)}, u32[]{:S(2)}) collective-permute-start(bf16[1,1040,128]{2,1,0:T(8,128)(2,1)S(1)} %get-tuple-element.149), channel_id=1, source_target_pairs={{0,8},{4,12},{8,0},{12,4},{16,24},{20,28},{24,16},{28,20},{1,9},{5... | collective-permute-start | bytes 798728 | tf_op jit(solution)/shard_map/ppermute | solution.py:284
  36.4 2.8 %collective-permute-start.12 = (bf16[1,1040,128]{2,1,0:T(8,128)(2,1)S(1)}, bf16[1,1040,128]{2,1,0:T(8,128)(2,1)}, u32[]{:S(2)}, u32[]{:S(2)}) collective-permute-start(bf16[1,1040,128]{2,1,0:T(8,128)(2,1)S(1)} %get-tuple-element.152), channel_id=1, source_target_pairs={{0,24},{4,28},{8,16},{12,20},{16,8},{20,12},{24,0},{28,4},{1,25},{... | collective-permute-start | bytes 798728 | tf_op jit(solution)/shard_map/ppermute | solution.py:284
  40.6 6.0 %ssm_mix.1 = (f32[256,2048]{1,0:T(8,128)}, f32[8,256]{1,0:T(8,128)}, bf16[2048,128]{1,0:T(8,128)(2,1)}) custom-call(s32[1]{0:T(128)} %bitcast.refs_0_.me_ref, bf16[256,2048]{1,0:T(8,128)(2,1)} %refs_2_.3, bf16[256,2048]{1,0:T(8,128)(2,1)} %refs_3_.6, bf16[256,2048]{1,0:T(8,128)(2,1)} %refs_4_.5, bf16[256,128]{1,0:T(8,128)(2,1)} %refs_3_.7, ...), custom_call_target="tpu_custom_call" | custom-call | bytes 6464516 | tf_op jit(solution)/shard_map/ssm_mix/pallas_call | solution.py:28
  46.5 24.3 %psum.21.refs_1_ = f32[8,256]{1,0:T(8,128)} all-reduce(f32[8,256]{1,0:T(8,128)} %get-tuple-element.145), channel_id=1, replica_groups=mesh['ctx'=8,'head'=4] {'head'}, use_global_device_ids=true, to_apply=%region_0.1 | all-reduce | flops 2048 | bytes 16384 | tf_op jit(solution)/shard_map/psum | solution.py:598
  70.8 5.9 %ssm_gate.1 = (bf16[256,2048]{1,0:T(8,128)(2,1)}, bf16[256,2048]{1,0:T(8,128)(2,1)}, bf16[256,2048]{1,0:T(8,128)(2,1)}, bf16[512,128]{1,0:T(8,128)(2,1)}, bf16[5...) custom-call(s32[1]{0:T(128)} %bitcast.refs_0_.me_ref, f32[8,256]{1,0:T(8,128)} %psum.21.refs_1_, ...), custom_call_target="tpu_custom_call" | custom-call | bytes 7955460 | tf_op jit(solution)/shard_map/ssm_gate/pallas_call | solution.py:28
  77.1 2.3 %collective-permute-start.15 = (bf16[512,128]{1,0:T(8,128)(2,1)}, bf16[512,128]{1,0:T(8,128)(2,1)S(1)}, u32[]{:S(2)}, u32[]{:S(2)}) collective-permute-start(bf16[512,128]{1,0:T(8,128)(2,1)} %get-tuple-element.160), channel_id=1, source_target_pairs={{0,12},{4,8},{8,4},{12,0},{16,28},{20,24},{24,20},{28,16},{1,13},{... | collective-permute-start | bytes 393224 | tf_op jit(solution)/shard_map/ppermute | solution.py:284
  79.5 15.0 %att_attend.1 = (bf16[1,1024,128]{2,1,0:T(8,128)(2,1)}, bf16[1,1024,128]{2,1,0:T(8,128)(2,1)}, bf16[1,1024,128]{2,1,0:T(8,128)(2,1)}, bf16[1,1024,128]{2,1,0:T(8...) custom-call(s32[1]{0:T(128)} %bitcast.refs_0_.me_ref, ...), custom_call_target="tpu_custom_call" | custom-call | flops 3221225472 | bytes 4227076 | tf_op jit(solution)/shard_map/att_attend/pallas_call | solution.py:28
  96.2 3.0 %collective-permute-start.24 = (bf16[1,1024,128]{2,1,0:T(8,128)(2,1)}, bf16[1,1024,128]{2,1,0:T(8,128)(2,1)S(1)}, u32[]{:S(2)}, u32[]{:S(2)}) collective-permute-start(bf16[1,1024,128]{2,1,0:T(8,128)(2,1)} %get-tuple-element.207), channel_id=1, source_target_pairs={{0,16},{4,20},{8,24},{12,28},{16,0},{20,4},{24,8},{28,12},{1,17},{... | collective-permute-start | bytes 786440 | tf_op jit(solution)/shard_map/ppermute | solution.py:284
  99.2 17.4 %collective-permute-done.17.refs_1_ = bf16[512,128]{1,0:T(8,128)(2,1)S(1)} collective-permute-done((bf16[512,128]{1,0:T(8,128)(2,1)S(1)}, bf16[512,128]{1,0:T(8,128)(2,1)S(1)}, u32[]{:S(2)}, u32[]{:S(2)}) %collective-permute-start.17) | collective-permute-done | bytes 131104 | tf_op jit(solution)/shard_map/ppermute | solution.py:291
  118.0 2.1 %collective-permute-start.20 = (bf16[512,128]{1,0:T(8,128)(2,1)S(1)}, bf16[512,128]{1,0:T(8,128)(2,1)S(1)}, u32[]{:S(2)}, u32[]{:S(2)}) collective-permute-start(bf16[512,128]{1,0:T(8,128)(2,1)S(1)} %get-tuple-element.200), channel_id=1, source_target_pairs={{0,12},{4,8},{8,4},{12,0},{16,28},{20,24},{24,20},{28,16},{1,13},{... | collective-permute-start | bytes 393224 | tf_op jit(solution)/shard_map/ppermute | solution.py:284
  120.1 4.9 %ssm_inner.1 = (f32[256,2048]{1,0:T(8,128)}, f32[256,128]{1,0:T(8,128)}, f32[256,128]{1,0:T(8,128)}) custom-call(s32[1]{0:T(128)} %bitcast.refs_0_.me_ref, bf16[256,2048]{1,0:T(8,128)(2,1)} %get-tuple-element.201.dmixed_ref, bf16[256,2048]{1,0:T(8,128)(2,1)} %refs_2_.3, bf16[256,128]{1,0:T(8,128)(2,1)} %refs_3_.7, bf16[256,128]{1,0:T(8,128)(2,1)} %r_ref.1, ...), custom_call_target="tpu_custom_call" | custom-call | bytes 5145604 | tf_op jit(solution)/shard_map/ssm_inner/pallas_call | solution.py:28
  125.1 6.1 %collective-permute-done.19.refs_9_ = bf16[512,128]{1,0:T(8,128)(2,1)S(1)} collective-permute-done((bf16[512,128]{1,0:T(8,128)(2,1)S(1)}, bf16[512,128]{1,0:T(8,128)(2,1)S(1)}, u32[]{:S(2)}, u32[]{:S(2)}) %collective-permute-start.19) | collective-permute-done | bytes 131104 | tf_op jit(solution)/shard_map/ppermute | solution.py:284
  131.2 2.8 %collective-permute-done.20.refs_10_ = bf16[512,128]{1,0:T(8,128)(2,1)S(1)} collective-permute-done((bf16[512,128]{1,0:T(8,128)(2,1)S(1)}, bf16[512,128]{1,0:T(8,128)(2,1)S(1)}, u32[]{:S(2)}, u32[]{:S(2)}) %collective-permute-start.20) | collective-permute-done | bytes 131104 | tf_op jit(solution)/shard_map/ppermute | solution.py:284
  136.7 4.1 %collective-permute-start.27 = (bf16[1,1024,128]{2,1,0:T(8,128)(2,1)S(1)}, bf16[1,1024,128]{2,1,0:T(8,128)(2,1)S(1)}, u32[]{:S(2)}, u32[]{:S(2)}) collective-permute-start(bf16[1,1024,128]{2,1,0:T(8,128)(2,1)S(1)} %copy-done.22), channel_id=1, source_target_pairs={{0,28},{4,24},{8,20},{12,16},{16,12},{20,8},{24,4},{28,0},{1,29},{... | collective-permute-start | bytes 786440 | tf_op jit(solution)/shard_map/ppermute | solution.py:284
  140.9 4.2 %ssm_last.1 = (bf16[256,2048]{1,0:T(8,128)(2,1)}, f32[256,128]{1,0:T(8,128)}) custom-call(s32[1]{0:T(128)} %bitcast.refs_0_.me_ref, f32[256,2048]{1,0:T(8,128)} %get-tuple-element.218.refs_1_, bf16[256,2048]{1,0:T(8,128)(2,1)} %refs_2_.3, bf16[256,128]{1,0:T(8,128)(2,1)} %refs_3_.7, s32[1,256]{1,0:T(1,128)} %bitcast.10, ...), custom_call_target="tpu_custom_call" | custom-call | bytes 5063684 | tf_op jit(solution)/shard_map/ssm_last/pallas_call | solution.py:28
  145.0 16.1 %all-reduce.3 = (bf16[256,128]{1,0:T(8,128)(2,1)}, bf16[256,128]{1,0:T(8,128)(2,1)}) all-reduce(f32[256,128]{1,0:T(8,128)} %get-tuple-element.226, f32[256,128]{1,0:T(8,128)S(1)} %copy-done.17), channel_id=1, replica_groups=mesh['ctx'=8,'head'=4] {'head'}, use_global_device_ids=true, to_apply=%region_1.2 | all-reduce | flops 65536 | bytes 393216 | tf_op jit(solution)/shard_map/psum | solution.py:665
  161.2 1.9 %att_unpack.1 = (bf16[256,1024]{1,0:T(8,128)(2,1)}, bf16[256,1024]{1,0:T(8,128)(2,1)}, bf16[256,1024]{1,0:T(8,128)(2,1)}, bf16[256,1024]{1,0:T(8,128)(2,1)}) custom-call(s32[1]{0:T(128)} %bitcast.refs_0_.me_ref, bf16[1,1024,128]{2,1,0:T(8,128)(2,1)S(1)} %copy-done.7, bf16[1,1024,128]{2,1,0:T(8,128)(2,1)S(1)} %collective-permute-done.21.refs_1_, ...), custom_call_target="tpu_custom_call" | custom-call | bytes 4194308 | tf_op jit(solution)/shard_map/att_unpack/pallas_call | solution.py:28
  (104 shorter events, 20.0 us)
Async XLA Ops:
  14.1 7.3 %collective-permute-start.3 = (bf16[512,128]{1,0:T(8,128)(2,1)S(1)}, bf16[512,128]{1,0:T(8,128)(2,1)S(1)}, u32[]{:S(2)}, u32[]{:S(2)}) collective-permute-start(bf16[512,128]{1,0:T(8,128)(2,1)S(1)} %ssm_total.2), channel_id=1, source_target_pairs={{0,16},{4,20},{8,24},{12,28},{1,17},{5,21},{9,25},{13,29},{2,18},{... | collective-permute-start | bytes 393224 | tf_op jit(solution)/shard_map/ppermute | solution.py:291
  21.4 15.0 %collective-permute-start.4 = (bf16[1,1040,128]{2,1,0:T(8,128)(2,1)S(1)}, bf16[1,1040,128]{2,1,0:T(8,128)(2,1)S(1)}, u32[]{:S(2)}, u32[]{:S(2)}) collective-permute-start(bf16[1,1040,128]{2,1,0:T(8,128)(2,1)S(1)} %get-tuple-element.135), channel_id=1, source_target_pairs={{0,16},{4,20},{8,24},{12,28},{16,0},{20,4},{24,8},{28,12},{1,17},{... | collective-permute-start | bytes 798728 | tf_op jit(solution)/shard_map/ppermute | solution.py:284
  23.5 15.7 %collective-permute-start.8 = (bf16[1,1040,128]{2,1,0:T(8,128)(2,1)S(1)}, bf16[1,1040,128]{2,1,0:T(8,128)(2,1)S(1)}, u32[]{:S(2)}, u32[]{:S(2)}) collective-permute-start(bf16[1,1040,128]{2,1,0:T(8,128)(2,1)S(1)} %get-tuple-element.148), channel_id=1, source_target_pairs={{0,4},{4,0},{8,12},{12,8},{16,20},{20,16},{24,28},{28,24},{1,5},{5... | collective-permute-start | bytes 798728 | tf_op jit(solution)/shard_map/ppermute | solution.py:284
  25.8 8.9 %collective-permute-start.6 = (bf16[512,128]{1,0:T(8,128)(2,1)S(1)}, bf16[512,128]{1,0:T(8,128)(2,1)S(1)}, u32[]{:S(2)}, u32[]{:S(2)}) collective-permute-start(bf16[512,128]{1,0:T(8,128)(2,1)S(1)} %get-tuple-element.139), channel_id=1, source_target_pairs={{0,8},{4,12},{8,0},{12,4},{16,24},{20,28},{24,16},{28,20},{1,9},{5... | collective-permute-start | bytes 393224 | tf_op jit(solution)/shard_map/ppermute | solution.py:284
  29.6 6.8 %collective-permute-start.7 = (bf16[512,128]{1,0:T(8,128)(2,1)S(1)}, bf16[512,128]{1,0:T(8,128)(2,1)S(1)}, u32[]{:S(2)}, u32[]{:S(2)}) collective-permute-start(bf16[512,128]{1,0:T(8,128)(2,1)S(1)} %get-tuple-element.140), channel_id=1, source_target_pairs={{0,12},{4,8},{8,4},{12,0},{16,28},{20,24},{24,20},{28,16},{1,13},{... | collective-permute-start | bytes 393224 | tf_op jit(solution)/shard_map/ppermute | solution.py:284
  31.2 45.5 %collective-permute-start.9 = (bf16[1,1040,128]{2,1,0:T(8,128)(2,1)S(1)}, bf16[1,1040,128]{2,1,0:T(8,128)(2,1)S(1)}, u32[]{:S(2)}, u32[]{:S(2)}) collective-permute-start(bf16[1,1040,128]{2,1,0:T(8,128)(2,1)S(1)} %get-tuple-element.149), channel_id=1, source_target_pairs={{0,8},{4,12},{8,0},{12,4},{16,24},{20,28},{24,16},{28,20},{1,9},{5... | collective-permute-start | bytes 798728 | tf_op jit(solution)/shard_map/ppermute | solution.py:284
  34.7 42.1 %collective-permute-start.10 = (bf16[1,1040,128]{2,1,0:T(8,128)(2,1)S(1)}, bf16[1,1040,128]{2,1,0:T(8,128)(2,1)S(1)}, u32[]{:S(2)}, u32[]{:S(2)}) collective-permute-start(bf16[1,1040,128]{2,1,0:T(8,128)(2,1)S(1)} %get-tuple-element.150), channel_id=1, source_target_pairs={{0,12},{4,8},{8,4},{12,0},{16,28},{20,24},{24,20},{28,16},{1,13},{... | collective-permute-start | bytes 798728 | tf_op jit(solution)/shard_map/ppermute | solution.py:284
  36.3 40.4 %collective-permute-start.11 = (bf16[1,1040,128]{2,1,0:T(8,128)(2,1)S(1)}, bf16[1,1040,128]{2,1,0:T(8,128)(2,1)}, u32[]{:S(2)}, u32[]{:S(2)}) collective-permute-start(bf16[1,1040,128]{2,1,0:T(8,128)(2,1)S(1)} %get-tuple-element.151), channel_id=1, source_target_pairs={{0,20},{4,16},{8,28},{12,24},{16,4},{20,0},{24,12},{28,8},{1,21},{... | collective-permute-start | bytes 798728 | tf_op jit(solution)/shard_map/ppermute | solution.py:284
  36.4 40.4 %collective-permute-start.12 = (bf16[1,1040,128]{2,1,0:T(8,128)(2,1)S(1)}, bf16[1,1040,128]{2,1,0:T(8,128)(2,1)}, u32[]{:S(2)}, u32[]{:S(2)}) collective-permute-start(bf16[1,1040,128]{2,1,0:T(8,128)(2,1)S(1)} %get-tuple-element.152), channel_id=1, source_target_pairs={{0,24},{4,28},{8,16},{12,20},{16,8},{20,12},{24,0},{28,4},{1,25},{... | collective-permute-start | bytes 798728 | tf_op jit(solution)/shard_map/ppermute | solution.py:284
  39.1 40.4 %collective-permute-start.16 = (bf16[1,1040,128]{2,1,0:T(8,128)(2,1)S(1)}, bf16[1,1040,128]{2,1,0:T(8,128)(2,1)}, u32[]{:S(2)}, u32[]{:S(2)}) collective-permute-start(bf16[1,1040,128]{2,1,0:T(8,128)(2,1)S(1)} %get-tuple-element.168), channel_id=1, source_target_pairs={{0,28},{4,24},{8,20},{12,16},{16,12},{20,8},{24,4},{28,0},{1,29},{... | collective-permute-start | bytes 798728 | tf_op jit(solution)/shard_map/ppermute | solution.py:284
  76.8 17.7 %collective-permute-start.13 = (bf16[512,128]{1,0:T(8,128)(2,1)}, bf16[512,128]{1,0:T(8,128)(2,1)S(1)}, u32[]{:S(2)}, u32[]{:S(2)}) collective-permute-start(bf16[512,128]{1,0:T(8,128)(2,1)} %get-tuple-element.158), channel_id=1, source_target_pairs={{0,4},{4,0},{8,12},{12,8},{16,20},{20,16},{24,28},{28,24},{1,5},{5... | collective-permute-start | bytes 393224 | tf_op jit(solution)/shard_map/ppermute | solution.py:284
  77.1 17.4 %collective-permute-start.14 = (bf16[512,128]{1,0:T(8,128)(2,1)}, bf16[512,128]{1,0:T(8,128)(2,1)S(1)}, u32[]{:S(2)}, u32[]{:S(2)}) collective-permute-start(bf16[512,128]{1,0:T(8,128)(2,1)} %get-tuple-element.159), channel_id=1, source_target_pairs={{0,8},{4,12},{8,0},{12,4},{16,24},{20,28},{24,16},{28,20},{1,9},{5... | collective-permute-start | bytes 393224 | tf_op jit(solution)/shard_map/ppermute | solution.py:284
  77.1 17.4 %collective-permute-start.15 = (bf16[512,128]{1,0:T(8,128)(2,1)}, bf16[512,128]{1,0:T(8,128)(2,1)S(1)}, u32[]{:S(2)}, u32[]{:S(2)}) collective-permute-start(bf16[512,128]{1,0:T(8,128)(2,1)} %get-tuple-element.160), channel_id=1, source_target_pairs={{0,12},{4,8},{8,4},{12,0},{16,28},{20,24},{24,20},{28,16},{1,13},{... | collective-permute-start | bytes 393224 | tf_op jit(solution)/shard_map/ppermute | solution.py:284
  94.8 21.8 %collective-permute-start.17 = (bf16[512,128]{1,0:T(8,128)(2,1)S(1)}, bf16[512,128]{1,0:T(8,128)(2,1)S(1)}, u32[]{:S(2)}, u32[]{:S(2)}) collective-permute-start(bf16[512,128]{1,0:T(8,128)(2,1)S(1)} %ssm_total.3), channel_id=1, source_target_pairs={{16,0},{20,4},{24,8},{28,12},{17,1},{21,5},{25,9},{29,13},{18,2},{... | collective-permute-start | bytes 393224 | tf_op jit(solution)/shard_map/ppermute | solution.py:291
  96.2 40.5 %collective-permute-start.24 = (bf16[1,1024,128]{2,1,0:T(8,128)(2,1)}, bf16[1,1024,128]{2,1,0:T(8,128)(2,1)S(1)}, u32[]{:S(2)}, u32[]{:S(2)}) collective-permute-start(bf16[1,1024,128]{2,1,0:T(8,128)(2,1)} %get-tuple-element.207), channel_id=1, source_target_pairs={{0,16},{4,20},{8,24},{12,28},{16,0},{20,4},{24,8},{28,12},{1,17},{... | collective-permute-start | bytes 786440 | tf_op jit(solution)/shard_map/ppermute | solution.py:284
  116.6 20.1 %collective-permute-start.25 = (bf16[1,1024,128]{2,1,0:T(8,128)(2,1)}, bf16[1,1024,128]{2,1,0:T(8,128)(2,1)S(1)}, u32[]{:S(2)}, u32[]{:S(2)}) collective-permute-start(bf16[1,1024,128]{2,1,0:T(8,128)(2,1)} %get-tuple-element.208), channel_id=1, source_target_pairs={{0,20},{4,16},{8,28},{12,24},{16,4},{20,0},{24,12},{28,8},{1,21},{... | collective-permute-start | bytes 786440 | tf_op jit(solution)/shard_map/ppermute | solution.py:284
  117.5 7.6 %collective-permute-start.18 = (bf16[512,128]{1,0:T(8,128)(2,1)S(1)}, bf16[512,128]{1,0:T(8,128)(2,1)S(1)}, u32[]{:S(2)}, u32[]{:S(2)}) collective-permute-start(bf16[512,128]{1,0:T(8,128)(2,1)S(1)} %get-tuple-element.198), channel_id=1, source_target_pairs={{0,4},{4,0},{8,12},{12,8},{16,20},{20,16},{24,28},{28,24},{1,5},{5... | collective-permute-start | bytes 393224 | tf_op jit(solution)/shard_map/ppermute | solution.py:284
  118.0 13.2 %collective-permute-start.19 = (bf16[512,128]{1,0:T(8,128)(2,1)S(1)}, bf16[512,128]{1,0:T(8,128)(2,1)S(1)}, u32[]{:S(2)}, u32[]{:S(2)}) collective-permute-start(bf16[512,128]{1,0:T(8,128)(2,1)S(1)} %get-tuple-element.199), channel_id=1, source_target_pairs={{0,8},{4,12},{8,0},{12,4},{16,24},{20,28},{24,16},{28,20},{1,9},{5... | collective-permute-start | bytes 393224 | tf_op jit(solution)/shard_map/ppermute | solution.py:284
  118.0 16.0 %collective-permute-start.20 = (bf16[512,128]{1,0:T(8,128)(2,1)S(1)}, bf16[512,128]{1,0:T(8,128)(2,1)S(1)}, u32[]{:S(2)}, u32[]{:S(2)}) collective-permute-start(bf16[512,128]{1,0:T(8,128)(2,1)S(1)} %get-tuple-element.200), channel_id=1, source_target_pairs={{0,12},{4,8},{8,4},{12,0},{16,28},{20,24},{24,20},{28,16},{1,13},{... | collective-permute-start | bytes 393224 | tf_op jit(solution)/shard_map/ppermute | solution.py:284
  134.0 27.1 %collective-permute-start.21 = (bf16[1,1024,128]{2,1,0:T(8,128)(2,1)S(1)}, bf16[1,1024,128]{2,1,0:T(8,128)(2,1)S(1)}, u32[]{:S(2)}, u32[]{:S(2)}) collective-permute-start(bf16[1,1024,128]{2,1,0:T(8,128)(2,1)S(1)} %copy-done.26), channel_id=1, source_target_pairs={{0,4},{4,0},{8,12},{12,8},{16,20},{20,16},{24,28},{28,24},{1,5},{5... | collective-permute-start | bytes 786440 | tf_op jit(solution)/shard_map/ppermute | solution.py:284
  135.2 26.0 %collective-permute-start.22 = (bf16[1,1024,128]{2,1,0:T(8,128)(2,1)S(1)}, bf16[1,1024,128]{2,1,0:T(8,128)(2,1)S(1)}, u32[]{:S(2)}, u32[]{:S(2)}) collective-permute-start(bf16[1,1024,128]{2,1,0:T(8,128)(2,1)S(1)} %copy-done.25), channel_id=1, source_target_pairs={{0,8},{4,12},{8,0},{12,4},{16,24},{20,28},{24,16},{28,20},{1,9},{5... | collective-permute-start | bytes 786440 | tf_op jit(solution)/shard_map/ppermute | solution.py:284
  135.2 26.0 %collective-permute-start.23 = (bf16[1,1024,128]{2,1,0:T(8,128)(2,1)S(1)}, bf16[1,1024,128]{2,1,0:T(8,128)(2,1)S(1)}, u32[]{:S(2)}, u32[]{:S(2)}) collective-permute-start(bf16[1,1024,128]{2,1,0:T(8,128)(2,1)S(1)} %copy-done.24), channel_id=1, source_target_pairs={{0,12},{4,8},{8,4},{12,0},{16,28},{20,24},{24,20},{28,16},{1,13},{... | collective-permute-start | bytes 786440 | tf_op jit(solution)/shard_map/ppermute | solution.py:284
  136.7 24.5 %collective-permute-start.26 = (bf16[1,1024,128]{2,1,0:T(8,128)(2,1)S(1)}, bf16[1,1024,128]{2,1,0:T(8,128)(2,1)S(1)}, u32[]{:S(2)}, u32[]{:S(2)}) collective-permute-start(bf16[1,1024,128]{2,1,0:T(8,128)(2,1)S(1)} %copy-done.23), channel_id=1, source_target_pairs={{0,24},{4,28},{8,16},{12,20},{16,8},{20,12},{24,0},{28,4},{1,25},{... | collective-permute-start | bytes 786440 | tf_op jit(solution)/shard_map/ppermute | solution.py:284
  136.7 24.5 %collective-permute-start.27 = (bf16[1,1024,128]{2,1,0:T(8,128)(2,1)S(1)}, bf16[1,1024,128]{2,1,0:T(8,128)(2,1)S(1)}, u32[]{:S(2)}, u32[]{:S(2)}) collective-permute-start(bf16[1,1024,128]{2,1,0:T(8,128)(2,1)S(1)} %copy-done.22), channel_id=1, source_target_pairs={{0,28},{4,24},{8,20},{12,16},{16,12},{20,8},{24,4},{28,0},{1,29},{... | collective-permute-start | bytes 786440 | tf_op jit(solution)/shard_map/ppermute | solution.py:284
  (31 other events, 472.9 us)

commit v7 on v6

--- a/solution.py
+++ b/solution.py
@@ -569,26 +569,26 @@
     )
     tails = [pass_block(block, n) for n, block in enumerate(sent)]
     total = carry_total(False, *tails)
-    start = cross(total, False)
     if dealt:
         marks = doc_start.reshape(length // 128, 128)
         marks = jnp.stack([marks // 128, marks % 128], axis=1).reshape(length // 64, 128)
         marks = jnp.pad(marks, ((0, TAIL - length // 64), (0, 0))).astype(BF16)
-        marks, total = lax.optimization_barrier((marks, total))
         packed = call(
             pack_kernel, [shape((per, 4 * length + TAIL, 128), BF16)] * parts,
             me, marks, att_queries, att_keys, att_values, att_grad,
             specs=[SMEM] + [VMEM] * 5, vmem=SMALL, name="att_pack",
         )
+        crossed, total = lax.optimization_barrier((pass_block(packed[shares], shares), total))
+        start = cross(total, False)
         packed, start = lax.optimization_barrier((packed, start))
-        att_got = {n: pass_block(block, n) for n, block in enumerate(packed)}
+        att_got = {n: pass_block(block, n) for n, block in enumerate(packed) if n != shares}
+        att_got[shares] = crossed
     else:
         att_out = ring_attention(att_queries, att_keys, att_values, att_grad, doc_start)
+        start = cross(total, False)
     state = [
         pass_block(block, n) for n, block in enumerate(carry_states(False, start, *tails))
     ]
-    if dealt:
-        att_got[shares], state = lax.optimization_barrier((att_got[shares], state))
     mixed, sums, state = call(
         lambda *refs: mix_kernel(shares, *refs),
         (shape((length, width), F32), shape((8, length), F32), shape((width, 128), BF16)),
@@ -628,9 +628,8 @@
         blocks, att_done = lax.optimization_barrier((blocks, att_done))
     total = carry_total(True, *tails, *blocks)
     start = cross(total, True)
-    back = [
-        pass_block(block, n) for n, block in enumerate(carry_states(True, start, *tails, *blocks))
-    ]
+    carried = carry_states(True, start, *tails, *blocks)
+    back = [pass_block(block, n) for n, block in enumerate(carried)]
     gin, read_part, write_part = call(
         inner_kernel,
         (shape((length, width), F32), shape((length, 128), F32), shape((length, 128), F32)),
@@ -639,12 +638,13 @@
     )
     if dealt:
         early = [shares, shares + 1]
-        late = [*range(shares + 2, parts), *range(1, shares)]
+        middle = [shares + 2]
+        late = [*range(shares + 3, parts), *range(1, shares)]
         att_back = {0: att_done[0]}
         held, total = lax.optimization_barrier((att_done, total))
-        att_back[early[0]] = pass_block(held[early[0]], early[0])
-        held, start = lax.optimization_barrier((att_done, start))
-        att_back[early[1]] = pass_block(held[early[1]], early[1])
+        att_back.update((n, pass_block(held[n], n)) for n in early)
+        held, carried = lax.optimization_barrier((att_done, carried))
+        att_back.update((n, pass_block(held[n], n)) for n in middle)
         held, back, gin = lax.optimization_barrier((att_done, back, gin))
         att_back.update((n, pass_block(held[n], n)) for n in late)
         done, back = lax.optimization_barrier(([att_back[n] for n in early], back))

time: 164 us -> 168 us (1.024)
  starting transfers between devices: 41.4 us -> 61.7 us
  blocking collectives: 40.4 us -> 26.2 us
  waiting for transfers between devices: 33 us -> 28.1 us
  local copies, waits for them, and re-layouts: 4.38 us -> 7.16 us
    ppermute x26, starting transfers between devices: 35.4 us -> 58.5 us  [pass_block(): lax.ppermute(block, 'ctx', [(i, i ^ n) for i in range(lax.axis_size('ctx'...]
    ppermute x2, waiting for transfers between devices: 17.4 us -> 1.93 us  [cross(): return lax.ppermute(total, 'ctx', pairs)]
    psum x1, blocking collectives: 24.3 us -> 10.2 us  [body(): sums = lax.psum(sums, 'head')]
    ppermute x26, waiting for transfers between devices: 15.7 us -> 26.2 us  [pass_block(): lax.ppermute(block, 'ctx', [(i, i ^ n) for i in range(lax.axis_size('ctx'...]
    unnamed x54 -> x56, local copies, waits for them, and re-layouts: 4.38 us -> 7.15 us
    ppermute x2, starting transfers between devices: 5.98 us -> 3.24 us  [cross(): return lax.ppermute(total, 'ctx', pairs)]
  transfers between devices with their start and end apart: 28 -> 28, of which waited for: 9 -> 6; matrix products, arithmetic and copies ran while one was open for 0% -> 0% of each run, Pallas kernels for 23% -> 24%
where the time goes in v7:
time: 168 us; the launch traced here: 167 us
  starting transfers between devices  61.7 us (37%)
  Pallas kernels  42.1 us (25%)
  waiting for transfers between devices  28.1 us (17%)
  blocking collectives  26.2 us (16%)
  local copies, waits for them, and re-layouts  7.16 us (4%)
    ppermute x26, starting transfers between devices, pass_block(): lax.ppermute(block, 'ctx', [(i, i ^ n) for i in range(lax.axis_size('ctx'...  58.5 us
    pallas_call x12, Pallas kernels, call(): pl.pallas_call(kernel, out_shape=out_shape, in_specs=specs or [VMEM] * le...  42.1 us
    ppermute x26, waiting for transfers between devices, pass_block(): lax.ppermute(block, 'ctx', [(i, i ^ n) for i in range(lax.axis_size('ctx'...  26.2 us
    psum x1, blocking collectives, body(): write_sum, read_sum = lax.psum((write_part, read_part), 'head')  15.9 us
    psum x1, blocking collectives, body(): sums = lax.psum(sums, 'head')  10.2 us
    unnamed x56, local copies, waits for them, and re-layouts  7.15 us
  transfers between devices with their start and end apart: 28, of which 6 were waited for; matrix products, arithmetic and copies ran while one was open for 0% of the time, Pallas kernels for 24%

profile of v7, /device:TPU:1, one launch (start us, length us, event | category | flops | bytes accessed | tf_op | source)
XLA Modules:
  0.0 167.1 jit_solution(8834222963481629704)
XLA Ops:
  6.8 3.1 %collective-permute-start = (bf16[1,1040,128]{2,1,0:T(8,128)(2,1)S(1)}, bf16[1,1040,128]{2,1,0:T(8,128)(2,1)S(1)}, u32[]{:S(2)}, u32[]{:S(2)}) collective-permute-start(bf16[1,1040,128]{2,1,0:T(8,128)(2,1)S(1)} %get-tuple-element.121), channel_id=1, source_target_pairs={{0,16},{4,20},{8,24},{12,28},{16,0},{20,4},{24,8},{28,12},{1,17},{... | collective-permute-start | bytes 798728 | tf_op jit(solution)/shard_map/ppermute | solution.py:284
  9.9 3.0 %ssm_first.1 = (f32[256,16]{1,0:T(8,128)}, f32[16,256]{1,0:T(8,128)}, bf16[528,128]{1,0:T(8,128)(2,1)}, bf16[528,128]{1,0:T(8,128)(2,1)}, bf16[528,128]{1,0:T(8,128)(2,1)}, /*index=5*/bf16[528,128]{1,0:T(8,128)(2,1)}) custom-call(s32[1]{0:T(128)} %bitcast.refs_0_.me_ref, f32[16,256]{1,0:T(8,128)} %bitcast.11, s32[1,256]{1,0:T(1,128)} %bitcast.6, ...), custom_call_target="tpu_custom_call" | custom-call | bytes 1704964 | tf_op jit(solution)/shard_map/ssm_first/pallas_call | solution.py:28
  17.3 6.2 %collective-permute-done.2.refs_3_.refs_4_ = bf16[528,128]{1,0:T(8,128)(2,1)S(1)} collective-permute-done((bf16[528,128]{1,0:T(8,128)(2,1)}, bf16[528,128]{1,0:T(8,128)(2,1)S(1)}, u32[]{:S(2)}, u32[]{:S(2)}) %collective-permute-start.2) | collective-permute-done | bytes 135200 | tf_op jit(solution)/shard_map/ppermute | solution.py:284
  23.6 2.5 %collective-permute-done.3.refs_4_.refs_5_ = bf16[528,128]{1,0:T(8,128)(2,1)S(1)} collective-permute-done((bf16[528,128]{1,0:T(8,128)(2,1)}, bf16[528,128]{1,0:T(8,128)(2,1)S(1)}, u32[]{:S(2)}, u32[]{:S(2)}) %collective-permute-start.3) | collective-permute-done | bytes 135200 | tf_op jit(solution)/shard_map/ppermute | solution.py:284
  29.0 1.9 %collective-permute-done.4.refs_1_ = bf16[512,128]{1,0:T(8,128)(2,1)S(1)} collective-permute-done((bf16[512,128]{1,0:T(8,128)(2,1)S(1)}, bf16[512,128]{1,0:T(8,128)(2,1)S(1)}, u32[]{:S(2)}, u32[]{:S(2)}) %collective-permute-start.4) | collective-permute-done | bytes 131104 | tf_op jit(solution)/shard_map/ppermute | solution.py:291
  33.2 4.0 %collective-permute-start.6 = (bf16[512,128]{1,0:T(8,128)(2,1)S(1)}, bf16[512,128]{1,0:T(8,128)(2,1)S(1)}, u32[]{:S(2)}, u32[]{:S(2)}) collective-permute-start(bf16[512,128]{1,0:T(8,128)(2,1)S(1)} %get-tuple-element.133), channel_id=1, source_target_pairs={{0,8},{4,12},{8,0},{12,4},{16,24},{20,28},{24,16},{28,20},{1,9},{5... | collective-permute-start | bytes 393224 | tf_op jit(solution)/shard_map/ppermute | solution.py:284
  39.9 7.3 %collective-permute-start.10 = (bf16[1,1040,128]{2,1,0:T(8,128)(2,1)S(1)}, bf16[1,1040,128]{2,1,0:T(8,128)(2,1)S(1)}, u32[]{:S(2)}, u32[]{:S(2)}) collective-permute-start(bf16[1,1040,128]{2,1,0:T(8,128)(2,1)S(1)} %get-tuple-element.140), channel_id=1, source_target_pairs={{0,12},{4,8},{8,4},{12,0},{16,28},{20,24},{24,20},{28,16},{1,13},{... | collective-permute-start | bytes 798728 | tf_op jit(solution)/shard_map/ppermute | solution.py:284
  47.2 2.1 %collective-permute-start.11 = (bf16[1,1040,128]{2,1,0:T(8,128)(2,1)S(1)}, bf16[1,1040,128]{2,1,0:T(8,128)(2,1)S(1)}, u32[]{:S(2)}, u32[]{:S(2)}) collective-permute-start(bf16[1,1040,128]{2,1,0:T(8,128)(2,1)S(1)} %get-tuple-element.141), channel_id=1, source_target_pairs={{0,20},{4,16},{8,28},{12,24},{16,4},{20,0},{24,12},{28,8},{1,21},{... | collective-permute-start | bytes 798728 | tf_op jit(solution)/shard_map/ppermute | solution.py:284
  49.4 5.1 %collective-permute-start.16 = (bf16[1,1040,128]{2,1,0:T(8,128)(2,1)S(1)}, bf16[1,1040,128]{2,1,0:T(8,128)(2,1)}, u32[]{:S(2)}, u32[]{:S(2)}) collective-permute-start(bf16[1,1040,128]{2,1,0:T(8,128)(2,1)S(1)} %get-tuple-element.158), channel_id=1, source_target_pairs={{0,28},{4,24},{8,20},{12,16},{16,12},{20,8},{24,4},{28,0},{1,29},{... | collective-permute-start | bytes 798728 | tf_op jit(solution)/shard_map/ppermute | solution.py:284
  54.5 6.0 %ssm_mix.1 = (f32[256,2048]{1,0:T(8,128)}, f32[8,256]{1,0:T(8,128)}, bf16[2048,128]{1,0:T(8,128)(2,1)}) custom-call(s32[1]{0:T(128)} %bitcast.refs_0_.me_ref, bf16[256,2048]{1,0:T(8,128)(2,1)} %refs_2_.3, bf16[256,2048]{1,0:T(8,128)(2,1)} %refs_3_.6, bf16[256,2048]{1,0:T(8,128)(2,1)} %refs_4_.5, bf16[256,128]{1,0:T(8,128)(2,1)} %refs_3_.7, ...), custom_call_target="tpu_custom_call" | custom-call | bytes 6464516 | tf_op jit(solution)/shard_map/ssm_mix/pallas_call | solution.py:28
  60.4 10.2 %psum.21.refs_1_ = f32[8,256]{1,0:T(8,128)} all-reduce(f32[8,256]{1,0:T(8,128)} %get-tuple-element.135), channel_id=1, replica_groups=mesh['ctx'=8,'head'=4] {'head'}, use_global_device_ids=true, to_apply=%region_0.1 | all-reduce | flops 2048 | bytes 16384 | tf_op jit(solution)/shard_map/psum | solution.py:598
  70.7 5.9 %ssm_gate.1 = (bf16[256,2048]{1,0:T(8,128)(2,1)}, bf16[256,2048]{1,0:T(8,128)(2,1)}, bf16[256,2048]{1,0:T(8,128)(2,1)}, bf16[512,128]{1,0:T(8,128)(2,1)}, bf16[5...) custom-call(s32[1]{0:T(128)} %bitcast.refs_0_.me_ref, f32[8,256]{1,0:T(8,128)} %psum.21.refs_1_, ...), custom_call_target="tpu_custom_call" | custom-call | bytes 7955460 | tf_op jit(solution)/shard_map/ssm_gate/pallas_call | solution.py:28
  76.8 2.6 %collective-permute-start.15 = (bf16[512,128]{1,0:T(8,128)(2,1)}, bf16[512,128]{1,0:T(8,128)(2,1)S(1)}, u32[]{:S(2)}, u32[]{:S(2)}) collective-permute-start(bf16[512,128]{1,0:T(8,128)(2,1)} %get-tuple-element.150), channel_id=1, source_target_pairs={{0,12},{4,8},{8,4},{12,0},{16,28},{20,24},{24,20},{28,16},{1,13},{... | collective-permute-start | bytes 393224 | tf_op jit(solution)/shard_map/ppermute | solution.py:284
  79.4 15.0 %att_attend.1 = (bf16[1,1024,128]{2,1,0:T(8,128)(2,1)}, bf16[1,1024,128]{2,1,0:T(8,128)(2,1)}, bf16[1,1024,128]{2,1,0:T(8,128)(2,1)}, bf16[1,1024,128]{2,1,0:T(8...) custom-call(s32[1]{0:T(128)} %bitcast.refs_0_.me_ref, ...), custom_call_target="tpu_custom_call" | custom-call | flops 3221225472 | bytes 4227076 | tf_op jit(solution)/shard_map/att_attend/pallas_call | solution.py:28
  96.1 3.0 %collective-permute-start.24 = (bf16[1,1024,128]{2,1,0:T(8,128)(2,1)}, bf16[1,1024,128]{2,1,0:T(8,128)(2,1)S(1)}, u32[]{:S(2)}, u32[]{:S(2)}) collective-permute-start(bf16[1,1024,128]{2,1,0:T(8,128)(2,1)} %get-tuple-element.197), channel_id=1, source_target_pairs={{0,16},{4,20},{8,24},{12,28},{16,0},{20,4},{24,8},{28,12},{1,17},{... | collective-permute-start | bytes 786440 | tf_op jit(solution)/shard_map/ppermute | solution.py:284
  99.1 2.9 %collective-permute-start.25 = (bf16[1,1024,128]{2,1,0:T(8,128)(2,1)}, bf16[1,1024,128]{2,1,0:T(8,128)(2,1)S(1)}, u32[]{:S(2)}, u32[]{:S(2)}) collective-permute-start(bf16[1,1024,128]{2,1,0:T(8,128)(2,1)} %get-tuple-element.198), channel_id=1, source_target_pairs={{0,20},{4,16},{8,28},{12,24},{16,4},{20,0},{24,12},{28,8},{1,21},{... | collective-permute-start | bytes 786440 | tf_op jit(solution)/shard_map/ppermute | solution.py:284
  102.9 17.5 %collective-permute-start.18 = (bf16[512,128]{1,0:T(8,128)(2,1)S(1)}, bf16[512,128]{1,0:T(8,128)(2,1)S(1)}, u32[]{:S(2)}, u32[]{:S(2)}) collective-permute-start(bf16[512,128]{1,0:T(8,128)(2,1)S(1)} %get-tuple-element.188), channel_id=1, source_target_pairs={{0,4},{4,0},{8,12},{12,8},{16,20},{20,16},{24,28},{28,24},{1,5},{5... | collective-permute-start | bytes 393224 | tf_op jit(solution)/shard_map/ppermute | solution.py:284
  121.6 4.9 %ssm_inner.1 = (f32[256,2048]{1,0:T(8,128)}, f32[256,128]{1,0:T(8,128)}, f32[256,128]{1,0:T(8,128)}) custom-call(s32[1]{0:T(128)} %bitcast.refs_0_.me_ref, bf16[256,2048]{1,0:T(8,128)(2,1)} %get-tuple-element.191.dmixed_ref, bf16[256,2048]{1,0:T(8,128)(2,1)} %refs_2_.3, bf16[256,128]{1,0:T(8,128)(2,1)} %refs_3_.7, bf16[256,128]{1,0:T(8,128)(2,1)} %r_ref.1, ...), custom_call_target="tpu_custom_call" | custom-call | bytes 5145604 | tf_op jit(solution)/shard_map/ssm_inner/pallas_call | solution.py:28
  126.7 4.4 %collective-permute-done.19.refs_9_ = bf16[512,128]{1,0:T(8,128)(2,1)S(1)} collective-permute-done((bf16[512,128]{1,0:T(8,128)(2,1)S(1)}, bf16[512,128]{1,0:T(8,128)(2,1)S(1)}, u32[]{:S(2)}, u32[]{:S(2)}) %collective-permute-start.19) | collective-permute-done | bytes 131104 | tf_op jit(solution)/shard_map/ppermute | solution.py:284
  131.1 11.2 %collective-permute-done.20.refs_10_ = bf16[512,128]{1,0:T(8,128)(2,1)S(1)} collective-permute-done((bf16[512,128]{1,0:T(8,128)(2,1)S(1)}, bf16[512,128]{1,0:T(8,128)(2,1)S(1)}, u32[]{:S(2)}, u32[]{:S(2)}) %collective-permute-start.20) | collective-permute-done | bytes 131104 | tf_op jit(solution)/shard_map/ppermute | solution.py:284
  142.5 2.5 %collective-permute-start.23 = (bf16[1,1024,128]{2,1,0:T(8,128)(2,1)S(1)}, bf16[1,1024,128]{2,1,0:T(8,128)(2,1)S(1)}, u32[]{:S(2)}, u32[]{:S(2)}) collective-permute-start(bf16[1,1024,128]{2,1,0:T(8,128)(2,1)S(1)} %copy-done.25), channel_id=1, source_target_pairs={{0,12},{4,8},{8,4},{12,0},{16,28},{20,24},{24,20},{28,16},{1,13},{... | collective-permute-start | bytes 786440 | tf_op jit(solution)/shard_map/ppermute | solution.py:284
  145.1 4.2 %ssm_last.1 = (bf16[256,2048]{1,0:T(8,128)(2,1)}, f32[256,128]{1,0:T(8,128)}) custom-call(s32[1]{0:T(128)} %bitcast.refs_0_.me_ref, f32[256,2048]{1,0:T(8,128)} %get-tuple-element.208.refs_1_, bf16[256,2048]{1,0:T(8,128)(2,1)} %refs_2_.3, bf16[256,128]{1,0:T(8,128)(2,1)} %refs_3_.7, s32[1,256]{1,0:T(1,128)} %bitcast.10, ...), custom_call_target="tpu_custom_call" | custom-call | bytes 5063684 | tf_op jit(solution)/shard_map/ssm_last/pallas_call | solution.py:28
  149.2 15.9 %all-reduce.3 = (bf16[256,128]{1,0:T(8,128)(2,1)}, bf16[256,128]{1,0:T(8,128)(2,1)}) all-reduce(f32[256,128]{1,0:T(8,128)} %get-tuple-element.216, f32[256,128]{1,0:T(8,128)S(1)} %copy-done.17), channel_id=1, replica_groups=mesh['ctx'=8,'head'=4] {'head'}, use_global_device_ids=true, to_apply=%region_1.2 | all-reduce | flops 65536 | bytes 393216 | tf_op jit(solution)/shard_map/psum | solution.py:665
  165.2 1.9 %att_unpack.1 = (bf16[256,1024]{1,0:T(8,128)(2,1)}, bf16[256,1024]{1,0:T(8,128)(2,1)}, bf16[256,1024]{1,0:T(8,128)(2,1)}, bf16[256,1024]{1,0:T(8,128)(2,1)}) custom-call(s32[1]{0:T(128)} %bitcast.refs_0_.me_ref, bf16[1,1024,128]{2,1,0:T(8,128)(2,1)S(1)} %copy-done.7, bf16[1,1024,128]{2,1,0:T(8,128)(2,1)S(1)} %collective-permute-done.21.refs_1_, ...), custom_call_target="tpu_custom_call" | custom-call | bytes 4194308 | tf_op jit(solution)/shard_map/att_unpack/pallas_call | solution.py:28
  (106 shorter events, 22.5 us)
Async XLA Ops:
  6.8 20.4 %collective-permute-start = (bf16[1,1040,128]{2,1,0:T(8,128)(2,1)S(1)}, bf16[1,1040,128]{2,1,0:T(8,128)(2,1)S(1)}, u32[]{:S(2)}, u32[]{:S(2)}) collective-permute-start(bf16[1,1040,128]{2,1,0:T(8,128)(2,1)S(1)} %get-tuple-element.121), channel_id=1, source_target_pairs={{0,16},{4,20},{8,24},{12,28},{16,0},{20,4},{24,8},{28,12},{1,17},{... | collective-permute-start | bytes 798728 | tf_op jit(solution)/shard_map/ppermute | solution.py:284
  14.2 9.4 %collective-permute-start.2 = (bf16[528,128]{1,0:T(8,128)(2,1)}, bf16[528,128]{1,0:T(8,128)(2,1)S(1)}, u32[]{:S(2)}, u32[]{:S(2)}) collective-permute-start(bf16[528,128]{1,0:T(8,128)(2,1)} %get-tuple-element.127), channel_id=1, source_target_pairs={{0,8},{4,12},{8,0},{12,4},{16,24},{20,28},{24,16},{28,20},{1,9},{5... | collective-permute-start | bytes 405512 | tf_op jit(solution)/shard_map/ppermute | solution.py:284
  15.5 10.6 %collective-permute-start.3 = (bf16[528,128]{1,0:T(8,128)(2,1)}, bf16[528,128]{1,0:T(8,128)(2,1)S(1)}, u32[]{:S(2)}, u32[]{:S(2)}) collective-permute-start(bf16[528,128]{1,0:T(8,128)(2,1)} %get-tuple-element.128), channel_id=1, source_target_pairs={{0,12},{4,8},{8,4},{12,0},{16,28},{20,24},{24,20},{28,16},{1,13},{... | collective-permute-start | bytes 405512 | tf_op jit(solution)/shard_map/ppermute | solution.py:284
  30.9 18.4 %collective-permute-start.8 = (bf16[1,1040,128]{2,1,0:T(8,128)(2,1)S(1)}, bf16[1,1040,128]{2,1,0:T(8,128)(2,1)S(1)}, u32[]{:S(2)}, u32[]{:S(2)}) collective-permute-start(bf16[1,1040,128]{2,1,0:T(8,128)(2,1)S(1)} %get-tuple-element.138), channel_id=1, source_target_pairs={{0,4},{4,0},{8,12},{12,8},{16,20},{20,16},{24,28},{28,24},{1,5},{5... | collective-permute-start | bytes 798728 | tf_op jit(solution)/shard_map/ppermute | solution.py:284
  33.2 13.9 %collective-permute-start.6 = (bf16[512,128]{1,0:T(8,128)(2,1)S(1)}, bf16[512,128]{1,0:T(8,128)(2,1)S(1)}, u32[]{:S(2)}, u32[]{:S(2)}) collective-permute-start(bf16[512,128]{1,0:T(8,128)(2,1)S(1)} %get-tuple-element.133), channel_id=1, source_target_pairs={{0,8},{4,12},{8,0},{12,4},{16,24},{20,28},{24,16},{28,20},{1,9},{5... | collective-permute-start | bytes 393224 | tf_op jit(solution)/shard_map/ppermute | solution.py:284
  37.2 12.0 %collective-permute-start.7 = (bf16[512,128]{1,0:T(8,128)(2,1)S(1)}, bf16[512,128]{1,0:T(8,128)(2,1)S(1)}, u32[]{:S(2)}, u32[]{:S(2)}) collective-permute-start(bf16[512,128]{1,0:T(8,128)(2,1)S(1)} %get-tuple-element.134), channel_id=1, source_target_pairs={{0,12},{4,8},{8,4},{12,0},{16,28},{20,24},{24,20},{28,16},{1,13},{... | collective-permute-start | bytes 393224 | tf_op jit(solution)/shard_map/ppermute | solution.py:284
  38.4 38.1 %collective-permute-start.9 = (bf16[1,1040,128]{2,1,0:T(8,128)(2,1)S(1)}, bf16[1,1040,128]{2,1,0:T(8,128)(2,1)S(1)}, u32[]{:S(2)}, u32[]{:S(2)}) collective-permute-start(bf16[1,1040,128]{2,1,0:T(8,128)(2,1)S(1)} %get-tuple-element.139), channel_id=1, source_target_pairs={{0,8},{4,12},{8,0},{12,4},{16,24},{20,28},{24,16},{28,20},{1,9},{5... | collective-permute-start | bytes 798728 | tf_op jit(solution)/shard_map/ppermute | solution.py:284
  39.9 36.7 %collective-permute-start.10 = (bf16[1,1040,128]{2,1,0:T(8,128)(2,1)S(1)}, bf16[1,1040,128]{2,1,0:T(8,128)(2,1)S(1)}, u32[]{:S(2)}, u32[]{:S(2)}) collective-permute-start(bf16[1,1040,128]{2,1,0:T(8,128)(2,1)S(1)} %get-tuple-element.140), channel_id=1, source_target_pairs={{0,12},{4,8},{8,4},{12,0},{16,28},{20,24},{24,20},{28,16},{1,13},{... | collective-permute-start | bytes 798728 | tf_op jit(solution)/shard_map/ppermute | solution.py:284
  47.2 29.4 %collective-permute-start.11 = (bf16[1,1040,128]{2,1,0:T(8,128)(2,1)S(1)}, bf16[1,1040,128]{2,1,0:T(8,128)(2,1)S(1)}, u32[]{:S(2)}, u32[]{:S(2)}) collective-permute-start(bf16[1,1040,128]{2,1,0:T(8,128)(2,1)S(1)} %get-tuple-element.141), channel_id=1, source_target_pairs={{0,20},{4,16},{8,28},{12,24},{16,4},{20,0},{24,12},{28,8},{1,21},{... | collective-permute-start | bytes 798728 | tf_op jit(solution)/shard_map/ppermute | solution.py:284
  49.3 27.3 %collective-permute-start.12 = (bf16[1,1040,128]{2,1,0:T(8,128)(2,1)S(1)}, bf16[1,1040,128]{2,1,0:T(8,128)(2,1)S(1)}, u32[]{:S(2)}, u32[]{:S(2)}) collective-permute-start(bf16[1,1040,128]{2,1,0:T(8,128)(2,1)S(1)} %get-tuple-element.142), channel_id=1, source_target_pairs={{0,24},{4,28},{8,16},{12,20},{16,8},{20,12},{24,0},{28,4},{1,25},{... | collective-permute-start | bytes 798728 | tf_op jit(solution)/shard_map/ppermute | solution.py:284
  49.4 30.0 %collective-permute-start.16 = (bf16[1,1040,128]{2,1,0:T(8,128)(2,1)S(1)}, bf16[1,1040,128]{2,1,0:T(8,128)(2,1)}, u32[]{:S(2)}, u32[]{:S(2)}) collective-permute-start(bf16[1,1040,128]{2,1,0:T(8,128)(2,1)S(1)} %get-tuple-element.158), channel_id=1, source_target_pairs={{0,28},{4,24},{8,20},{12,16},{16,12},{20,8},{24,4},{28,0},{1,29},{... | collective-permute-start | bytes 798728 | tf_op jit(solution)/shard_map/ppermute | solution.py:284
  76.6 17.8 %collective-permute-start.13 = (bf16[512,128]{1,0:T(8,128)(2,1)}, bf16[512,128]{1,0:T(8,128)(2,1)S(1)}, u32[]{:S(2)}, u32[]{:S(2)}) collective-permute-start(bf16[512,128]{1,0:T(8,128)(2,1)} %get-tuple-element.148), channel_id=1, source_target_pairs={{0,4},{4,0},{8,12},{12,8},{16,20},{20,16},{24,28},{28,24},{1,5},{5... | collective-permute-start | bytes 393224 | tf_op jit(solution)/shard_map/ppermute | solution.py:284
  76.7 17.7 %collective-permute-start.14 = (bf16[512,128]{1,0:T(8,128)(2,1)}, bf16[512,128]{1,0:T(8,128)(2,1)S(1)}, u32[]{:S(2)}, u32[]{:S(2)}) collective-permute-start(bf16[512,128]{1,0:T(8,128)(2,1)} %get-tuple-element.149), channel_id=1, source_target_pairs={{0,8},{4,12},{8,0},{12,4},{16,24},{20,28},{24,16},{28,20},{1,9},{5... | collective-permute-start | bytes 393224 | tf_op jit(solution)/shard_map/ppermute | solution.py:284
  76.8 17.6 %collective-permute-start.15 = (bf16[512,128]{1,0:T(8,128)(2,1)}, bf16[512,128]{1,0:T(8,128)(2,1)S(1)}, u32[]{:S(2)}, u32[]{:S(2)}) collective-permute-start(bf16[512,128]{1,0:T(8,128)(2,1)} %get-tuple-element.150), channel_id=1, source_target_pairs={{0,12},{4,8},{8,4},{12,0},{16,28},{20,24},{24,20},{28,16},{1,13},{... | collective-permute-start | bytes 393224 | tf_op jit(solution)/shard_map/ppermute | solution.py:284
  96.1 46.4 %collective-permute-start.24 = (bf16[1,1024,128]{2,1,0:T(8,128)(2,1)}, bf16[1,1024,128]{2,1,0:T(8,128)(2,1)S(1)}, u32[]{:S(2)}, u32[]{:S(2)}) collective-permute-start(bf16[1,1024,128]{2,1,0:T(8,128)(2,1)} %get-tuple-element.197), channel_id=1, source_target_pairs={{0,16},{4,20},{8,24},{12,28},{16,0},{20,4},{24,8},{28,12},{1,17},{... | collective-permute-start | bytes 786440 | tf_op jit(solution)/shard_map/ppermute | solution.py:284
  99.1 45.9 %collective-permute-start.25 = (bf16[1,1024,128]{2,1,0:T(8,128)(2,1)}, bf16[1,1024,128]{2,1,0:T(8,128)(2,1)S(1)}, u32[]{:S(2)}, u32[]{:S(2)}) collective-permute-start(bf16[1,1024,128]{2,1,0:T(8,128)(2,1)} %get-tuple-element.198), channel_id=1, source_target_pairs={{0,20},{4,16},{8,28},{12,24},{16,4},{20,0},{24,12},{28,8},{1,21},{... | collective-permute-start | bytes 786440 | tf_op jit(solution)/shard_map/ppermute | solution.py:284
  102.9 23.6 %collective-permute-start.18 = (bf16[512,128]{1,0:T(8,128)(2,1)S(1)}, bf16[512,128]{1,0:T(8,128)(2,1)S(1)}, u32[]{:S(2)}, u32[]{:S(2)}) collective-permute-start(bf16[512,128]{1,0:T(8,128)(2,1)S(1)} %get-tuple-element.188), channel_id=1, source_target_pairs={{0,4},{4,0},{8,12},{12,8},{16,20},{20,16},{24,28},{28,24},{1,5},{5... | collective-permute-start | bytes 393224 | tf_op jit(solution)/shard_map/ppermute | solution.py:284
  120.5 10.6 %collective-permute-start.19 = (bf16[512,128]{1,0:T(8,128)(2,1)S(1)}, bf16[512,128]{1,0:T(8,128)(2,1)S(1)}, u32[]{:S(2)}, u32[]{:S(2)}) collective-permute-start(bf16[512,128]{1,0:T(8,128)(2,1)S(1)} %get-tuple-element.189), channel_id=1, source_target_pairs={{0,8},{4,12},{8,0},{12,4},{16,24},{20,28},{24,16},{28,20},{1,9},{5... | collective-permute-start | bytes 393224 | tf_op jit(solution)/shard_map/ppermute | solution.py:284
  120.5 21.9 %collective-permute-start.20 = (bf16[512,128]{1,0:T(8,128)(2,1)S(1)}, bf16[512,128]{1,0:T(8,128)(2,1)S(1)}, u32[]{:S(2)}, u32[]{:S(2)}) collective-permute-start(bf16[512,128]{1,0:T(8,128)(2,1)S(1)} %get-tuple-element.190), channel_id=1, source_target_pairs={{0,12},{4,8},{8,4},{12,0},{16,28},{20,24},{24,20},{28,16},{1,13},{... | collective-permute-start | bytes 393224 | tf_op jit(solution)/shard_map/ppermute | solution.py:284
  126.6 38.6 %collective-permute-start.26 = (bf16[1,1024,128]{2,1,0:T(8,128)(2,1)}, bf16[1,1024,128]{2,1,0:T(8,128)(2,1)S(1)}, u32[]{:S(2)}, u32[]{:S(2)}) collective-permute-start(bf16[1,1024,128]{2,1,0:T(8,128)(2,1)} %get-tuple-element.205), channel_id=1, source_target_pairs={{0,24},{4,28},{8,16},{12,20},{16,8},{20,12},{24,0},{28,4},{1,25},{... | collective-permute-start | bytes 786440 | tf_op jit(solution)/shard_map/ppermute | solution.py:284
  142.3 22.8 %collective-permute-start.21 = (bf16[1,1024,128]{2,1,0:T(8,128)(2,1)S(1)}, bf16[1,1024,128]{2,1,0:T(8,128)(2,1)S(1)}, u32[]{:S(2)}, u32[]{:S(2)}) collective-permute-start(bf16[1,1024,128]{2,1,0:T(8,128)(2,1)S(1)} %copy-done.27), channel_id=1, source_target_pairs={{0,4},{4,0},{8,12},{12,8},{16,20},{20,16},{24,28},{28,24},{1,5},{5... | collective-permute-start | bytes 786440 | tf_op jit(solution)/shard_map/ppermute | solution.py:284
  142.4 22.8 %collective-permute-start.22 = (bf16[1,1024,128]{2,1,0:T(8,128)(2,1)S(1)}, bf16[1,1024,128]{2,1,0:T(8,128)(2,1)S(1)}, u32[]{:S(2)}, u32[]{:S(2)}) collective-permute-start(bf16[1,1024,128]{2,1,0:T(8,128)(2,1)S(1)} %copy-done.26), channel_id=1, source_target_pairs={{0,8},{4,12},{8,0},{12,4},{16,24},{20,28},{24,16},{28,20},{1,9},{5... | collective-permute-start | bytes 786440 | tf_op jit(solution)/shard_map/ppermute | solution.py:284
  142.5 22.7 %collective-permute-start.23 = (bf16[1,1024,128]{2,1,0:T(8,128)(2,1)S(1)}, bf16[1,1024,128]{2,1,0:T(8,128)(2,1)S(1)}, u32[]{:S(2)}, u32[]{:S(2)}) collective-permute-start(bf16[1,1024,128]{2,1,0:T(8,128)(2,1)S(1)} %copy-done.25), channel_id=1, source_target_pairs={{0,12},{4,8},{8,4},{12,0},{16,28},{20,24},{24,20},{28,16},{1,13},{... | collective-permute-start | bytes 786440 | tf_op jit(solution)/shard_map/ppermute | solution.py:284
  145.0 20.2 %collective-permute-start.27 = (bf16[1,1024,128]{2,1,0:T(8,128)(2,1)S(1)}, bf16[1,1024,128]{2,1,0:T(8,128)(2,1)S(1)}, u32[]{:S(2)}, u32[]{:S(2)}) collective-permute-start(bf16[1,1024,128]{2,1,0:T(8,128)(2,1)S(1)} %copy-done.24), channel_id=1, source_target_pairs={{0,28},{4,24},{8,20},{12,16},{16,12},{20,8},{24,4},{28,0},{1,29},{... | collective-permute-start | bytes 786440 | tf_op jit(solution)/shard_map/ppermute | solution.py:284
  (32 other events, 435.5 us)

commit v8 on v5

--- a/solution.py
+++ b/solution.py
@@ -568,21 +568,22 @@
         specs=[SMEM] + [VMEM] * 4, scratch=[held_tails], name="ssm_first",
     )
     tails = [pass_block(block, n) for n, block in enumerate(sent)]
+    total = carry_total(False, *tails)
+    start = cross(total, False)
     if dealt:
         marks = doc_start.reshape(length // 128, 128)
         marks = jnp.stack([marks // 128, marks % 128], axis=1).reshape(length // 64, 128)
         marks = jnp.pad(marks, ((0, TAIL - length // 64), (0, 0))).astype(BF16)
-        marks, tails = lax.optimization_barrier((marks, tails))
+        marks, total = lax.optimization_barrier((marks, total))
         packed = call(
             pack_kernel, [shape((per, 4 * length + TAIL, 128), BF16)] * parts,
             me, marks, att_queries, att_keys, att_values, att_grad,
             specs=[SMEM] + [VMEM] * 5, vmem=SMALL, name="att_pack",
         )
+        packed, start = lax.optimization_barrier((packed, start))
         att_got = {n: pass_block(block, n) for n, block in enumerate(packed)}
     else:
         att_out = ring_attention(att_queries, att_keys, att_values, att_grad, doc_start)
-    total = carry_total(False, *tails)
-    start = cross(total, False)
     state = [
         pass_block(block, n) for n, block in enumerate(carry_states(False, start, *tails))
     ]
@@ -607,6 +608,13 @@
         done, sent = lax.optimization_barrier(([att_got[n] for n in rest], sent))
         att_got.update(zip(rest, done))
     blocks = [pass_block(block, n) for n, block in enumerate(sent)]
+    gin, read_part, write_part = call(
+        inner_kernel,
+        (shape((length, width), F32), shape((length, 128), F32), shape((length, 128), F32)),
+        me, dmixed, ssm_input, write_map, read_map, starts, lcol, lrow, state,
+        specs=[SMEM] + [VMEM] * 8, name="ssm_inner",
+    )
+    blocks, gin = lax.optimization_barrier((blocks, gin))
     total = carry_total(True, *tails, *blocks)
     start = cross(total, True)
     if dealt:
@@ -627,20 +635,14 @@
             flops=6 * per * (parts * length) ** 2 * ATT_DIM, name="att_attend",
         )
         start, att_done = lax.optimization_barrier((start, att_done))
-    back = [
-        pass_block(block, n) for n, block in enumerate(carry_states(True, start, *tails, *blocks))
-    ]
-    gin, read_part, write_part = call(
-        inner_kernel,
-        (shape((length, width), F32), shape((length, 128), F32), shape((length, 128), F32)),
-        me, dmixed, ssm_input, write_map, read_map, starts, lcol, lrow, state,
-        specs=[SMEM] + [VMEM] * 8, name="ssm_inner",
-    )
+    carried = carry_states(True, start, *tails, *blocks)
+    back = [pass_block(block, n) for n, block in enumerate(carried)]
     if dealt:
-        att_back = {shares: pass_block(att_done[shares], shares)}
-        held, back, gin = lax.optimization_barrier((att_done, back, gin))
-        for n in [n for n in range(parts)[::-1] if n != shares]:
-            att_back[n] = pass_block(held[n], n)
+        held, carried = lax.optimization_barrier((att_done, carried))
+        att_back = {n: pass_block(held[n], n) for n in (0, shares)}
+        held, back = lax.optimization_barrier((att_done, back))
+        late = [*range(shares + 1, parts), *range(1, shares)]
+        att_back.update((n, pass_block(held[n], n)) for n in late)
         att_out = call(
             unpack_kernel, (shape((length, att_width), BF16),) * 4,
             me, *[att_back[n] for n in range(parts)],

time: 163 us -> 155 us (0.951)
  the two profiles are of different devices: /device:TPU:1 before, /device:TPU:20 now
where the time goes in v8:
time: 155 us; the launch traced here: 154 us
  starting transfers between devices  56.3 us (36%)
  Pallas kernels  41.9 us (27%)
  waiting for transfers between devices  28.5 us (18%)
  blocking collectives  21.6 us (14%)
  local copies, waits for them, and re-layouts  4.36 us (3%)
    ppermute x26, starting transfers between devices, pass_block(): lax.ppermute(block, 'ctx', [(i, i ^ n) for i in range(lax.axis_size('ctx'...  52.6 us
    pallas_call x12, Pallas kernels, call(): pl.pallas_call(kernel, out_shape=out_shape, in_specs=specs or [VMEM] * le...  41.9 us
    ppermute x26, waiting for transfers between devices, pass_block(): lax.ppermute(block, 'ctx', [(i, i ^ n) for i in range(lax.axis_size('ctx'...  24.6 us
    psum x1, blocking collectives, body(): write_sum, read_sum = lax.psum((write_part, read_part), 'head')  15 us
    psum x1, blocking collectives, body(): sums = lax.psum(sums, 'head')  6.65 us
    unnamed x44, local copies, waits for them, and re-layouts  4.36 us
    ppermute x2, waiting for transfers between devices, cross(): return lax.ppermute(total, 'ctx', pairs)  3.85 us
    ppermute x2, starting transfers between devices, cross(): return lax.ppermute(total, 'ctx', pairs)  3.75 us
  transfers between devices with their start and end apart: 28, of which 13 were waited for; matrix products, arithmetic and copies ran while one was open for 0% of the time, Pallas kernels for 24%

profile of v8, /device:TPU:20, one launch (start us, length us, event | category | flops | bytes accessed | tf_op | source)
XLA Modules:
  0.0 154.3 jit_solution(10891075137484062688)
XLA Ops:
  0.7 3.1 %ssm_first.1 = (f32[256,16]{1,0:T(8,128)}, f32[16,256]{1,0:T(8,128)}, bf16[528,128]{1,0:T(8,128)(2,1)}, bf16[528,128]{1,0:T(8,128)(2,1)}, bf16[528,128]{1,0:T(8,128)(2,1)}, /*index=5*/bf16[528,128]{1,0:T(8,128)(2,1)}) custom-call(s32[1]{0:T(128)} %bitcast.refs_0_.me_ref, f32[16,256]{1,0:T(8,128)} %bitcast.11, s32[1,256]{1,0:T(1,128)} %bitcast.5, ...), custom_call_target="tpu_custom_call" | custom-call | bytes 1704964 | tf_op jit(solution)/shard_map/ssm_first/pallas_call | solution.py:28
  9.3 2.7 %collective-permute-done.1.refs_3_.refs_4_ = bf16[528,128]{1,0:T(8,128)(2,1)S(1)} collective-permute-done((bf16[528,128]{1,0:T(8,128)(2,1)}, bf16[528,128]{1,0:T(8,128)(2,1)S(1)}, u32[]{:S(2)}, u32[]{:S(2)}) %collective-permute-start.1) | collective-permute-done | bytes 135200 | tf_op jit(solution)/shard_map/ppermute | solution.py:284
  18.4 3.9 %collective-permute-done.3.refs_1_ = bf16[512,128]{1,0:T(8,128)(2,1)S(1)} collective-permute-done((bf16[512,128]{1,0:T(8,128)(2,1)S(1)}, bf16[512,128]{1,0:T(8,128)(2,1)S(1)}, u32[]{:S(2)}, u32[]{:S(2)}) %collective-permute-start.3) | collective-permute-done | bytes 131104 | tf_op jit(solution)/shard_map/ppermute | solution.py:291
  25.2 9.0 %collective-permute-start.6 = (bf16[512,128]{1,0:T(8,128)(2,1)S(1)}, bf16[512,128]{1,0:T(8,128)(2,1)S(1)}, u32[]{:S(2)}, u32[]{:S(2)}) collective-permute-start(bf16[512,128]{1,0:T(8,128)(2,1)S(1)} %get-tuple-element.135), channel_id=1, source_target_pairs={{0,8},{4,12},{8,0},{12,4},{16,24},{20,28},{24,16},{28,20},{1,9},{5... | collective-permute-start | bytes 393224 | tf_op jit(solution)/shard_map/ppermute | solution.py:284
  35.4 5.9 %collective-permute-start.9 = (bf16[1,1040,128]{2,1,0:T(8,128)(2,1)S(1)}, bf16[1,1040,128]{2,1,0:T(8,128)(2,1)S(1)}, u32[]{:S(2)}, u32[]{:S(2)}) collective-permute-start(bf16[1,1040,128]{2,1,0:T(8,128)(2,1)S(1)} %get-tuple-element.145), channel_id=1, source_target_pairs={{0,8},{4,12},{8,0},{12,4},{16,24},{20,28},{24,16},{28,20},{1,9},{5... | collective-permute-start | bytes 798728 | tf_op jit(solution)/shard_map/ppermute | solution.py:284
  41.9 3.8 %collective-permute-start.10 = (bf16[1,1040,128]{2,1,0:T(8,128)(2,1)S(1)}, bf16[1,1040,128]{2,1,0:T(8,128)(2,1)S(1)}, u32[]{:S(2)}, u32[]{:S(2)}) collective-permute-start(bf16[1,1040,128]{2,1,0:T(8,128)(2,1)S(1)} %get-tuple-element.146), channel_id=1, source_target_pairs={{0,12},{4,8},{8,4},{12,0},{16,28},{20,24},{24,20},{28,16},{1,13},{... | collective-permute-start | bytes 798728 | tf_op jit(solution)/shard_map/ppermute | solution.py:284
  45.9 6.7 %collective-permute-start.11 = (bf16[1,1040,128]{2,1,0:T(8,128)(2,1)S(1)}, bf16[1,1040,128]{2,1,0:T(8,128)(2,1)}, u32[]{:S(2)}, u32[]{:S(2)}) collective-permute-start(bf16[1,1040,128]{2,1,0:T(8,128)(2,1)S(1)} %get-tuple-element.147), channel_id=1, source_target_pairs={{0,20},{4,16},{8,28},{12,24},{16,4},{20,0},{24,12},{28,8},{1,21},{... | collective-permute-start | bytes 798728 | tf_op jit(solution)/shard_map/ppermute | solution.py:284
  53.2 2.4 %collective-permute-start.17 = (bf16[1,1040,128]{2,1,0:T(8,128)(2,1)S(1)}, bf16[1,1040,128]{2,1,0:T(8,128)(2,1)}, u32[]{:S(2)}, u32[]{:S(2)}) collective-permute-start(bf16[1,1040,128]{2,1,0:T(8,128)(2,1)S(1)} %get-tuple-element.171), channel_id=1, source_target_pairs={{0,28},{4,24},{8,20},{12,16},{16,12},{20,8},{24,4},{28,0},{1,29},{... | collective-permute-start | bytes 798728 | tf_op jit(solution)/shard_map/ppermute | solution.py:284
  55.6 6.0 %ssm_mix.1 = (f32[256,2048]{1,0:T(8,128)}, f32[8,256]{1,0:T(8,128)}, bf16[2048,128]{1,0:T(8,128)(2,1)}) custom-call(s32[1]{0:T(128)} %bitcast.refs_0_.me_ref, bf16[256,2048]{1,0:T(8,128)(2,1)} %refs_2_.3, bf16[256,2048]{1,0:T(8,128)(2,1)} %refs_3_.6, bf16[256,2048]{1,0:T(8,128)(2,1)} %refs_4_.5, bf16[256,128]{1,0:T(8,128)(2,1)} %refs_3_.7, ...), custom_call_target="tpu_custom_call" | custom-call | bytes 6464516 | tf_op jit(solution)/shard_map/ssm_mix/pallas_call | solution.py:28
  61.5 6.7 %psum.21.refs_1_ = f32[8,256]{1,0:T(8,128)} all-reduce(f32[8,256]{1,0:T(8,128)} %get-tuple-element.141), channel_id=1, replica_groups=mesh['ctx'=8,'head'=4] {'head'}, use_global_device_ids=true, to_apply=%region_0.1 | all-reduce | flops 2048 | bytes 16384 | tf_op jit(solution)/shard_map/psum | solution.py:598
  68.2 5.9 %ssm_gate.1 = (bf16[256,2048]{1,0:T(8,128)(2,1)}, bf16[256,2048]{1,0:T(8,128)(2,1)}, bf16[256,2048]{1,0:T(8,128)(2,1)}, bf16[512,128]{1,0:T(8,128)(2,1)}, bf16[5...) custom-call(s32[1]{0:T(128)} %bitcast.refs_0_.me_ref, f32[8,256]{1,0:T(8,128)} %psum.21.refs_1_, ...), custom_call_target="tpu_custom_call" | custom-call | bytes 7955460 | tf_op jit(solution)/shard_map/ssm_gate/pallas_call | solution.py:28
  75.0 3.3 %collective-permute-start.14 = (bf16[512,128]{1,0:T(8,128)(2,1)}, bf16[512,128]{1,0:T(8,128)(2,1)S(1)}, u32[]{:S(2)}, u32[]{:S(2)}) collective-permute-start(bf16[512,128]{1,0:T(8,128)(2,1)} %get-tuple-element.155), channel_id=1, source_target_pairs={{0,8},{4,12},{8,0},{12,4},{16,24},{20,28},{24,16},{28,20},{1,9},{5... | collective-permute-start | bytes 393224 | tf_op jit(solution)/shard_map/ppermute | solution.py:284
  79.6 4.9 %ssm_inner.1 = (f32[256,2048]{1,0:T(8,128)}, f32[256,128]{1,0:T(8,128)}, f32[256,128]{1,0:T(8,128)}) custom-call(s32[1]{0:T(128)} %bitcast.refs_0_.me_ref, bf16[256,2048]{1,0:T(8,128)(2,1)} %get-tuple-element.157.dmixed_ref, bf16[256,2048]{1,0:T(8,128)(2,1)} %refs_2_.3, bf16[256,128]{1,0:T(8,128)(2,1)} %refs_3_.7, bf16[256,128]{1,0:T(8,128)(2,1)} %r_ref.1, ...), custom_call_target="tpu_custom_call" | custom-call | bytes 5145604 | tf_op jit(solution)/shard_map/ssm_inner/pallas_call | solution.py:28
  85.6 2.5 %collective-permute-start.16 = (bf16[512,128]{1,0:T(8,128)(2,1)S(1)}, bf16[512,128]{1,0:T(8,128)(2,1)S(1)}, u32[]{:S(2)}, u32[]{:S(2)}) collective-permute-start(bf16[512,128]{1,0:T(8,128)(2,1)S(1)} %ssm_total.3), channel_id=1, source_target_pairs={{16,0},{20,4},{24,8},{28,12},{17,1},{21,5},{25,9},{29,13},{18,2},{... | collective-permute-start | bytes 393224 | tf_op jit(solution)/shard_map/ppermute | solution.py:291
  88.1 14.7 %att_attend.1 = (bf16[1,1024,128]{2,1,0:T(8,128)(2,1)}, bf16[1,1024,128]{2,1,0:T(8,128)(2,1)}, bf16[1,1024,128]{2,1,0:T(8,128)(2,1)}, bf16[1,1024,128]{2,1,0:T(8...) custom-call(s32[1]{0:T(128)} %bitcast.refs_0_.me_ref, ...), custom_call_target="tpu_custom_call" | custom-call | flops 3221225472 | bytes 4227076 | tf_op jit(solution)/shard_map/att_attend/pallas_call | solution.py:28
  104.8 2.4 %collective-permute-start.20 = (bf16[512,128]{1,0:T(8,128)(2,1)S(1)}, bf16[512,128]{1,0:T(8,128)(2,1)S(1)}, u32[]{:S(2)}, u32[]{:S(2)}) collective-permute-start(bf16[512,128]{1,0:T(8,128)(2,1)S(1)} %get-tuple-element.200), channel_id=1, source_target_pairs={{0,12},{4,8},{8,4},{12,0},{16,28},{20,24},{24,20},{28,16},{1,13},{... | collective-permute-start | bytes 393224 | tf_op jit(solution)/shard_map/ppermute | solution.py:284
  110.7 3.7 %collective-permute-done.20.refs_10_ = bf16[512,128]{1,0:T(8,128)(2,1)S(1)} collective-permute-done((bf16[512,128]{1,0:T(8,128)(2,1)S(1)}, bf16[512,128]{1,0:T(8,128)(2,1)S(1)}, u32[]{:S(2)}, u32[]{:S(2)}) %collective-permute-start.20) | collective-permute-done | bytes 131104 | tf_op jit(solution)/shard_map/ppermute | solution.py:284
  115.2 2.7 %collective-permute-start.23 = (bf16[1,1024,128]{2,1,0:T(8,128)(2,1)}, bf16[1,1024,128]{2,1,0:T(8,128)(2,1)S(1)}, u32[]{:S(2)}, u32[]{:S(2)}) collective-permute-start(bf16[1,1024,128]{2,1,0:T(8,128)(2,1)} %get-tuple-element.204), channel_id=1, source_target_pairs={{0,12},{4,8},{8,4},{12,0},{16,28},{20,24},{24,20},{28,16},{1,13},{... | collective-permute-start | bytes 786440 | tf_op jit(solution)/shard_map/ppermute | solution.py:284
  117.9 5.0 %collective-permute-start.25 = (bf16[1,1024,128]{2,1,0:T(8,128)(2,1)}, bf16[1,1024,128]{2,1,0:T(8,128)(2,1)S(1)}, u32[]{:S(2)}, u32[]{:S(2)}) collective-permute-start(bf16[1,1024,128]{2,1,0:T(8,128)(2,1)} %get-tuple-element.206), channel_id=1, source_target_pairs={{0,20},{4,16},{8,28},{12,24},{16,4},{20,0},{24,12},{28,8},{1,21},{... | collective-permute-start | bytes 786440 | tf_op jit(solution)/shard_map/ppermute | solution.py:284
  123.0 4.6 %collective-permute-done.21.refs_1_ = bf16[1,1024,128]{2,1,0:T(8,128)(2,1)S(1)} collective-permute-done((bf16[1,1024,128]{2,1,0:T(8,128)(2,1)}, bf16[1,1024,128]{2,1,0:T(8,128)(2,1)S(1)}, u32[]{:S(2)}, u32[]{:S(2)}) %collective-permute-start.21) | collective-permute-done | bytes 262176 | tf_op jit(solution)/shard_map/ppermute | solution.py:284
  127.6 4.2 %ssm_last.1 = (bf16[256,2048]{1,0:T(8,128)(2,1)}, f32[256,128]{1,0:T(8,128)}) custom-call(s32[1]{0:T(128)} %bitcast.refs_0_.me_ref, f32[256,2048]{1,0:T(8,128)} %get-tuple-element.210.refs_1_, bf16[256,2048]{1,0:T(8,128)(2,1)} %refs_2_.3, bf16[256,128]{1,0:T(8,128)(2,1)} %refs_3_.7, s32[1,256]{1,0:T(1,128)} %bitcast.10, ...), custom_call_target="tpu_custom_call" | custom-call | bytes 5063684 | tf_op jit(solution)/shard_map/ssm_last/pallas_call | solution.py:28
  131.8 15.0 %all-reduce.3 = (bf16[256,128]{1,0:T(8,128)(2,1)}, bf16[256,128]{1,0:T(8,128)(2,1)}) all-reduce(f32[256,128]{1,0:T(8,128)} %get-tuple-element.218, f32[256,128]{1,0:T(8,128)S(1)} %copy-done.17), channel_id=1, replica_groups=mesh['ctx'=8,'head'=4] {'head'}, use_global_device_ids=true, to_apply=%region_1.2 | all-reduce | flops 65536 | bytes 393216 | tf_op jit(solution)/shard_map/psum | solution.py:659
  146.8 2.8 %collective-permute-done.26.refs_6_ = bf16[1,1024,128]{2,1,0:T(8,128)(2,1)S(1)} collective-permute-done((bf16[1,1024,128]{2,1,0:T(8,128)(2,1)}, bf16[1,1024,128]{2,1,0:T(8,128)(2,1)S(1)}, u32[]{:S(2)}, u32[]{:S(2)}) %collective-permute-start.26) | collective-permute-done | bytes 262176 | tf_op jit(solution)/shard_map/ppermute | solution.py:284
  149.6 2.8 %collective-permute-done.27.refs_7_ = bf16[1,1024,128]{2,1,0:T(8,128)(2,1)S(1)} collective-permute-done((bf16[1,1024,128]{2,1,0:T(8,128)(2,1)}, bf16[1,1024,128]{2,1,0:T(8,128)(2,1)S(1)}, u32[]{:S(2)}, u32[]{:S(2)}) %collective-permute-start.27) | collective-permute-done | bytes 262176 | tf_op jit(solution)/shard_map/ppermute | solution.py:284
  (94 shorter events, 29.1 us)
Async XLA Ops:
  5.3 6.7 %collective-permute-start.1 = (bf16[528,128]{1,0:T(8,128)(2,1)}, bf16[528,128]{1,0:T(8,128)(2,1)S(1)}, u32[]{:S(2)}, u32[]{:S(2)}) collective-permute-start(bf16[528,128]{1,0:T(8,128)(2,1)} %get-tuple-element.120), channel_id=1, source_target_pairs={{0,8},{4,12},{8,0},{12,4},{16,24},{20,28},{24,16},{28,20},{1,9},{5... | collective-permute-start | bytes 405512 | tf_op jit(solution)/shard_map/ppermute | solution.py:284
  14.4 7.9 %collective-permute-start.3 = (bf16[512,128]{1,0:T(8,128)(2,1)S(1)}, bf16[512,128]{1,0:T(8,128)(2,1)S(1)}, u32[]{:S(2)}, u32[]{:S(2)}) collective-permute-start(bf16[512,128]{1,0:T(8,128)(2,1)S(1)} %ssm_total.2), channel_id=1, source_target_pairs={{0,16},{4,20},{8,24},{12,28},{1,17},{5,21},{9,25},{13,29},{2,18},{... | collective-permute-start | bytes 393224 | tf_op jit(solution)/shard_map/ppermute | solution.py:291
  22.3 30.3 %collective-permute-start.4 = (bf16[1,1040,128]{2,1,0:T(8,128)(2,1)S(1)}, bf16[1,1040,128]{2,1,0:T(8,128)(2,1)S(1)}, u32[]{:S(2)}, u32[]{:S(2)}) collective-permute-start(bf16[1,1040,128]{2,1,0:T(8,128)(2,1)S(1)} %get-tuple-element.131), channel_id=1, source_target_pairs={{0,16},{4,20},{8,24},{12,28},{16,0},{20,4},{24,8},{28,12},{1,17},{... | collective-permute-start | bytes 798728 | tf_op jit(solution)/shard_map/ppermute | solution.py:284
  22.3 30.9 %collective-permute-start.8 = (bf16[1,1040,128]{2,1,0:T(8,128)(2,1)S(1)}, bf16[1,1040,128]{2,1,0:T(8,128)(2,1)S(1)}, u32[]{:S(2)}, u32[]{:S(2)}) collective-permute-start(bf16[1,1040,128]{2,1,0:T(8,128)(2,1)S(1)} %get-tuple-element.144), channel_id=1, source_target_pairs={{0,4},{4,0},{8,12},{12,8},{16,20},{20,16},{24,28},{28,24},{1,5},{5... | collective-permute-start | bytes 798728 | tf_op jit(solution)/shard_map/ppermute | solution.py:284
  24.7 10.8 %collective-permute-start.5 = (bf16[512,128]{1,0:T(8,128)(2,1)S(1)}, bf16[512,128]{1,0:T(8,128)(2,1)S(1)}, u32[]{:S(2)}, u32[]{:S(2)}) collective-permute-start(bf16[512,128]{1,0:T(8,128)(2,1)S(1)} %get-tuple-element.134), channel_id=1, source_target_pairs={{0,4},{4,0},{8,12},{12,8},{16,20},{20,16},{24,28},{28,24},{1,5},{5... | collective-permute-start | bytes 393224 | tf_op jit(solution)/shard_map/ppermute | solution.py:284
  25.2 16.7 %collective-permute-start.6 = (bf16[512,128]{1,0:T(8,128)(2,1)S(1)}, bf16[512,128]{1,0:T(8,128)(2,1)S(1)}, u32[]{:S(2)}, u32[]{:S(2)}) collective-permute-start(bf16[512,128]{1,0:T(8,128)(2,1)S(1)} %get-tuple-element.135), channel_id=1, source_target_pairs={{0,8},{4,12},{8,0},{12,4},{16,24},{20,28},{24,16},{28,20},{1,9},{5... | collective-permute-start | bytes 393224 | tf_op jit(solution)/shard_map/ppermute | solution.py:284
  34.2 11.8 %collective-permute-start.7 = (bf16[512,128]{1,0:T(8,128)(2,1)S(1)}, bf16[512,128]{1,0:T(8,128)(2,1)S(1)}, u32[]{:S(2)}, u32[]{:S(2)}) collective-permute-start(bf16[512,128]{1,0:T(8,128)(2,1)S(1)} %get-tuple-element.136), channel_id=1, source_target_pairs={{0,12},{4,8},{8,4},{12,0},{16,28},{20,24},{24,20},{28,16},{1,13},{... | collective-permute-start | bytes 393224 | tf_op jit(solution)/shard_map/ppermute | solution.py:284
  35.4 38.6 %collective-permute-start.9 = (bf16[1,1040,128]{2,1,0:T(8,128)(2,1)S(1)}, bf16[1,1040,128]{2,1,0:T(8,128)(2,1)S(1)}, u32[]{:S(2)}, u32[]{:S(2)}) collective-permute-start(bf16[1,1040,128]{2,1,0:T(8,128)(2,1)S(1)} %get-tuple-element.145), channel_id=1, source_target_pairs={{0,8},{4,12},{8,0},{12,4},{16,24},{20,28},{24,16},{28,20},{1,9},{5... | collective-permute-start | bytes 798728 | tf_op jit(solution)/shard_map/ppermute | solution.py:284
  41.9 32.2 %collective-permute-start.10 = (bf16[1,1040,128]{2,1,0:T(8,128)(2,1)S(1)}, bf16[1,1040,128]{2,1,0:T(8,128)(2,1)S(1)}, u32[]{:S(2)}, u32[]{:S(2)}) collective-permute-start(bf16[1,1040,128]{2,1,0:T(8,128)(2,1)S(1)} %get-tuple-element.146), channel_id=1, source_target_pairs={{0,12},{4,8},{8,4},{12,0},{16,28},{20,24},{24,20},{28,16},{1,13},{... | collective-permute-start | bytes 798728 | tf_op jit(solution)/shard_map/ppermute | solution.py:284
  45.9 28.2 %collective-permute-start.11 = (bf16[1,1040,128]{2,1,0:T(8,128)(2,1)S(1)}, bf16[1,1040,128]{2,1,0:T(8,128)(2,1)}, u32[]{:S(2)}, u32[]{:S(2)}) collective-permute-start(bf16[1,1040,128]{2,1,0:T(8,128)(2,1)S(1)} %get-tuple-element.147), channel_id=1, source_target_pairs={{0,20},{4,16},{8,28},{12,24},{16,4},{20,0},{24,12},{28,8},{1,21},{... | collective-permute-start | bytes 798728 | tf_op jit(solution)/shard_map/ppermute | solution.py:284
  52.6 21.5 %collective-permute-start.12 = (bf16[1,1040,128]{2,1,0:T(8,128)(2,1)S(1)}, bf16[1,1040,128]{2,1,0:T(8,128)(2,1)}, u32[]{:S(2)}, u32[]{:S(2)}) collective-permute-start(bf16[1,1040,128]{2,1,0:T(8,128)(2,1)S(1)} %get-tuple-element.148), channel_id=1, source_target_pairs={{0,24},{4,28},{8,16},{12,20},{16,8},{20,12},{24,0},{28,4},{1,25},{... | collective-permute-start | bytes 798728 | tf_op jit(solution)/shard_map/ppermute | solution.py:284
  53.2 34.9 %collective-permute-start.17 = (bf16[1,1040,128]{2,1,0:T(8,128)(2,1)S(1)}, bf16[1,1040,128]{2,1,0:T(8,128)(2,1)}, u32[]{:S(2)}, u32[]{:S(2)}) collective-permute-start(bf16[1,1040,128]{2,1,0:T(8,128)(2,1)S(1)} %get-tuple-element.171), channel_id=1, source_target_pairs={{0,28},{4,24},{8,20},{12,16},{16,12},{20,8},{24,4},{28,0},{1,29},{... | collective-permute-start | bytes 798728 | tf_op jit(solution)/shard_map/ppermute | solution.py:284
  74.1 10.4 %collective-permute-start.13 = (bf16[512,128]{1,0:T(8,128)(2,1)}, bf16[512,128]{1,0:T(8,128)(2,1)S(1)}, u32[]{:S(2)}, u32[]{:S(2)}) collective-permute-start(bf16[512,128]{1,0:T(8,128)(2,1)} %get-tuple-element.154), channel_id=1, source_target_pairs={{0,4},{4,0},{8,12},{12,8},{16,20},{20,16},{24,28},{28,24},{1,5},{5... | collective-permute-start | bytes 393224 | tf_op jit(solution)/shard_map/ppermute | solution.py:284
  75.0 9.6 %collective-permute-start.14 = (bf16[512,128]{1,0:T(8,128)(2,1)}, bf16[512,128]{1,0:T(8,128)(2,1)S(1)}, u32[]{:S(2)}, u32[]{:S(2)}) collective-permute-start(bf16[512,128]{1,0:T(8,128)(2,1)} %get-tuple-element.155), channel_id=1, source_target_pairs={{0,8},{4,12},{8,0},{12,4},{16,24},{20,28},{24,16},{28,20},{1,9},{5... | collective-permute-start | bytes 393224 | tf_op jit(solution)/shard_map/ppermute | solution.py:284
  78.2 7.2 %collective-permute-start.15 = (bf16[512,128]{1,0:T(8,128)(2,1)}, bf16[512,128]{1,0:T(8,128)(2,1)S(1)}, u32[]{:S(2)}, u32[]{:S(2)}) collective-permute-start(bf16[512,128]{1,0:T(8,128)(2,1)} %get-tuple-element.156), channel_id=1, source_target_pairs={{0,12},{4,8},{8,4},{12,0},{16,28},{20,24},{24,20},{28,16},{1,13},{... | collective-permute-start | bytes 393224 | tf_op jit(solution)/shard_map/ppermute | solution.py:284
  85.6 17.2 %collective-permute-start.16 = (bf16[512,128]{1,0:T(8,128)(2,1)S(1)}, bf16[512,128]{1,0:T(8,128)(2,1)S(1)}, u32[]{:S(2)}, u32[]{:S(2)}) collective-permute-start(bf16[512,128]{1,0:T(8,128)(2,1)S(1)} %ssm_total.3), channel_id=1, source_target_pairs={{16,0},{20,4},{24,8},{28,12},{17,1},{21,5},{25,9},{29,13},{18,2},{... | collective-permute-start | bytes 393224 | tf_op jit(solution)/shard_map/ppermute | solution.py:291
  104.8 9.6 %collective-permute-start.20 = (bf16[512,128]{1,0:T(8,128)(2,1)S(1)}, bf16[512,128]{1,0:T(8,128)(2,1)S(1)}, u32[]{:S(2)}, u32[]{:S(2)}) collective-permute-start(bf16[512,128]{1,0:T(8,128)(2,1)S(1)} %get-tuple-element.200), channel_id=1, source_target_pairs={{0,12},{4,8},{8,4},{12,0},{16,28},{20,24},{24,20},{28,16},{1,13},{... | collective-permute-start | bytes 393224 | tf_op jit(solution)/shard_map/ppermute | solution.py:284
  107.2 15.8 %collective-permute-start.24 = (bf16[1,1024,128]{2,1,0:T(8,128)(2,1)}, bf16[1,1024,128]{2,1,0:T(8,128)(2,1)S(1)}, u32[]{:S(2)}, u32[]{:S(2)}) collective-permute-start(bf16[1,1024,128]{2,1,0:T(8,128)(2,1)} %get-tuple-element.205), channel_id=1, source_target_pairs={{0,16},{4,20},{8,24},{12,28},{16,0},{20,4},{24,8},{28,12},{1,17},{... | collective-permute-start | bytes 786440 | tf_op jit(solution)/shard_map/ppermute | solution.py:284
  114.4 13.2 %collective-permute-start.21 = (bf16[1,1024,128]{2,1,0:T(8,128)(2,1)}, bf16[1,1024,128]{2,1,0:T(8,128)(2,1)S(1)}, u32[]{:S(2)}, u32[]{:S(2)}) collective-permute-start(bf16[1,1024,128]{2,1,0:T(8,128)(2,1)} %get-tuple-element.202), channel_id=1, source_target_pairs={{0,4},{4,0},{8,12},{12,8},{16,20},{20,16},{24,28},{28,24},{1,5},{5... | collective-permute-start | bytes 786440 | tf_op jit(solution)/shard_map/ppermute | solution.py:284
  115.0 31.8 %collective-permute-start.22 = (bf16[1,1024,128]{2,1,0:T(8,128)(2,1)}, bf16[1,1024,128]{2,1,0:T(8,128)(2,1)S(1)}, u32[]{:S(2)}, u32[]{:S(2)}) collective-permute-start(bf16[1,1024,128]{2,1,0:T(8,128)(2,1)} %get-tuple-element.203), channel_id=1, source_target_pairs={{0,8},{4,12},{8,0},{12,4},{16,24},{20,28},{24,16},{28,20},{1,9},{5... | collective-permute-start | bytes 786440 | tf_op jit(solution)/shard_map/ppermute | solution.py:284
  115.2 31.6 %collective-permute-start.23 = (bf16[1,1024,128]{2,1,0:T(8,128)(2,1)}, bf16[1,1024,128]{2,1,0:T(8,128)(2,1)S(1)}, u32[]{:S(2)}, u32[]{:S(2)}) collective-permute-start(bf16[1,1024,128]{2,1,0:T(8,128)(2,1)} %get-tuple-element.204), channel_id=1, source_target_pairs={{0,12},{4,8},{8,4},{12,0},{16,28},{20,24},{24,20},{28,16},{1,13},{... | collective-permute-start | bytes 786440 | tf_op jit(solution)/shard_map/ppermute | solution.py:284
  117.9 28.9 %collective-permute-start.25 = (bf16[1,1024,128]{2,1,0:T(8,128)(2,1)}, bf16[1,1024,128]{2,1,0:T(8,128)(2,1)S(1)}, u32[]{:S(2)}, u32[]{:S(2)}) collective-permute-start(bf16[1,1024,128]{2,1,0:T(8,128)(2,1)} %get-tuple-element.206), channel_id=1, source_target_pairs={{0,20},{4,16},{8,28},{12,24},{16,4},{20,0},{24,12},{28,8},{1,21},{... | collective-permute-start | bytes 786440 | tf_op jit(solution)/shard_map/ppermute | solution.py:284
  123.0 26.6 %collective-permute-start.26 = (bf16[1,1024,128]{2,1,0:T(8,128)(2,1)}, bf16[1,1024,128]{2,1,0:T(8,128)(2,1)S(1)}, u32[]{:S(2)}, u32[]{:S(2)}) collective-permute-start(bf16[1,1024,128]{2,1,0:T(8,128)(2,1)} %get-tuple-element.207), channel_id=1, source_target_pairs={{0,24},{4,28},{8,16},{12,20},{16,8},{20,12},{24,0},{28,4},{1,25},{... | collective-permute-start | bytes 786440 | tf_op jit(solution)/shard_map/ppermute | solution.py:284
  127.6 24.8 %collective-permute-start.27 = (bf16[1,1024,128]{2,1,0:T(8,128)(2,1)}, bf16[1,1024,128]{2,1,0:T(8,128)(2,1)S(1)}, u32[]{:S(2)}, u32[]{:S(2)}) collective-permute-start(bf16[1,1024,128]{2,1,0:T(8,128)(2,1)} %get-tuple-element.208), channel_id=1, source_target_pairs={{0,28},{4,24},{8,20},{12,16},{16,12},{20,8},{24,4},{28,0},{1,29},{... | collective-permute-start | bytes 786440 | tf_op jit(solution)/shard_map/ppermute | solution.py:284
  (26 other events, 300.0 us)

commit v9 on v8

--- a/solution.py
+++ b/solution.py
@@ -581,7 +581,7 @@
             specs=[SMEM] + [VMEM] * 5, vmem=SMALL, name="att_pack",
         )
         packed, start = lax.optimization_barrier((packed, start))
-        att_got = {n: pass_block(block, n) for n, block in enumerate(packed)}
+        att_got = {n: pass_block(packed[n], n) for n in (0, shares)}
     else:
         att_out = ring_attention(att_queries, att_keys, att_values, att_grad, doc_start)
     state = [
@@ -589,6 +589,10 @@
     ]
     if dealt:
         att_got[shares], state = lax.optimization_barrier((att_got[shares], state))
+    if dealt:
+        packed, att_got[shares], state = lax.optimization_barrier((packed, att_got[shares], state))
+        soon = [*range(shares + 1, parts), 1]
+        att_got.update((n, pass_block(packed[n], n)) for n in soon)
     mixed, sums, state = call(
         lambda *refs: mix_kernel(shares, *refs),
         (shape((length, width), F32), shape((8, length), F32), shape((width, 128), BF16)),
@@ -604,10 +608,13 @@
     )
 
     if dealt:
-        rest = [n for n in range(1, parts - 1) if n != shares]
+        rest = [*range(shares + 1, parts - 1), 1]
         done, sent = lax.optimization_barrier(([att_got[n] for n in rest], sent))
         att_got.update(zip(rest, done))
     blocks = [pass_block(block, n) for n, block in enumerate(sent)]
+    if dealt:
+        packed, blocks = lax.optimization_barrier((packed, blocks))
+        att_got.update((n, pass_block(packed[n], n)) for n in range(2, shares))
     gin, read_part, write_part = call(
         inner_kernel,
         (shape((length, width), F32), shape((length, 128), F32), shape((length, 128), F32)),

time: 155 us -> 162 us (1.045)
  the two profiles are of different devices: /device:TPU:20 before, /device:TPU:1 now
where the time goes in v9:
time: 162 us; the launch traced here: 159 us
  blocking collectives  44.3 us (27%)
  starting transfers between devices  42 us (26%)
  Pallas kernels  41.9 us (26%)
  waiting for transfers between devices  23.9 us (15%)
  local copies, waits for them, and re-layouts  5.06 us (3%)
    pallas_call x12, Pallas kernels, call(): pl.pallas_call(kernel, out_shape=out_shape, in_specs=specs or [VMEM] * le...  41.9 us
    ppermute x26, starting transfers between devices, pass_block(): lax.ppermute(block, 'ctx', [(i, i ^ n) for i in range(lax.axis_size('ctx'...  36 us
    psum x1, blocking collectives, body(): write_sum, read_sum = lax.psum((write_part, read_part), 'head')  26.8 us
    ppermute x26, waiting for transfers between devices, pass_block(): lax.ppermute(block, 'ctx', [(i, i ^ n) for i in range(lax.axis_size('ctx'...  23.9 us
    psum x1, blocking collectives, body(): sums = lax.psum(sums, 'head')  17.5 us
    ppermute x2, starting transfers between devices, cross(): return lax.ppermute(total, 'ctx', pairs)  6.02 us
    unnamed x48, local copies, waits for them, and re-layouts  5.06 us
  transfers between devices with their start and end apart: 28, of which 12 were waited for; matrix products, arithmetic and copies ran while one was open for 0% of the time, Pallas kernels for 23%

profile of v9, /device:TPU:1, one launch (start us, length us, event | category | flops | bytes accessed | tf_op | source)
XLA Modules:
  0.0 159.0 jit_solution(699937973030577783)
XLA Ops:
  0.7 3.1 %ssm_first.1 = (f32[256,16]{1,0:T(8,128)}, f32[16,256]{1,0:T(8,128)}, bf16[528,128]{1,0:T(8,128)(2,1)}, bf16[528,128]{1,0:T(8,128)(2,1)}, bf16[528,128]{1,0:T(8,128)(2,1)}, /*index=5*/bf16[528,128]{1,0:T(8,128)(2,1)}) custom-call(s32[1]{0:T(128)} %bitcast.refs_0_.me_ref, f32[16,256]{1,0:T(8,128)} %bitcast.11, s32[1,256]{1,0:T(1,128)} %bitcast.5, ...), custom_call_target="tpu_custom_call" | custom-call | bytes 1704964 | tf_op jit(solution)/shard_map/ssm_first/pallas_call | solution.py:28
  3.8 2.0 %collective-permute-start = (bf16[528,128]{1,0:T(8,128)(2,1)}, bf16[528,128]{1,0:T(8,128)(2,1)S(1)}, u32[]{:S(2)}, u32[]{:S(2)}) collective-permute-start(bf16[528,128]{1,0:T(8,128)(2,1)} %get-tuple-element.134), channel_id=1, source_target_pairs={{0,4},{4,0},{8,12},{12,8},{16,20},{20,16},{24,28},{28,24},{1,5},{5... | collective-permute-start | bytes 405512 | tf_op jit(solution)/shard_map/ppermute | solution.py:284
  10.2 2.9 %collective-permute-done.2.refs_4_.refs_5_ = bf16[528,128]{1,0:T(8,128)(2,1)S(1)} collective-permute-done((bf16[528,128]{1,0:T(8,128)(2,1)}, bf16[528,128]{1,0:T(8,128)(2,1)S(1)}, u32[]{:S(2)}, u32[]{:S(2)}) %collective-permute-start.2) | collective-permute-done | bytes 135200 | tf_op jit(solution)/shard_map/ppermute | solution.py:284
  14.1 4.6 %collective-permute-start.3 = (bf16[512,128]{1,0:T(8,128)(2,1)S(1)}, bf16[512,128]{1,0:T(8,128)(2,1)S(1)}, u32[]{:S(2)}, u32[]{:S(2)}) collective-permute-start(bf16[512,128]{1,0:T(8,128)(2,1)S(1)} %ssm_total.2), channel_id=1, source_target_pairs={{0,16},{4,20},{8,24},{12,28},{1,17},{5,21},{9,25},{13,29},{2,18},{... | collective-permute-start | bytes 393224 | tf_op jit(solution)/shard_map/ppermute | solution.py:291
  21.4 2.1 %collective-permute-start.4 = (bf16[1,1040,128]{2,1,0:T(8,128)(2,1)S(1)}, bf16[1,1040,128]{2,1,0:T(8,128)(2,1)S(1)}, u32[]{:S(2)}, u32[]{:S(2)}) collective-permute-start(bf16[1,1040,128]{2,1,0:T(8,128)(2,1)S(1)} %get-tuple-element.150), channel_id=1, source_target_pairs={{0,16},{4,20},{8,24},{12,28},{16,0},{20,4},{24,8},{28,12},{1,17},{... | collective-permute-start | bytes 798728 | tf_op jit(solution)/shard_map/ppermute | solution.py:284
  24.9 4.2 %collective-permute-start.6 = (bf16[512,128]{1,0:T(8,128)(2,1)S(1)}, bf16[512,128]{1,0:T(8,128)(2,1)S(1)}, u32[]{:S(2)}, u32[]{:S(2)}) collective-permute-start(bf16[512,128]{1,0:T(8,128)(2,1)S(1)} %get-tuple-element.157), channel_id=1, source_target_pairs={{0,8},{4,12},{8,0},{12,4},{16,24},{20,28},{24,16},{28,20},{1,9},{5... | collective-permute-start | bytes 393224 | tf_op jit(solution)/shard_map/ppermute | solution.py:284
  29.3 4.6 %collective-permute-done.6.refs_11_ = bf16[512,128]{1,0:T(8,128)(2,1)S(1)} collective-permute-done((bf16[512,128]{1,0:T(8,128)(2,1)S(1)}, bf16[512,128]{1,0:T(8,128)(2,1)S(1)}, u32[]{:S(2)}, u32[]{:S(2)}) %collective-permute-start.6) | collective-permute-done | bytes 131104 | tf_op jit(solution)/shard_map/ppermute | solution.py:284
  36.6 2.4 %collective-permute-start.9 = (bf16[1,1040,128]{2,1,0:T(8,128)(2,1)S(1)}, bf16[1,1040,128]{2,1,0:T(8,128)(2,1)}, u32[]{:S(2)}, u32[]{:S(2)}) collective-permute-start(bf16[1,1040,128]{2,1,0:T(8,128)(2,1)S(1)} %get-tuple-element.175), channel_id=1, source_target_pairs={{0,24},{4,28},{8,16},{12,20},{16,8},{20,12},{24,0},{28,4},{1,25},{... | collective-permute-start | bytes 798728 | tf_op jit(solution)/shard_map/ppermute | solution.py:284
  39.0 6.0 %ssm_mix.1 = (f32[256,2048]{1,0:T(8,128)}, f32[8,256]{1,0:T(8,128)}, bf16[2048,128]{1,0:T(8,128)(2,1)}) custom-call(s32[1]{0:T(128)} %bitcast.refs_0_.me_ref, bf16[256,2048]{1,0:T(8,128)(2,1)} %refs_2_.3, bf16[256,2048]{1,0:T(8,128)(2,1)} %refs_3_.6, bf16[256,2048]{1,0:T(8,128)(2,1)} %refs_4_.5, bf16[256,128]{1,0:T(8,128)(2,1)} %refs_3_.7, ...), custom_call_target="tpu_custom_call" | custom-call | bytes 6464516 | tf_op jit(solution)/shard_map/ssm_mix/pallas_call | solution.py:28
  44.9 17.5 %psum.21.refs_1_ = f32[8,256]{1,0:T(8,128)} all-reduce(f32[8,256]{1,0:T(8,128)} %get-tuple-element.168), channel_id=1, replica_groups=mesh['ctx'=8,'head'=4] {'head'}, use_global_device_ids=true, to_apply=%region_0.1 | all-reduce | flops 2048 | bytes 16384 | tf_op jit(solution)/shard_map/psum | solution.py:602
  62.5 5.9 %ssm_gate.1 = (bf16[256,2048]{1,0:T(8,128)(2,1)}, bf16[256,2048]{1,0:T(8,128)(2,1)}, bf16[256,2048]{1,0:T(8,128)(2,1)}, bf16[512,128]{1,0:T(8,128)(2,1)}, bf16[5...) custom-call(s32[1]{0:T(128)} %bitcast.refs_0_.me_ref, f32[8,256]{1,0:T(8,128)} %psum.21.refs_1_, ...), custom_call_target="tpu_custom_call" | custom-call | bytes 7955460 | tf_op jit(solution)/shard_map/ssm_gate/pallas_call | solution.py:28
  69.5 1.6 collective-permute-start.13
  73.8 2.2 %collective-permute-done.13.refs_8_.refs_9_ = bf16[512,128]{1,0:T(8,128)(2,1)S(1)} collective-permute-done((bf16[512,128]{1,0:T(8,128)(2,1)}, bf16[512,128]{1,0:T(8,128)(2,1)S(1)}, u32[]{:S(2)}, u32[]{:S(2)}) %collective-permute-start.13) | collective-permute-done | bytes 131104 | tf_op jit(solution)/shard_map/ppermute | solution.py:284
  76.1 1.6 %collective-permute-start.15 = (bf16[1,1040,128]{2,1,0:T(8,128)(2,1)S(1)}, bf16[1,1040,128]{2,1,0:T(8,128)(2,1)S(1)}, u32[]{:S(2)}, u32[]{:S(2)}) collective-permute-start(bf16[1,1040,128]{2,1,0:T(8,128)(2,1)S(1)} %get-tuple-element.197), channel_id=1, source_target_pairs={{0,8},{4,12},{8,0},{12,4},{16,24},{20,28},{24,16},{28,20},{1,9},{5... | collective-permute-start | bytes 798728 | tf_op jit(solution)/shard_map/ppermute | solution.py:284
  78.3 4.9 %ssm_inner.1 = (f32[256,2048]{1,0:T(8,128)}, f32[256,128]{1,0:T(8,128)}, f32[256,128]{1,0:T(8,128)}) custom-call(s32[1]{0:T(128)} %bitcast.refs_0_.me_ref, bf16[256,2048]{1,0:T(8,128)(2,1)} %get-tuple-element.189.dmixed_ref, bf16[256,2048]{1,0:T(8,128)(2,1)} %refs_2_.3, bf16[256,128]{1,0:T(8,128)(2,1)} %refs_3_.7, bf16[256,128]{1,0:T(8,128)(2,1)} %r_ref.1, ...), custom_call_target="tpu_custom_call" | custom-call | bytes 5145604 | tf_op jit(solution)/shard_map/ssm_inner/pallas_call | solution.py:28
  86.3 5.2 %collective-permute-done.16.refs_4_ = bf16[1,1040,128]{2,1,0:T(8,128)(2,1)S(1)} collective-permute-done((bf16[1,1040,128]{2,1,0:T(8,128)(2,1)S(1)}, bf16[1,1040,128]{2,1,0:T(8,128)(2,1)S(1)}, u32[]{:S(2)}, u32[]{:S(2)}) %collective-permute-start.16) | collective-permute-done | bytes 266272 | tf_op jit(solution)/shard_map/ppermute | solution.py:284
  92.2 14.7 %att_attend.1 = (bf16[1,1024,128]{2,1,0:T(8,128)(2,1)}, bf16[1,1024,128]{2,1,0:T(8,128)(2,1)}, bf16[1,1024,128]{2,1,0:T(8,128)(2,1)}, bf16[1,1024,128]{2,1,0:T(8...) custom-call(s32[1]{0:T(128)} %bitcast.refs_0_.me_ref, ...), custom_call_target="tpu_custom_call" | custom-call | flops 3221225472 | bytes 4227076 | tf_op jit(solution)/shard_map/att_attend/pallas_call | solution.py:28
  107.9 1.6 collective-permute-start.18
  110.6 2.2 %collective-permute-start.24 = (bf16[1,1024,128]{2,1,0:T(8,128)(2,1)}, bf16[1,1024,128]{2,1,0:T(8,128)(2,1)S(1)}, u32[]{:S(2)}, u32[]{:S(2)}) collective-permute-start(bf16[1,1024,128]{2,1,0:T(8,128)(2,1)} %get-tuple-element.235), channel_id=1, source_target_pairs={{0,16},{4,20},{8,24},{12,28},{16,0},{20,4},{24,8},{28,12},{1,17},{... | collective-permute-start | bytes 786440 | tf_op jit(solution)/shard_map/ppermute | solution.py:284
  114.4 3.8 %collective-permute-start.21 = (bf16[1,1024,128]{2,1,0:T(8,128)(2,1)}, bf16[1,1024,128]{2,1,0:T(8,128)(2,1)S(1)}, u32[]{:S(2)}, u32[]{:S(2)}) collective-permute-start(bf16[1,1024,128]{2,1,0:T(8,128)(2,1)} %get-tuple-element.232), channel_id=1, source_target_pairs={{0,4},{4,0},{8,12},{12,8},{16,20},{20,16},{24,28},{28,24},{1,5},{5... | collective-permute-start | bytes 786440 | tf_op jit(solution)/shard_map/ppermute | solution.py:284
  120.2 5.3 %collective-permute-start.26 = (bf16[1,1024,128]{2,1,0:T(8,128)(2,1)}, bf16[1,1024,128]{2,1,0:T(8,128)(2,1)S(1)}, u32[]{:S(2)}, u32[]{:S(2)}) collective-permute-start(bf16[1,1024,128]{2,1,0:T(8,128)(2,1)} %get-tuple-element.237), channel_id=1, source_target_pairs={{0,24},{4,28},{8,16},{12,20},{16,8},{20,12},{24,0},{28,4},{1,25},{... | collective-permute-start | bytes 786440 | tf_op jit(solution)/shard_map/ppermute | solution.py:284
  126.0 4.2 %ssm_last.1 = (bf16[256,2048]{1,0:T(8,128)(2,1)}, f32[256,128]{1,0:T(8,128)}) custom-call(s32[1]{0:T(128)} %bitcast.refs_0_.me_ref, f32[256,2048]{1,0:T(8,128)} %get-tuple-element.240.refs_1_, bf16[256,2048]{1,0:T(8,128)(2,1)} %refs_2_.3, bf16[256,128]{1,0:T(8,128)(2,1)} %refs_3_.7, s32[1,256]{1,0:T(1,128)} %bitcast.10, ...), custom_call_target="tpu_custom_call" | custom-call | bytes 5063684 | tf_op jit(solution)/shard_map/ssm_last/pallas_call | solution.py:28
  130.2 26.8 %all-reduce.3 = (bf16[256,128]{1,0:T(8,128)(2,1)}, bf16[256,128]{1,0:T(8,128)(2,1)}) all-reduce(f32[256,128]{1,0:T(8,128)} %get-tuple-element.248, f32[256,128]{1,0:T(8,128)S(1)} %copy-done.17), channel_id=1, replica_groups=mesh['ctx'=8,'head'=4] {'head'}, use_global_device_ids=true, to_apply=%region_1.2 | all-reduce | flops 65536 | bytes 393216 | tf_op jit(solution)/shard_map/psum | solution.py:666
  157.0 1.9 %att_unpack.1 = (bf16[256,1024]{1,0:T(8,128)(2,1)}, bf16[256,1024]{1,0:T(8,128)(2,1)}, bf16[256,1024]{1,0:T(8,128)(2,1)}, bf16[256,1024]{1,0:T(8,128)(2,1)}) custom-call(s32[1]{0:T(128)} %bitcast.refs_0_.me_ref, bf16[1,1024,128]{2,1,0:T(8,128)(2,1)S(1)} %copy-done.7, bf16[1,1024,128]{2,1,0:T(8,128)(2,1)S(1)} %collective-permute-done.21.refs_1_, ...), custom_call_target="tpu_custom_call" | custom-call | bytes 4194308 | tf_op jit(solution)/shard_map/att_unpack/pallas_call | solution.py:28
  (98 shorter events, 26.8 us)
Async XLA Ops:
  3.8 5.6 %collective-permute-start = (bf16[528,128]{1,0:T(8,128)(2,1)}, bf16[528,128]{1,0:T(8,128)(2,1)S(1)}, u32[]{:S(2)}, u32[]{:S(2)}) collective-permute-start(bf16[528,128]{1,0:T(8,128)(2,1)} %get-tuple-element.134), channel_id=1, source_target_pairs={{0,4},{4,0},{8,12},{12,8},{16,20},{20,16},{24,28},{28,24},{1,5},{5... | collective-permute-start | bytes 405512 | tf_op jit(solution)/shard_map/ppermute | solution.py:284
  7.1 5.9 %collective-permute-start.2 = (bf16[528,128]{1,0:T(8,128)(2,1)}, bf16[528,128]{1,0:T(8,128)(2,1)S(1)}, u32[]{:S(2)}, u32[]{:S(2)}) collective-permute-start(bf16[528,128]{1,0:T(8,128)(2,1)} %get-tuple-element.136), channel_id=1, source_target_pairs={{0,12},{4,8},{8,4},{12,0},{16,28},{20,24},{24,20},{28,16},{1,13},{... | collective-permute-start | bytes 405512 | tf_op jit(solution)/shard_map/ppermute | solution.py:284
  14.1 7.3 %collective-permute-start.3 = (bf16[512,128]{1,0:T(8,128)(2,1)S(1)}, bf16[512,128]{1,0:T(8,128)(2,1)S(1)}, u32[]{:S(2)}, u32[]{:S(2)}) collective-permute-start(bf16[512,128]{1,0:T(8,128)(2,1)S(1)} %ssm_total.2), channel_id=1, source_target_pairs={{0,16},{4,20},{8,24},{12,28},{1,17},{5,21},{9,25},{13,29},{2,18},{... | collective-permute-start | bytes 393224 | tf_op jit(solution)/shard_map/ppermute | solution.py:291
  21.4 14.0 %collective-permute-start.4 = (bf16[1,1040,128]{2,1,0:T(8,128)(2,1)S(1)}, bf16[1,1040,128]{2,1,0:T(8,128)(2,1)S(1)}, u32[]{:S(2)}, u32[]{:S(2)}) collective-permute-start(bf16[1,1040,128]{2,1,0:T(8,128)(2,1)S(1)} %get-tuple-element.150), channel_id=1, source_target_pairs={{0,16},{4,20},{8,24},{12,28},{16,0},{20,4},{24,8},{28,12},{1,17},{... | collective-permute-start | bytes 798728 | tf_op jit(solution)/shard_map/ppermute | solution.py:284
  24.3 5.0 %collective-permute-start.5 = (bf16[512,128]{1,0:T(8,128)(2,1)S(1)}, bf16[512,128]{1,0:T(8,128)(2,1)S(1)}, u32[]{:S(2)}, u32[]{:S(2)}) collective-permute-start(bf16[512,128]{1,0:T(8,128)(2,1)S(1)} %get-tuple-element.156), channel_id=1, source_target_pairs={{0,4},{4,0},{8,12},{12,8},{16,20},{20,16},{24,28},{28,24},{1,5},{5... | collective-permute-start | bytes 393224 | tf_op jit(solution)/shard_map/ppermute | solution.py:284
  24.9 9.0 %collective-permute-start.6 = (bf16[512,128]{1,0:T(8,128)(2,1)S(1)}, bf16[512,128]{1,0:T(8,128)(2,1)S(1)}, u32[]{:S(2)}, u32[]{:S(2)}) collective-permute-start(bf16[512,128]{1,0:T(8,128)(2,1)S(1)} %get-tuple-element.157), channel_id=1, source_target_pairs={{0,8},{4,12},{8,0},{12,4},{16,24},{20,28},{24,16},{28,20},{1,9},{5... | collective-permute-start | bytes 393224 | tf_op jit(solution)/shard_map/ppermute | solution.py:284
  29.1 6.3 %collective-permute-start.7 = (bf16[512,128]{1,0:T(8,128)(2,1)S(1)}, bf16[512,128]{1,0:T(8,128)(2,1)S(1)}, u32[]{:S(2)}, u32[]{:S(2)}) collective-permute-start(bf16[512,128]{1,0:T(8,128)(2,1)S(1)} %get-tuple-element.158), channel_id=1, source_target_pairs={{0,12},{4,8},{8,4},{12,0},{16,28},{20,24},{24,20},{28,16},{1,13},{... | collective-permute-start | bytes 393224 | tf_op jit(solution)/shard_map/ppermute | solution.py:284
  35.4 33.0 %collective-permute-start.10 = (bf16[1,1040,128]{2,1,0:T(8,128)(2,1)S(1)}, bf16[1,1040,128]{2,1,0:T(8,128)(2,1)S(1)}, u32[]{:S(2)}, u32[]{:S(2)}) collective-permute-start(bf16[1,1040,128]{2,1,0:T(8,128)(2,1)S(1)} %get-tuple-element.171), channel_id=1, source_target_pairs={{0,4},{4,0},{8,12},{12,8},{16,20},{20,16},{24,28},{28,24},{1,5},{5... | collective-permute-start | bytes 798728 | tf_op jit(solution)/shard_map/ppermute | solution.py:284
  36.6 31.8 %collective-permute-start.8 = (bf16[1,1040,128]{2,1,0:T(8,128)(2,1)S(1)}, bf16[1,1040,128]{2,1,0:T(8,128)(2,1)S(1)}, u32[]{:S(2)}, u32[]{:S(2)}) collective-permute-start(bf16[1,1040,128]{2,1,0:T(8,128)(2,1)S(1)} %get-tuple-element.174), channel_id=1, source_target_pairs={{0,20},{4,16},{8,28},{12,24},{16,4},{20,0},{24,12},{28,8},{1,21},{... | collective-permute-start | bytes 798728 | tf_op jit(solution)/shard_map/ppermute | solution.py:284
  36.6 31.8 %collective-permute-start.9 = (bf16[1,1040,128]{2,1,0:T(8,128)(2,1)S(1)}, bf16[1,1040,128]{2,1,0:T(8,128)(2,1)}, u32[]{:S(2)}, u32[]{:S(2)}) collective-permute-start(bf16[1,1040,128]{2,1,0:T(8,128)(2,1)S(1)} %get-tuple-element.175), channel_id=1, source_target_pairs={{0,24},{4,28},{8,16},{12,20},{16,8},{20,12},{24,0},{28,4},{1,25},{... | collective-permute-start | bytes 798728 | tf_op jit(solution)/shard_map/ppermute | solution.py:284
  69.5 6.6 %collective-permute-start.13 = (bf16[512,128]{1,0:T(8,128)(2,1)}, bf16[512,128]{1,0:T(8,128)(2,1)S(1)}, u32[]{:S(2)}, u32[]{:S(2)}) collective-permute-start(bf16[512,128]{1,0:T(8,128)(2,1)} %get-tuple-element.184), channel_id=1, source_target_pairs={{0,12},{4,8},{8,4},{12,0},{16,28},{20,24},{24,20},{28,16},{1,13},{... | collective-permute-start | bytes 393224 | tf_op jit(solution)/shard_map/ppermute | solution.py:284
  71.1 13.8 %collective-permute-start.17 = (bf16[1,1040,128]{2,1,0:T(8,128)(2,1)S(1)}, bf16[1,1040,128]{2,1,0:T(8,128)(2,1)S(1)}, u32[]{:S(2)}, u32[]{:S(2)}) collective-permute-start(bf16[1,1040,128]{2,1,0:T(8,128)(2,1)S(1)} %get-tuple-element.176), channel_id=1, source_target_pairs={{0,28},{4,24},{8,20},{12,16},{16,12},{20,8},{24,4},{28,0},{1,29},{... | collective-permute-start | bytes 798728 | tf_op jit(solution)/shard_map/ppermute | solution.py:284
  76.1 10.2 %collective-permute-start.15 = (bf16[1,1040,128]{2,1,0:T(8,128)(2,1)S(1)}, bf16[1,1040,128]{2,1,0:T(8,128)(2,1)S(1)}, u32[]{:S(2)}, u32[]{:S(2)}) collective-permute-start(bf16[1,1040,128]{2,1,0:T(8,128)(2,1)S(1)} %get-tuple-element.197), channel_id=1, source_target_pairs={{0,8},{4,12},{8,0},{12,4},{16,24},{20,28},{24,16},{28,20},{1,9},{5... | collective-permute-start | bytes 798728 | tf_op jit(solution)/shard_map/ppermute | solution.py:284
  77.7 13.8 %collective-permute-start.16 = (bf16[1,1040,128]{2,1,0:T(8,128)(2,1)S(1)}, bf16[1,1040,128]{2,1,0:T(8,128)(2,1)S(1)}, u32[]{:S(2)}, u32[]{:S(2)}) collective-permute-start(bf16[1,1040,128]{2,1,0:T(8,128)(2,1)S(1)} %get-tuple-element.198), channel_id=1, source_target_pairs={{0,12},{4,8},{8,4},{12,0},{16,28},{20,24},{24,20},{28,16},{1,13},{... | collective-permute-start | bytes 798728 | tf_op jit(solution)/shard_map/ppermute | solution.py:284
  83.5 23.5 %collective-permute-start.14 = (bf16[512,128]{1,0:T(8,128)(2,1)S(1)}, bf16[512,128]{1,0:T(8,128)(2,1)S(1)}, u32[]{:S(2)}, u32[]{:S(2)}) collective-permute-start(bf16[512,128]{1,0:T(8,128)(2,1)S(1)} %ssm_total.3), channel_id=1, source_target_pairs={{16,0},{20,4},{24,8},{28,12},{17,1},{21,5},{25,9},{29,13},{18,2},{... | collective-permute-start | bytes 393224 | tf_op jit(solution)/shard_map/ppermute | solution.py:291
  107.9 4.9 %collective-permute-start.18 = (bf16[512,128]{1,0:T(8,128)(2,1)S(1)}, bf16[512,128]{1,0:T(8,128)(2,1)S(1)}, u32[]{:S(2)}, u32[]{:S(2)}) collective-permute-start(bf16[512,128]{1,0:T(8,128)(2,1)S(1)} %get-tuple-element.228), channel_id=1, source_target_pairs={{0,4},{4,0},{8,12},{12,8},{16,20},{20,16},{24,28},{28,24},{1,5},{5... | collective-permute-start | bytes 393224 | tf_op jit(solution)/shard_map/ppermute | solution.py:284
  109.4 4.9 %collective-permute-start.20 = (bf16[512,128]{1,0:T(8,128)(2,1)S(1)}, bf16[512,128]{1,0:T(8,128)(2,1)S(1)}, u32[]{:S(2)}, u32[]{:S(2)}) collective-permute-start(bf16[512,128]{1,0:T(8,128)(2,1)S(1)} %get-tuple-element.230), channel_id=1, source_target_pairs={{0,12},{4,8},{8,4},{12,0},{16,28},{20,24},{24,20},{28,16},{1,13},{... | collective-permute-start | bytes 393224 | tf_op jit(solution)/shard_map/ppermute | solution.py:284
  110.6 9.6 %collective-permute-start.24 = (bf16[1,1024,128]{2,1,0:T(8,128)(2,1)}, bf16[1,1024,128]{2,1,0:T(8,128)(2,1)S(1)}, u32[]{:S(2)}, u32[]{:S(2)}) collective-permute-start(bf16[1,1024,128]{2,1,0:T(8,128)(2,1)} %get-tuple-element.235), channel_id=1, source_target_pairs={{0,16},{4,20},{8,24},{12,28},{16,0},{20,4},{24,8},{28,12},{1,17},{... | collective-permute-start | bytes 786440 | tf_op jit(solution)/shard_map/ppermute | solution.py:284
  114.4 11.1 %collective-permute-start.21 = (bf16[1,1024,128]{2,1,0:T(8,128)(2,1)}, bf16[1,1024,128]{2,1,0:T(8,128)(2,1)S(1)}, u32[]{:S(2)}, u32[]{:S(2)}) collective-permute-start(bf16[1,1024,128]{2,1,0:T(8,128)(2,1)} %get-tuple-element.232), channel_id=1, source_target_pairs={{0,4},{4,0},{8,12},{12,8},{16,20},{20,16},{24,28},{28,24},{1,5},{5... | collective-permute-start | bytes 786440 | tf_op jit(solution)/shard_map/ppermute | solution.py:284
  118.1 38.8 %collective-permute-start.22 = (bf16[1,1024,128]{2,1,0:T(8,128)(2,1)}, bf16[1,1024,128]{2,1,0:T(8,128)(2,1)S(1)}, u32[]{:S(2)}, u32[]{:S(2)}) collective-permute-start(bf16[1,1024,128]{2,1,0:T(8,128)(2,1)} %get-tuple-element.233), channel_id=1, source_target_pairs={{0,8},{4,12},{8,0},{12,4},{16,24},{20,28},{24,16},{28,20},{1,9},{5... | collective-permute-start | bytes 786440 | tf_op jit(solution)/shard_map/ppermute | solution.py:284
  118.1 38.8 %collective-permute-start.23 = (bf16[1,1024,128]{2,1,0:T(8,128)(2,1)}, bf16[1,1024,128]{2,1,0:T(8,128)(2,1)S(1)}, u32[]{:S(2)}, u32[]{:S(2)}) collective-permute-start(bf16[1,1024,128]{2,1,0:T(8,128)(2,1)} %get-tuple-element.234), channel_id=1, source_target_pairs={{0,12},{4,8},{8,4},{12,0},{16,28},{20,24},{24,20},{28,16},{1,13},{... | collective-permute-start | bytes 786440 | tf_op jit(solution)/shard_map/ppermute | solution.py:284
  119.3 37.7 %collective-permute-start.25 = (bf16[1,1024,128]{2,1,0:T(8,128)(2,1)}, bf16[1,1024,128]{2,1,0:T(8,128)(2,1)S(1)}, u32[]{:S(2)}, u32[]{:S(2)}) collective-permute-start(bf16[1,1024,128]{2,1,0:T(8,128)(2,1)} %get-tuple-element.236), channel_id=1, source_target_pairs={{0,20},{4,16},{8,28},{12,24},{16,4},{20,0},{24,12},{28,8},{1,21},{... | collective-permute-start | bytes 786440 | tf_op jit(solution)/shard_map/ppermute | solution.py:284
  120.2 36.8 %collective-permute-start.26 = (bf16[1,1024,128]{2,1,0:T(8,128)(2,1)}, bf16[1,1024,128]{2,1,0:T(8,128)(2,1)S(1)}, u32[]{:S(2)}, u32[]{:S(2)}) collective-permute-start(bf16[1,1024,128]{2,1,0:T(8,128)(2,1)} %get-tuple-element.237), channel_id=1, source_target_pairs={{0,24},{4,28},{8,16},{12,20},{16,8},{20,12},{24,0},{28,4},{1,25},{... | collective-permute-start | bytes 786440 | tf_op jit(solution)/shard_map/ppermute | solution.py:284
  125.5 31.5 %collective-permute-start.27 = (bf16[1,1024,128]{2,1,0:T(8,128)(2,1)}, bf16[1,1024,128]{2,1,0:T(8,128)(2,1)S(1)}, u32[]{:S(2)}, u32[]{:S(2)}) collective-permute-start(bf16[1,1024,128]{2,1,0:T(8,128)(2,1)} %get-tuple-element.238), channel_id=1, source_target_pairs={{0,28},{4,24},{8,20},{12,16},{16,12},{20,8},{24,4},{28,0},{1,29},{... | collective-permute-start | bytes 786440 | tf_op jit(solution)/shard_map/ppermute | solution.py:284
  (28 other events, 284.8 us)

commit v10 on v8

--- a/solution.py
+++ b/solution.py
@@ -364,10 +364,9 @@
                 top = new
                 tops.append(new)
             out = jnp.zeros((ATT_DIM, length), F32)
+            factors = [jnp.exp2((tops[j] - top) * rate) / total for j in range(i + 1)]
             for j in range(i + 1):
-                probs = expo_ref[j] * (jnp.exp2((tops[j] - top) * rate) / total)
-                expo_ref[j] = probs
-                weights = probs.astype(BF16)
+                weights = (expo_ref[j] * factors[j]).astype(BF16)
                 dvalue = dot(weights, grads)
                 dv_ref[j] = dvalue if j == i else dv_ref[j] + dvalue
                 out = out + dot(vt_ref[j], weights)
@@ -375,7 +374,7 @@
             dquery = jnp.zeros((ATT_DIM, length), F32)
             for j in range(i + 1):
                 dprobs = dot_nt(piece(j, 2), grads)
-                dscore = (expo_ref[j] * ((dprobs - delta) * scale)).astype(BF16)
+                dscore = (expo_ref[j] * ((dprobs - delta) * (factors[j] * scale))).astype(BF16)
                 dkey = dot(dscore, queries)
                 dk_ref[j] = dkey if j == i else dk_ref[j] + dkey
                 dquery = dquery + dot(kt_ref[j], dscore)

time: 155 us -> 155 us (level)
  no operation moved by 1% of the time
where the time goes in v10:
time: 155 us; the launch traced here: 154 us
  starting transfers between devices  56.3 us (36%)
  Pallas kernels  41.9 us (27%)
  waiting for transfers between devices  28.5 us (18%)
  blocking collectives  21.6 us (14%)
  local copies, waits for them, and re-layouts  4.36 us (3%)
    ppermute x26, starting transfers between devices, pass_block(): lax.ppermute(block, 'ctx', [(i, i ^ n) for i in range(lax.axis_size('ctx'...  52.6 us
    pallas_call x12, Pallas kernels, call(): pl.pallas_call(kernel, out_shape=out_shape, in_specs=specs or [VMEM] * le...  41.9 us
    ppermute x26, waiting for transfers between devices, pass_block(): lax.ppermute(block, 'ctx', [(i, i ^ n) for i in range(lax.axis_size('ctx'...  24.6 us
    psum x1, blocking collectives, body(): write_sum, read_sum = lax.psum((write_part, read_part), 'head')  15 us
    psum x1, blocking collectives, body(): sums = lax.psum(sums, 'head')  6.65 us
    unnamed x44, local copies, waits for them, and re-layouts  4.36 us
    ppermute x2, waiting for transfers between devices, cross(): return lax.ppermute(total, 'ctx', pairs)  3.85 us
    ppermute x2, starting transfers between devices, cross(): return lax.ppermute(total, 'ctx', pairs)  3.75 us
  transfers between devices with their start and end apart: 28, of which 13 were waited for; matrix products, arithmetic and copies ran while one was open for 0% of the time, Pallas kernels for 24%

profile of v10, /device:TPU:20, one launch (start us, length us, event | category | flops | bytes accessed | tf_op | source)
XLA Modules:
  0.0 154.3 jit_solution(8614253016462162793)
XLA Ops:
  0.7 3.1 %ssm_first.1 = (f32[256,16]{1,0:T(8,128)}, f32[16,256]{1,0:T(8,128)}, bf16[528,128]{1,0:T(8,128)(2,1)}, bf16[528,128]{1,0:T(8,128)(2,1)}, bf16[528,128]{1,0:T(8,128)(2,1)}, /*index=5*/bf16[528,128]{1,0:T(8,128)(2,1)}) custom-call(s32[1]{0:T(128)} %bitcast.refs_0_.me_ref, f32[16,256]{1,0:T(8,128)} %bitcast.11, s32[1,256]{1,0:T(1,128)} %bitcast.5, ...), custom_call_target="tpu_custom_call" | custom-call | bytes 1704964 | tf_op jit(solution)/shard_map/ssm_first/pallas_call | solution.py:28
  9.3 2.7 %collective-permute-done.1.refs_3_.refs_4_ = bf16[528,128]{1,0:T(8,128)(2,1)S(1)} collective-permute-done((bf16[528,128]{1,0:T(8,128)(2,1)}, bf16[528,128]{1,0:T(8,128)(2,1)S(1)}, u32[]{:S(2)}, u32[]{:S(2)}) %collective-permute-start.1) | collective-permute-done | bytes 135200 | tf_op jit(solution)/shard_map/ppermute | solution.py:284
  18.4 3.9 %collective-permute-done.3.refs_1_ = bf16[512,128]{1,0:T(8,128)(2,1)S(1)} collective-permute-done((bf16[512,128]{1,0:T(8,128)(2,1)S(1)}, bf16[512,128]{1,0:T(8,128)(2,1)S(1)}, u32[]{:S(2)}, u32[]{:S(2)}) %collective-permute-start.3) | collective-permute-done | bytes 131104 | tf_op jit(solution)/shard_map/ppermute | solution.py:291
  25.2 9.0 %collective-permute-start.6 = (bf16[512,128]{1,0:T(8,128)(2,1)S(1)}, bf16[512,128]{1,0:T(8,128)(2,1)S(1)}, u32[]{:S(2)}, u32[]{:S(2)}) collective-permute-start(bf16[512,128]{1,0:T(8,128)(2,1)S(1)} %get-tuple-element.135), channel_id=1, source_target_pairs={{0,8},{4,12},{8,0},{12,4},{16,24},{20,28},{24,16},{28,20},{1,9},{5... | collective-permute-start | bytes 393224 | tf_op jit(solution)/shard_map/ppermute | solution.py:284
  35.4 5.9 %collective-permute-start.9 = (bf16[1,1040,128]{2,1,0:T(8,128)(2,1)S(1)}, bf16[1,1040,128]{2,1,0:T(8,128)(2,1)S(1)}, u32[]{:S(2)}, u32[]{:S(2)}) collective-permute-start(bf16[1,1040,128]{2,1,0:T(8,128)(2,1)S(1)} %get-tuple-element.145), channel_id=1, source_target_pairs={{0,8},{4,12},{8,0},{12,4},{16,24},{20,28},{24,16},{28,20},{1,9},{5... | collective-permute-start | bytes 798728 | tf_op jit(solution)/shard_map/ppermute | solution.py:284
  41.9 3.8 %collective-permute-start.10 = (bf16[1,1040,128]{2,1,0:T(8,128)(2,1)S(1)}, bf16[1,1040,128]{2,1,0:T(8,128)(2,1)S(1)}, u32[]{:S(2)}, u32[]{:S(2)}) collective-permute-start(bf16[1,1040,128]{2,1,0:T(8,128)(2,1)S(1)} %get-tuple-element.146), channel_id=1, source_target_pairs={{0,12},{4,8},{8,4},{12,0},{16,28},{20,24},{24,20},{28,16},{1,13},{... | collective-permute-start | bytes 798728 | tf_op jit(solution)/shard_map/ppermute | solution.py:284
  45.9 6.7 %collective-permute-start.11 = (bf16[1,1040,128]{2,1,0:T(8,128)(2,1)S(1)}, bf16[1,1040,128]{2,1,0:T(8,128)(2,1)}, u32[]{:S(2)}, u32[]{:S(2)}) collective-permute-start(bf16[1,1040,128]{2,1,0:T(8,128)(2,1)S(1)} %get-tuple-element.147), channel_id=1, source_target_pairs={{0,20},{4,16},{8,28},{12,24},{16,4},{20,0},{24,12},{28,8},{1,21},{... | collective-permute-start | bytes 798728 | tf_op jit(solution)/shard_map/ppermute | solution.py:284
  53.2 2.4 %collective-permute-start.17 = (bf16[1,1040,128]{2,1,0:T(8,128)(2,1)S(1)}, bf16[1,1040,128]{2,1,0:T(8,128)(2,1)}, u32[]{:S(2)}, u32[]{:S(2)}) collective-permute-start(bf16[1,1040,128]{2,1,0:T(8,128)(2,1)S(1)} %get-tuple-element.171), channel_id=1, source_target_pairs={{0,28},{4,24},{8,20},{12,16},{16,12},{20,8},{24,4},{28,0},{1,29},{... | collective-permute-start | bytes 798728 | tf_op jit(solution)/shard_map/ppermute | solution.py:284
  55.6 6.0 %ssm_mix.1 = (f32[256,2048]{1,0:T(8,128)}, f32[8,256]{1,0:T(8,128)}, bf16[2048,128]{1,0:T(8,128)(2,1)}) custom-call(s32[1]{0:T(128)} %bitcast.refs_0_.me_ref, bf16[256,2048]{1,0:T(8,128)(2,1)} %refs_2_.3, bf16[256,2048]{1,0:T(8,128)(2,1)} %refs_3_.6, bf16[256,2048]{1,0:T(8,128)(2,1)} %refs_4_.5, bf16[256,128]{1,0:T(8,128)(2,1)} %refs_3_.7, ...), custom_call_target="tpu_custom_call" | custom-call | bytes 6464516 | tf_op jit(solution)/shard_map/ssm_mix/pallas_call | solution.py:28
  61.5 6.7 %psum.21.refs_1_ = f32[8,256]{1,0:T(8,128)} all-reduce(f32[8,256]{1,0:T(8,128)} %get-tuple-element.141), channel_id=1, replica_groups=mesh['ctx'=8,'head'=4] {'head'}, use_global_device_ids=true, to_apply=%region_0.1 | all-reduce | flops 2048 | bytes 16384 | tf_op jit(solution)/shard_map/psum | solution.py:597
  68.2 5.9 %ssm_gate.1 = (bf16[256,2048]{1,0:T(8,128)(2,1)}, bf16[256,2048]{1,0:T(8,128)(2,1)}, bf16[256,2048]{1,0:T(8,128)(2,1)}, bf16[512,128]{1,0:T(8,128)(2,1)}, bf16[5...) custom-call(s32[1]{0:T(128)} %bitcast.refs_0_.me_ref, f32[8,256]{1,0:T(8,128)} %psum.21.refs_1_, ...), custom_call_target="tpu_custom_call" | custom-call | bytes 7955460 | tf_op jit(solution)/shard_map/ssm_gate/pallas_call | solution.py:28
  75.0 3.3 %collective-permute-start.14 = (bf16[512,128]{1,0:T(8,128)(2,1)}, bf16[512,128]{1,0:T(8,128)(2,1)S(1)}, u32[]{:S(2)}, u32[]{:S(2)}) collective-permute-start(bf16[512,128]{1,0:T(8,128)(2,1)} %get-tuple-element.155), channel_id=1, source_target_pairs={{0,8},{4,12},{8,0},{12,4},{16,24},{20,28},{24,16},{28,20},{1,9},{5... | collective-permute-start | bytes 393224 | tf_op jit(solution)/shard_map/ppermute | solution.py:284
  79.6 4.9 %ssm_inner.1 = (f32[256,2048]{1,0:T(8,128)}, f32[256,128]{1,0:T(8,128)}, f32[256,128]{1,0:T(8,128)}) custom-call(s32[1]{0:T(128)} %bitcast.refs_0_.me_ref, bf16[256,2048]{1,0:T(8,128)(2,1)} %get-tuple-element.157.dmixed_ref, bf16[256,2048]{1,0:T(8,128)(2,1)} %refs_2_.3, bf16[256,128]{1,0:T(8,128)(2,1)} %refs_3_.7, bf16[256,128]{1,0:T(8,128)(2,1)} %r_ref.1, ...), custom_call_target="tpu_custom_call" | custom-call | bytes 5145604 | tf_op jit(solution)/shard_map/ssm_inner/pallas_call | solution.py:28
  85.6 2.5 %collective-permute-start.16 = (bf16[512,128]{1,0:T(8,128)(2,1)S(1)}, bf16[512,128]{1,0:T(8,128)(2,1)S(1)}, u32[]{:S(2)}, u32[]{:S(2)}) collective-permute-start(bf16[512,128]{1,0:T(8,128)(2,1)S(1)} %ssm_total.3), channel_id=1, source_target_pairs={{16,0},{20,4},{24,8},{28,12},{17,1},{21,5},{25,9},{29,13},{18,2},{... | collective-permute-start | bytes 393224 | tf_op jit(solution)/shard_map/ppermute | solution.py:291
  88.1 14.7 %att_attend.1 = (bf16[1,1024,128]{2,1,0:T(8,128)(2,1)}, bf16[1,1024,128]{2,1,0:T(8,128)(2,1)}, bf16[1,1024,128]{2,1,0:T(8,128)(2,1)}, bf16[1,1024,128]{2,1,0:T(8...) custom-call(s32[1]{0:T(128)} %bitcast.refs_0_.me_ref, ...), custom_call_target="tpu_custom_call" | custom-call | flops 3221225472 | bytes 4227076 | tf_op jit(solution)/shard_map/att_attend/pallas_call | solution.py:28
  104.8 2.4 %collective-permute-start.20 = (bf16[512,128]{1,0:T(8,128)(2,1)S(1)}, bf16[512,128]{1,0:T(8,128)(2,1)S(1)}, u32[]{:S(2)}, u32[]{:S(2)}) collective-permute-start(bf16[512,128]{1,0:T(8,128)(2,1)S(1)} %get-tuple-element.200), channel_id=1, source_target_pairs={{0,12},{4,8},{8,4},{12,0},{16,28},{20,24},{24,20},{28,16},{1,13},{... | collective-permute-start | bytes 393224 | tf_op jit(solution)/shard_map/ppermute | solution.py:284
  110.7 3.7 %collective-permute-done.20.refs_10_ = bf16[512,128]{1,0:T(8,128)(2,1)S(1)} collective-permute-done((bf16[512,128]{1,0:T(8,128)(2,1)S(1)}, bf16[512,128]{1,0:T(8,128)(2,1)S(1)}, u32[]{:S(2)}, u32[]{:S(2)}) %collective-permute-start.20) | collective-permute-done | bytes 131104 | tf_op jit(solution)/shard_map/ppermute | solution.py:284
  115.2 2.7 %collective-permute-start.23 = (bf16[1,1024,128]{2,1,0:T(8,128)(2,1)}, bf16[1,1024,128]{2,1,0:T(8,128)(2,1)S(1)}, u32[]{:S(2)}, u32[]{:S(2)}) collective-permute-start(bf16[1,1024,128]{2,1,0:T(8,128)(2,1)} %get-tuple-element.204), channel_id=1, source_target_pairs={{0,12},{4,8},{8,4},{12,0},{16,28},{20,24},{24,20},{28,16},{1,13},{... | collective-permute-start | bytes 786440 | tf_op jit(solution)/shard_map/ppermute | solution.py:284
  117.9 5.0 %collective-permute-start.25 = (bf16[1,1024,128]{2,1,0:T(8,128)(2,1)}, bf16[1,1024,128]{2,1,0:T(8,128)(2,1)S(1)}, u32[]{:S(2)}, u32[]{:S(2)}) collective-permute-start(bf16[1,1024,128]{2,1,0:T(8,128)(2,1)} %get-tuple-element.206), channel_id=1, source_target_pairs={{0,20},{4,16},{8,28},{12,24},{16,4},{20,0},{24,12},{28,8},{1,21},{... | collective-permute-start | bytes 786440 | tf_op jit(solution)/shard_map/ppermute | solution.py:284
  123.0 4.6 %collective-permute-done.21.refs_1_ = bf16[1,1024,128]{2,1,0:T(8,128)(2,1)S(1)} collective-permute-done((bf16[1,1024,128]{2,1,0:T(8,128)(2,1)}, bf16[1,1024,128]{2,1,0:T(8,128)(2,1)S(1)}, u32[]{:S(2)}, u32[]{:S(2)}) %collective-permute-start.21) | collective-permute-done | bytes 262176 | tf_op jit(solution)/shard_map/ppermute | solution.py:284
  127.6 4.2 %ssm_last.1 = (bf16[256,2048]{1,0:T(8,128)(2,1)}, f32[256,128]{1,0:T(8,128)}) custom-call(s32[1]{0:T(128)} %bitcast.refs_0_.me_ref, f32[256,2048]{1,0:T(8,128)} %get-tuple-element.210.refs_1_, bf16[256,2048]{1,0:T(8,128)(2,1)} %refs_2_.3, bf16[256,128]{1,0:T(8,128)(2,1)} %refs_3_.7, s32[1,256]{1,0:T(1,128)} %bitcast.10, ...), custom_call_target="tpu_custom_call" | custom-call | bytes 5063684 | tf_op jit(solution)/shard_map/ssm_last/pallas_call | solution.py:28
  131.8 15.0 %all-reduce.3 = (bf16[256,128]{1,0:T(8,128)(2,1)}, bf16[256,128]{1,0:T(8,128)(2,1)}) all-reduce(f32[256,128]{1,0:T(8,128)} %get-tuple-element.218, f32[256,128]{1,0:T(8,128)S(1)} %copy-done.17), channel_id=1, replica_groups=mesh['ctx'=8,'head'=4] {'head'}, use_global_device_ids=true, to_apply=%region_1.2 | all-reduce | flops 65536 | bytes 393216 | tf_op jit(solution)/shard_map/psum | solution.py:658
  146.8 2.8 %collective-permute-done.26.refs_6_ = bf16[1,1024,128]{2,1,0:T(8,128)(2,1)S(1)} collective-permute-done((bf16[1,1024,128]{2,1,0:T(8,128)(2,1)}, bf16[1,1024,128]{2,1,0:T(8,128)(2,1)S(1)}, u32[]{:S(2)}, u32[]{:S(2)}) %collective-permute-start.26) | collective-permute-done | bytes 262176 | tf_op jit(solution)/shard_map/ppermute | solution.py:284
  149.6 2.8 %collective-permute-done.27.refs_7_ = bf16[1,1024,128]{2,1,0:T(8,128)(2,1)S(1)} collective-permute-done((bf16[1,1024,128]{2,1,0:T(8,128)(2,1)}, bf16[1,1024,128]{2,1,0:T(8,128)(2,1)S(1)}, u32[]{:S(2)}, u32[]{:S(2)}) %collective-permute-start.27) | collective-permute-done | bytes 262176 | tf_op jit(solution)/shard_map/ppermute | solution.py:284
  (94 shorter events, 29.1 us)
Async XLA Ops:
  5.3 6.7 %collective-permute-start.1 = (bf16[528,128]{1,0:T(8,128)(2,1)}, bf16[528,128]{1,0:T(8,128)(2,1)S(1)}, u32[]{:S(2)}, u32[]{:S(2)}) collective-permute-start(bf16[528,128]{1,0:T(8,128)(2,1)} %get-tuple-element.120), channel_id=1, source_target_pairs={{0,8},{4,12},{8,0},{12,4},{16,24},{20,28},{24,16},{28,20},{1,9},{5... | collective-permute-start | bytes 405512 | tf_op jit(solution)/shard_map/ppermute | solution.py:284
  14.4 7.9 %collective-permute-start.3 = (bf16[512,128]{1,0:T(8,128)(2,1)S(1)}, bf16[512,128]{1,0:T(8,128)(2,1)S(1)}, u32[]{:S(2)}, u32[]{:S(2)}) collective-permute-start(bf16[512,128]{1,0:T(8,128)(2,1)S(1)} %ssm_total.2), channel_id=1, source_target_pairs={{0,16},{4,20},{8,24},{12,28},{1,17},{5,21},{9,25},{13,29},{2,18},{... | collective-permute-start | bytes 393224 | tf_op jit(solution)/shard_map/ppermute | solution.py:291
  22.3 30.3 %collective-permute-start.4 = (bf16[1,1040,128]{2,1,0:T(8,128)(2,1)S(1)}, bf16[1,1040,128]{2,1,0:T(8,128)(2,1)S(1)}, u32[]{:S(2)}, u32[]{:S(2)}) collective-permute-start(bf16[1,1040,128]{2,1,0:T(8,128)(2,1)S(1)} %get-tuple-element.131), channel_id=1, source_target_pairs={{0,16},{4,20},{8,24},{12,28},{16,0},{20,4},{24,8},{28,12},{1,17},{... | collective-permute-start | bytes 798728 | tf_op jit(solution)/shard_map/ppermute | solution.py:284
  22.3 30.9 %collective-permute-start.8 = (bf16[1,1040,128]{2,1,0:T(8,128)(2,1)S(1)}, bf16[1,1040,128]{2,1,0:T(8,128)(2,1)S(1)}, u32[]{:S(2)}, u32[]{:S(2)}) collective-permute-start(bf16[1,1040,128]{2,1,0:T(8,128)(2,1)S(1)} %get-tuple-element.144), channel_id=1, source_target_pairs={{0,4},{4,0},{8,12},{12,8},{16,20},{20,16},{24,28},{28,24},{1,5},{5... | collective-permute-start | bytes 798728 | tf_op jit(solution)/shard_map/ppermute | solution.py:284
  24.7 10.8 %collective-permute-start.5 = (bf16[512,128]{1,0:T(8,128)(2,1)S(1)}, bf16[512,128]{1,0:T(8,128)(2,1)S(1)}, u32[]{:S(2)}, u32[]{:S(2)}) collective-permute-start(bf16[512,128]{1,0:T(8,128)(2,1)S(1)} %get-tuple-element.134), channel_id=1, source_target_pairs={{0,4},{4,0},{8,12},{12,8},{16,20},{20,16},{24,28},{28,24},{1,5},{5... | collective-permute-start | bytes 393224 | tf_op jit(solution)/shard_map/ppermute | solution.py:284
  25.2 16.7 %collective-permute-start.6 = (bf16[512,128]{1,0:T(8,128)(2,1)S(1)}, bf16[512,128]{1,0:T(8,128)(2,1)S(1)}, u32[]{:S(2)}, u32[]{:S(2)}) collective-permute-start(bf16[512,128]{1,0:T(8,128)(2,1)S(1)} %get-tuple-element.135), channel_id=1, source_target_pairs={{0,8},{4,12},{8,0},{12,4},{16,24},{20,28},{24,16},{28,20},{1,9},{5... | collective-permute-start | bytes 393224 | tf_op jit(solution)/shard_map/ppermute | solution.py:284
  34.2 11.8 %collective-permute-start.7 = (bf16[512,128]{1,0:T(8,128)(2,1)S(1)}, bf16[512,128]{1,0:T(8,128)(2,1)S(1)}, u32[]{:S(2)}, u32[]{:S(2)}) collective-permute-start(bf16[512,128]{1,0:T(8,128)(2,1)S(1)} %get-tuple-element.136), channel_id=1, source_target_pairs={{0,12},{4,8},{8,4},{12,0},{16,28},{20,24},{24,20},{28,16},{1,13},{... | collective-permute-start | bytes 393224 | tf_op jit(solution)/shard_map/ppermute | solution.py:284
  35.4 38.6 %collective-permute-start.9 = (bf16[1,1040,128]{2,1,0:T(8,128)(2,1)S(1)}, bf16[1,1040,128]{2,1,0:T(8,128)(2,1)S(1)}, u32[]{:S(2)}, u32[]{:S(2)}) collective-permute-start(bf16[1,1040,128]{2,1,0:T(8,128)(2,1)S(1)} %get-tuple-element.145), channel_id=1, source_target_pairs={{0,8},{4,12},{8,0},{12,4},{16,24},{20,28},{24,16},{28,20},{1,9},{5... | collective-permute-start | bytes 798728 | tf_op jit(solution)/shard_map/ppermute | solution.py:284
  41.9 32.2 %collective-permute-start.10 = (bf16[1,1040,128]{2,1,0:T(8,128)(2,1)S(1)}, bf16[1,1040,128]{2,1,0:T(8,128)(2,1)S(1)}, u32[]{:S(2)}, u32[]{:S(2)}) collective-permute-start(bf16[1,1040,128]{2,1,0:T(8,128)(2,1)S(1)} %get-tuple-element.146), channel_id=1, source_target_pairs={{0,12},{4,8},{8,4},{12,0},{16,28},{20,24},{24,20},{28,16},{1,13},{... | collective-permute-start | bytes 798728 | tf_op jit(solution)/shard_map/ppermute | solution.py:284
  45.9 28.2 %collective-permute-start.11 = (bf16[1,1040,128]{2,1,0:T(8,128)(2,1)S(1)}, bf16[1,1040,128]{2,1,0:T(8,128)(2,1)}, u32[]{:S(2)}, u32[]{:S(2)}) collective-permute-start(bf16[1,1040,128]{2,1,0:T(8,128)(2,1)S(1)} %get-tuple-element.147), channel_id=1, source_target_pairs={{0,20},{4,16},{8,28},{12,24},{16,4},{20,0},{24,12},{28,8},{1,21},{... | collective-permute-start | bytes 798728 | tf_op jit(solution)/shard_map/ppermute | solution.py:284
  52.6 21.5 %collective-permute-start.12 = (bf16[1,1040,128]{2,1,0:T(8,128)(2,1)S(1)}, bf16[1,1040,128]{2,1,0:T(8,128)(2,1)}, u32[]{:S(2)}, u32[]{:S(2)}) collective-permute-start(bf16[1,1040,128]{2,1,0:T(8,128)(2,1)S(1)} %get-tuple-element.148), channel_id=1, source_target_pairs={{0,24},{4,28},{8,16},{12,20},{16,8},{20,12},{24,0},{28,4},{1,25},{... | collective-permute-start | bytes 798728 | tf_op jit(solution)/shard_map/ppermute | solution.py:284
  53.2 34.9 %collective-permute-start.17 = (bf16[1,1040,128]{2,1,0:T(8,128)(2,1)S(1)}, bf16[1,1040,128]{2,1,0:T(8,128)(2,1)}, u32[]{:S(2)}, u32[]{:S(2)}) collective-permute-start(bf16[1,1040,128]{2,1,0:T(8,128)(2,1)S(1)} %get-tuple-element.171), channel_id=1, source_target_pairs={{0,28},{4,24},{8,20},{12,16},{16,12},{20,8},{24,4},{28,0},{1,29},{... | collective-permute-start | bytes 798728 | tf_op jit(solution)/shard_map/ppermute | solution.py:284
  74.1 10.4 %collective-permute-start.13 = (bf16[512,128]{1,0:T(8,128)(2,1)}, bf16[512,128]{1,0:T(8,128)(2,1)S(1)}, u32[]{:S(2)}, u32[]{:S(2)}) collective-permute-start(bf16[512,128]{1,0:T(8,128)(2,1)} %get-tuple-element.154), channel_id=1, source_target_pairs={{0,4},{4,0},{8,12},{12,8},{16,20},{20,16},{24,28},{28,24},{1,5},{5... | collective-permute-start | bytes 393224 | tf_op jit(solution)/shard_map/ppermute | solution.py:284
  75.0 9.6 %collective-permute-start.14 = (bf16[512,128]{1,0:T(8,128)(2,1)}, bf16[512,128]{1,0:T(8,128)(2,1)S(1)}, u32[]{:S(2)}, u32[]{:S(2)}) collective-permute-start(bf16[512,128]{1,0:T(8,128)(2,1)} %get-tuple-element.155), channel_id=1, source_target_pairs={{0,8},{4,12},{8,0},{12,4},{16,24},{20,28},{24,16},{28,20},{1,9},{5... | collective-permute-start | bytes 393224 | tf_op jit(solution)/shard_map/ppermute | solution.py:284
  78.2 7.2 %collective-permute-start.15 = (bf16[512,128]{1,0:T(8,128)(2,1)}, bf16[512,128]{1,0:T(8,128)(2,1)S(1)}, u32[]{:S(2)}, u32[]{:S(2)}) collective-permute-start(bf16[512,128]{1,0:T(8,128)(2,1)} %get-tuple-element.156), channel_id=1, source_target_pairs={{0,12},{4,8},{8,4},{12,0},{16,28},{20,24},{24,20},{28,16},{1,13},{... | collective-permute-start | bytes 393224 | tf_op jit(solution)/shard_map/ppermute | solution.py:284
  85.6 17.2 %collective-permute-start.16 = (bf16[512,128]{1,0:T(8,128)(2,1)S(1)}, bf16[512,128]{1,0:T(8,128)(2,1)S(1)}, u32[]{:S(2)}, u32[]{:S(2)}) collective-permute-start(bf16[512,128]{1,0:T(8,128)(2,1)S(1)} %ssm_total.3), channel_id=1, source_target_pairs={{16,0},{20,4},{24,8},{28,12},{17,1},{21,5},{25,9},{29,13},{18,2},{... | collective-permute-start | bytes 393224 | tf_op jit(solution)/shard_map/ppermute | solution.py:291
  104.8 9.6 %collective-permute-start.20 = (bf16[512,128]{1,0:T(8,128)(2,1)S(1)}, bf16[512,128]{1,0:T(8,128)(2,1)S(1)}, u32[]{:S(2)}, u32[]{:S(2)}) collective-permute-start(bf16[512,128]{1,0:T(8,128)(2,1)S(1)} %get-tuple-element.200), channel_id=1, source_target_pairs={{0,12},{4,8},{8,4},{12,0},{16,28},{20,24},{24,20},{28,16},{1,13},{... | collective-permute-start | bytes 393224 | tf_op jit(solution)/shard_map/ppermute | solution.py:284
  107.2 15.8 %collective-permute-start.24 = (bf16[1,1024,128]{2,1,0:T(8,128)(2,1)}, bf16[1,1024,128]{2,1,0:T(8,128)(2,1)S(1)}, u32[]{:S(2)}, u32[]{:S(2)}) collective-permute-start(bf16[1,1024,128]{2,1,0:T(8,128)(2,1)} %get-tuple-element.205), channel_id=1, source_target_pairs={{0,16},{4,20},{8,24},{12,28},{16,0},{20,4},{24,8},{28,12},{1,17},{... | collective-permute-start | bytes 786440 | tf_op jit(solution)/shard_map/ppermute | solution.py:284
  114.4 13.2 %collective-permute-start.21 = (bf16[1,1024,128]{2,1,0:T(8,128)(2,1)}, bf16[1,1024,128]{2,1,0:T(8,128)(2,1)S(1)}, u32[]{:S(2)}, u32[]{:S(2)}) collective-permute-start(bf16[1,1024,128]{2,1,0:T(8,128)(2,1)} %get-tuple-element.202), channel_id=1, source_target_pairs={{0,4},{4,0},{8,12},{12,8},{16,20},{20,16},{24,28},{28,24},{1,5},{5... | collective-permute-start | bytes 786440 | tf_op jit(solution)/shard_map/ppermute | solution.py:284
  115.0 31.8 %collective-permute-start.22 = (bf16[1,1024,128]{2,1,0:T(8,128)(2,1)}, bf16[1,1024,128]{2,1,0:T(8,128)(2,1)S(1)}, u32[]{:S(2)}, u32[]{:S(2)}) collective-permute-start(bf16[1,1024,128]{2,1,0:T(8,128)(2,1)} %get-tuple-element.203), channel_id=1, source_target_pairs={{0,8},{4,12},{8,0},{12,4},{16,24},{20,28},{24,16},{28,20},{1,9},{5... | collective-permute-start | bytes 786440 | tf_op jit(solution)/shard_map/ppermute | solution.py:284
  115.2 31.5 %collective-permute-start.23 = (bf16[1,1024,128]{2,1,0:T(8,128)(2,1)}, bf16[1,1024,128]{2,1,0:T(8,128)(2,1)S(1)}, u32[]{:S(2)}, u32[]{:S(2)}) collective-permute-start(bf16[1,1024,128]{2,1,0:T(8,128)(2,1)} %get-tuple-element.204), channel_id=1, source_target_pairs={{0,12},{4,8},{8,4},{12,0},{16,28},{20,24},{24,20},{28,16},{1,13},{... | collective-permute-start | bytes 786440 | tf_op jit(solution)/shard_map/ppermute | solution.py:284
  117.9 28.9 %collective-permute-start.25 = (bf16[1,1024,128]{2,1,0:T(8,128)(2,1)}, bf16[1,1024,128]{2,1,0:T(8,128)(2,1)S(1)}, u32[]{:S(2)}, u32[]{:S(2)}) collective-permute-start(bf16[1,1024,128]{2,1,0:T(8,128)(2,1)} %get-tuple-element.206), channel_id=1, source_target_pairs={{0,20},{4,16},{8,28},{12,24},{16,4},{20,0},{24,12},{28,8},{1,21},{... | collective-permute-start | bytes 786440 | tf_op jit(solution)/shard_map/ppermute | solution.py:284
  123.0 26.6 %collective-permute-start.26 = (bf16[1,1024,128]{2,1,0:T(8,128)(2,1)}, bf16[1,1024,128]{2,1,0:T(8,128)(2,1)S(1)}, u32[]{:S(2)}, u32[]{:S(2)}) collective-permute-start(bf16[1,1024,128]{2,1,0:T(8,128)(2,1)} %get-tuple-element.207), channel_id=1, source_target_pairs={{0,24},{4,28},{8,16},{12,20},{16,8},{20,12},{24,0},{28,4},{1,25},{... | collective-permute-start | bytes 786440 | tf_op jit(solution)/shard_map/ppermute | solution.py:284
  127.6 24.8 %collective-permute-start.27 = (bf16[1,1024,128]{2,1,0:T(8,128)(2,1)}, bf16[1,1024,128]{2,1,0:T(8,128)(2,1)S(1)}, u32[]{:S(2)}, u32[]{:S(2)}) collective-permute-start(bf16[1,1024,128]{2,1,0:T(8,128)(2,1)} %get-tuple-element.208), channel_id=1, source_target_pairs={{0,28},{4,24},{8,20},{12,16},{16,12},{20,8},{24,4},{28,0},{1,29},{... | collective-permute-start | bytes 786440 | tf_op jit(solution)/shard_map/ppermute | solution.py:284
  (26 other events, 300.0 us)
